TPU v7x, 32 devices: a whole 2x2x4 slice. The times are simulated.
32 devices in a mesh: stream: 2 (over core), batch: 16 (over z, y, x).
Axes of the slice: x: 2, y: 2, z: 4, core: 2. Of those that a mesh axis runs over, the one named last changes fastest.
Arguments:
- tokens: bfloat16 [2, 16384, 1152], P('stream', 'batch'), may hold values from -6 to 6
- segments: int32 [16384], P('batch'), may hold values from 0 to 63, as said below
- timesteps: int32 [64], P('batch'), may hold values from 0 to 999
- labels: int32 [64], replicated, may hold values from 0 to 999
- head_keep: int32 [64, 16], P('batch'), may hold values 0 or 1
- token_keep: int32 [2, 16384], P('stream', 'batch'), may hold values 0 or 1
- class_table: bfloat16 [1001, 1152], replicated, may hold values from -6 to 6
- w_ada: bfloat16 [1152, 6912], replicated, may hold values from -0.1875 to 0.1875
- b_ada: float32 [6912], replicated, may hold values from -3 to 3
- w_qkv: bfloat16 [1152, 3456], replicated, may hold values from -0.1875 to 0.1875
- b_qv: float32 [2304], replicated, may hold values from -2 to 2
- w_proj: bfloat16 [1152, 1152], replicated, may hold values from -2 to 2
- b_proj: float32 [1152], replicated, may hold values from -3 to 3
- w_fc1: bfloat16 [1152, 4608], replicated, may hold values from -0.1875 to 0.1875
- b_fc1: float32 [4608], replicated, may hold values from -3 to 3
- w_fc2: bfloat16 [4608, 1152], replicated, may hold values from -0.1875 to 0.1875
- b_fc2: float32 [1152], replicated, may hold values from -3 to 3
- out_grad: bfloat16 [2, 16384, 1152], P('stream', 'batch'), may hold values from -6 to 6
Outputs:
- out: bfloat16 [2, 16384, 1152], P('stream', 'batch')
- grad_tokens: float32 [2, 16384, 1152], P('stream', 'batch')
- grad_table: float32 [1001, 1152], replicated
- grad_w_ada: float32 [1152, 6912], P(('stream', 'batch'))
- grad_b_ada: float32 [6912], P(('stream', 'batch'))
- grad_w_qkv: float32 [1152, 3456], P(('stream', 'batch'))
- grad_b_qv: float32 [2304], P(('stream', 'batch'))
- grad_w_proj: float32 [1152, 1152], P(('stream', 'batch'))
- grad_b_proj: float32 [1152], P(('stream', 'batch'))
- grad_w_fc1: float32 [1152, 4608], P(('stream', 'batch'))
- grad_b_fc1: float32 [4608], P(('stream', 'batch'))
- grad_w_fc2: float32 [4608, 1152], P(('stream', 'batch'))
- grad_b_fc2: float32 [1152], P(('stream', 'batch'))
Inputs may be any that keep to these rules, and one draw needn't show every extreme that they name: `segments`: the g-th aligned group of 1024 tokens is either one image, all its tokens numbered 4 g, or four images of 256 tokens numbered 4 g, 4 g + 1, 4 g + 2, 4 g + 3 in order. The first group is four images, the second one image, and the last four images. Numbers that no token carries have timesteps, labels and head masks that nothing reads.
All inputs are finite; a program needn't handle non-finite values. No bound on the sum of `head_keep` or of `token_keep` on one device may be relied on, other than what follows from the above.
Results may differ from a plain program's by a relative error of at most 0.015.
The roundings to bfloat16 on the way count: a program that leaves them out, or rounds other values in their place, can miss the bound.
Values sent between devices are 32-bit elements; how exact they have to be, the bound alone decides.
A program may use at most 448 MiB of HBM per device.

v0:
```python
from functools import partial
import math

import jax
import jax.numpy as jnp
from jax import lax
from jax.sharding import PartitionSpec as P

SMALL_LEN = 256


NORM_EPS = 1e-06
MASKED = -1e30
HIGHEST = lax.Precision.HIGHEST
CONTRACT_ROWS = (((0,), (0,)), ((), ()))
CONTRACT_COLS = (((1,), (1,)), ((), ()))


def product(left, right):
    return jnp.dot(left, right, preferred_element_type=jnp.float32)


def product_rows(left, right):
    return lax.dot_general(left, right, CONTRACT_ROWS, preferred_element_type=jnp.float32)


def product_cols(left, right):
    return lax.dot_general(left, right, CONTRACT_COLS, preferred_element_type=jnp.float32)


def exact_rows(left, right):
    return lax.dot_general(
        left, right, CONTRACT_ROWS, precision=HIGHEST, preferred_element_type=jnp.float32
    )


def time_embed(steps_in, width):
    half_width = width // 2
    frequency = jnp.exp(-math.log(10000.0) * jnp.arange(half_width, dtype=jnp.float32) / half_width)
    angles = steps_in.astype(jnp.float32)[:, None] * frequency[None, :]
    return jnp.concatenate([jnp.cos(angles), jnp.sin(angles)], axis=1)


def layer_norm(values):
    centre = values - jnp.mean(values, axis=-1, keepdims=True)
    spread = jnp.mean(centre * centre, axis=-1, keepdims=True)
    return centre * lax.rsqrt(spread + NORM_EPS)


def modulate(values, shift_part, scale_part):
    return layer_norm(values) * (1.0 + scale_part) + shift_part


def block_scores(queries, keys, query_items, key_items):
    factor = 1.0 / math.sqrt(queries.shape[-1])
    scores = jnp.einsum("qhd,khd->hqk", queries, keys, preferred_element_type=jnp.float32) * factor
    same_item = (query_items[:, None] == key_items[None, :])[None]
    return jnp.where(same_item, scores, MASKED)


def forward_block(queries, keys, values, query_items, key_items):
    scores = block_scores(queries, keys, query_items, key_items)
    top_score = jnp.max(scores, axis=-1, keepdims=True)
    expo = jnp.exp(scores - top_score)
    total = jnp.sum(expo, axis=-1, keepdims=True)
    weights = (expo / total).astype(jnp.bfloat16)
    mixture = jnp.einsum("hqk,khd->qhd", weights, values, preferred_element_type=jnp.float32)
    return (mixture, (top_score + jnp.log(total))[..., 0])


def backward_block(queries, keys, values, query_items, key_items, grad_out, log_total):
    factor = 1.0 / math.sqrt(queries.shape[-1])
    scores = block_scores(queries, keys, query_items, key_items)
    probs = jnp.exp(scores - log_total[..., None])
    grad_probs = jnp.einsum("qhd,khd->hqk", grad_out, values, preferred_element_type=jnp.float32)
    centre = jnp.sum(grad_probs * probs, axis=-1, keepdims=True)
    grad_scores = (probs * (grad_probs - centre)).astype(jnp.bfloat16)
    grad_values = jnp.einsum(
        "hqk,qhd->khd", probs.astype(jnp.bfloat16), grad_out, preferred_element_type=jnp.float32
    )
    grad_queries = (
        jnp.einsum("hqk,khd->qhd", grad_scores, keys, preferred_element_type=jnp.float32) * factor
    )
    grad_keys = (
        jnp.einsum("hqk,qhd->khd", grad_scores, queries, preferred_element_type=jnp.float32)
        * factor
    )
    return (grad_queries, grad_keys, grad_values)


def group_forward(queries, keys, values, items):
    length = items.shape[0]
    block_rows = min(512, length)
    block_count = length // block_rows
    tail = queries.shape[1:]
    query_blocks = queries.reshape((block_count, block_rows) + tail)
    key_blocks = keys.reshape((block_count, block_rows) + tail)
    value_blocks = values.reshape((block_count, block_rows) + tail)
    item_blocks = items.reshape(block_count, block_rows)

    def whole_group(unused):
        return lax.map(
            lambda pieces: forward_block(pieces[0], keys, values, pieces[1], items),
            (query_blocks, item_blocks),
        )

    def diagonal(unused):
        return lax.map(
            lambda pieces: forward_block(*pieces),
            (query_blocks, key_blocks, value_blocks, item_blocks, item_blocks),
        )

    mixture, log_total = lax.cond(items[0] == items[length - 1], whole_group, diagonal, 0)
    return (mixture.reshape((length,) + tail), log_total)


def group_backward(queries, keys, values, items, grad_out, log_total):
    length = items.shape[0]
    block_rows = min(512, length)
    block_count = length // block_rows
    tail = queries.shape[1:]
    query_blocks = queries.reshape((block_count, block_rows) + tail)
    key_blocks = keys.reshape((block_count, block_rows) + tail)
    value_blocks = values.reshape((block_count, block_rows) + tail)
    grad_blocks = grad_out.reshape((block_count, block_rows) + tail)
    item_blocks = items.reshape(block_count, block_rows)

    def whole_group(unused):

        def per_block(carry, pieces):
            grad_query, grad_key, grad_value = backward_block(
                pieces[0], keys, values, pieces[1], items, pieces[2], pieces[3]
            )
            return ((carry[0] + grad_key, carry[1] + grad_value), grad_query)

        empty = jnp.zeros(keys.shape, jnp.float32)
        totals, grad_query = lax.scan(
            per_block, (empty, empty), (query_blocks, item_blocks, grad_blocks, log_total)
        )
        return (grad_query.reshape((length,) + tail), totals[0], totals[1])

    def diagonal(unused):
        grad_query, grad_key, grad_value = lax.map(
            lambda pieces: backward_block(*pieces),
            (
                query_blocks,
                key_blocks,
                value_blocks,
                item_blocks,
                item_blocks,
                grad_blocks,
                log_total,
            ),
        )
        return (
            grad_query.reshape((length,) + tail),
            grad_key.reshape((length,) + tail),
            grad_value.reshape((length,) + tail),
        )

    return lax.cond(items[0] == items[length - 1], whole_group, diagonal, 0)


def per_device(
    tokens,
    segments,
    timesteps,
    labels,
    head_keep,
    token_keep,
    class_table,
    w_ada,
    b_ada,
    w_qkv,
    b_qv,
    w_proj,
    b_proj,
    w_fc1,
    b_fc1,
    w_fc2,
    b_fc2,
    out_grad,
):
    width = tokens.shape[2]
    token_dev = tokens.shape[1]
    heads_count = head_keep.shape[1]
    head_width = width // heads_count
    item_dev = timesteps.shape[0]
    group_len = 4 * SMALL_LEN
    group_dev = token_dev // group_len
    null_class = class_table.shape[0] - 1
    stream_index = lax.axis_index("stream")
    batch_index = lax.axis_index("batch")
    item_start = batch_index * item_dev
    own_labels = lax.dynamic_slice_in_dim(labels, item_start, item_dev)
    used_labels = jnp.where(stream_index == 0, own_labels, null_class)
    cond = time_embed(timesteps, width) + jnp.take(class_table, used_labels, axis=0).astype(
        jnp.float32
    )
    activated = jax.nn.silu(cond).astype(jnp.bfloat16)
    modulation = product(activated, w_ada) + b_ada
    local_items = segments - item_start
    selector = (local_items[:, None] == jnp.arange(item_dev, dtype=jnp.int32)[None, :]).astype(
        jnp.float32
    )
    mod_tokens = jnp.dot(
        selector, modulation, precision=HIGHEST, preferred_element_type=jnp.float32
    )
    shift_one, scale_one, gate_one, shift_two, scale_two, gate_two = jnp.split(
        mod_tokens, 6, axis=1
    )
    head_rows = jnp.dot(
        selector,
        head_keep.astype(jnp.float32),
        precision=HIGHEST,
        preferred_element_type=jnp.float32,
    )
    head_mask = jnp.repeat(head_rows, head_width, axis=1)
    keep_mask = token_keep[0].astype(jnp.float32)[:, None]
    inputs = tokens[0].astype(jnp.float32)
    normed_one = modulate(inputs, shift_one, scale_one).astype(jnp.bfloat16)
    bias_full = jnp.concatenate([b_qv[:width], jnp.zeros((width,), jnp.float32), b_qv[width:]])
    projected = (product(normed_one, w_qkv) + bias_full).astype(jnp.bfloat16)
    split_heads = projected.reshape(group_dev, group_len, 3, heads_count, head_width)
    queries = split_heads[:, :, 0]
    keys = split_heads[:, :, 1]
    values = split_heads[:, :, 2]
    items_grouped = segments.reshape(group_dev, group_len)
    mixture, log_total = lax.map(
        lambda pieces: group_forward(*pieces), (queries, keys, values, items_grouped)
    )
    attended = (mixture.reshape(token_dev, width) * head_mask).astype(jnp.bfloat16)
    branch_one = product(attended, w_proj) + b_proj
    middle = inputs + gate_one * branch_one
    normed_two = modulate(middle, shift_two, scale_two).astype(jnp.bfloat16)
    hidden_pre = product(normed_two, w_fc1) + b_fc1
    hidden = jax.nn.gelu(hidden_pre, approximate=True).astype(jnp.bfloat16)
    branch_two = product(hidden, w_fc2) + b_fc2
    result = (middle + gate_two * keep_mask * branch_two).astype(jnp.bfloat16)
    grad_top = out_grad[0].astype(jnp.float32)
    grad_gate_two = grad_top * keep_mask * branch_two
    grad_branch_two = (grad_top * gate_two * keep_mask).astype(jnp.bfloat16)
    grad_w_fc2 = product_rows(hidden, grad_branch_two)
    grad_b_fc2 = jnp.sum(grad_branch_two.astype(jnp.float32), axis=0)
    grad_hidden = product_cols(grad_branch_two, w_fc2)
    grad_pre = jax.vjp(partial(jax.nn.gelu, approximate=True), hidden_pre)[1](grad_hidden)[
        0
    ].astype(jnp.bfloat16)
    grad_w_fc1 = product_rows(normed_two, grad_pre)
    grad_b_fc1 = jnp.sum(grad_pre.astype(jnp.float32), axis=0)
    grad_normed_two = product_cols(grad_pre, w_fc1)
    grad_middle_norm, grad_shift_two, grad_scale_two = jax.vjp(
        modulate, middle, shift_two, scale_two
    )[1](grad_normed_two)
    grad_middle = grad_top + grad_middle_norm
    grad_gate_one = grad_middle * branch_one
    grad_branch_one = (grad_middle * gate_one).astype(jnp.bfloat16)
    grad_w_proj = product_rows(attended, grad_branch_one)
    grad_b_proj = jnp.sum(grad_branch_one.astype(jnp.float32), axis=0)
    grad_attended = (product_cols(grad_branch_one, w_proj) * head_mask).astype(jnp.bfloat16)
    grad_grouped = grad_attended.reshape(group_dev, group_len, heads_count, head_width)
    grad_queries, grad_keys, grad_values = lax.map(
        lambda pieces: group_backward(*pieces),
        (queries, keys, values, items_grouped, grad_grouped, log_total),
    )
    grad_projected = (
        jnp.stack([grad_queries, grad_keys, grad_values], axis=2)
        .reshape(token_dev, 3 * width)
        .astype(jnp.bfloat16)
    )
    grad_w_qkv = product_rows(normed_one, grad_projected)
    column_sums = jnp.sum(grad_projected.astype(jnp.float32), axis=0)
    grad_b_qv = jnp.concatenate([column_sums[:width], column_sums[2 * width :]])
    grad_normed_one = product_cols(grad_projected, w_qkv)
    grad_input_norm, grad_shift_one, grad_scale_one = jax.vjp(
        modulate, inputs, shift_one, scale_one
    )[1](grad_normed_one)
    grad_tokens = grad_middle + grad_input_norm
    grad_mod_tokens = jnp.concatenate(
        [
            grad_shift_one,
            grad_scale_one,
            grad_gate_one,
            grad_shift_two,
            grad_scale_two,
            grad_gate_two,
        ],
        axis=1,
    )
    grad_modulation = exact_rows(selector, grad_mod_tokens).astype(jnp.bfloat16)
    grad_w_ada = product_rows(activated, grad_modulation)
    grad_b_ada = jnp.sum(grad_modulation.astype(jnp.float32), axis=0)
    grad_activated = product_cols(grad_modulation, w_ada)
    grad_cond = jax.vjp(jax.nn.silu, cond)[1](grad_activated)[0]
    class_index = jnp.arange(null_class + 1, dtype=jnp.int32)
    label_select = (used_labels[:, None] == class_index[None, :]).astype(jnp.float32)
    local_table = exact_rows(label_select, grad_cond)
    grad_table = lax.psum(local_table, ("stream", "batch"))
    halves = (
        lax.psum_scatter(grad_w_ada, "stream", scatter_dimension=0, tiled=True),
        lax.psum_scatter(grad_b_ada, "stream", scatter_dimension=0, tiled=True),
        lax.psum_scatter(grad_w_qkv, "stream", scatter_dimension=0, tiled=True),
        lax.psum_scatter(grad_b_qv, "stream", scatter_dimension=0, tiled=True),
        lax.psum_scatter(grad_w_proj, "stream", scatter_dimension=0, tiled=True),
        lax.psum_scatter(grad_b_proj, "stream", scatter_dimension=0, tiled=True),
        lax.psum_scatter(grad_w_fc1, "stream", scatter_dimension=0, tiled=True),
        lax.psum_scatter(grad_b_fc1, "stream", scatter_dimension=0, tiled=True),
        lax.psum_scatter(grad_w_fc2, "stream", scatter_dimension=0, tiled=True),
        lax.psum_scatter(grad_b_fc2, "stream", scatter_dimension=0, tiled=True),
    )
    shards = (
        lax.psum_scatter(halves[0], "batch", scatter_dimension=0, tiled=True),
        lax.psum_scatter(halves[1], "batch", scatter_dimension=0, tiled=True),
        lax.psum_scatter(halves[2], "batch", scatter_dimension=0, tiled=True),
        lax.psum_scatter(halves[3], "batch", scatter_dimension=0, tiled=True),
        lax.psum_scatter(halves[4], "batch", scatter_dimension=0, tiled=True),
        lax.psum_scatter(halves[5], "batch", scatter_dimension=0, tiled=True),
        lax.psum_scatter(halves[6], "batch", scatter_dimension=0, tiled=True),
        lax.psum_scatter(halves[7], "batch", scatter_dimension=0, tiled=True),
        lax.psum_scatter(halves[8], "batch", scatter_dimension=0, tiled=True),
        lax.psum_scatter(halves[9], "batch", scatter_dimension=0, tiled=True),
    )
    return (
        result[None],
        grad_tokens[None],
        grad_table,
        shards[0],
        shards[1],
        shards[2],
        shards[3],
        shards[4],
        shards[5],
        shards[6],
        shards[7],
        shards[8],
        shards[9],
    )


def solution(mesh):
    return jax.shard_map(
        per_device,
        mesh=mesh,
        in_specs=(
            P("stream", "batch", None),
            P("batch"),
            P("batch"),
            P(),
            P("batch", None),
            P("stream", "batch"),
            P(),
            P(),
            P(),
            P(),
            P(),
            P(),
            P(),
            P(),
            P(),
            P(),
            P(),
            P("stream", "batch", None),
        ),
        out_specs=(
            P("stream", "batch", None),
            P("stream", "batch", None),
            P(),
            P(("stream", "batch"), None),
            P(("stream", "batch")),
            P(("stream", "batch"), None),
            P(("stream", "batch")),
            P(("stream", "batch"), None),
            P(("stream", "batch")),
            P(("stream", "batch"), None),
            P(("stream", "batch")),
            P(("stream", "batch"), None),
            P(("stream", "batch")),
        ),
        check_vma=False,
    )
```

profile of v0, /device:TPU:0, one launch (start us, length us, event | category | flops | bytes accessed | tf_op | source)
XLA Modules:
  0.0 2088.5 jit_solution(7586704675484491546)
XLA Ops:
  24.5 7.7 convolution_add_fusion
  32.3 12.0 fusion.104
  44.3 9.3 copy-done.3
  56.6 14.6 add_convert_fusion
  71.2 10.3 copy.74
  81.6 6.6 slice_bitcast_fusion.1
  88.1 6.6 reshape.390
  94.7 6.6 reshape.389
  101.4 6.8 reshape.387
  108.2 68.8 %conditional.2 = (f32[2,512,16,72]{1,3,2,0:T(8,128)}, f32[2,16,512]{2,1,0:T(8,128)}) conditional(s32[]{:T(128)} %bitcast.27, (bf16[2,512,16,72]{1,0,3,2:T(2,128)(2,1)}, s32[2,512]{1,0:T(2,128)}, bf16[2,512,16,72]{1,0,3,2:T(2,128)(2,1)}, bf16[2,512,16,72]{1,0,3,2:T(2,128)(2,1)}) %tuple.55, (s32[2,512]{1,0:T(2,128)}, s32[1024]{0:T(1024)}, ...), branch_computations={%region_2.0_spmd, %region_7.12_spmd} | conditional | flops 2517098496 | bytes 163227984 | solution.py:113
  117.1 59.5 %while.49 = (s32[]{:T(128)}, f32[2,512,16,72]{1,3,2,0:T(8,128)}, f32[2,16,512]{2,1,0:T(8,128)}, bf16[2,512,16,72]{1,3,2,0:T(8,128)(2,1)}, s32[2,512]{1,0:T(2,128...) while((s32[]{:T(128)}, f32[2,512,16,72]{1,3,2,0:T(8,128)}, ...), condition=%wide.region_6.6_spmd, body=%wide.region_3.5_spmd.sunk | while | flops 1258545152 | bytes 57548900 | solution.py:108
  117.3 10.2 fusion.225
  127.6 9.2 fusion.226
  136.8 9.5 bitcast_dynamic-update-slice_fusion.16
  147.1 10.2 fusion.225
  157.3 9.2 fusion.226
  166.5 9.5 bitcast_dynamic-update-slice_fusion.16
  177.0 6.0 copy.79
  186.3 7.6 fusion.127
  197.3 6.6 convert_reduce_fusion.3
  204.0 20.3 fusion.133
  224.3 24.1 %fusion.121 = f32[4608,1152]{1,0:T(8,128)} fusion(bf16[1024,1152]{1,0:T(8,128)(2,1)S(1)} %get-tuple-element.528, f32[1024,4608]{1,0:T(8,128)} %fusion.133, f32[4608]{0:T(1024)S(1)} %copy-done.83), kind=kOutput, calls=%fused_computation.208 | convolution fusion | flops 10918821888 | bytes 42485760 | tf_op jit(solution)/shard_map/dot_general | solution.py:24
  248.6 30.3 %convert_reduce_fusion = (f32[4608]{0:T(1024)}, bf16[1024,4608]{1,0:T(8,128)(2,1)}) fusion(f32[1024,4608]{1,0:T(8,128)} %fusion.133, f32[4608]{0:T(1024)S(1)} %copy-done.83, bf16[1024,1152]{1,0:T(8,128)(2,1)} %copy-done.29, bf16[4608,1152]{1,0:T(8,128)(2,1)} %param.45), kind=kOutput, calls=%fused_computation.106 | convolution fusion | flops 10980159488 | bytes 41324544 | tf_op jit(solution)/shard_map/dot_general | solution.py:28
  278.9 21.8 %multiply_reduce_fusion.2 = (f32[1024]{0:T(1024)S(1)}, f32[1024,1152]{1,0:T(8,128)}) fusion(f32[1024,1152]{1,0:T(8,128)} %copy-done.8, f32[1024]{0:T(1024)S(1)} %copy-done.55, f32[1024,6912]{1,0:T(8,128)} %copy-done.3, bf16[1024,4608]{1,0:T(8,128)(2,1)} %get-tuple-element.530, bf16[1152,4608]{1,0:T(8,128)(2,1)} %param.43), kind=kOutput, calls=%fused_computation.149 | convolution fusion | flops 10877533184 | bytes 34217984 | tf_op jit(solution)/shard_map/dot_general | solution.py:28
  300.8 27.3 %convolution_add_fusion.1 = f32[1024,1152]{1,0:T(8,128)} fusion(bf16[4608,1152]{1,0:T(8,128)(2,1)} %param.45, f32[1152]{0:T(1024)S(1)} %copy-done.85, f32[1024,4608]{1,0:T(8,128)} %fusion.133, f32[4608]{0:T(1024)S(1)} %copy-done.83), kind=kOutput, calls=%fused_computation.128 | convolution fusion | flops 10920001536 | bytes 34232832 | tf_op jit(solution)/shard_map/dot_general | solution.py:20
  328.1 7.6 fusion.126
  335.7 5.7 convert_reduce_fusion.4
  351.3 6.2 copy.80
  357.5 8.0 fusion.101
  369.9 6.6 reshape.393
  376.5 334.9 %conditional.3 = (f32[1,1024,1,16,72]{1,4,3,2,0:T(8,128)}, f32[1,1024,1,16,72]{1,4,3,2,0:T(8,128)}, bf16[2,512,16,72]{1,3,2,0:T(8,128)(2,1)}) conditional(s32[]{:T(128)} %bitcast.27, (bf16[2,512,16,72]{1,0,3,2:T(2,128)(2,1)}, s32[2,512]{1,0:T(2,128)}, bf16[2,512,16,72]{1,0,3,2:T(2,128)(2,1)S(1)}, f32[2,16,512]{2,1,0:T(8,128)}, ...), branch_computations={%region_16.20_spmd, %region_20.24_spmd} | conditional | flops 6172631040 | bytes 334244288 | solution.py:161
  385.5 305.4 %while.51 = (s32[]{:T(128)}, bf16[2,512,16,72]{1,3,2,0:T(8,128)(2,1)}, f32[2,512,16,72]{1,0,3,2:T(2,128)}, f32[2,512,16,72]{1,0,3,2:T(2,128)}, bf16[2,512,16,72]...) while((s32[]{:T(128)}, ...), condition=%wide.region_19.19_spmd, body=%wide.region_17.18_spmd.sunk | while | flops 3059081216 | bytes 179610832 | solution.py:143
  386.7 11.9 subtract_exponential_fusion.5
  398.6 8.5 fusion.219
  410.9 47.4 %dynamic_update_slice.56 = f32[2,512,16,72]{1,0,3,2:T(2,128)} dynamic-update-slice(f32[2,512,16,72]{1,0,3,2:T(2,128)} %get-tuple-element.869, f32[1,512,16,72]{1,0,3,2:T(1,128)} %copy.101, s32[]{:T(128)S(6)} %copy.122, s32[]{:T(128)} %constant.171.clone..sunk, s32[]{:T(128)} %constant.171.clone..sunk, s32[]{:T(128)} %constant.171.clone..sunk) | dynamic-update-slice | bytes 4718596 | tf_op jit(solution)/shard_map/while/body/eval_jaxpr/cond/branch_0_fun/while/body/jit(dynamic_update_index_in_dim)/dynamic_update_slice | solution.py:108
  458.3 11.0 multiply_reduce_fusion.7
  469.3 11.6 multiply_convert_fusion.14
  491.0 47.2 %dynamic_update_slice.55 = f32[2,512,16,72]{1,0,3,2:T(2,128)} dynamic-update-slice(f32[2,512,16,72]{1,0,3,2:T(2,128)} %get-tuple-element.868, f32[1,512,16,72]{1,0,3,2:T(1,128)S(1)} %copy.100, s32[]{:T(128)S(6)} %copy.122, s32[]{:T(128)} %constant.171.clone..sunk, s32[]{:T(128)} %constant.171.clone..sunk, s32[]{:T(128)} %constant.171.clone..sunk) | dynamic-update-slice | bytes 4718596 | tf_op jit(solution)/shard_map/while/body/eval_jaxpr/cond/branch_0_fun/while/body/jit(dynamic_update_index_in_dim)/dynamic_update_slice | solution.py:108
  539.1 11.8 subtract_exponential_fusion.5
  550.9 8.5 fusion.219
  563.2 47.4 %dynamic_update_slice.56 = f32[2,512,16,72]{1,0,3,2:T(2,128)} dynamic-update-slice(f32[2,512,16,72]{1,0,3,2:T(2,128)} %get-tuple-element.869, f32[1,512,16,72]{1,0,3,2:T(1,128)} %copy.101, s32[]{:T(128)S(6)} %copy.122, s32[]{:T(128)} %constant.171.clone..sunk, s32[]{:T(128)} %constant.171.clone..sunk, s32[]{:T(128)} %constant.171.clone..sunk) | dynamic-update-slice | bytes 4718596 | tf_op jit(solution)/shard_map/while/body/eval_jaxpr/cond/branch_0_fun/while/body/jit(dynamic_update_index_in_dim)/dynamic_update_slice | solution.py:108
  610.6 11.0 multiply_reduce_fusion.7
  621.6 11.6 multiply_convert_fusion.14
  643.3 47.2 %dynamic_update_slice.55 = f32[2,512,16,72]{1,0,3,2:T(2,128)} dynamic-update-slice(f32[2,512,16,72]{1,0,3,2:T(2,128)} %get-tuple-element.868, f32[1,512,16,72]{1,0,3,2:T(1,128)S(1)} %copy.100, s32[]{:T(128)S(6)} %copy.122, s32[]{:T(128)} %constant.171.clone..sunk, s32[]{:T(128)} %constant.171.clone..sunk, s32[]{:T(128)} %constant.171.clone..sunk) | dynamic-update-slice | bytes 4718596 | tf_op jit(solution)/shard_map/while/body/eval_jaxpr/cond/branch_0_fun/while/body/jit(dynamic_update_index_in_dim)/dynamic_update_slice | solution.py:108
  690.8 7.4 stack.18
  698.2 7.4 stack.17
  717.0 5.5 stack.23
  730.3 11.7 fusion.135
  743.7 20.1 fusion.137
  764.0 18.1 constant_dynamic-update-slice_fusion.1
  782.2 7.4 fusion.91
  789.7 7.7 fusion.125
  797.9 8.7 multiply_dynamic-update-slice_fusion.1
  815.0 13.9 convert_reduce_fusion.5
  828.9 12.8 fusion.120
  841.8 9.7 fusion.134
  857.4 31.6 %reduce-scatter.15.cloned.1.call-done = f32[576,6912]{1,0:T(8,128)} async-done(((f32[1152,6912]{1,0:T(8,128)}), f32[576,6912]{1,0:T(8,128)}) %reduce-scatter.15.cloned.1.call-update) | async-done | bytes 15925264 | tf_op jit(solution)/shard_map/reduce_scatter | solution.py:300
  889.0 957.6 %fusion.122 = (f32[40,6912]{1,0:T(8,128)S(1)}, f32[48,3456]{1,0:T(8,128)S(1)}, f32[48,1152]{1,0:T(8,128)S(1)}, f32[40,4608]{1,0:T(8,128)S(1)}) fusion(f32[576,6912]{1,0:T(8,128)} %reduce-scatter.15.cloned.1.call-done, f32[576,3456]{1,0:T(8,128)} %reduce-scatter.17.cloned.1.call-done, f32[576,1152]{1,0:T(8,128)} %reduce-scatter.19.cloned.1.call-done, ...), kind=kCustom, calls=%all-reduce-scatter.4 | all-reduce-scatter fusion | flops 10911746 | bytes 39887360
  1880.2 14.3 collective-permute-done.6
  1903.9 101.6 %all-reduce.18 = (f32[3456]{0:T(1024)S(1)}, f32[1152]{0:T(1024)S(1)}, f32[576]{0:T(1024)S(1)}, f32[2304]{0:T(1024)S(1)}, f32[576]{0:T(1024)S(1)}) all-reduce(f32[3456]{0:T(1024)S(1)} %dynamic-slice.5, f32[1152]{0:T(1024)S(1)} %dynamic-slice.11, f32[576]{0:T(1024)S(1)} %dynamic-slice.17, ...), channel_id=5, replica_groups=mesh['stream'=2,'batch'=16] {'batch'}, use_global_device_ids=true, to_apply=%region_31.32.clone | all-reduce | flops 8064 | bytes 64512
  2010.2 8.2 concatenate.24
  2026.5 18.8 concatenate.23
  2047.3 10.9 concatenate.25
  2060.3 13.2 concatenate.22
  (321 shorter events, 179.1 us)
Async XLA Ops:
  8.0 178.3 %copy-start = (bf16[1152,1152]{1,0:T(8,128)(2,1)S(1)}, bf16[1152,1152]{1,0:T(8,128)(2,1)}, u32[]{:S(2)}) copy-start(bf16[1152,1152]{1,0:T(8,128)(2,1)} %param.41) | copy-start | bytes 7962628
  8.0 12.6 copy-start.78
  8.0 15.3 copy-start.86
  8.0 16.5 copy-start.75
  8.1 848.7 %reduce-scatter.23.cloned.1.call-start = ((), (), s32[]{:S(2)}) async-start(), calls=%async_computation.11 | async-start | bytes 31850496 | tf_op jit(solution)/shard_map/reduce_scatter | solution.py:308
  11.5 20.7 copy-start.41
  12.3 20.0 copy-start.76
  17.6 26.7 %copy-start.57 = (f32[1024]{0:T(1024)}, f32[1024]{0:T(1024)S(1)}, u32[]{:S(2)}) copy-start(f32[1024]{0:T(1024)S(1)} %broadcast_multiply_fusion.1) | copy-start | bytes 12292
  20.7 23.7 %copy-start.65 = (f32[1024]{0:T(1024)}, f32[1024]{0:T(1024)S(1)}, u32[]{:S(2)}) copy-start(f32[1024]{0:T(1024)S(1)} %fusion.116) | copy-start | bytes 12292
  32.3 21.4 %copy-start.9 = (bf16[1,1024,1152]{2,1,0:T(8,128)(2,1)S(1)}, bf16[1,1024,1152]{2,1,0:T(8,128)(2,1)}, u32[]{:S(2)}) copy-start(bf16[1,1024,1152]{2,1,0:T(8,128)(2,1)} %param.30) | copy-start | bytes 7077892
  193.9 10.0 copy-start.8
  194.0 10.0 copy-start.54
  204.0 20.4 copy-start.27
  204.0 20.4 copy-start.29
  204.0 20.3 copy-start.83
  248.5 30.4 %copy-start.55 = (f32[1024]{0:T(1024)S(1)}, f32[1024]{0:T(1024)}, u32[]{:S(2)}) copy-start(f32[1024]{0:T(1024)} %copy-done.54) | copy-start | bytes 12292
  248.5 608.8 %reduce-scatter.19.cloned.1.call-start = ((), (), s32[]{:S(2)}) async-start(), calls=%async_computation.9 | async-start | bytes 7962624 | tf_op jit(solution)/shard_map/reduce_scatter | solution.py:304
  278.9 21.8 %copy-start.72 = (f32[1024]{0:T(1024)S(1)}, f32[1024]{0:T(1024)}, u32[]{:S(2)}) copy-start(f32[1024]{0:T(1024)} %copy-done.71) | copy-start | bytes 12292
  278.9 21.8 %copy-start.85 = (f32[1152]{0:T(1024)S(1)}, f32[1152]{0:T(1024)}, u32[]{:S(2)}) copy-start(f32[1152]{0:T(1024)} %param.46) | copy-start | bytes 13828
  278.9 49.1 %slice-start = ((s8[4718592]{0:T(1024)(128)(4,1)}), s8[524288]{0:T(1024)(128)(4,1)S(1)}, s32[]{:S(2)}) async-start(s8[4718592]{0:T(1024)(128)(4,1)} %bitcast.307), calls=%async_computation.13 | async-start | bytes 1048576
  300.7 27.3 %slice-start.1 = ((s8[4718592]{0:T(1024)(128)(4,1)}), s8[4194304]{0:T(1024)(128)(4,1)S(1)}, s32[]{:S(2)}) async-start(s8[4718592]{0:T(1024)(128)(4,1)} %bitcast.307), calls=%async_computation.14 | async-start | bytes 8388608
  300.7 27.3 %copy-start.15 = (f32[1024,1152]{1,0:T(8,128)S(1)}, f32[1024,1152]{1,0:T(8,128)}, u32[]{:S(2)}) copy-start(f32[1024,1152]{1,0:T(8,128)} %get-tuple-element.574) | copy-start | bytes 14155780
  300.7 27.3 %copy-start.60 = (f32[1,1024]{1,0:T(1,128)S(1)}, f32[1,1024]{1,0:T(1,128)}, u32[]{:S(2)}) copy-start(f32[1,1024]{1,0:T(1,128)} %convert_element_type.142) | copy-start | bytes 12292
  300.8 27.3 %copy-start.63 = (f32[1024]{0:T(1024)S(1)}, f32[1024]{0:T(1024)}, u32[]{:S(2)}) copy-start(f32[1024]{0:T(1024)} %copy-done.62) | copy-start | bytes 12292
  347.6 509.7 %reduce-scatter.17.cloned.1.call-start = ((), (), s32[]{:S(2)}) async-start(), calls=%async_computation.8 | async-start | bytes 23887872 | tf_op jit(solution)/shard_map/reduce_scatter | solution.py:302
  365.5 11.0 copy-start.12
  386.7 11.9 copy-start.5
  410.9 47.4 %copy-start.6 = (bf16[2,512,16,72]{1,3,2,0:T(8,128)(2,1)S(1)}, bf16[2,512,16,72]{1,3,2,0:T(8,128)(2,1)}, u32[]{:S(2)}) copy-start(bf16[2,512,16,72]{1,3,2,0:T(8,128)(2,1)} %get-tuple-element.886) | copy-start | bytes 7077892 | tf_op jit(solution)/shard_map/while/body/eval_jaxpr/cond/branch_0_fun/while
  539.1 11.8 copy-start.5
  563.2 47.4 %copy-start.6 = (bf16[2,512,16,72]{1,3,2,0:T(8,128)(2,1)S(1)}, bf16[2,512,16,72]{1,3,2,0:T(8,128)(2,1)}, u32[]{:S(2)}) copy-start(bf16[2,512,16,72]{1,3,2,0:T(8,128)(2,1)} %get-tuple-element.886) | copy-start | bytes 7077892 | tf_op jit(solution)/shard_map/while/body/eval_jaxpr/cond/branch_0_fun/while
  742.0 115.4 %reduce-scatter.21.cloned.1.call-start = ((), (), s32[]{:S(2)}) async-start(), calls=%async_computation.10 | async-start | bytes 31850496 | tf_op jit(solution)/shard_map/reduce_scatter | solution.py:306
  763.8 18.4 copy-start.11
  763.8 18.3 copy-start.58
  763.8 18.3 copy-start.66
  763.8 125.2 %reduce-scatter.15.cloned.1.call-start = ((), (), s32[]{:S(2)}) async-start(), calls=%async_computation.7 | async-start | bytes 47775744 | tf_op jit(solution)/shard_map/reduce_scatter | solution.py:300
  782.2 15.2 slice-start.6
  789.6 17.0 slice-start.4
  789.7 19.7 slice-start.2
  797.9 11.5 slice-start.3
  815.0 13.9 copy-start.48
  815.0 13.9 copy-start.51
  815.0 13.9 copy-start.53
  815.0 13.9 copy-start.77
  841.8 9.8 copy-start.81
  841.8 1234.3 %all-reduce.23.cloned.1.call-start = ((), (), s32[]{:S(2)}) async-start(), calls=%async_computation.6 | async-start | bytes 9289728 | tf_op jit(solution)/shard_map/psum | solution.py:298
  856.7 1219.4 %reduce-scatter.25.cloned.1.call-start = ((), (), s32[]{:S(2)}) async-start(), calls=%async_computation.12 | async-start | bytes 11280384 | tf_op jit(solution)/shard_map/reduce_scatter | solution.py:320
  857.3 1015.1 %copy-start.87 = (u32[32]{0:T(128)S(1)}, u32[32]{0:T(128)}, u32[]{:S(2)}) copy-start(u32[32]{0:T(128)} %constant.212) | copy-start | bytes 388
  857.3 1018.2 %copy-start.82 = (u32[32]{0:T(128)S(1)}, u32[32]{0:T(128)}, u32[]{:S(2)}) copy-start(u32[32]{0:T(128)} %constant.208) | copy-start | bytes 388
  857.3 1042.5 %copy-start.73 = (f32[1152]{0:T(1024)S(1)}, f32[1152]{0:T(1024)}, u32[]{:S(2)}) copy-start(f32[1152]{0:T(1024)} %get-tuple-element.531) | copy-start | bytes 13828
  857.3 1042.5 %copy-start.74 = (f32[1152]{0:T(1024)S(1)}, f32[1152]{0:T(1024)}, u32[]{:S(2)}) copy-start(f32[1152]{0:T(1024)} %get-tuple-element.527) | copy-start | bytes 13828
  857.3 1042.5 %copy-start.79 = (f32[4608]{0:T(1024)S(1)}, f32[4608]{0:T(1024)}, u32[]{:S(2)}) copy-start(f32[4608]{0:T(1024)} %get-tuple-element.529) | copy-start | bytes 55300
  1846.6 19.7 collective-permute-start.8
  1848.8 21.5 %collective-permute-start.7 = (f32[48,1152]{1,0:T(8,128)S(1)}, f32[48,1152]{1,0:T(8,128)S(1)}, u32[]{:S(2)}, u32[]{:S(2)}) collective-permute-start(f32[48,1152]{1,0:T(8,128)S(1)} %get-tuple-element.525), channel_id=1, source_target_pairs={{0,2},{1,3},{2,4},{3,5},{4,6},{5,7},{6,8},{7,9},{8,10},{9,11},{10,... | collective-permute-start | bytes 663560
  1851.1 11.4 collective-permute-start.9
  1855.3 163.1 %collective-permute-start.5 = (f32[36,3456]{1,0:T(8,128)}, f32[36,3456]{1,0:T(8,128)}, u32[]{:S(2)}, u32[]{:S(2)}) collective-permute-start(f32[36,3456]{1,0:T(8,128)} %slice.59), channel_id=1, source_target_pairs={{0,4},{1,5},{2,6},{3,7},{4,8},{5,9},{6,10},{7,11},{8,12},{9,13},{1... | collective-permute-start | bytes 1493000
  1859.7 162.6 %collective-permute-start.4 = (f32[48,3456]{1,0:T(8,128)S(1)}, f32[48,3456]{1,0:T(8,128)S(1)}, u32[]{:S(2)}, u32[]{:S(2)}) collective-permute-start(f32[48,3456]{1,0:T(8,128)S(1)} %get-tuple-element.524), channel_id=1, source_target_pairs={{0,3},{1,4},{2,5},{3,6},{4,7},{5,8},{6,9},{7,10},{8,11},{9,12},{10... | collective-permute-start | bytes 1990664
  1862.5 9.8 copy-start.49
  1862.5 161.9 %collective-permute-start.3 = (f32[48,3456]{1,0:T(8,128)S(1)}, f32[48,3456]{1,0:T(8,128)}, u32[]{:S(2)}, u32[]{:S(2)}) collective-permute-start(f32[48,3456]{1,0:T(8,128)S(1)} %get-tuple-element.524), channel_id=1, source_target_pairs={{0,2},{1,3},{2,4},{3,5},{4,6},{5,7},{6,8},{7,9},{8,10},{9,11},{10,... | collective-permute-start | bytes 1990664
  1866.3 160.2 %collective-permute-start.2 = (f32[48,3456]{1,0:T(8,128)S(1)}, f32[48,3456]{1,0:T(8,128)}, u32[]{:S(2)}, u32[]{:S(2)}) collective-permute-start(f32[48,3456]{1,0:T(8,128)S(1)} %get-tuple-element.524), channel_id=1, source_target_pairs={{0,1},{1,2},{2,3},{3,4},{4,5},{5,6},{6,7},{7,8},{8,9},{9,10},{10,1... | collective-permute-start | bytes 1990664
  1870.3 24.1 %collective-permute-start.6 = (f32[48,1152]{1,0:T(8,128)S(1)}, f32[48,1152]{1,0:T(8,128)}, u32[]{:S(2)}, u32[]{:S(2)}) collective-permute-start(f32[48,1152]{1,0:T(8,128)S(1)} %get-tuple-element.525), channel_id=1, source_target_pairs={{0,1},{1,2},{2,3},{3,4},{4,5},{5,6},{6,7},{7,8},{8,9},{9,10},{10,1... | collective-permute-start | bytes 663560
  1894.4 152.9 %collective-permute-start.10 = (f32[40,4608]{1,0:T(8,128)S(1)}, f32[40,4608]{1,0:T(8,128)}, u32[]{:S(2)}, u32[]{:S(2)}) collective-permute-start(f32[40,4608]{1,0:T(8,128)S(1)} %get-tuple-element.526), channel_id=1, source_target_pairs={{0,1},{1,2},{2,3},{3,4},{4,5},{5,6},{6,7},{7,8},{8,9},{9,10},{10,1... | collective-permute-start | bytes 2211848
  2018.4 41.9 %collective-permute-start = (f32[40,6912]{1,0:T(8,128)S(1)}, f32[40,6912]{1,0:T(8,128)}, u32[]{:S(2)}, u32[]{:S(2)}) collective-permute-start(f32[40,6912]{1,0:T(8,128)S(1)} %get-tuple-element.523), channel_id=1, source_target_pairs={{0,1},{1,2},{2,3},{3,4},{4,5},{5,6},{6,7},{7,8},{8,9},{9,10},{10,1... | collective-permute-start | bytes 3317768
  2022.3 25.0 %collective-permute-start.11 = (f32[20,4608]{1,0:T(8,128)}, f32[20,4608]{1,0:T(8,128)}, u32[]{:S(2)}, u32[]{:S(2)}) collective-permute-start(f32[20,4608]{1,0:T(8,128)} %slice.61), channel_id=1, source_target_pairs={{0,2},{1,3},{2,4},{3,5},{4,6},{5,7},{6,8},{7,9},{8,10},{9,11},{10,... | collective-permute-start | bytes 1105928
  2024.4 35.9 %collective-permute-start.1 = (f32[20,6912]{1,0:T(8,128)}, f32[20,6912]{1,0:T(8,128)}, u32[]{:S(2)}, u32[]{:S(2)}) collective-permute-start(f32[20,6912]{1,0:T(8,128)} %slice.58), channel_id=1, source_target_pairs={{0,2},{1,3},{2,4},{3,5},{4,6},{5,7},{6,8},{7,9},{8,10},{9,11},{10,... | collective-permute-start | bytes 1658888
  (44 other events, 204.5 us)
Sparse Core Ops, SparseCore 0:
  248.6 68.6 reduce-scatter.22
  347.8 46.4 reduce-scatter.18
  742.1 28.8 reduce-scatter.16
  773.3 32.2 reduce-scatter.20
  841.9 47.0 reduce-scatter.14
  896.2 350.2 reduce-scatter.24
Sparse Core Ops, SparseCore 1:
  856.8 271.2 all-reduce.22
where the time goes:
time: 2110 us; the launch traced here: 2090 us
  blocking collectives  1060 us (50%)
  local copies, waits for them, and re-layouts  413 us (20%)
  matrix products  388 us (18%)
  other arithmetic  109 us (5%)
  waiting for transfers between devices  46.5 us (2%)
  starting transfers between devices  37.5 us (2%)
  between operations  24.6 us (1%)
    unnamed x3, blocking collectives  1060 us
    dynamic_update_slice x8, local copies, waits for them, and re-layouts, diagonal(): lax.map(lambda pieces: forward_block(*pieces), (query_blocks, key_blocks,...  202 us
    unnamed x187, local copies, waits for them, and re-layouts  97.5 us
    dot_general x5, matrix products, product_cols(): lax.dot_general(left, right, CONTRACT_COLS, preferred_element_type=jnp.fl...  87.9 us
    dot_general x5, matrix products, product(): return jnp.dot(left, right, preferred_element_type=jnp.float32)  77.6 us
    dot_general x5, matrix products, product_rows(): lax.dot_general(left, right, CONTRACT_ROWS, preferred_element_type=jnp.fl...  73.6 us
    dot_general x4, matrix products, block_scores(): jnp.einsum('qhd,khd->hqk', queries, keys, preferred_element_type=jnp.floa...  44.1 us
  transfers between devices with their start and end apart: 19, of which 2 were waited for; matrix products, arithmetic and copies ran while one was open for 77% of the time, Pallas kernels for 0%

commit v1 on v0

v1 whole, which is shorter than its diff:
```python
import functools
import math

import jax
import jax.numpy as jnp
from jax import lax
from jax.experimental import pallas as pl
from jax.experimental.pallas import tpu as pltpu
from jax.sharding import PartitionSpec as P

F32 = jnp.float32
BF16 = jnp.bfloat16
HIGHEST = lax.Precision.HIGHEST
NORM_EPS = 1e-06
ROW = 256
GROUP = 1024
NN = (((1,), (0,)), ((), ()))
NT = (((1,), (1,)), ((), ()))
TN = (((0,), (0,)), ((), ()))
TT = (((0,), (1,)), ((), ()))
VMEM_LIMIT = 60 << 20


def dot(left, right, dims=NN, precision=None):
    return lax.dot_general(left, right, dims, precision=precision, preferred_element_type=F32)


def call(body, name, flops, moved, **kwargs):
    return pl.pallas_call(
        body,
        name=name,
        compiler_params=pltpu.CompilerParams(vmem_limit_bytes=VMEM_LIMIT),
        cost_estimate=pl.CostEstimate(flops=flops, bytes_accessed=moved, transcendentals=0),
        **kwargs,
    )


def shaped(shape, kind):
    return jax.ShapeDtypeStruct(shape, kind)


def normed(values):
    centre = values - jnp.mean(values, axis=-1, keepdims=True)
    spread = jnp.mean(centre * centre, axis=-1, keepdims=True)
    inverse = lax.rsqrt(spread + NORM_EPS)
    return centre * inverse, inverse


def normed_back(grad, normal, inverse):
    first = jnp.mean(grad, axis=-1, keepdims=True)
    second = jnp.mean(grad * normal, axis=-1, keepdims=True)
    return inverse * (grad - first - normal * second)


def qkv_body(x_ref, mod_ref, w_ref, b_ref, h_ref, out_ref):
    @pl.when(pl.program_id(0) == 0)
    def _():
        for tile in range(x_ref.shape[0] // ROW):
            rows = slice(tile * ROW, tile * ROW + ROW)
            normal, _ = normed(x_ref[rows].astype(F32))
            h_ref[rows] = (normal * (1.0 + mod_ref[tile, 1:2]) + mod_ref[tile, 0:1]).astype(BF16)

    out_ref[...] = (dot(h_ref[...], w_ref[...]) + b_ref[...]).astype(BF16)


def qkv_call(x, mod, w, bias):
    tokens, width = x.shape
    wide = w.shape[1]
    block = 384
    return call(
        qkv_body,
        "qkv",
        2 * tokens * width * wide,
        2 * (2 * tokens * width + width * wide + tokens * wide),
        grid=(wide // block,),
        in_specs=[
            pl.BlockSpec((tokens, width), lambda j: (0, 0)),
            pl.BlockSpec(mod.shape, lambda j: (0, 0, 0)),
            pl.BlockSpec((width, block), lambda j: (0, j)),
            pl.BlockSpec((1, block), lambda j: (0, j)),
        ],
        out_specs=[
            pl.BlockSpec((tokens, width), lambda j: (0, 0)),
            pl.BlockSpec((tokens, block), lambda j: (0, j)),
        ],
        out_shape=[shaped((tokens, width), BF16), shaped((tokens, wide), BF16)],
    )(x, mod, w, bias)


def pair_select(offset, head_width):
    row = lax.broadcasted_iota(jnp.int32, (256, 256), 0)
    col = lax.broadcasted_iota(jnp.int32, (256, 256), 1)
    lane = col & 127
    base = offset + jnp.where(col >= 128, head_width, 0)
    return jnp.where((lane < head_width) & (row == base + lane), 1.0, 0.0).astype(BF16)


def attention_body(flag_ref, qkv_ref, keep_ref, p_ref, ot_ref, om_ref, *, width, head_width):
    pair = pl.program_id(1)
    column = pair * (2 * head_width)
    start = pl.multiple_of(column // 128 * 128, 128)
    select = pair_select(column - start, head_width)
    scale = math.log2(math.e) / math.sqrt(head_width)
    tokens = qkv_ref.shape[0]

    @pl.when(pair == 0)
    def _():
        om_ref[...] = jnp.zeros_like(om_ref)

    q = dot(qkv_ref[:, pl.ds(start, 256)], select).astype(BF16)
    k = dot(qkv_ref[:, pl.ds(width + start, 256)], select).astype(BF16)
    v = dot(qkv_ref[:, pl.ds(2 * width + start, 256)], select)
    lane = lax.broadcasted_iota(jnp.int32, v.shape, 1) & 127
    v = jnp.where(lane == head_width, 1.0, v).astype(BF16)

    def part(head, first, count):
        rows = slice(first, first + count)
        lanes = slice(128 * head, 128 * head + 128)
        scores = dot(k[rows, lanes], q[rows, lanes], NT)
        top = jnp.max(scores, axis=0, keepdims=True)
        expo = jnp.exp2((scores - top) * scale)
        total = jnp.sum(expo, axis=0, keepdims=True)
        probs = (expo * (1.0 / total)).astype(BF16)
        p_ref[head, rows, rows] = probs
        mixed = dot(v[rows, lanes], probs, TN)
        ot_ref[head, :, rows] = mixed[:head_width] * (1.0 / mixed[head_width : head_width + 1])
        return (mixed * keep_ref[head, :, rows]).astype(BF16)

    def finish(parts):
        mixed = jnp.concatenate([jnp.concatenate(row, axis=1) for row in parts], axis=0)
        new = dot(mixed, select, TT)
        om_ref[:, pl.ds(start, 256)] = (om_ref[:, pl.ds(start, 256)].astype(F32) + new).astype(BF16)

    whole = flag_ref[pl.program_id(0)] == 1

    @pl.when(whole)
    def _():
        finish([[part(head, 0, tokens)] for head in range(2)])

    @pl.when(jnp.logical_not(whole))
    def _():
        finish([[part(head, at, ROW) for at in range(0, tokens, ROW)] for head in range(2)])


def attention_call(flag, qkv, keep, heads):
    tokens, wide = qkv.shape
    width = wide // 3
    head_width = width // heads
    groups = tokens // GROUP
    return call(
        functools.partial(attention_body, width=width, head_width=head_width),
        "attention",
        2 * 2 * heads * tokens * GROUP * 256,
        2 * tokens * wide + 2 * heads * tokens * GROUP + 6 * tokens * width,
        grid=(groups, heads // 2),
        in_specs=[
            pl.BlockSpec(memory_space=pltpu.SMEM),
            pl.BlockSpec((GROUP, wide), lambda g, h: (g, 0)),
            pl.BlockSpec((2, 1, GROUP), lambda g, h: (h, 0, g)),
        ],
        out_specs=[
            pl.BlockSpec((2, GROUP, GROUP), lambda g, h: (h, 0, g)),
            pl.BlockSpec((2, head_width, GROUP), lambda g, h: (h, 0, g)),
            pl.BlockSpec((GROUP, width), lambda g, h: (g, 0)),
        ],
        out_shape=[
            shaped((heads, GROUP, tokens), BF16),
            shaped((heads, head_width, tokens), F32),
            shaped((tokens, width), BF16),
        ],
    )(flag, qkv, keep)


def attention_back_body(
    flag_ref, qkv_ref, do_ref, p_ref, ot_ref, out_ref, ds_ref, *, width, head_width
):
    pair = pl.program_id(1)
    column = pair * (2 * head_width)
    start = pl.multiple_of(column // 128 * 128, 128)
    select = pair_select(column - start, head_width)
    scale = 1.0 / math.sqrt(head_width)
    tokens = qkv_ref.shape[0]

    @pl.when(pair == 0)
    def _():
        out_ref[...] = jnp.zeros_like(out_ref)

    q = dot(qkv_ref[:, pl.ds(start, 256)], select).astype(BF16)
    k = dot(qkv_ref[:, pl.ds(width + start, 256)], select).astype(BF16)
    v = dot(qkv_ref[:, pl.ds(2 * width + start, 256)], select).astype(BF16)
    window = do_ref[:, pl.ds(start, 256)]
    do = dot(window, select).astype(BF16)
    do_t = dot(select, window, TT)
    delta = [
        jnp.sum(do_t[128 * head : 128 * head + head_width] * ot_ref[head], axis=0, keepdims=True)
        for head in range(2)
    ]

    def grad_scores(head, first, count):
        rows = slice(first, first + count)
        lanes = slice(128 * head, 128 * head + 128)
        dp = dot(v[rows, lanes], do[rows, lanes], NT)
        probs = p_ref[head, rows, rows].astype(F32)
        return (probs * (dp - delta[head][:, rows])).astype(BF16)

    def add(base, value, dims):
        new = dot(value, select, dims)
        spot = pl.ds(base + start, 256)
        out_ref[:, spot] = (out_ref[:, spot].astype(F32) + new).astype(BF16)

    def run(count):
        dq, dk, dv = [], [], []
        for head in range(2):
            lanes = slice(128 * head, 128 * head + 128)
            dq_row, dk_col, dv_col = [], [], []
            for first in range(0, tokens, count):
                rows = slice(first, first + count)
                ds = grad_scores(head, first, count)
                if count == tokens:
                    ds_ref[head] = ds
                    ds = ds_ref[head]
                dq_row.append((dot(k[rows, lanes], ds, TN) * scale).astype(BF16))
                dk_col.append((dot(ds, q[rows, lanes]) * scale).astype(BF16))
                dv_col.append(dot(p_ref[head, rows, rows], do[rows, lanes]).astype(BF16))
            dq.append(jnp.concatenate(dq_row, axis=1))
            dk.append(jnp.concatenate(dk_col, axis=0))
            dv.append(jnp.concatenate(dv_col, axis=0))
        add(0, jnp.concatenate(dq, axis=0), TT)
        add(width, jnp.concatenate(dk, axis=1), NT)
        add(2 * width, jnp.concatenate(dv, axis=1), NT)

    whole = flag_ref[pl.program_id(0)] == 1

    @pl.when(whole)
    def _():
        run(tokens)

    @pl.when(jnp.logical_not(whole))
    def _():
        run(ROW)


def attention_back_call(flag, qkv, do, probs, mixed):
    tokens, wide = qkv.shape
    width = wide // 3
    heads, head_width = mixed.shape[:2]
    groups = tokens // GROUP
    return call(
        functools.partial(attention_back_body, width=width, head_width=head_width),
        "attention_back",
        4 * 2 * heads * tokens * GROUP * 256,
        4 * tokens * wide + 2 * heads * tokens * GROUP + 6 * tokens * width,
        grid=(groups, heads // 2),
        in_specs=[
            pl.BlockSpec(memory_space=pltpu.SMEM),
            pl.BlockSpec((GROUP, wide), lambda g, h: (g, 0)),
            pl.BlockSpec((GROUP, width), lambda g, h: (g, 0)),
            pl.BlockSpec((2, GROUP, GROUP), lambda g, h: (h, 0, g)),
            pl.BlockSpec((2, head_width, GROUP), lambda g, h: (h, 0, g)),
        ],
        out_specs=pl.BlockSpec((GROUP, wide), lambda g, h: (g, 0)),
        out_shape=shaped((tokens, wide), BF16),
        scratch_shapes=[pltpu.VMEM((2, GROUP, GROUP), BF16)],
    )(flag, qkv, do, probs, mixed)


def middle_body(
    om_ref, w_ref, b_ref, x_ref, mod_ref, top_ref, keep_ref, perm_ref,
    a_ref, x1_ref, h_ref, hp_ref, dm_ref, sum_ref,
):
    tile = pl.program_id(0)
    branch = dot(om_ref[...], w_ref[...]) + b_ref[...]
    a_ref[...] = branch
    middle = x_ref[...].astype(F32) + mod_ref[tile, 2:3] * branch
    x1_ref[...] = middle
    normal, _ = normed(middle)
    hidden = (normal * (1.0 + mod_ref[tile, 4:5]) + mod_ref[tile, 3:4]).astype(BF16)
    h_ref[...] = hidden
    hp_ref[...] = dot(hidden, perm_ref[...]).astype(BF16)
    grad = (top_ref[...].astype(F32) * mod_ref[tile, 5:6] * keep_ref[...]).astype(BF16)
    dm_ref[...] = grad
    sum_ref[0] = jnp.sum(grad.astype(F32), axis=0, keepdims=True)


def middle_call(om, w, bias, x, mod, top, keep, perm):
    tokens, width = x.shape
    tiles = tokens // ROW
    rows = pl.BlockSpec((ROW, width), lambda i: (i, 0))
    fixed = pl.BlockSpec((width, width), lambda i: (0, 0))
    return call(
        middle_body,
        "middle",
        4 * tokens * width * width,
        26 * tokens * width,
        grid=(tiles,),
        in_specs=[
            rows,
            fixed,
            pl.BlockSpec((1, width), lambda i: (0, 0)),
            rows,
            pl.BlockSpec(mod.shape, lambda i: (0, 0, 0)),
            rows,
            pl.BlockSpec((ROW, 1), lambda i: (i, 0)),
            fixed,
        ],
        out_specs=[rows, rows, rows, rows, rows, pl.BlockSpec((1, 1, width), lambda i: (i, 0, 0))],
        out_shape=[
            shaped((tokens, width), F32),
            shaped((tokens, width), F32),
            shaped((tokens, width), BF16),
            shaped((tokens, width), BF16),
            shaped((tokens, width), BF16),
            shaped((tiles, 1, width), F32),
        ],
    )(om, w, bias, x, mod, top, keep, perm)


def hidden_body(h_ref, hp_ref, dm_ref, w1_ref, b1_ref, w2_ref, g_ref, df_ref, sum_ref, send_ref, keep_ref):
    first, second = math.sqrt(2.0 / math.pi), 0.044715
    pre = dot(h_ref[...], w1_ref[...]) + b1_ref[...]
    square = pre * pre
    tanh = jnp.tanh(first * pre * (1.0 + second * square))
    half = 0.5 * (1.0 + tanh)
    g_ref[...] = (pre * half).astype(BF16)
    slope = half + (0.5 * first) * pre * (1.0 - tanh * tanh) * (1.0 + (3.0 * second) * square)
    grad = (dot(dm_ref[...], w2_ref[...], NT) * slope).astype(BF16)
    df_ref[...] = grad
    sum_ref[...] = jnp.sum(grad.astype(F32), axis=0, keepdims=True)
    half_rows = send_ref.shape[0]
    send_ref[...] = dot(hp_ref[:, half_rows:], grad, TN)
    keep_ref[...] = dot(hp_ref[:, :half_rows], grad, TN)


def hidden_call(h, hp, dm, w1, b1, w2, first, count):
    tokens, width = h.shape
    block = 384
    base = first // block
    full = pl.BlockSpec((tokens, width), lambda j: (0, 0))
    half = width // 2
    return call(
        hidden_body,
        "hidden",
        6 * tokens * width * count,
        6 * tokens * width + 4 * tokens * count + 8 * width * count,
        grid=(count // block,),
        in_specs=[
            full,
            full,
            full,
            pl.BlockSpec((width, block), lambda j: (0, base + j)),
            pl.BlockSpec((1, block), lambda j: (0, base + j)),
            pl.BlockSpec((block, width), lambda j: (base + j, 0)),
        ],
        out_specs=[
            pl.BlockSpec((tokens, block), lambda j: (0, j)),
            pl.BlockSpec((tokens, block), lambda j: (0, j)),
            pl.BlockSpec((1, block), lambda j: (0, j)),
            pl.BlockSpec((half, block), lambda j: (0, j)),
            pl.BlockSpec((half, block), lambda j: (0, j)),
        ],
        out_shape=[
            shaped((tokens, count), BF16),
            shaped((tokens, count), BF16),
            shaped((1, count), F32),
            shaped((half, count), F32),
            shaped((half, count), F32),
        ],
    )(h, hp, dm, w1, b1, w2)


def rows_grad_body(side_ref, spot_ref, *refs, pieces):
    g_refs, dm_ref, out_ref = refs[:pieces], refs[pieces], refs[pieces + 1]
    shard = out_ref.shape[1]
    grad = dm_ref[...]
    place = 0
    for g_ref in g_refs:
        made = dot(g_ref[...], grad, TN)
        for at in range(0, made.shape[0], shard):
            out_ref[spot_ref[place]] = made[at : at + shard]
            place += 1


def rows_grad_call(side, spots, g, dm, first, count, shards):
    tokens, hidden = g.shape
    half = hidden // 2
    block = 128
    pieces = 2
    base = first // block
    specs = [
        pl.BlockSpec((tokens, half // pieces), functools.partial(lambda j, side, spots, n: (0, side[0] * pieces + n), n=n))
        for n in range(pieces)
    ]
    return call(
        functools.partial(rows_grad_body, pieces=pieces),
        "rows_grad",
        2 * tokens * half * count,
        2 * tokens * half + 2 * tokens * count + 4 * half * count,
        grid_spec=pltpu.PrefetchScalarGridSpec(
            num_scalar_prefetch=2,
            grid=(count // block,),
            in_specs=specs + [pl.BlockSpec((tokens, block), lambda j, side, spots: (0, base + j))],
            out_specs=pl.BlockSpec((shards, half // shards, block), lambda j, side, spots: (0, 0, j)),
        ),
        out_shape=shaped((shards, half // shards, count), F32),
    )(side, spots, *([g] * pieces), dm)


def result_body(g_ref, w_ref, b_ref, x1_ref, mod_ref, top_ref, keep_ref, out_ref, sum_ref):
    tile = pl.program_id(0)
    branch = dot(g_ref[...], w_ref[...]) + b_ref[...]
    out_ref[...] = (x1_ref[...] + mod_ref[tile, 5:6] * keep_ref[...] * branch).astype(BF16)
    sum_ref[0] = jnp.sum(top_ref[...].astype(F32) * keep_ref[...] * branch, axis=0, keepdims=True)


def result_call(g, w, bias, x1, mod, top, keep):
    tokens, width = x1.shape
    hidden = g.shape[1]
    tiles = tokens // ROW
    rows = pl.BlockSpec((ROW, width), lambda i: (i, 0))
    return call(
        result_body,
        "result",
        2 * tokens * width * hidden,
        2 * tokens * hidden + 2 * hidden * width + 8 * tokens * width,
        grid=(tiles,),
        in_specs=[
            pl.BlockSpec((ROW, hidden), lambda i: (i, 0)),
            pl.BlockSpec((hidden, width), lambda i: (0, 0)),
            pl.BlockSpec((1, width), lambda i: (0, 0)),
            rows,
            pl.BlockSpec(mod.shape, lambda i: (0, 0, 0)),
            rows,
            pl.BlockSpec((ROW, 1), lambda i: (i, 0)),
        ],
        out_specs=[rows, pl.BlockSpec((1, 1, width), lambda i: (i, 0, 0))],
        out_shape=[shaped((tokens, width), BF16), shaped((tiles, 1, width), F32)],
    )(g, w, bias, x1, mod, top, keep)


def middle_back_body(
    df_ref, w1_ref, x1_ref, mod_ref, top_ref, a_ref, wp_ref, head_ref,
    dx_ref, da_ref, do_ref, sum_ref,
):
    tile = pl.program_id(0)
    grad = dot(df_ref[...], w1_ref[...], NT)
    normal, inverse = normed(x1_ref[...])
    back = normed_back(grad * (1.0 + mod_ref[tile, 4:5]), normal, inverse)
    dx = top_ref[...].astype(F32) + back
    dx_ref[...] = dx
    da = (dx * mod_ref[tile, 2:3]).astype(BF16)
    da_ref[...] = da
    do_ref[...] = (dot(da, wp_ref[...], NT) * head_ref[tile]).astype(BF16)
    sum_ref[0, 0:1] = jnp.sum(dx * a_ref[...], axis=0, keepdims=True)
    sum_ref[0, 1:2] = jnp.sum(grad, axis=0, keepdims=True)
    sum_ref[0, 2:3] = jnp.sum(grad * normal, axis=0, keepdims=True)
    sum_ref[0, 3:4] = jnp.sum(da.astype(F32), axis=0, keepdims=True)


def middle_back_call(df, w1, x1, mod, top, a, wp, head_rows):
    tokens, width = x1.shape
    hidden = df.shape[1]
    tiles = tokens // ROW
    rows = pl.BlockSpec((ROW, width), lambda i: (i, 0))
    return call(
        middle_back_body,
        "middle_back",
        2 * tokens * width * (hidden + width),
        2 * tokens * hidden + 2 * hidden * width + 18 * tokens * width,
        grid=(tiles,),
        in_specs=[
            pl.BlockSpec((ROW, hidden), lambda i: (i, 0)),
            pl.BlockSpec((width, hidden), lambda i: (0, 0)),
            rows,
            pl.BlockSpec(mod.shape, lambda i: (0, 0, 0)),
            rows,
            rows,
            pl.BlockSpec((width, width), lambda i: (0, 0)),
            pl.BlockSpec(head_rows.shape, lambda i: (0, 0, 0)),
        ],
        out_specs=[rows, rows, rows, pl.BlockSpec((1, 4, width), lambda i: (i, 0, 0))],
        out_shape=[
            shaped((tokens, width), F32),
            shaped((tokens, width), BF16),
            shaped((tokens, width), BF16),
            shaped((tiles, 4, width), F32),
        ],
    )(df, w1, x1, mod, top, a, wp, head_rows)


def columns_grad_body(left_ref, perm_ref, right_ref, send_ref, keep_ref, sum_ref, moved_ref):
    @pl.when(pl.program_id(0) == 0)
    def _():
        moved_ref[...] = dot(left_ref[...], perm_ref[...]).astype(BF16)

    half = send_ref.shape[0]
    grad = right_ref[...]
    send_ref[...] = dot(moved_ref[:, half:], grad, TN)
    keep_ref[...] = dot(moved_ref[:, :half], grad, TN)
    sum_ref[...] = jnp.sum(grad.astype(F32), axis=0, keepdims=True)


def columns_grad_call(left, perm, right, name):
    tokens, width = left.shape
    wide = right.shape[1]
    half = width // 2
    block = 384
    out = pl.BlockSpec((half, block), lambda j: (0, j))
    return call(
        columns_grad_body,
        name,
        2 * tokens * width * (wide + width),
        2 * tokens * (wide + width) + 2 * width * width + 4 * width * wide,
        grid=(wide // block,),
        in_specs=[
            pl.BlockSpec((tokens, width), lambda j: (0, 0)),
            pl.BlockSpec((width, width), lambda j: (0, 0)),
            pl.BlockSpec((tokens, block), lambda j: (0, j)),
        ],
        out_specs=[out, out, pl.BlockSpec((1, block), lambda j: (0, j))],
        out_shape=[shaped((half, wide), F32), shaped((half, wide), F32), shaped((1, wide), F32)],
        scratch_shapes=[pltpu.VMEM((tokens, width), BF16)],
    )(left, perm, right)


def first_back_body(dqkv_ref, w_ref, x_ref, mod_ref, dx_ref, out_ref, sum_ref):
    tile = pl.program_id(0)
    grad = dot(dqkv_ref[...], w_ref[...], NT)
    normal, inverse = normed(x_ref[...].astype(F32))
    out_ref[...] = dx_ref[...] + normed_back(grad * (1.0 + mod_ref[tile, 1:2]), normal, inverse)
    sum_ref[0, 0:1] = jnp.sum(grad, axis=0, keepdims=True)
    sum_ref[0, 1:2] = jnp.sum(grad * normal, axis=0, keepdims=True)


def first_back_call(dqkv, w, x, mod, dx):
    tokens, wide = dqkv.shape
    width = x.shape[1]
    tiles = tokens // ROW
    rows = pl.BlockSpec((ROW, width), lambda i: (i, 0))
    return call(
        first_back_body,
        "first_back",
        2 * tokens * width * wide,
        2 * tokens * wide + 2 * width * wide + 10 * tokens * width,
        grid=(tiles,),
        in_specs=[
            pl.BlockSpec((ROW, wide), lambda i: (i, 0)),
            pl.BlockSpec((width, wide), lambda i: (0, 0)),
            rows,
            pl.BlockSpec(mod.shape, lambda i: (0, 0, 0)),
            rows,
        ],
        out_specs=[rows, pl.BlockSpec((1, 2, width), lambda i: (i, 0, 0))],
        out_shape=[shaped((tokens, width), F32), shaped((tiles, 2, width), F32)],
    )(dqkv, w, x, mod, dx)


def bit_order(lead, bits):
    return [lead] + [bit for bit in range(bits) if bit != lead]


def part_orders(bits):
    if bits < 3:
        return [list(range(bits))]
    return [bit_order(lead, bits) for lead in range(3)]


def scatter_sum(send, keep, bits, orders=None):
    received = lax.ppermute(send, "stream", [(0, 1), (1, 0)])
    rows, wide = keep.shape
    orders = orders or part_orders(bits)
    share = wide // len(orders)
    results = []
    for number, order in enumerate(orders):
        columns = slice(number * share, number * share + share)
        terms = [keep[:, columns], received[:, columns]]
        left = list(range(bits))
        count = rows
        for bit in order:
            before = 1 << left.index(bit)
            after = count // (2 * before)

            def pick(term, which):
                return term.reshape(before, 2, after, share)[:, which].reshape(count // 2, share)

            sent = functools.reduce(lambda x, y: x + y, [pick(term, 1) for term in terms])
            pairs = [(i, i ^ (1 << bit)) for i in range(1 << bits)]
            terms = [pick(term, 0) for term in terms] + [lax.ppermute(sent, "batch", pairs)]
            left.remove(bit)
            count //= 2
        results.append(functools.reduce(lambda x, y: x + y, terms))
    return results


def device_offsets(bits):
    places = jnp.arange(1 << bits, dtype=jnp.int32)
    offset = jnp.zeros_like(places)
    for bit in range(bits):
        offset = offset | (((places >> (bits - 1 - bit)) & 1) << bit)
    return offset


def time_embed(steps_in, width):
    half_width = width // 2
    frequency = jnp.exp(-math.log(10000.0) * jnp.arange(half_width, dtype=F32) / half_width)
    angles = steps_in.astype(F32)[:, None] * frequency[None, :]
    return jnp.concatenate([jnp.cos(angles), jnp.sin(angles)], axis=1)


def per_device(
    tokens, segments, timesteps, labels, head_keep, token_keep, class_table, w_ada, b_ada,
    w_qkv, b_qv, w_proj, b_proj, w_fc1, b_fc1, w_fc2, b_fc2, out_grad, *, batch,
):
    x, top = tokens[0], out_grad[0]
    count, width = x.shape
    hidden = w_fc1.shape[1]
    heads = head_keep.shape[1]
    head_width = width // heads
    items = timesteps.shape[0]
    tiles = count // ROW
    groups = count // GROUP
    null_class = class_table.shape[0] - 1
    bits = batch.bit_length() - 1
    devices = 2 * batch
    stream = lax.axis_index("stream")
    index = lax.axis_index("batch")

    own_labels = lax.dynamic_slice_in_dim(labels, index * items, items)
    used = jnp.where(stream == 0, own_labels, null_class)
    cond = time_embed(timesteps, width) + jnp.take(class_table, used, axis=0).astype(F32)
    act = jax.nn.silu(cond).astype(BF16)
    modulation = dot(act, w_ada) + b_ada
    tile_item = segments[::ROW] - index * items
    chosen = tile_item[:, None] == jnp.arange(items, dtype=jnp.int32)[None, :]
    mod = jnp.sum(jnp.where(chosen[:, :, None], modulation[None], 0.0), axis=1)
    mod = mod.reshape(tiles, 6, width)
    tile_heads = jnp.sum(jnp.where(chosen[:, :, None], head_keep[None], 0), axis=1).astype(F32)
    head_rows = jnp.repeat(tile_heads, head_width, axis=1).reshape(tiles, 1, width)
    head_columns = jnp.repeat(tile_heads.T, ROW, axis=1).reshape(heads, 1, count)
    keep = token_keep[0].astype(F32)[:, None]
    grouped = segments.reshape(groups, GROUP)
    flag = (grouped[:, 0] == grouped[:, -1]).astype(jnp.int32)

    offset = device_offsets(bits)
    own_order = jnp.concatenate([stream * batch + (index ^ offset), (1 - stream) * batch + (index ^ offset)])
    shard = width // devices
    source = (own_order[:, None] * shard + jnp.arange(shard, dtype=jnp.int32)[None, :]).reshape(width)
    perm = (jnp.arange(width, dtype=jnp.int32)[:, None] == source[None, :]).astype(BF16)
    inverse = device_offsets(bits)
    spots = inverse[jnp.arange(batch, dtype=jnp.int32) ^ index]

    bias_full = jnp.concatenate([b_qv[:width], jnp.zeros((width,), F32), b_qv[width:]])[None]
    h1, qkv = qkv_call(x, mod, w_qkv, bias_full)
    probs, mixed, om = attention_call(flag, qkv, head_columns, heads)
    a, x1, h2, h2p, dm, sum_dm = middle_call(om, w_proj, b_proj[None], x, mod, top, keep, perm)

    cuts = [0, hidden // 4, hidden // 2, hidden]
    pieces, fc1 = [], []
    for low, high in zip(cuts[:-1], cuts[1:]):
        got = hidden_call(h2, h2p, dm, w_fc1, b_fc1[None], w_fc2, low, high - low)
        pieces.append(got[:3])
        fc1 += scatter_sum(got[3], got[4], bits)
    g = jnp.concatenate([piece[0] for piece in pieces], axis=1)
    df = jnp.concatenate([piece[1] for piece in pieces], axis=1)
    sum_df = jnp.concatenate([piece[2] for piece in pieces], axis=1)[0]
    fc2 = []
    for low, high in ((0, width // 3), (width // 3, width)):
        halves = [
            rows_grad_call(side[None], spots, g, dm, low, high - low, batch).reshape(hidden // 2, high - low)
            for side in (1 - stream, stream)
        ]
        fc2 += scatter_sum(halves[0], halves[1], bits)
    result, sum_gate = result_call(g, w_fc2, b_fc2[None], x1, mod, top, keep)
    dx1, da, do, sums_two = middle_back_call(df, w_fc1, x1, mod, top, a, w_proj, head_rows)
    send, kept, _ = columns_grad_call(om, perm, da, "proj_grad")
    proj = scatter_sum(send, kept, bits)

    dqkv = attention_back_call(flag, qkv, do, probs, mixed)
    send, kept, sum_dqkv = columns_grad_call(h1, perm, dqkv, "qkv_grad")
    wide = scatter_sum(send, kept, bits)
    grad_tokens, sums_one = first_back_call(dqkv, w_qkv, x, mod, dx1)

    biases = jnp.concatenate(
        [
            part.reshape(devices, -1)
            for part in (
                sum_df,
                jnp.sum(sum_dm, axis=(0, 1)),
                jnp.sum(sums_two[:, 3], axis=0),
                jnp.concatenate([sum_dqkv[0, :width], sum_dqkv[0, 2 * width :]]),
            )
        ],
        axis=1,
    )
    biases = biases[own_order]
    bias = scatter_sum(biases[batch:], biases[:batch], bits, [list(range(bits))])[0][0]
    ends = [hidden // devices, width // devices, width // devices, 2 * width // devices]
    at = [sum(ends[:n]) for n in range(5)]
    grad_b_fc1, grad_b_fc2, grad_b_proj, grad_b_qv = [bias[at[n] : at[n + 1]] for n in range(4)]

    by_tile = jnp.stack(
        [sums_one[:, 0], sums_one[:, 1], sums_two[:, 0], sums_two[:, 1], sums_two[:, 2], sum_gate[:, 0]],
        axis=1,
    ).reshape(tiles, 6 * width)
    grad_mod = jnp.sum(jnp.where(chosen[:, :, None], by_tile[:, None], 0.0), axis=0)
    grad_mod = grad_mod.astype(BF16).astype(F32)
    gathered = lax.all_gather(
        jnp.concatenate([grad_mod, cond], axis=1), ("stream", "batch"), axis=0, tiled=True
    )
    all_mod = gathered[:, : 6 * width]
    all_cond = gathered[:, 6 * width :]
    all_mod16 = all_mod.astype(BF16)
    me = stream * batch + index
    all_act = jax.nn.silu(all_cond).astype(BF16)
    own_act = lax.dynamic_slice_in_dim(all_act, me * shard, shard, axis=1)
    grad_w_ada = dot(own_act, all_mod16, TN)
    share = 6 * width // devices
    grad_b_ada = jnp.sum(lax.dynamic_slice_in_dim(all_mod, me * share, share, axis=1), axis=0)
    grad_act = dot(all_mod16, w_ada, NT)
    grad_cond = jax.vjp(jax.nn.silu, all_cond)[1](grad_act)[0]
    all_labels = jnp.concatenate([labels, jnp.full_like(labels, null_class)])
    class_index = jnp.arange(null_class + 1, dtype=jnp.int32)
    label_select = (all_labels[:, None] == class_index[None, :]).astype(F32)
    grad_table = dot(label_select, grad_cond, TN, HIGHEST)

    return (
        result[None],
        grad_tokens[None],
        grad_table,
        grad_w_ada,
        grad_b_ada,
        jnp.concatenate(wide, axis=1),
        grad_b_qv,
        jnp.concatenate(proj, axis=1),
        grad_b_proj,
        jnp.concatenate(fc1, axis=1),
        grad_b_fc1,
        jnp.concatenate(fc2, axis=1),
        grad_b_fc2,
    )


def solution(mesh):
    both = ("stream", "batch")
    return jax.shard_map(
        functools.partial(per_device, batch=mesh.shape["batch"]),
        mesh=mesh,
        in_specs=(
            P("stream", "batch", None),
            P("batch"),
            P("batch"),
            P(),
            P("batch", None),
            P("stream", "batch"),
            P(), P(), P(), P(), P(), P(), P(), P(), P(), P(), P(),
            P("stream", "batch", None),
        ),
        out_specs=(
            P("stream", "batch", None),
            P("stream", "batch", None),
            P(),
            P(both, None),
            P(both),
            P(both, None),
            P(both),
            P(both, None),
            P(both),
            P(both, None),
            P(both),
            P(both, None),
            P(both),
        ),
        check_vma=False,
    )
```

time: 2110 us -> 923 us (0.44)
  blocking collectives: 1060 us -> 0 us
  matrix products: 388 us -> 26.4 us
  Pallas kernels: 0 us -> 323 us
  local copies, waits for them, and re-layouts: 413 us -> 175 us
  starting transfers between devices: 37.5 us -> 126 us
  waiting for transfers between devices: 46.5 us -> 135 us
    unnamed x3 -> x0, blocking collectives: 1060 us -> none
    dot_general x33 -> x4, matrix products: 388 us -> 26.4 us  [dot(): lax.dot_general(left, right, dims, precision=precision, preferred_element...]
    pallas_call x0 -> x16, Pallas kernels: none -> 323 us  [the longest x3 62.9 us: hidden_call(): call(hidden_body, 'hidden', 6 * tokens * width * count, 6 * tokens * widt...]
    dynamic_update_slice x8 -> x0, local copies, waits for them, and re-layouts: 202 us -> none  [diagonal(): lax.map(lambda pieces: forward_block(*pieces), (query_blocks, key_blocks,...]
    ppermute x0 -> x96, waiting for transfers between devices: none -> 135 us  [the longest x88 134 us: scatter_sum(): lax.ppermute(sent, 'batch', pairs)]
    ppermute x0 -> x96, starting transfers between devices: none -> 126 us  [the longest x88 124 us: scatter_sum(): lax.ppermute(sent, 'batch', pairs)]
    unnamed x187 -> x231, local copies, waits for them, and re-layouts: 97.5 us -> 18.7 us
    slice x0 -> x59, other arithmetic: none -> 55.5 us  [the longest x58 55.3 us: pick(): term.reshape(before, 2, after, share)[:, which].reshape(count // 2, share)]
  transfers between devices with their start and end apart: 19 -> 97, of which waited for: 2 -> 37; matrix products, arithmetic and copies ran while one was open for 77% -> 31% of each run, Pallas kernels for 0% -> 26%
where the time goes in v1:
time: 923 us; the launch traced here: 915 us
  Pallas kernels  323 us (35%)
  local copies, waits for them, and re-layouts  175 us (19%)
  waiting for transfers between devices  135 us (15%)
  starting transfers between devices  126 us (14%)
  other arithmetic  113 us (12%)
  matrix products  26.4 us (3%)
  between operations  17.3 us (2%)
    ppermute x88, waiting for transfers between devices, scatter_sum(): lax.ppermute(sent, 'batch', pairs)  134 us
    ppermute x88, starting transfers between devices, scatter_sum(): lax.ppermute(sent, 'batch', pairs)  124 us
    another operation x65, local copies, waits for them, and re-layouts, pick(): term.reshape(before, 2, after, share)[:, which].reshape(count // 2, share)  72.3 us
    pallas_call x3, Pallas kernels, hidden_call(): call(hidden_body, 'hidden', 6 * tokens * width * count, 6 * tokens * widt...  62.9 us
    slice x58, other arithmetic, pick(): term.reshape(before, 2, after, share)[:, which].reshape(count // 2, share)  55.3 us
    slice x14, local copies, waits for them, and re-layouts, scatter_sum(): terms = [keep[:, columns], received[:, columns]]  45.2 us
    pallas_call x4, Pallas kernels, rows_grad_call(): call(functools.partial(rows_grad_body, pieces=pieces), 'rows_grad', 2 * t...  43.8 us
    pallas_call x1, Pallas kernels, attention_back_call(): call(functools.partial(attention_back_body, width=width, head_width=head_...  41 us
  transfers between devices with their start and end apart: 97, of which 37 were waited for; matrix products, arithmetic and copies ran while one was open for 31% of the time, Pallas kernels for 26%

profile of v1, /device:TPU:0, one launch (start us, length us, event | category | flops | bytes accessed | tf_op | source)
XLA Modules:
  0.0 915.3 jit_solution(3614776388331817366)
XLA Ops:
  20.8 7.7 convolution_add_fusion
  30.6 2.6 fusion.perm_ref
  33.2 18.0 %qkv.1 = (bf16[1024,1152]{1,0:T(8,128)(2,1)}, bf16[1024,3456]{1,0:T(8,128)(2,1)}) custom-call(bf16[1024,1152]{1,0:T(8,128)(2,1)} %bitcast.968, f32[4,6,1152]{2,1,0:T(8,128)} %reshape.1066.mod_ref, bf16[1152,3456]{1,0:T(8,128)(2,1)} %w_ref.7, f32[1,3456]{1,0:T(1,128)} %broadcast_in_dim.138.b_ref), custom_call_target="tpu_custom_call" | custom-call | flops 8153726976 | bytes 19759104 | tf_op jit(solution)/shard_map/qkv/pallas_call | solution.py:70
  51.2 36.1 %attention.1 = (bf16[16,1024,1024]{2,1,0:T(8,128)(2,1)}, f32[16,72,1024]{2,1,0:T(8,128)}, bf16[1024,1152]{1,0:T(8,128)(2,1)}) custom-call(s32[1]{0:T(128)} %bitcast.1.flag_ref, bf16[1024,3456]{1,0:T(8,128)(2,1)} %get-tuple-element.52.qkv_ref, f32[16,1,1024]{2,1,0:T(1,128)} %reshape_reshape.6.keep_ref), custom_call_target="tpu_custom_call" | custom-call | flops 17179869184 | bytes 47710208 | tf_op jit(solution)/shard_map/attention/pallas_call | solution.py:150
  87.2 14.1 %middle.1 = (f32[1024,1152]{1,0:T(8,128)}, f32[1024,1152]{1,0:T(8,128)}, bf16[1024,1152]{1,0:T(8,128)(2,1)}, bf16[1024,1152]{1,0:T(8,128)(2,1)}, bf16[1024,1152]{1,0:T(8,128)(2,1)}, /*index=5*/f32[4,1,1152]{2,1,0:T(1,128)}) custom-call(bf16[1024,1152]{1,0:T(8,128)(2,1)} %get-tuple-element.53.om_ref.left_ref, bf16[1152,1152]{1,0:T(8,128)(2,1)} %wp_ref.1, ...), custom_call_target="tpu_custom_call" | custom-call | flops 5435817984 | bytes 30670848 | tf_op jit(solution)/shard_map/middle/pallas_call | solution.py:290
  101.4 17.1 %hidden.4 = (bf16[1024,1152]{1,0:T(8,128)(2,1)}, bf16[1024,1152]{1,0:T(8,128)(2,1)}, f32[1,1152]{1,0:T(1,128)}, f32[576,1152]{1,0:T(8,128)}, f32[576,1152]{1,0:T(8,128)}) custom-call(bf16[1024,1152]{1,0:T(8,128)(2,1)} %get-tuple-element.54.h_ref, bf16[1024,1152]{1,0:T(8,128)(2,1)} %get-tuple-element.55.hp_ref, ...), custom_call_target="tpu_custom_call" | custom-call | flops 8153726976 | bytes 22413312 | tf_op jit(solution)/shard_map/hidden/pallas_call | solution.py:340
  118.9 16.8 %hidden.3 = (bf16[1024,1152]{1,0:T(8,128)(2,1)}, bf16[1024,1152]{1,0:T(8,128)(2,1)}, f32[1,1152]{1,0:T(1,128)}, f32[576,1152]{1,0:T(8,128)}, f32[576,1152]{1,0:T(8,128)}) custom-call(bf16[1024,1152]{1,0:T(8,128)(2,1)} %get-tuple-element.54.h_ref, bf16[1024,1152]{1,0:T(8,128)(2,1)} %get-tuple-element.55.hp_ref, ...), custom_call_target="tpu_custom_call" | custom-call | flops 8153726976 | bytes 22413312 | tf_op jit(solution)/shard_map/hidden/pallas_call | solution.py:340
  135.8 29.0 %hidden.5 = (bf16[1024,2304]{1,0:T(8,128)(2,1)}, bf16[1024,2304]{1,0:T(8,128)(2,1)}, f32[1,2304]{1,0:T(1,128)}, f32[576,2304]{1,0:T(8,128)}, f32[576,2304]{1,0:T(8,128)}) custom-call(bf16[1024,1152]{1,0:T(8,128)(2,1)} %get-tuple-element.54.h_ref, bf16[1024,1152]{1,0:T(8,128)(2,1)} %get-tuple-element.55.hp_ref, ...), custom_call_target="tpu_custom_call" | custom-call | flops 16307453952 | bytes 37748736 | tf_op jit(solution)/shard_map/hidden/pallas_call | solution.py:340
  166.2 3.4 constant_dynamic-update-slice_fusion.2
  169.7 3.3 constant_dynamic-update-slice_fusion.1
  173.0 2.5 constant_dynamic-update-slice_fusion.g_ref.refs_0_.refs_1_
  175.5 20.1 %result.1 = (bf16[1024,1152]{1,0:T(8,128)(2,1)}, f32[4,1,1152]{2,1,0:T(1,128)}) custom-call(bf16[1024,4608]{1,0:T(8,128)(2,1)} %constant_dynamic-update-slice_fusion.g_ref.refs_0_.refs_1_, bf16[4608,1152]{1,0:T(8,128)(2,1)} %w_ref.6, f32[1,1152]{1,0:T(1,128)} %broadcast_in_dim.145.b_ref, f32[1024,1152]{1,0:T(8,128)} %get-tuple-element.60.x1_ref, ...), custom_call_target="tpu_custom_call" | custom-call | flops 10871635968 | bytes 29491200 | tf_op jit(solution)/shard_map/result/pallas_call | solution.py:420
  195.5 9.0 pad_maximum_fusion.df_ref
  204.5 30.7 %middle_back.1 = (f32[1024,1152]{1,0:T(8,128)}, bf16[1024,1152]{1,0:T(8,128)(2,1)}, bf16[1024,1152]{1,0:T(8,128)(2,1)}, f32[4,4,1152]{2,1,0:T(4,128)}) custom-call(bf16[1024,4608]{1,0:T(8,128)(2,1)} %pad_maximum_fusion.df_ref, bf16[1152,4608]{1,0:T(8,128)(2,1)} %w1_ref.7, f32[1024,1152]{1,0:T(8,128)} %get-tuple-element.60.x1_ref, ...), custom_call_target="tpu_custom_call" | custom-call | flops 13589544960 | bytes 41287680 | tf_op jit(solution)/shard_map/middle_back/pallas_call | solution.py:464
  235.2 41.0 %attention_back.1.dqkv_ref.right_ref = bf16[1024,3456]{1,0:T(8,128)(2,1)} custom-call(s32[1]{0:T(128)} %bitcast.1.flag_ref, bf16[1024,3456]{1,0:T(8,128)(2,1)} %get-tuple-element.52.qkv_ref, bf16[1024,1152]{1,0:T(8,128)(2,1)} %get-tuple-element.66.do_ref, bf16[16,1024,1024]{2,1,0:T(8,128)(2,1)} %get-tuple-element.67.p_ref, ...), custom_call_target="tpu_custom_call" | custom-call | flops 34359738368 | bytes 54788096 | tf_op jit(solution)/shard_map/attention_back/pallas_call | solution.py:248
  276.3 17.3 %first_back.1 = (f32[1024,1152]{1,0:T(8,128)}, f32[4,2,1152]{2,1,0:T(2,128)}) custom-call(bf16[1024,3456]{1,0:T(8,128)(2,1)} %attention_back.1.dqkv_ref.right_ref, bf16[1152,3456]{1,0:T(8,128)(2,1)} %w_ref.7, bf16[1024,1152]{1,0:T(8,128)(2,1)} %bitcast.970, f32[4,6,1152]{2,1,0:T(8,128)} %reshape.1066.mod_ref, f32[1024,1152]{1,0:T(8,128)} %get-tuple-element.69.dx_ref), custom_call_target="tpu_custom_call" | custom-call | flops 8153726976 | bytes 26836992 | tf_op jit(solution)/shard_map/first_back/pallas_call | solution.py:539
  295.4 13.5 %proj_grad.1 = (f32[576,1152]{1,0:T(8,128)}, f32[576,1152]{1,0:T(8,128)}, f32[1,1152]{1,0:T(1,128)}) custom-call(bf16[1024,1152]{1,0:T(8,128)(2,1)} %get-tuple-element.53.om_ref.left_ref, bf16[1152,1152]{1,0:T(8,128)(2,1)} %fusion.perm_ref, bf16[1024,1152]{1,0:T(8,128)(2,1)} %get-tuple-element.82.right_ref), custom_call_target="tpu_custom_call" | custom-call | flops 5435817984 | bytes 12681216 | tf_op jit(solution)/shard_map/proj_grad/pallas_call | solution.py:508
  309.9 25.0 %qkv_grad.1 = (f32[576,3456]{1,0:T(8,128)}, f32[576,3456]{1,0:T(8,128)}, f32[1,3456]{1,0:T(1,128)}) custom-call(bf16[1024,1152]{1,0:T(8,128)(2,1)} %get-tuple-element.74.left_ref, bf16[1152,1152]{1,0:T(8,128)(2,1)} %fusion.perm_ref, bf16[1024,3456]{1,0:T(8,128)(2,1)} %attention_back.1.dqkv_ref.right_ref), custom_call_target="tpu_custom_call" | custom-call | flops 10871635968 | bytes 28016640 | tf_op jit(solution)/shard_map/qkv_grad/pallas_call | solution.py:508
  338.0 8.7 rows_grad.4
  346.7 13.2 %rows_grad.6 = f32[16,144,768]{2,1,0:T(8,128)} custom-call(s32[1]{0:T(128)} %bitcast.228.side_ref, s32[16]{0:T(128)} %gather_fusion.2, bf16[1024,4608]{1,0:T(8,128)(2,1)} %constant_dynamic-update-slice_fusion.g_ref.refs_0_.refs_1_, bf16[1024,4608]{1,0:T(8,128)(2,1)} %constant_dynamic-update-slice_fusion.g_ref.refs_0_.refs_1_, ...), custom_call_target="tpu_custom_call" | custom-call | flops 3623878656 | bytes 13369344 | tf_op jit(solution)/shard_map/rows_grad/pallas_call | solution.py:393
  359.9 4.0 fusion.177
  363.9 7.2 fusion.170
  373.3 3.2 fusion.172
  376.4 13.2 %rows_grad.7 = f32[16,144,768]{2,1,0:T(8,128)} custom-call(s32[1]{0:T(128)} %bitcast.235.side_ref, s32[16]{0:T(128)} %gather_fusion.2, bf16[1024,4608]{1,0:T(8,128)(2,1)} %constant_dynamic-update-slice_fusion.g_ref.refs_0_.refs_1_, bf16[1024,4608]{1,0:T(8,128)(2,1)} %constant_dynamic-update-slice_fusion.g_ref.refs_0_.refs_1_, ...), custom_call_target="tpu_custom_call" | custom-call | flops 3623878656 | bytes 13369344 | tf_op jit(solution)/shard_map/rows_grad/pallas_call | solution.py:393
  389.6 21.1 %collective-permute-start.14 = (f32[8,288]{1,0:T(8,128)S(1)}, f32[8,288]{1,0:T(8,128)S(1)}, u32[]{:S(2)}, u32[]{:S(2)}) collective-permute-start(f32[8,288]{1,0:T(8,128)S(1)} %get-tuple-element.439), channel_id=1, source_target_pairs={{0,1},{1,0},{2,3},{3,2},{4,5},{5,4},{6,7},{7,6},{8,9},{9,8},{10,11... | collective-permute-start | bytes 27656 | tf_op jit(solution)/shard_map/ppermute | solution.py:587
  410.7 3.3 fusion.179
  415.7 3.3 fusion.181
  420.6 3.3 fusion.183
  425.3 8.7 rows_grad.5
  466.9 5.0 collective-permute-done.23
  586.9 4.2 collective-permute-done.30
  591.1 5.2 collective-permute-done.35
  596.3 5.6 collective-permute-done.22
  602.0 5.1 collective-permute-done.39
  607.2 6.6 collective-permute-done.43
  613.8 3.0 collective-permute-start.56
  629.1 3.8 collective-permute-done.71
  637.5 5.1 collective-permute-done.72
  646.7 3.8 collective-permute-done.80
  658.8 2.7 collective-permute-done.74
  661.4 2.5 collective-permute-start.82
  664.6 3.0 fusion.175
  673.9 11.8 %collective-permute-done.58 = f32[288,768]{1,0:T(8,128)S(1)} collective-permute-done((f32[288,768]{1,0:T(8,128)S(1)}, f32[288,768]{1,0:T(8,128)S(1)}, u32[]{:S(2)}, u32[]{:S(2)}) %collective-permute-start.58) | collective-permute-done | bytes 884768 | tf_op jit(solution)/shard_map/ppermute | solution.py:587
  687.0 3.5 collective-permute-done.62
  721.1 3.6 collective-permute-done.65
  726.9 3.7 fusion.173
  738.6 4.0 fusion.171
  751.7 5.9 reshape.1210
  757.6 11.7 %fusion.6 = f32[128,1152]{1,0:T(8,128)S(1)} fusion(bf16[1152,6912]{1,0:T(8,128)(2,1)} %param.25, f32[128,8064]{1,0:T(8,128)} %reshape.1210), kind=kOutput, calls=%fused_computation.27 | convolution fusion | flops 2038431744 | bytes 18284544 | tf_op jit(solution)/shard_map/dot_general | solution.py:25
  769.3 5.5 fusion.13
  787.2 15.0 %collective-permute-done.85 = f32[576,256]{1,0:T(8,128)S(1)} collective-permute-done((f32[576,256]{1,0:T(8,128)S(1)}, f32[576,256]{1,0:T(8,128)S(1)}, u32[]{:S(2)}, u32[]{:S(2)}) %collective-permute-start.85) | collective-permute-done | bytes 589856 | tf_op jit(solution)/shard_map/ppermute | solution.py:587
  805.8 3.4 collective-permute-start.90
  809.4 2.5 collective-permute-done.86
  813.0 3.2 collective-permute-done.90
  816.2 2.4 collective-permute-done.94
  819.3 2.4 collective-permute-start.95
  824.4 3.0 fusion.193
  827.4 7.0 collective-permute-done.1
  840.0 8.6 collective-permute-done.6
  850.9 3.4 collective-permute-start.7
  860.6 2.4 fusion.209
  885.6 2.9 collective-permute-start.12
  892.7 8.7 collective-permute-done.8
  902.6 2.8 collective-permute-done.12
  (670 shorter events, 328.8 us)
Async XLA Ops:
  7.2 744.5 %all-gather.3.cloned.1.call-start = ((), (), s32[]{:S(2)}) async-start(), calls=%async_computation | async-start | bytes 4257792 | tf_op jit(solution)/shard_map/all_gather | solution.py:706
  118.4 317.4 %collective-permute-start.44 = (f32[576,1152]{1,0:T(8,128)}, f32[576,1152]{1,0:T(8,128)}, u32[]{:S(2)}, u32[]{:S(2)}) collective-permute-start(f32[576,1152]{1,0:T(8,128)} %get-tuple-element.88), channel_id=1, source_target_pairs={{0,16},{16,0},{1,17},{17,1},{2,18},{18,2},{3,19},{19,3},{4,20},{20... | collective-permute-start | bytes 7962632 | tf_op jit(solution)/shard_map/ppermute | solution.py:568
  135.7 305.9 %collective-permute-start.31 = (f32[576,1152]{1,0:T(8,128)}, f32[576,1152]{1,0:T(8,128)}, u32[]{:S(2)}, u32[]{:S(2)}) collective-permute-start(f32[576,1152]{1,0:T(8,128)} %get-tuple-element.86), channel_id=1, source_target_pairs={{0,16},{16,0},{1,17},{17,1},{2,18},{18,2},{3,19},{19,3},{4,20},{20... | collective-permute-start | bytes 7962632 | tf_op jit(solution)/shard_map/ppermute | solution.py:568
  308.9 136.1 %collective-permute-start.18 = (f32[576,1152]{1,0:T(8,128)}, f32[576,1152]{1,0:T(8,128)}, u32[]{:S(2)}, u32[]{:S(2)}) collective-permute-start(f32[576,1152]{1,0:T(8,128)} %get-tuple-element.84), channel_id=1, source_target_pairs={{0,16},{16,0},{1,17},{17,1},{2,18},{18,2},{3,19},{19,3},{4,20},{20... | collective-permute-start | bytes 7962632 | tf_op jit(solution)/shard_map/ppermute | solution.py:568
  336.5 53.1 %collective-permute-start.13 = (f32[16,288]{1,0:T(8,128)S(1)}, f32[16,288]{1,0:T(8,128)S(1)}, u32[]{:S(2)}, u32[]{:S(2)}) collective-permute-start(f32[16,288]{1,0:T(8,128)S(1)} %get-tuple-element.437), channel_id=1, source_target_pairs={{0,16},{16,0},{1,17},{17,1},{2,18},{18,2},{3,19},{19,3},{4,20},{20... | collective-permute-start | bytes 55304 | tf_op jit(solution)/shard_map/ppermute | solution.py:568
  389.6 24.4 %collective-permute-start.14 = (f32[8,288]{1,0:T(8,128)S(1)}, f32[8,288]{1,0:T(8,128)S(1)}, u32[]{:S(2)}, u32[]{:S(2)}) collective-permute-start(f32[8,288]{1,0:T(8,128)S(1)} %get-tuple-element.439), channel_id=1, source_target_pairs={{0,1},{1,0},{2,3},{3,2},{4,5},{5,4},{6,7},{7,6},{8,9},{9,8},{10,11... | collective-permute-start | bytes 27656 | tf_op jit(solution)/shard_map/ppermute | solution.py:587
  423.9 10.1 %collective-permute-start.17 = (f32[1,288]{1,0:T(1,128)S(1)}, f32[1,288]{1,0:T(1,128)S(1)}, u32[]{:S(2)}, u32[]{:S(2)}) collective-permute-start(f32[1,288]{1,0:T(1,128)S(1)} %fusion.148), channel_id=1, source_target_pairs={{0,8},{1,9},{2,10},{3,11},{4,12},{5,13},{6,14},{7,15},{8,0},{9,1},... | collective-permute-start | bytes 3464 | tf_op jit(solution)/shard_map/ppermute | solution.py:587
  437.9 13.2 %collective-permute-start.45 = (f32[288,384]{1,0:T(8,128)S(1)}, f32[288,384]{1,0:T(8,128)S(1)}, u32[]{:S(2)}, u32[]{:S(2)}) collective-permute-start(f32[288,384]{1,0:T(8,128)S(1)} %get-tuple-element.218), channel_id=1, source_target_pairs={{0,1},{1,0},{2,3},{3,2},{4,5},{5,4},{6,7},{7,6},{8,9},{9,8},{10,11... | collective-permute-start | bytes 1327112 | tf_op jit(solution)/shard_map/ppermute | solution.py:587
  439.8 13.2 %collective-permute-start.49 = (f32[288,384]{1,0:T(8,128)S(1)}, f32[288,384]{1,0:T(8,128)S(1)}, u32[]{:S(2)}, u32[]{:S(2)}) collective-permute-start(f32[288,384]{1,0:T(8,128)S(1)} %bitcast.921), channel_id=1, source_target_pairs={{0,2},{1,3},{2,0},{3,1},{4,6},{5,7},{6,4},{7,5},{8,10},{9,11},{10,... | collective-permute-start | bytes 1327112 | tf_op jit(solution)/shard_map/ppermute | solution.py:587
  440.5 13.9 %collective-permute-start.53 = (f32[288,384]{1,0:T(8,128)S(1)}, f32[288,384]{1,0:T(8,128)S(1)}, u32[]{:S(2)}, u32[]{:S(2)}) collective-permute-start(f32[288,384]{1,0:T(8,128)S(1)} %bitcast.919), channel_id=1, source_target_pairs={{0,4},{1,5},{2,6},{3,7},{4,0},{5,1},{6,2},{7,3},{8,12},{9,13},{10,... | collective-permute-start | bytes 1327112 | tf_op jit(solution)/shard_map/ppermute | solution.py:587
  443.6 15.0 %collective-permute-start.32 = (f32[288,384]{1,0:T(8,128)S(1)}, f32[288,384]{1,0:T(8,128)S(1)}, u32[]{:S(2)}, u32[]{:S(2)}) collective-permute-start(f32[288,384]{1,0:T(8,128)S(1)} %get-tuple-element.227), channel_id=1, source_target_pairs={{0,1},{1,0},{2,3},{3,2},{4,5},{5,4},{6,7},{7,6},{8,9},{9,8},{10,11... | collective-permute-start | bytes 1327112 | tf_op jit(solution)/shard_map/ppermute | solution.py:587
  445.0 17.4 %collective-permute-start.36 = (f32[288,384]{1,0:T(8,128)S(1)}, f32[288,384]{1,0:T(8,128)S(1)}, u32[]{:S(2)}, u32[]{:S(2)}) collective-permute-start(f32[288,384]{1,0:T(8,128)S(1)} %bitcast.920), channel_id=1, source_target_pairs={{0,2},{1,3},{2,0},{3,1},{4,6},{5,7},{6,4},{7,5},{8,10},{9,11},{10,... | collective-permute-start | bytes 1327112 | tf_op jit(solution)/shard_map/ppermute | solution.py:587
  451.1 13.1 %collective-permute-start.40 = (f32[288,384]{1,0:T(8,128)S(1)}, f32[288,384]{1,0:T(8,128)S(1)}, u32[]{:S(2)}, u32[]{:S(2)}) collective-permute-start(f32[288,384]{1,0:T(8,128)S(1)} %bitcast.917), channel_id=1, source_target_pairs={{0,4},{1,5},{2,6},{3,7},{4,0},{5,1},{6,2},{7,3},{8,12},{9,13},{10,... | collective-permute-start | bytes 1327112 | tf_op jit(solution)/shard_map/ppermute | solution.py:587
  452.9 19.0 %collective-permute-start.23 = (f32[288,384]{1,0:T(8,128)S(1)}, f32[288,384]{1,0:T(8,128)S(1)}, u32[]{:S(2)}, u32[]{:S(2)}) collective-permute-start(f32[288,384]{1,0:T(8,128)S(1)} %bitcast.918), channel_id=1, source_target_pairs={{0,2},{1,3},{2,0},{3,1},{4,6},{5,7},{6,4},{7,5},{8,10},{9,11},{10,... | collective-permute-start | bytes 1327112 | tf_op jit(solution)/shard_map/ppermute | solution.py:587
  454.5 19.4 %collective-permute-start.27 = (f32[288,384]{1,0:T(8,128)S(1)}, f32[288,384]{1,0:T(8,128)S(1)}, u32[]{:S(2)}, u32[]{:S(2)}) collective-permute-start(f32[288,384]{1,0:T(8,128)S(1)} %bitcast.916), channel_id=1, source_target_pairs={{0,4},{1,5},{2,6},{3,7},{4,0},{5,1},{6,2},{7,3},{8,12},{9,13},{10,... | collective-permute-start | bytes 1327112 | tf_op jit(solution)/shard_map/ppermute | solution.py:587
  458.6 16.7 %collective-permute-start.19 = (f32[288,384]{1,0:T(8,128)S(1)}, f32[288,384]{1,0:T(8,128)S(1)}, u32[]{:S(2)}, u32[]{:S(2)}) collective-permute-start(f32[288,384]{1,0:T(8,128)S(1)} %get-tuple-element.230), channel_id=1, source_target_pairs={{0,1},{1,0},{2,3},{3,2},{4,5},{5,4},{6,7},{7,6},{8,9},{9,8},{10,11... | collective-permute-start | bytes 1327112 | tf_op jit(solution)/shard_map/ppermute | solution.py:587
  462.4 14.9 %collective-permute-start.46 = (f32[144,384]{1,0:T(8,128)S(1)}, f32[144,384]{1,0:T(8,128)S(1)}, u32[]{:S(2)}, u32[]{:S(2)}) collective-permute-start(f32[144,384]{1,0:T(8,128)S(1)} %get-tuple-element.304), channel_id=1, source_target_pairs={{0,2},{1,3},{2,0},{3,1},{4,6},{5,7},{6,4},{7,5},{8,10},{9,11},{10,... | collective-permute-start | bytes 663560 | tf_op jit(solution)/shard_map/ppermute | solution.py:587
  464.2 17.9 %collective-permute-start.50 = (f32[144,384]{1,0:T(8,128)}, f32[144,384]{1,0:T(8,128)}, u32[]{:S(2)}, u32[]{:S(2)}) collective-permute-start(f32[144,384]{1,0:T(8,128)} %get-tuple-element.300), channel_id=1, source_target_pairs={{0,1},{1,0},{2,3},{3,2},{4,5},{5,4},{6,7},{7,6},{8,9},{9,8},{10,11... | collective-permute-start | bytes 663560 | tf_op jit(solution)/shard_map/ppermute | solution.py:587
  471.9 18.9 %collective-permute-start.54 = (f32[144,384]{1,0:T(8,128)}, f32[144,384]{1,0:T(8,128)}, u32[]{:S(2)}, u32[]{:S(2)}) collective-permute-start(f32[144,384]{1,0:T(8,128)} %get-tuple-element.296), channel_id=1, source_target_pairs={{0,1},{1,0},{2,3},{3,2},{4,5},{5,4},{6,7},{7,6},{8,9},{9,8},{10,11... | collective-permute-start | bytes 663560 | tf_op jit(solution)/shard_map/ppermute | solution.py:587
  473.8 25.7 %collective-permute-start.33 = (f32[144,384]{1,0:T(8,128)}, f32[144,384]{1,0:T(8,128)}, u32[]{:S(2)}, u32[]{:S(2)}) collective-permute-start(f32[144,384]{1,0:T(8,128)} %get-tuple-element.316), channel_id=1, source_target_pairs={{0,2},{1,3},{2,0},{3,1},{4,6},{5,7},{6,4},{7,5},{8,10},{9,11},{10,... | collective-permute-start | bytes 663560 | tf_op jit(solution)/shard_map/ppermute | solution.py:587
  475.3 34.5 %collective-permute-start.37 = (f32[144,384]{1,0:T(8,128)}, f32[144,384]{1,0:T(8,128)}, u32[]{:S(2)}, u32[]{:S(2)}) collective-permute-start(f32[144,384]{1,0:T(8,128)} %get-tuple-element.312), channel_id=1, source_target_pairs={{0,1},{1,0},{2,3},{3,2},{4,5},{5,4},{6,7},{7,6},{8,9},{9,8},{10,11... | collective-permute-start | bytes 663560 | tf_op jit(solution)/shard_map/ppermute | solution.py:587
  477.4 38.3 %collective-permute-start.41 = (f32[144,384]{1,0:T(8,128)}, f32[144,384]{1,0:T(8,128)}, u32[]{:S(2)}, u32[]{:S(2)}) collective-permute-start(f32[144,384]{1,0:T(8,128)} %get-tuple-element.308), channel_id=1, source_target_pairs={{0,1},{1,0},{2,3},{3,2},{4,5},{5,4},{6,7},{7,6},{8,9},{9,8},{10,11... | collective-permute-start | bytes 663560 | tf_op jit(solution)/shard_map/ppermute | solution.py:587
  482.1 21.6 %collective-permute-start.24 = (f32[144,384]{1,0:T(8,128)}, f32[144,384]{1,0:T(8,128)}, u32[]{:S(2)}, u32[]{:S(2)}) collective-permute-start(f32[144,384]{1,0:T(8,128)} %get-tuple-element.324), channel_id=1, source_target_pairs={{0,1},{1,0},{2,3},{3,2},{4,5},{5,4},{6,7},{7,6},{8,9},{9,8},{10,11... | collective-permute-start | bytes 663560 | tf_op jit(solution)/shard_map/ppermute | solution.py:587
  490.8 16.0 %collective-permute-start.28 = (f32[144,384]{1,0:T(8,128)}, f32[144,384]{1,0:T(8,128)}, u32[]{:S(2)}, u32[]{:S(2)}) collective-permute-start(f32[144,384]{1,0:T(8,128)} %get-tuple-element.328), channel_id=1, source_target_pairs={{0,1},{1,0},{2,3},{3,2},{4,5},{5,4},{6,7},{7,6},{8,9},{9,8},{10,11... | collective-permute-start | bytes 663560 | tf_op jit(solution)/shard_map/ppermute | solution.py:587
  499.5 13.0 %collective-permute-start.20 = (f32[144,384]{1,0:T(8,128)}, f32[144,384]{1,0:T(8,128)}, u32[]{:S(2)}, u32[]{:S(2)}) collective-permute-start(f32[144,384]{1,0:T(8,128)} %get-tuple-element.320), channel_id=1, source_target_pairs={{0,2},{1,3},{2,0},{3,1},{4,6},{5,7},{6,4},{7,5},{8,10},{9,11},{10,... | collective-permute-start | bytes 663560 | tf_op jit(solution)/shard_map/ppermute | solution.py:587
  503.6 48.3 %collective-permute-start.47 = (f32[72,384]{1,0:T(8,128)}, f32[72,384]{1,0:T(8,128)}, u32[]{:S(2)}, u32[]{:S(2)}) collective-permute-start(f32[72,384]{1,0:T(8,128)} %get-tuple-element.366), channel_id=1, source_target_pairs={{0,4},{1,5},{2,6},{3,7},{4,0},{5,1},{6,2},{7,3},{8,12},{9,13},{10,... | collective-permute-start | bytes 331784 | tf_op jit(solution)/shard_map/ppermute | solution.py:587
  506.8 47.5 %collective-permute-start.51 = (f32[72,384]{1,0:T(8,128)}, f32[72,384]{1,0:T(8,128)}, u32[]{:S(2)}, u32[]{:S(2)}) collective-permute-start(f32[72,384]{1,0:T(8,128)} %get-tuple-element.361), channel_id=1, source_target_pairs={{0,4},{1,5},{2,6},{3,7},{4,0},{5,1},{6,2},{7,3},{8,12},{9,13},{10,... | collective-permute-start | bytes 331784 | tf_op jit(solution)/shard_map/ppermute | solution.py:587
  509.9 52.5 %collective-permute-start.55 = (f32[72,384]{1,0:T(8,128)}, f32[72,384]{1,0:T(8,128)}, u32[]{:S(2)}, u32[]{:S(2)}) collective-permute-start(f32[72,384]{1,0:T(8,128)} %get-tuple-element.356), channel_id=1, source_target_pairs={{0,2},{1,3},{2,0},{3,1},{4,6},{5,7},{6,4},{7,5},{8,10},{9,11},{10,... | collective-permute-start | bytes 331784 | tf_op jit(solution)/shard_map/ppermute | solution.py:587
  512.5 55.8 %collective-permute-start.34 = (f32[72,384]{1,0:T(8,128)}, f32[72,384]{1,0:T(8,128)}, u32[]{:S(2)}, u32[]{:S(2)}) collective-permute-start(f32[72,384]{1,0:T(8,128)} %get-tuple-element.381), channel_id=1, source_target_pairs={{0,4},{1,5},{2,6},{3,7},{4,0},{5,1},{6,2},{7,3},{8,12},{9,13},{10,... | collective-permute-start | bytes 331784 | tf_op jit(solution)/shard_map/ppermute | solution.py:587
  515.7 54.2 %collective-permute-start.38 = (f32[72,384]{1,0:T(8,128)}, f32[72,384]{1,0:T(8,128)}, u32[]{:S(2)}, u32[]{:S(2)}) collective-permute-start(f32[72,384]{1,0:T(8,128)} %get-tuple-element.376), channel_id=1, source_target_pairs={{0,4},{1,5},{2,6},{3,7},{4,0},{5,1},{6,2},{7,3},{8,12},{9,13},{10,... | collective-permute-start | bytes 331784 | tf_op jit(solution)/shard_map/ppermute | solution.py:587
  551.9 19.4 %collective-permute-start.42 = (f32[72,384]{1,0:T(8,128)}, f32[72,384]{1,0:T(8,128)}, u32[]{:S(2)}, u32[]{:S(2)}) collective-permute-start(f32[72,384]{1,0:T(8,128)} %get-tuple-element.371), channel_id=1, source_target_pairs={{0,2},{1,3},{2,0},{3,1},{4,6},{5,7},{6,4},{7,5},{8,10},{9,11},{10,... | collective-permute-start | bytes 331784 | tf_op jit(solution)/shard_map/ppermute | solution.py:587
  560.3 15.4 %collective-permute-start.29 = (f32[72,384]{1,0:T(8,128)}, f32[72,384]{1,0:T(8,128)}, u32[]{:S(2)}, u32[]{:S(2)}) collective-permute-start(f32[72,384]{1,0:T(8,128)} %get-tuple-element.397), channel_id=1, source_target_pairs={{0,2},{1,3},{2,0},{3,1},{4,6},{5,7},{6,4},{7,5},{8,10},{9,11},{10,... | collective-permute-start | bytes 331784 | tf_op jit(solution)/shard_map/ppermute | solution.py:587
  562.4 11.1 %collective-permute-start.21 = (f32[72,384]{1,0:T(8,128)}, f32[72,384]{1,0:T(8,128)}, u32[]{:S(2)}, u32[]{:S(2)}) collective-permute-start(f32[72,384]{1,0:T(8,128)} %get-tuple-element.386), channel_id=1, source_target_pairs={{0,4},{1,5},{2,6},{3,7},{4,0},{5,1},{6,2},{7,3},{8,12},{9,13},{10,... | collective-permute-start | bytes 331784 | tf_op jit(solution)/shard_map/ppermute | solution.py:587
  568.3 52.2 %collective-permute-start.70 = (f32[2304,384]{1,0:T(8,128)}, f32[2304,384]{1,0:T(8,128)}, u32[]{:S(2)}, u32[]{:S(2)}) collective-permute-start(f32[2304,384]{1,0:T(8,128)} %bitcast.751), channel_id=1, source_target_pairs={{0,16},{16,0},{1,17},{17,1},{2,18},{18,2},{3,19},{19,3},{4,20},{20... | collective-permute-start | bytes 10616840 | tf_op jit(solution)/shard_map/ppermute | solution.py:568
  569.9 94.7 %collective-permute-start.57 = (f32[576,2304]{1,0:T(8,128)}, f32[576,2304]{1,0:T(8,128)}, u32[]{:S(2)}, u32[]{:S(2)}) collective-permute-start(f32[576,2304]{1,0:T(8,128)} %get-tuple-element.90), channel_id=1, source_target_pairs={{0,16},{16,0},{1,17},{17,1},{2,18},{18,2},{3,19},{19,3},{4,20},{20... | collective-permute-start | bytes 15925256 | tf_op jit(solution)/shard_map/ppermute | solution.py:568
  572.0 155.0 %collective-permute-start.83 = (f32[2304,768]{1,0:T(8,128)}, f32[2304,768]{1,0:T(8,128)}, u32[]{:S(2)}, u32[]{:S(2)}) collective-permute-start(f32[2304,768]{1,0:T(8,128)} %bitcast.726), channel_id=1, source_target_pairs={{0,16},{16,0},{1,17},{17,1},{2,18},{18,2},{3,19},{19,3},{4,20},{20... | collective-permute-start | bytes 21233672 | tf_op jit(solution)/shard_map/ppermute | solution.py:568
  573.5 40.3 %collective-permute-start.48 = (f32[36,384]{1,0:T(8,128)}, f32[36,384]{1,0:T(8,128)}, u32[]{:S(2)}, u32[]{:S(2)}) collective-permute-start(f32[36,384]{1,0:T(8,128)} %bitcast.952), channel_id=1, source_target_pairs={{0,8},{1,9},{2,10},{3,11},{4,12},{5,13},{6,14},{7,15},{8,0},{9,1},... | collective-permute-start | bytes 165896 | tf_op jit(solution)/shard_map/ppermute | solution.py:587
  632.9 105.7 %collective-permute-start = (f32[576,3456]{1,0:T(8,128)}, f32[576,3456]{1,0:T(8,128)}, u32[]{:S(2)}, u32[]{:S(2)}) collective-permute-start(f32[576,3456]{1,0:T(8,128)} %get-tuple-element.76), channel_id=1, source_target_pairs={{0,16},{16,0},{1,17},{17,1},{2,18},{18,2},{3,19},{19,3},{4,20},{20... | collective-permute-start | bytes 23887880 | tf_op jit(solution)/shard_map/ppermute | solution.py:568
  658.1 11.9 %collective-permute-start.78 = (f32[144,128]{1,0:T(8,128)S(1)}, f32[144,128]{1,0:T(8,128)S(1)}, u32[]{:S(2)}, u32[]{:S(2)}) collective-permute-start(f32[144,128]{1,0:T(8,128)S(1)} %fusion.99), channel_id=1, source_target_pairs={{0,8},{1,9},{2,10},{3,11},{4,12},{5,13},{6,14},{7,15},{8,0},{9,1},... | collective-permute-start | bytes 221192 | tf_op jit(solution)/shard_map/ppermute | solution.py:587
  667.9 17.8 %collective-permute-start.58 = (f32[288,768]{1,0:T(8,128)S(1)}, f32[288,768]{1,0:T(8,128)S(1)}, u32[]{:S(2)}, u32[]{:S(2)}) collective-permute-start(f32[288,768]{1,0:T(8,128)S(1)} %get-tuple-element.164), channel_id=1, source_target_pairs={{0,1},{1,0},{2,3},{3,2},{4,5},{5,4},{6,7},{7,6},{8,9},{9,8},{10,11... | collective-permute-start | bytes 2654216 | tf_op jit(solution)/shard_map/ppermute | solution.py:587
  670.0 20.6 %collective-permute-start.62 = (f32[288,768]{1,0:T(8,128)S(1)}, f32[288,768]{1,0:T(8,128)S(1)}, u32[]{:S(2)}, u32[]{:S(2)}) collective-permute-start(f32[288,768]{1,0:T(8,128)S(1)} %bitcast.852), channel_id=1, source_target_pairs={{0,2},{1,3},{2,0},{3,1},{4,6},{5,7},{6,4},{7,5},{8,10},{9,11},{10,... | collective-permute-start | bytes 2654216 | tf_op jit(solution)/shard_map/ppermute | solution.py:587
  671.5 21.6 %collective-permute-start.66 = (f32[288,768]{1,0:T(8,128)S(1)}, f32[288,768]{1,0:T(8,128)S(1)}, u32[]{:S(2)}, u32[]{:S(2)}) collective-permute-start(f32[288,768]{1,0:T(8,128)S(1)} %bitcast.851), channel_id=1, source_target_pairs={{0,4},{1,5},{2,6},{3,7},{4,0},{5,1},{6,2},{7,3},{8,12},{9,13},{10,... | collective-permute-start | bytes 2654216 | tf_op jit(solution)/shard_map/ppermute | solution.py:587
  694.1 12.0 %collective-permute-start.67 = (f32[144,768]{1,0:T(8,128)}, f32[144,768]{1,0:T(8,128)}, u32[]{:S(2)}, u32[]{:S(2)}) collective-permute-start(f32[144,768]{1,0:T(8,128)} %get-tuple-element.200), channel_id=1, source_target_pairs={{0,1},{1,0},{2,3},{3,2},{4,5},{5,4},{6,7},{7,6},{8,9},{9,8},{10,11... | collective-permute-start | bytes 1327112 | tf_op jit(solution)/shard_map/ppermute | solution.py:587
  732.7 42.2 %collective-permute-start.84 = (f32[1152,256]{1,0:T(8,128)}, f32[1152,256]{1,0:T(8,128)}, u32[]{:S(2)}, u32[]{:S(2)}) collective-permute-start(f32[1152,256]{1,0:T(8,128)} %get-tuple-element.155), channel_id=1, source_target_pairs={{0,1},{1,0},{2,3},{3,2},{4,5},{5,4},{6,7},{7,6},{8,9},{9,8},{10,11... | collective-permute-start | bytes 3538952 | tf_op jit(solution)/shard_map/ppermute | solution.py:587
  735.7 41.9 %collective-permute-start.88 = (f32[1152,256]{1,0:T(8,128)}, f32[1152,256]{1,0:T(8,128)}, u32[]{:S(2)}, u32[]{:S(2)}) collective-permute-start(f32[1152,256]{1,0:T(8,128)} %bitcast.319), channel_id=1, source_target_pairs={{0,2},{1,3},{2,0},{3,1},{4,6},{5,7},{6,4},{7,5},{8,10},{9,11},{10,... | collective-permute-start | bytes 3538952 | tf_op jit(solution)/shard_map/ppermute | solution.py:587
  738.6 41.7 %collective-permute-start.92 = (f32[1152,256]{1,0:T(8,128)}, f32[1152,256]{1,0:T(8,128)}, u32[]{:S(2)}, u32[]{:S(2)}) collective-permute-start(f32[1152,256]{1,0:T(8,128)} %bitcast.338), channel_id=1, source_target_pairs={{0,4},{1,5},{2,6},{3,7},{4,0},{5,1},{6,2},{7,3},{8,12},{9,13},{10,... | collective-permute-start | bytes 3538952 | tf_op jit(solution)/shard_map/ppermute | solution.py:587
  744.8 74.4 %collective-permute-start.5 = (f32[288,1152]{1,0:T(8,128)}, f32[288,1152]{1,0:T(8,128)}, u32[]{:S(2)}, u32[]{:S(2)}) collective-permute-start(f32[288,1152]{1,0:T(8,128)} %bitcast.28), channel_id=1, source_target_pairs={{0,2},{1,3},{2,0},{3,1},{4,6},{5,7},{6,4},{7,5},{8,10},{9,11},{10,... | collective-permute-start | bytes 3981320 | tf_op jit(solution)/shard_map/ppermute | solution.py:587
  748.1 75.3 %collective-permute-start.9 = (f32[288,1152]{1,0:T(8,128)}, f32[288,1152]{1,0:T(8,128)}, u32[]{:S(2)}, u32[]{:S(2)}) collective-permute-start(f32[288,1152]{1,0:T(8,128)} %bitcast.42), channel_id=1, source_target_pairs={{0,4},{1,5},{2,6},{3,7},{4,0},{5,1},{6,2},{7,3},{8,12},{9,13},{10,... | collective-permute-start | bytes 3981320 | tf_op jit(solution)/shard_map/ppermute | solution.py:587
  776.6 25.7 %collective-permute-start.85 = (f32[576,256]{1,0:T(8,128)S(1)}, f32[576,256]{1,0:T(8,128)S(1)}, u32[]{:S(2)}, u32[]{:S(2)}) collective-permute-start(f32[576,256]{1,0:T(8,128)S(1)} %get-tuple-element.187), channel_id=1, source_target_pairs={{0,2},{1,3},{2,0},{3,1},{4,6},{5,7},{6,4},{7,5},{8,10},{9,11},{10,... | collective-permute-start | bytes 1769480 | tf_op jit(solution)/shard_map/ppermute | solution.py:587
  779.3 24.3 %collective-permute-start.89 = (f32[576,256]{1,0:T(8,128)S(1)}, f32[576,256]{1,0:T(8,128)S(1)}, u32[]{:S(2)}, u32[]{:S(2)}) collective-permute-start(f32[576,256]{1,0:T(8,128)S(1)} %get-tuple-element.183), channel_id=1, source_target_pairs={{0,1},{1,0},{2,3},{3,2},{4,5},{5,4},{6,7},{7,6},{8,9},{9,8},{10,11... | collective-permute-start | bytes 1769480 | tf_op jit(solution)/shard_map/ppermute | solution.py:587
  782.0 23.8 %collective-permute-start.93 = (f32[576,256]{1,0:T(8,128)S(1)}, f32[576,256]{1,0:T(8,128)S(1)}, u32[]{:S(2)}, u32[]{:S(2)}) collective-permute-start(f32[576,256]{1,0:T(8,128)S(1)} %get-tuple-element.179), channel_id=1, source_target_pairs={{0,1},{1,0},{2,3},{3,2},{4,5},{5,4},{6,7},{7,6},{8,9},{9,8},{10,11... | collective-permute-start | bytes 1769480 | tf_op jit(solution)/shard_map/ppermute | solution.py:587
  802.3 32.1 %collective-permute-start.1 = (f32[288,1152]{1,0:T(8,128)S(1)}, f32[288,1152]{1,0:T(8,128)S(1)}, u32[]{:S(2)}, u32[]{:S(2)}) collective-permute-start(f32[288,1152]{1,0:T(8,128)S(1)} %copy-done.48), channel_id=1, source_target_pairs={{0,1},{1,0},{2,3},{3,2},{4,5},{5,4},{6,7},{7,6},{8,9},{9,8},{10,11... | collective-permute-start | bytes 3981320 | tf_op jit(solution)/shard_map/ppermute | solution.py:587
  805.8 10.4 %collective-permute-start.90 = (f32[288,256]{1,0:T(8,128)S(1)}, f32[288,256]{1,0:T(8,128)S(1)}, u32[]{:S(2)}, u32[]{:S(2)}) collective-permute-start(f32[288,256]{1,0:T(8,128)S(1)} %get-tuple-element.259), channel_id=1, source_target_pairs={{0,4},{1,5},{2,6},{3,7},{4,0},{5,1},{6,2},{7,3},{8,12},{9,13},{10,... | collective-permute-start | bytes 884744 | tf_op jit(solution)/shard_map/ppermute | solution.py:587
  816.2 20.6 %collective-permute-start.87 = (f32[144,256]{1,0:T(8,128)S(1)}, f32[144,256]{1,0:T(8,128)S(1)}, u32[]{:S(2)}, u32[]{:S(2)}) collective-permute-start(f32[144,256]{1,0:T(8,128)S(1)} %fusion.67), channel_id=1, source_target_pairs={{0,8},{1,9},{2,10},{3,11},{4,12},{5,13},{6,14},{7,15},{8,0},{9,1},... | collective-permute-start | bytes 442376 | tf_op jit(solution)/shard_map/ppermute | solution.py:587
  818.6 19.9 %collective-permute-start.91 = (f32[144,256]{1,0:T(8,128)S(1)}, f32[144,256]{1,0:T(8,128)S(1)}, u32[]{:S(2)}, u32[]{:S(2)}) collective-permute-start(f32[144,256]{1,0:T(8,128)S(1)} %fusion.63), channel_id=1, source_target_pairs={{0,8},{1,9},{2,10},{3,11},{4,12},{5,13},{6,14},{7,15},{8,0},{9,1},... | collective-permute-start | bytes 442376 | tf_op jit(solution)/shard_map/ppermute | solution.py:587
  819.3 20.0 %collective-permute-start.95 = (f32[144,256]{1,0:T(8,128)S(1)}, f32[144,256]{1,0:T(8,128)S(1)}, u32[]{:S(2)}, u32[]{:S(2)}) collective-permute-start(f32[144,256]{1,0:T(8,128)S(1)} %fusion.59), channel_id=1, source_target_pairs={{0,8},{1,9},{2,10},{3,11},{4,12},{5,13},{6,14},{7,15},{8,0},{9,1},... | collective-permute-start | bytes 442376 | tf_op jit(solution)/shard_map/ppermute | solution.py:587
  823.4 25.2 %collective-permute-start.6 = (f32[144,1152]{1,0:T(8,128)S(1)}, f32[144,1152]{1,0:T(8,128)S(1)}, u32[]{:S(2)}, u32[]{:S(2)}) collective-permute-start(f32[144,1152]{1,0:T(8,128)S(1)} %get-tuple-element.171), channel_id=1, source_target_pairs={{0,1},{1,0},{2,3},{3,2},{4,5},{5,4},{6,7},{7,6},{8,9},{9,8},{10,11... | collective-permute-start | bytes 1990664 | tf_op jit(solution)/shard_map/ppermute | solution.py:587
  834.3 26.2 %collective-permute-start.10 = (f32[144,1152]{1,0:T(8,128)}, f32[144,1152]{1,0:T(8,128)}, u32[]{:S(2)}, u32[]{:S(2)}) collective-permute-start(f32[144,1152]{1,0:T(8,128)} %get-tuple-element.175), channel_id=1, source_target_pairs={{0,1},{1,0},{2,3},{3,2},{4,5},{5,4},{6,7},{7,6},{8,9},{9,8},{10,11... | collective-permute-start | bytes 1990664 | tf_op jit(solution)/shard_map/ppermute | solution.py:587
  836.7 32.7 %collective-permute-start.2 = (f32[144,1152]{1,0:T(8,128)}, f32[144,1152]{1,0:T(8,128)}, u32[]{:S(2)}, u32[]{:S(2)}) collective-permute-start(f32[144,1152]{1,0:T(8,128)} %get-tuple-element.167), channel_id=1, source_target_pairs={{0,2},{1,3},{2,0},{3,1},{4,6},{5,7},{6,4},{7,5},{8,10},{9,11},{10,... | collective-permute-start | bytes 1990664 | tf_op jit(solution)/shard_map/ppermute | solution.py:587
  850.9 29.4 %collective-permute-start.7 = (f32[72,1152]{1,0:T(8,128)}, f32[72,1152]{1,0:T(8,128)}, u32[]{:S(2)}, u32[]{:S(2)}) collective-permute-start(f32[72,1152]{1,0:T(8,128)} %get-tuple-element.244), channel_id=1, source_target_pairs={{0,4},{1,5},{2,6},{3,7},{4,0},{5,1},{6,2},{7,3},{8,12},{9,13},{10,... | collective-permute-start | bytes 995336 | tf_op jit(solution)/shard_map/ppermute | solution.py:587
  864.1 19.6 %collective-permute-start.11 = (f32[72,1152]{1,0:T(8,128)}, f32[72,1152]{1,0:T(8,128)}, u32[]{:S(2)}, u32[]{:S(2)}) collective-permute-start(f32[72,1152]{1,0:T(8,128)} %get-tuple-element.249), channel_id=1, source_target_pairs={{0,2},{1,3},{2,0},{3,1},{4,6},{5,7},{6,4},{7,5},{8,10},{9,11},{10,... | collective-permute-start | bytes 995336 | tf_op jit(solution)/shard_map/ppermute | solution.py:587
  883.7 17.8 %collective-permute-start.8 = (f32[36,1152]{1,0:T(8,128)}, f32[36,1152]{1,0:T(8,128)S(1)}, u32[]{:S(2)}, u32[]{:S(2)}) collective-permute-start(f32[36,1152]{1,0:T(8,128)} %fusion.53), channel_id=1, source_target_pairs={{0,8},{1,9},{2,10},{3,11},{4,12},{5,13},{6,14},{7,15},{8,0},{9,1},... | collective-permute-start | bytes 497672 | tf_op jit(solution)/shard_map/ppermute | solution.py:587
  885.6 19.9 %collective-permute-start.12 = (f32[36,1152]{1,0:T(8,128)}, f32[36,1152]{1,0:T(8,128)}, u32[]{:S(2)}, u32[]{:S(2)}) collective-permute-start(f32[36,1152]{1,0:T(8,128)} %fusion.50), channel_id=1, source_target_pairs={{0,8},{1,9},{2,10},{3,11},{4,12},{5,13},{6,14},{7,15},{8,0},{9,1},... | collective-permute-start | bytes 497672 | tf_op jit(solution)/shard_map/ppermute | solution.py:587
  892.7 14.7 %collective-permute-start.4 = (f32[36,1152]{1,0:T(8,128)S(1)}, f32[36,1152]{1,0:T(8,128)S(1)}, u32[]{:S(2)}, u32[]{:S(2)}) collective-permute-start(f32[36,1152]{1,0:T(8,128)S(1)} %bitcast.943), channel_id=1, source_target_pairs={{0,8},{1,9},{2,10},{3,11},{4,12},{5,13},{6,14},{7,15},{8,0},{9,1},... | collective-permute-start | bytes 497672 | tf_op jit(solution)/shard_map/ppermute | solution.py:587
  (145 other events, 1435.7 us)
Sparse Core Ops, SparseCore 0:
  295.5 81.3 all-gather.2

commit v2 on v1

--- a/solution.py
+++ b/solution.py
@@ -12,6 +12,7 @@
 BF16 = jnp.bfloat16
 HIGHEST = lax.Precision.HIGHEST
 NORM_EPS = 1e-06
+ROW_PARTS = ((2, 0), (1, 2))
 ROW = 256
 GROUP = 1024
 NN = (((1,), (0,)), ((), ()))
@@ -19,6 +20,8 @@
 TN = (((0,), (0,)), ((), ()))
 TT = (((0,), (1,)), ((), ()))
 VMEM_LIMIT = 60 << 20
+COLUMNS = 384
+UNITS = 512
 
 
 def dot(left, right, dims=NN, precision=None):
@@ -30,7 +33,7 @@
         body,
         name=name,
         compiler_params=pltpu.CompilerParams(vmem_limit_bytes=VMEM_LIMIT),
-        cost_estimate=pl.CostEstimate(flops=flops, bytes_accessed=moved, transcendentals=0),
+        cost_estimate=pl.CostEstimate(flops=flops // 8, bytes_accessed=moved // 8, transcendentals=0),
         **kwargs,
     )
 
@@ -66,7 +69,7 @@
 def qkv_call(x, mod, w, bias):
     tokens, width = x.shape
     wide = w.shape[1]
-    block = 384
+    block = width
     return call(
         qkv_body,
         "qkv",
@@ -172,18 +175,20 @@
 
 
 def attention_back_body(
-    flag_ref, qkv_ref, do_ref, p_ref, ot_ref, out_ref, ds_ref, *, width, head_width
+    flag_ref, qkv_ref, do_ref, p_ref, ot_ref, *refs, width, head_width, first_pair, span
 ):
-    pair = pl.program_id(1)
+    out_ref, ready_ref, ds_ref = refs[-3:]
+    step = pl.program_id(1)
+    pair = step + first_pair
     column = pair * (2 * head_width)
     start = pl.multiple_of(column // 128 * 128, 128)
     select = pair_select(column - start, head_width)
     scale = 1.0 / math.sqrt(head_width)
     tokens = qkv_ref.shape[0]
 
-    @pl.when(pair == 0)
+    @pl.when(step == 0)
     def _():
-        out_ref[...] = jnp.zeros_like(out_ref)
+        out_ref[...] = refs[0][...] if len(refs) > 3 else jnp.zeros_like(out_ref)
 
     q = dot(qkv_ref[:, pl.ds(start, 256)], select).astype(BF16)
     k = dot(qkv_ref[:, pl.ds(width + start, 256)], select).astype(BF16)
@@ -239,34 +244,47 @@
     def _():
         run(ROW)
 
-
-def attention_back_call(flag, qkv, do, probs, mixed):
+    @pl.when(step == pl.num_programs(1) - 1)
+    def _():
+        first, size = span
+        for third in range(3):
+            at = third * width + first
+            ready_ref[:, third * size : (third + 1) * size] = out_ref[:, at : at + size]
+
+
+def attention_back_call(flag, qkv, do, probs, mixed, part, *before):
     tokens, wide = qkv.shape
     width = wide // 3
     heads, head_width = mixed.shape[:2]
     groups = tokens // GROUP
-    return call(
-        functools.partial(attention_back_body, width=width, head_width=head_width),
+    pairs = heads // 4
+    base = part * pairs
+    cut = width // 2 // 128 * 128
+    span = (cut, width - cut) if part else (0, cut)
+    whole = pl.BlockSpec((GROUP, wide), lambda g, h: (g, 0))
+    return call(
+        functools.partial(attention_back_body, width=width, head_width=head_width, first_pair=base, span=span),
         "attention_back",
-        4 * 2 * heads * tokens * GROUP * 256,
-        4 * tokens * wide + 2 * heads * tokens * GROUP + 6 * tokens * width,
-        grid=(groups, heads // 2),
+        2 * 2 * heads * tokens * GROUP * 256,
+        4 * tokens * wide + heads * tokens * GROUP + 6 * tokens * width,
+        grid=(groups, pairs),
         in_specs=[
             pl.BlockSpec(memory_space=pltpu.SMEM),
-            pl.BlockSpec((GROUP, wide), lambda g, h: (g, 0)),
+            whole,
             pl.BlockSpec((GROUP, width), lambda g, h: (g, 0)),
-            pl.BlockSpec((2, GROUP, GROUP), lambda g, h: (h, 0, g)),
-            pl.BlockSpec((2, head_width, GROUP), lambda g, h: (h, 0, g)),
-        ],
-        out_specs=pl.BlockSpec((GROUP, wide), lambda g, h: (g, 0)),
-        out_shape=shaped((tokens, wide), BF16),
+            pl.BlockSpec((2, GROUP, GROUP), lambda g, h: (base + h, 0, g)),
+            pl.BlockSpec((2, head_width, GROUP), lambda g, h: (base + h, 0, g)),
+        ]
+        + [whole] * len(before),
+        out_specs=[whole, pl.BlockSpec((GROUP, 3 * span[1]), lambda g, h: (g, 0))],
+        out_shape=[shaped((tokens, wide), BF16), shaped((tokens, 3 * span[1]), BF16)],
         scratch_shapes=[pltpu.VMEM((2, GROUP, GROUP), BF16)],
-    )(flag, qkv, do, probs, mixed)
+    )(flag, qkv, do, probs, mixed, *before)
 
 
 def middle_body(
-    om_ref, w_ref, b_ref, x_ref, mod_ref, top_ref, keep_ref, perm_ref,
-    a_ref, x1_ref, h_ref, hp_ref, dm_ref, sum_ref,
+    om_ref, w_ref, b_ref, x_ref, mod_ref, top_ref, keep_ref, away_ref, own_ref,
+    a_ref, x1_ref, h_ref, h_away_ref, h_own_ref, dm_ref, sum_ref,
 ):
     tile = pl.program_id(0)
     branch = dot(om_ref[...], w_ref[...]) + b_ref[...]
@@ -276,16 +294,18 @@
     normal, _ = normed(middle)
     hidden = (normal * (1.0 + mod_ref[tile, 4:5]) + mod_ref[tile, 3:4]).astype(BF16)
     h_ref[...] = hidden
-    hp_ref[...] = dot(hidden, perm_ref[...]).astype(BF16)
+    h_away_ref[...] = dot(hidden, away_ref[...]).astype(BF16)
+    h_own_ref[...] = dot(hidden, own_ref[...]).astype(BF16)
     grad = (top_ref[...].astype(F32) * mod_ref[tile, 5:6] * keep_ref[...]).astype(BF16)
     dm_ref[...] = grad
     sum_ref[0] = jnp.sum(grad.astype(F32), axis=0, keepdims=True)
 
 
-def middle_call(om, w, bias, x, mod, top, keep, perm):
+def middle_call(om, w, bias, x, mod, top, keep, away, own):
     tokens, width = x.shape
     tiles = tokens // ROW
     rows = pl.BlockSpec((ROW, width), lambda i: (i, 0))
+    half = pl.BlockSpec((ROW, width // 2), lambda i: (i, 0))
     fixed = pl.BlockSpec((width, width), lambda i: (0, 0))
     return call(
         middle_body,
@@ -301,21 +321,24 @@
             pl.BlockSpec(mod.shape, lambda i: (0, 0, 0)),
             rows,
             pl.BlockSpec((ROW, 1), lambda i: (i, 0)),
-            fixed,
-        ],
-        out_specs=[rows, rows, rows, rows, rows, pl.BlockSpec((1, 1, width), lambda i: (i, 0, 0))],
+            pl.BlockSpec((width, width // 2), lambda i: (0, 0)),
+            pl.BlockSpec((width, width // 2), lambda i: (0, 0)),
+        ],
+        out_specs=[rows, rows, rows, half, half, rows, pl.BlockSpec((1, 1, width), lambda i: (i, 0, 0))],
         out_shape=[
             shaped((tokens, width), F32),
             shaped((tokens, width), F32),
             shaped((tokens, width), BF16),
-            shaped((tokens, width), BF16),
+            shaped((tokens, width // 2), BF16),
+            shaped((tokens, width // 2), BF16),
             shaped((tokens, width), BF16),
             shaped((tiles, 1, width), F32),
         ],
-    )(om, w, bias, x, mod, top, keep, perm)
-
-
-def hidden_body(h_ref, hp_ref, dm_ref, w1_ref, b1_ref, w2_ref, g_ref, df_ref, sum_ref, send_ref, keep_ref):
+    )(om, w, bias, x, mod, top, keep, away, own)
+
+
+def hidden_body(h_ref, away_ref, dm_ref, w1_ref, b1_ref, w2_ref, *refs):
+    g_ref, df_ref, sum_ref, send_ref = refs[-4:]
     first, second = math.sqrt(2.0 / math.pi), 0.044715
     pre = dot(h_ref[...], w1_ref[...]) + b1_ref[...]
     square = pre * pre
@@ -326,17 +349,17 @@
     grad = (dot(dm_ref[...], w2_ref[...], NT) * slope).astype(BF16)
     df_ref[...] = grad
     sum_ref[...] = jnp.sum(grad.astype(F32), axis=0, keepdims=True)
-    half_rows = send_ref.shape[0]
-    send_ref[...] = dot(hp_ref[:, half_rows:], grad, TN)
-    keep_ref[...] = dot(hp_ref[:, :half_rows], grad, TN)
-
-
-def hidden_call(h, hp, dm, w1, b1, w2, first, count):
+    send_ref[...] = dot(away_ref[...], grad, TN)
+
+
+def hidden_call(h, away, dm, w1, b1, w2, first, count, before):
     tokens, width = h.shape
-    block = 384
+    hidden = w1.shape[1]
+    block = UNITS
     base = first // block
     full = pl.BlockSpec((tokens, width), lambda j: (0, 0))
     half = width // 2
+    place = pl.BlockSpec(memory_space=pl.ANY)
     return call(
         hidden_body,
         "hidden",
@@ -345,64 +368,132 @@
         grid=(count // block,),
         in_specs=[
             full,
-            full,
+            pl.BlockSpec((tokens, half), lambda j: (0, 0)),
             full,
             pl.BlockSpec((width, block), lambda j: (0, base + j)),
             pl.BlockSpec((1, block), lambda j: (0, base + j)),
             pl.BlockSpec((block, width), lambda j: (base + j, 0)),
-        ],
+        ]
+        + [place] * len(before),
         out_specs=[
-            pl.BlockSpec((tokens, block), lambda j: (0, j)),
-            pl.BlockSpec((tokens, block), lambda j: (0, j)),
-            pl.BlockSpec((1, block), lambda j: (0, j)),
+            pl.BlockSpec((tokens, block), lambda j: (0, base + j)),
+            pl.BlockSpec((tokens, block), lambda j: (0, base + j)),
+            pl.BlockSpec((1, block), lambda j: (0, base + j)),
             pl.BlockSpec((half, block), lambda j: (0, j)),
-            pl.BlockSpec((half, block), lambda j: (0, j)),
         ],
         out_shape=[
-            shaped((tokens, count), BF16),
-            shaped((tokens, count), BF16),
-            shaped((1, count), F32),
+            shaped((tokens, hidden), BF16),
+            shaped((tokens, hidden), BF16),
+            shaped((1, hidden), F32),
             shaped((half, count), F32),
-            shaped((half, count), F32),
-        ],
-    )(h, hp, dm, w1, b1, w2)
-
-
-def rows_grad_body(side_ref, spot_ref, *refs, pieces):
-    g_refs, dm_ref, out_ref = refs[:pieces], refs[pieces], refs[pieces + 1]
-    shard = out_ref.shape[1]
-    grad = dm_ref[...]
+        ],
+        input_output_aliases={6 + n: n for n in range(len(before))},
+    )(h, away, dm, w1, b1, w2, *before)
+
+
+def shard_rows(spot_ref, g_ref, grad, put):
+    shards = spot_ref.shape[1]
+    rows = g_ref.shape[1] // 2
+    shard = g_ref.shape[1] // shards
+    part = pl.program_id(0)
     place = 0
-    for g_ref in g_refs:
-        made = dot(g_ref[...], grad, TN)
-        for at in range(0, made.shape[0], shard):
-            out_ref[spot_ref[place]] = made[at : at + shard]
+    for piece in range(2):
+        made = dot(g_ref[:, piece * rows : (piece + 1) * rows], grad, TN)
+        for at in range(0, rows, shard):
+            put(spot_ref[part, place], made[at : at + shard])
             place += 1
 
 
-def rows_grad_call(side, spots, g, dm, first, count, shards):
+def rows_send_body(side_ref, spot_ref, g_ref, dm_ref, out_ref):
+    def put(spot, value):
+        out_ref[spot] = value
+
+    shard_rows(spot_ref, g_ref, dm_ref[...], put)
+
+
+def rows_send_call(side, spots, g, dm):
     tokens, hidden = g.shape
+    width = dm.shape[1]
     half = hidden // 2
-    block = 128
-    pieces = 2
-    base = first // block
-    specs = [
-        pl.BlockSpec((tokens, half // pieces), functools.partial(lambda j, side, spots, n: (0, side[0] * pieces + n), n=n))
-        for n in range(pieces)
-    ]
-    return call(
-        functools.partial(rows_grad_body, pieces=pieces),
-        "rows_grad",
-        2 * tokens * half * count,
-        2 * tokens * half + 2 * tokens * count + 4 * half * count,
+    shards = spots.shape[1]
+    return call(
+        rows_send_body,
+        "rows_send",
+        2 * tokens * half * width,
+        2 * tokens * (half + width) + 4 * half * width,
         grid_spec=pltpu.PrefetchScalarGridSpec(
             num_scalar_prefetch=2,
-            grid=(count // block,),
-            in_specs=specs + [pl.BlockSpec((tokens, block), lambda j, side, spots: (0, base + j))],
-            out_specs=pl.BlockSpec((shards, half // shards, block), lambda j, side, spots: (0, 0, j)),
+            grid=(width // COLUMNS,),
+            in_specs=[
+                pl.BlockSpec((tokens, half), lambda j, side, spots: (0, side[0])),
+                pl.BlockSpec((tokens, COLUMNS), lambda j, side, spots: (0, j)),
+            ],
+            out_specs=pl.BlockSpec((shards, half // shards, COLUMNS), lambda j, side, spots: (0, 0, j)),
         ),
-        out_shape=shaped((shards, half // shards, count), F32),
-    )(side, spots, *([g] * pieces), dm)
+        out_shape=shaped((shards, half // shards, width), F32),
+    )(side, spots, g, dm)
+
+
+def rows_keep_body(side_ref, spot_ref, g_ref, dm_ref, got_ref, *outs, bounds):
+    half = spot_ref.shape[1] // 2
+    step = pl.program_id(0)
+    for part in range(len(bounds) - 1):
+
+        @pl.when((step >= bounds[part]) & (step < bounds[part + 1]))
+        def _():
+            def put(spot, value):
+                value = value + got_ref[spot]
+
+                @pl.when(spot < half)
+                def _():
+                    outs[2 * part + 1][jnp.minimum(spot, half - 1)] = value
+
+                @pl.when(spot >= half)
+                def _():
+                    outs[2 * part][jnp.maximum(spot - half, 0)] = value
+
+            shard_rows(spot_ref, g_ref, dm_ref[...], put)
+
+
+def rows_keep_call(side, spots, g, dm, got, counts):
+    tokens, hidden = g.shape
+    width = dm.shape[1]
+    half = hidden // 2
+    steps, shards = spots.shape
+    bounds = [sum(counts[:n]) for n in range(len(counts) + 1)]
+    specs, shapes = [], []
+    for part, count in enumerate(counts):
+        for _ in range(2):
+            specs.append(
+                pl.BlockSpec(
+                    (shards // 2, half // shards, COLUMNS),
+                    functools.partial(
+                        lambda j, side, spots, first, count: (0, 0, jnp.clip(j - first, 0, count - 1)),
+                        first=bounds[part],
+                        count=count,
+                    ),
+                )
+            )
+            shapes.append(shaped((shards // 2, half // shards, count * COLUMNS), F32))
+    made = call(
+        functools.partial(rows_keep_body, bounds=bounds),
+        "rows_keep",
+        2 * tokens * half * width,
+        2 * tokens * (half + width) + 8 * half * width,
+        grid_spec=pltpu.PrefetchScalarGridSpec(
+            num_scalar_prefetch=2,
+            grid=(steps,),
+            in_specs=[
+                pl.BlockSpec((tokens, half), lambda j, side, spots: (0, side[0])),
+                pl.BlockSpec((tokens, COLUMNS), lambda j, side, spots: (0, j)),
+                pl.BlockSpec((shards, half // shards, COLUMNS), lambda j, side, spots: (0, 0, j)),
+            ],
+            out_specs=specs,
+        ),
+        out_shape=shapes,
+    )(side, spots, g, dm, got)
+    made = [array.reshape(-1, array.shape[2]) for array in made]
+    return list(zip(made[::2], made[1::2]))
 
 
 def result_body(g_ref, w_ref, b_ref, x1_ref, mod_ref, top_ref, keep_ref, out_ref, sum_ref):
@@ -487,39 +578,118 @@
     )(df, w1, x1, mod, top, a, wp, head_rows)
 
 
-def columns_grad_body(left_ref, perm_ref, right_ref, send_ref, keep_ref, sum_ref, moved_ref):
-    @pl.when(pl.program_id(0) == 0)
-    def _():
-        moved_ref[...] = dot(left_ref[...], perm_ref[...]).astype(BF16)
-
-    half = send_ref.shape[0]
-    grad = right_ref[...]
-    send_ref[...] = dot(moved_ref[:, half:], grad, TN)
-    keep_ref[...] = dot(moved_ref[:, :half], grad, TN)
-    sum_ref[...] = jnp.sum(grad.astype(F32), axis=0, keepdims=True)
-
-
-def columns_grad_call(left, perm, right, name):
+def step_of(counts):
+    return next(size for size in (512, 640, 384, 128) if all(count % size == 0 for count in counts))
+
+
+def operand_specs(pairs, step):
+    specs, starts, at = [], [], 0
+    for left, _, first, count in pairs:
+        base, steps = first // step, count // step
+        specs.append(pl.BlockSpec(left.shape, lambda j: (0, 0)))
+        specs.append(
+            pl.BlockSpec(
+                (left.shape[0], step),
+                functools.partial(lambda j, at, base, steps: (0, base + jnp.clip(j - at, 0, steps - 1)), at=at, base=base, steps=steps),
+            )
+        )
+        starts.append(at)
+        at += steps
+    return specs, starts + [at]
+
+
+def each_pair(starts, body):
+    if len(starts) == 2:
+        body(0)
+        return
+    step = pl.program_id(0)
+    for number in range(len(starts) - 1):
+        pl.when((step >= starts[number]) & (step < starts[number + 1]))(functools.partial(body, number))
+
+
+def columns_send_body(*refs, starts):
+    send_ref, sum_ref = refs[-2:]
+
+    def run(number):
+        grad = refs[2 * number + 1][...]
+        send_ref[...] = dot(refs[2 * number][...], grad, TN)
+        sum_ref[...] = jnp.sum(grad.astype(F32), axis=0, keepdims=True)
+
+    each_pair(starts, run)
+
+
+def columns_send_call(pairs, name):
+    tokens, half = pairs[0][0].shape
+    count = sum(pair[3] for pair in pairs)
+    step = step_of([pair[3] for pair in pairs])
+    specs, starts = operand_specs(pairs, step)
+    return call(
+        functools.partial(columns_send_body, starts=starts),
+        name,
+        2 * tokens * half * count,
+        2 * tokens * (count + half) + 4 * half * count,
+        grid=(count // step,),
+        in_specs=specs,
+        out_specs=[
+            pl.BlockSpec((half, step), lambda j: (0, j)),
+            pl.BlockSpec((1, step), lambda j: (0, j)),
+        ],
+        out_shape=[shaped((half, count), F32), shaped((1, count), F32)],
+    )(*[array for pair in pairs for array in pair[:2]])
+
+
+def columns_keep_body(*refs, starts):
+    got_ref, send_ref, keep_ref = refs[-3:]
+    rows = keep_ref.shape[0]
+
+    def run(number):
+        made = dot(refs[2 * number][...], refs[2 * number + 1][...], TN) + got_ref[...]
+        send_ref[...] = made[rows:]
+        keep_ref[...] = made[:rows]
+
+    each_pair(starts, run)
+
+
+def columns_keep_call(pairs, got, name):
+    tokens, half = pairs[0][0].shape
+    count = got.shape[1]
+    step = step_of([pair[3] for pair in pairs])
+    specs, starts = operand_specs(pairs, step)
+    out = pl.BlockSpec((half // 2, step), lambda j: (0, j))
+    made = call(
+        functools.partial(columns_keep_body, starts=starts),
+        name,
+        2 * tokens * half * count,
+        2 * tokens * (count + half) + 8 * half * count,
+        grid=(count // step,),
+        in_specs=specs + [pl.BlockSpec((half, step), lambda j: (0, j))],
+        out_specs=[out, out],
+        out_shape=[shaped((half // 2, count), F32)] * 2,
+    )(*[array for pair in pairs for array in pair[:2]], got)
+    return [tuple(made)]
+
+
+def moved_body(left_ref, away_ref, own_ref, left_away_ref, left_own_ref):
+    left_away_ref[...] = dot(left_ref[...], away_ref[...]).astype(BF16)
+    left_own_ref[...] = dot(left_ref[...], own_ref[...]).astype(BF16)
+
+
+def moved_call(left, away, own):
     tokens, width = left.shape
-    wide = right.shape[1]
     half = width // 2
-    block = 384
-    out = pl.BlockSpec((half, block), lambda j: (0, j))
-    return call(
-        columns_grad_body,
-        name,
-        2 * tokens * width * (wide + width),
-        2 * tokens * (wide + width) + 2 * width * width + 4 * width * wide,
-        grid=(wide // block,),
-        in_specs=[
-            pl.BlockSpec((tokens, width), lambda j: (0, 0)),
-            pl.BlockSpec((width, width), lambda j: (0, 0)),
-            pl.BlockSpec((tokens, block), lambda j: (0, j)),
-        ],
-        out_specs=[out, out, pl.BlockSpec((1, block), lambda j: (0, j))],
-        out_shape=[shaped((half, wide), F32), shaped((half, wide), F32), shaped((1, wide), F32)],
-        scratch_shapes=[pltpu.VMEM((tokens, width), BF16)],
-    )(left, perm, right)
+    block = tokens // 2
+    fixed = pl.BlockSpec((width, half), lambda i: (0, 0))
+    out = pl.BlockSpec((block, half), lambda i: (i, 0))
+    return call(
+        moved_body,
+        "moved",
+        2 * tokens * width * width,
+        4 * tokens * width + 2 * width * width,
+        grid=(2,),
+        in_specs=[pl.BlockSpec((block, width), lambda i: (i, 0)), fixed, fixed],
+        out_specs=[out, out],
+        out_shape=[shaped((tokens, half), BF16)] * 2,
+    )(left, away, own)
 
 
 def first_back_body(dqkv_ref, w_ref, x_ref, mod_ref, dx_ref, out_ref, sum_ref):
@@ -554,49 +724,248 @@
     )(dqkv, w, x, mod, dx)
 
 
-def bit_order(lead, bits):
-    return [lead] + [bit for bit in range(bits) if bit != lead]
-
-
-def part_orders(bits):
-    if bits < 3:
-        return [list(range(bits))]
-    return [bit_order(lead, bits) for lead in range(3)]
-
-
-def scatter_sum(send, keep, bits, orders=None):
-    received = lax.ppermute(send, "stream", [(0, 1), (1, 0)])
-    rows, wide = keep.shape
-    orders = orders or part_orders(bits)
-    share = wide // len(orders)
-    results = []
-    for number, order in enumerate(orders):
-        columns = slice(number * share, number * share + share)
-        terms = [keep[:, columns], received[:, columns]]
-        left = list(range(bits))
-        count = rows
-        for bit in order:
-            before = 1 << left.index(bit)
-            after = count // (2 * before)
-
-            def pick(term, which):
-                return term.reshape(before, 2, after, share)[:, which].reshape(count // 2, share)
-
-            sent = functools.reduce(lambda x, y: x + y, [pick(term, 1) for term in terms])
-            pairs = [(i, i ^ (1 << bit)) for i in range(1 << bits)]
-            terms = [pick(term, 0) for term in terms] + [lax.ppermute(sent, "batch", pairs)]
-            left.remove(bit)
-            count //= 2
-        results.append(functools.reduce(lambda x, y: x + y, terms))
-    return results
-
-
-def device_offsets(bits):
+def modulation_back_body(
+    me_ref, own_ref, other_ref, own_cond_ref, other_cond_ref, label_ref, w_ref,
+    grad_ref, sum_ref, table_ref, act_ref, total_ref,
+):
+    step = pl.program_id(0)
+    half = own_ref.shape[0]
+    width = act_ref.shape[1]
+
+    @pl.when(step == 0)
+    def _():
+        for at, cond_ref in ((0, own_cond_ref), (half, other_cond_ref)):
+            cond = cond_ref[...]
+            act_ref[at : at + half] = (cond / (1.0 + jnp.exp(-cond))).astype(BF16)
+
+    mod = jnp.concatenate([own_ref[...], other_ref[...]], axis=0)
+    sum_ref[...] = jnp.sum(mod, axis=0, keepdims=True)
+    mod = mod.astype(BF16)
+    shard = grad_ref.shape[0]
+    row = lax.broadcasted_iota(jnp.int32, (width, 128), 0)
+    column = lax.broadcasted_iota(jnp.int32, (width, 128), 1)
+    picked = jnp.where((column < shard) & (row == me_ref[0] * shard + column), 1.0, 0.0).astype(BF16)
+    own_act = dot(act_ref[...], picked).astype(BF16)
+    grad_ref[...] = dot(own_act, mod, TN)[:shard]
+    part = dot(mod, w_ref[...], NT)
+
+    @pl.when(step == 0)
+    def _():
+        total_ref[...] = part
+
+    @pl.when(step > 0)
+    def _():
+        total_ref[...] += part
+
+    @pl.when(step == pl.num_programs(0) - 1)
+    def _():
+        cond = jnp.concatenate([own_cond_ref[...], other_cond_ref[...]], axis=0)
+        gate = 1.0 / (1.0 + jnp.exp(-cond))
+        grad = total_ref[...] * (gate * (1.0 + cond * (1.0 - gate)))
+        classes = table_ref.shape[0]
+        select = (label_ref[...] == lax.broadcasted_iota(jnp.int32, (2 * half, classes), 1)).astype(F32)
+        table_ref[...] = dot(select, grad, TN, HIGHEST)
+
+
+def modulation_back_call(me, own, other, used, w, classes, shard):
+    rows = own.shape[0]
+    width, wide = w.shape
+    block = 768
+    at = wide // width
+    part = pl.BlockSpec((rows, block), lambda j: (0, j))
+    cond = pl.BlockSpec((rows, width), lambda j: (0, at))
+    return call(
+        modulation_back_body,
+        "modulation_back",
+        4 * rows * width * wide,
+        2 * width * wide,
+        grid=(wide // block,),
+        in_specs=[
+            pl.BlockSpec(memory_space=pltpu.SMEM),
+            part,
+            part,
+            cond,
+            cond,
+            pl.BlockSpec(used.shape, lambda j: (0, 0)),
+            pl.BlockSpec((width, block), lambda j: (0, j)),
+        ],
+        out_specs=[
+            pl.BlockSpec((shard, block), lambda j: (0, j)),
+            pl.BlockSpec((1, block), lambda j: (0, j)),
+            pl.BlockSpec((classes, width), lambda j: (0, 0)),
+        ],
+        out_shape=[shaped((shard, wide), F32), shaped((1, wide), F32), shaped((classes, width), F32)],
+        scratch_shapes=[pltpu.VMEM((2 * rows, width), BF16), pltpu.VMEM((2 * rows, width), F32)],
+    )(me, own, other, own, other, used, w)
+
+
+def add_body(*refs, plans):
+    outs = refs[-len(plans) :]
+    at = 0
+    for out_ref, (count, first, rows) in zip(outs, plans):
+        value = refs[at][first : first + rows]
+        for term in range(1, count):
+            value = value + refs[at + term][first : first + rows]
+        out_ref[...] = value
+        at += count
+
+
+def add_call(jobs):
+    steps = 3 if all(terms[0].shape[1] % 384 == 0 for terms, _, _ in jobs) else 2
+    if any(terms[0].shape[1] % (128 * steps) for terms, _, _ in jobs):
+        steps = 1
+    operands, specs, outs, shapes, plans = [], [], [], [], []
+    moved = 0
+    for terms, first, rows in jobs:
+        wide = terms[0].shape[1]
+        block = wide // steps
+        for term in terms:
+            size, index, at = rows, first // rows, 0
+            while size % 8 and size < term.shape[0]:
+                size, index, at = size * 2, 0, first
+            operands.append(term)
+            specs.append(pl.BlockSpec((size, block), functools.partial(lambda j, index: (index, j), index=index)))
+        plans.append((len(terms), at, rows))
+        outs.append(pl.BlockSpec((rows, block), lambda j: (0, j)))
+        shapes.append(shaped((rows, wide), F32))
+        moved += 4 * rows * wide * (len(terms) + 1)
+    return call(
+        functools.partial(add_body, plans=plans),
+        "add",
+        moved // 4,
+        moved,
+        grid=(steps,),
+        in_specs=specs,
+        out_specs=outs,
+        out_shape=shapes,
+    )(*operands)
+
+
+def bit_order(bits, core, lead):
+    order = list(range(bits))
+    if bits >= 2 and core:
+        order[:2] = [1, 0]
+    if lead and lead < bits:
+        order.remove(lead)
+        order.insert(0, lead)
+    return order
+
+
+class Chunk:
+    def __init__(self, send, kept, wait, lead):
+        self.send, self.terms, self.wait, self.lead = send, [kept], wait, lead
+        self.rows = kept.shape[0]
+        self.stage = 0
+
+
+class Spread:
+    def __init__(self, rows):
+        self.own, self.other = rows, None
+        self.stage = 0
+
+
+class Flow:
+    def __init__(self, bits):
+        self.bits = bits
+        self.fresh, self.crossing, self.chunks, self.last = [], [], [], []
+        self.blocks = ([], [], [])
+        self.spreads = []
+
+    def emit(self, send, keep, store, waits=(0,), leads=(0,)):
+        self.fresh.append((send, keep, store, waits, leads))
+
+    def spread(self, rows):
+        self.spreads.append(Spread(rows))
+        return self.spreads[-1]
+
+    def busy(self):
+        moving = self.fresh or self.crossing or any(chunk.stage < self.bits for chunk in self.chunks)
+        return moving or any(spread.stage <= self.bits for spread in self.spreads)
+
+    def pairs(self, stage, lead):
+        size = 1 << self.bits
+        flips = [1 << bit_order(self.bits, core, lead)[stage] for core in range(2)]
+        return [(core * size + i, core * size + (i ^ flips[core])) for core in range(2) for i in range(size)]
+
+    def received(self, live):
+        live, (cores, blocks, doubles) = lax.optimization_barrier((live, self.blocks))
+        for spread, block in zip([spread for spread in self.spreads if spread.other is None and spread.stage], doubles):
+            if spread.stage > self.bits:
+                spread.other = block
+            else:
+                spread.own = jnp.concatenate([spread.own, block], axis=0)
+        jobs, waiting = [], []
+        for chunk, block in zip(self.last, blocks):
+            chunk.terms.append(block)
+            if chunk.stage < self.bits:
+                chunk.rows //= 2
+                jobs.append((chunk.terms, chunk.rows, chunk.rows))
+                waiting.append(chunk)
+        for (_, keep, store, waits, leads), core in zip(self.crossing, cores):
+            new = [Chunk(*pair, wait, lead) for pair, wait, lead in zip(keep(core), waits, leads)]
+            store += new
+            self.chunks += new
+        for chunk, value in zip(waiting, add_call(jobs) if jobs else []):
+            chunk.send = value
+        return live
+
+    def round(self, live):
+        live = self.received(live)
+        moving = [chunk for chunk in self.chunks if chunk.stage < self.bits and not chunk.wait]
+        for chunk in self.chunks:
+            chunk.wait = max(0, chunk.wait - 1)
+        crossing, self.fresh = self.fresh, []
+        doubling = [spread for spread in self.spreads if spread.stage <= self.bits]
+        live, cores, sends, doubles = lax.optimization_barrier(
+            (
+                live,
+                [entry[0] for entry in crossing],
+                [chunk.send for chunk in moving],
+                [spread.own for spread in doubling],
+            )
+        )
+        blocks = []
+        for chunk, send in zip(moving, sends):
+            blocks.append(lax.ppermute(send, ("stream", "batch"), self.pairs(chunk.stage, chunk.lead)))
+            chunk.stage += 1
+        cores = [lax.ppermute(send, "stream", [(0, 1), (1, 0)]) for send in cores]
+        for number, (spread, rows) in enumerate(zip(doubling, doubles)):
+            spread.own = rows
+            if spread.stage < self.bits:
+                pairs = self.pairs(self.bits - 1 - spread.stage, 0)
+                doubles[number] = lax.ppermute(rows, ("stream", "batch"), pairs)
+            else:
+                doubles[number] = lax.ppermute(rows, "stream", [(0, 1), (1, 0)])
+            spread.stage += 1
+        self.crossing, self.last, self.blocks = crossing, moving, (cores, blocks, doubles)
+        return live
+
+    def totals(self, live):
+        while self.busy():
+            live = self.round(live)
+        live = self.received(live)
+        return live, add_call([(chunk.terms, 0, chunk.rows) for chunk in self.chunks])
+
+
+def offsets_of(bits, side, lead):
     places = jnp.arange(1 << bits, dtype=jnp.int32)
-    offset = jnp.zeros_like(places)
-    for bit in range(bits):
-        offset = offset | (((places >> (bits - 1 - bit)) & 1) << bit)
-    return offset
+    made = []
+    for core in range(2):
+        offset = jnp.zeros_like(places)
+        for stage, bit in enumerate(bit_order(bits, core, lead)):
+            offset = offset | (((places >> (bits - 1 - stage)) & 1) << bit)
+        made.append(offset)
+    return jnp.where(side == 0, made[0], made[1])
+
+
+def places_of(bits, side, lead, offset):
+    made = []
+    for core in range(2):
+        place = jnp.zeros_like(offset)
+        for stage, bit in enumerate(bit_order(bits, core, lead)):
+            place = place | (((offset >> bit) & 1) << (bits - 1 - stage))
+        made.append(place)
+    return jnp.where(side == 0, made[0], made[1])
 
 
 def time_embed(steps_in, width):
@@ -640,87 +1009,137 @@
     grouped = segments.reshape(groups, GROUP)
     flag = (grouped[:, 0] == grouped[:, -1]).astype(jnp.int32)
 
-    offset = device_offsets(bits)
-    own_order = jnp.concatenate([stream * batch + (index ^ offset), (1 - stream) * batch + (index ^ offset)])
     shard = width // devices
-    source = (own_order[:, None] * shard + jnp.arange(shard, dtype=jnp.int32)[None, :]).reshape(width)
-    perm = (jnp.arange(width, dtype=jnp.int32)[:, None] == source[None, :]).astype(BF16)
-    inverse = device_offsets(bits)
-    spots = inverse[jnp.arange(batch, dtype=jnp.int32) ^ index]
+
+    def picked(side):
+        order = side * batch + (index ^ offsets_of(bits, side, 0))
+        source = (order[:, None] * shard + jnp.arange(shard, dtype=jnp.int32)[None, :]).reshape(width // 2)
+        return (jnp.arange(width, dtype=jnp.int32)[:, None] == source[None, :]).astype(BF16)
+
+    def spots(side):
+        return jnp.stack([places_of(bits, side, lead, jnp.arange(batch, dtype=jnp.int32) ^ index) for steps, lead in ROW_PARTS for _ in range(steps)])
+
+    other = 1 - stream
+    away, own = picked(other), picked(stream)
 
     bias_full = jnp.concatenate([b_qv[:width], jnp.zeros((width,), F32), b_qv[width:]])[None]
     h1, qkv = qkv_call(x, mod, w_qkv, bias_full)
     probs, mixed, om = attention_call(flag, qkv, head_columns, heads)
-    a, x1, h2, h2p, dm, sum_dm = middle_call(om, w_proj, b_proj[None], x, mod, top, keep, perm)
-
-    cuts = [0, hidden // 4, hidden // 2, hidden]
-    pieces, fc1 = [], []
-    for low, high in zip(cuts[:-1], cuts[1:]):
-        got = hidden_call(h2, h2p, dm, w_fc1, b_fc1[None], w_fc2, low, high - low)
-        pieces.append(got[:3])
-        fc1 += scatter_sum(got[3], got[4], bits)
-    g = jnp.concatenate([piece[0] for piece in pieces], axis=1)
-    df = jnp.concatenate([piece[1] for piece in pieces], axis=1)
-    sum_df = jnp.concatenate([piece[2] for piece in pieces], axis=1)[0]
-    fc2 = []
-    for low, high in ((0, width // 3), (width // 3, width)):
-        halves = [
-            rows_grad_call(side[None], spots, g, dm, low, high - low, batch).reshape(hidden // 2, high - low)
-            for side in (1 - stream, stream)
+    a, x1, h2, h2_away, h2_own, dm, sum_dm = middle_call(om, w_proj, b_proj[None], x, mod, top, keep, away, own)
+
+    flow = Flow(bits)
+    fc1, fc2, wide = [], [], []
+
+    filled, latest = (), {}
+    for low, high in ((0, 2 * UNITS), (2 * UNITS, 5 * UNITS), (5 * UNITS, hidden)):
+        *filled, send = hidden_call(h2, h2_away, dm, w_fc1, b_fc1[None], w_fc2, low, high - low, filled)
+        latest["df"] = filled[1]
+
+        def hidden_keep(got, low=low, count=high - low):
+            return columns_keep_call([(h2_own, latest["df"], low, count)], got, "hidden_keep")
+
+        flow.emit(send, hidden_keep, fc1)
+        h2, filled = flow.round((h2, filled))
+        latest["df"] = filled[1]
+    g, df, sum_df = filled
+
+    rows_send = rows_send_call(other[None], spots(other), g, dm)
+    flow.emit(
+        rows_send.reshape(-1, width),
+        lambda got: rows_keep_call(
+            stream[None], spots(stream), g, dm, got.reshape(rows_send.shape), [steps for steps, _ in ROW_PARTS]
+        ),
+        fc2,
+        [0] * len(ROW_PARTS),
+        [lead for _, lead in ROW_PARTS],
+    )
+    om_away, om_own = moved_call(om, away, own)
+    h1_away, h1_own = moved_call(h1, away, own)
+    df, x1, om_away, om_own, h1_away, h1_own = flow.round((df, x1, om_away, om_own, h1_away, h1_own))
+    dx1, da, do, sums_two = middle_back_call(df, w_fc1, x1, mod, top, a, w_proj, head_rows)
+
+    def by_item(*sums):
+        by_tile = jnp.concatenate(sums, axis=1)
+        return jnp.sum(jnp.where(chosen[:, :, None], by_tile[:, None], 0.0), axis=0).astype(BF16).astype(F32)
+
+    def in_rows(*sums):
+        made = jnp.concatenate([part.reshape(devices, -1) for part in sums], axis=1).reshape(items, -1)
+        return jnp.pad(made, ((0, 0), (0, -made.shape[1] % 128)))
+
+    def own_part(gathered, first, count):
+        each = devices // items
+        rows = lax.dynamic_index_in_dim(gathered.reshape(batch, items, -1), me // each, axis=1, keepdims=False)
+        return jnp.sum(lax.dynamic_slice_in_dim(rows, first + me % each * count, count, axis=1), axis=0)
+
+    me = stream * batch + index
+
+    def used_labels(side):
+        order = bit_order(bits, 0, 0)[::-1], bit_order(bits, 1, 0)[::-1]
+        places = jnp.arange(batch, dtype=jnp.int32)
+        offsets = [sum(((places >> n) & 1) << bit for n, bit in enumerate(bits_of)) for bits_of in order]
+        from_device = index ^ jnp.where(side == 0, offsets[0], offsets[1])
+        return jnp.where(side == 0, jnp.take(labels.reshape(batch, items), from_device, axis=0).reshape(-1), null_class)
+
+    used_rows = jnp.concatenate([used_labels(stream), used_labels(other)])[:, None]
+    dx1, da, do, sums_two = flow.round((dx1, da, do, sums_two))
+    dqkv, ready = attention_back_call(flag, qkv, do, probs, mixed, 0)
+    first_pairs = [(om_away, da, 0, width), (h1_away, ready, 0, ready.shape[1])]
+    own_pairs = [(om_own, da, 0, width), (h1_own, ready, 0, ready.shape[1])]
+    send, first_sums = columns_send_call(first_pairs, "first_send")
+    low_sums = first_sums[:, width:]
+    flow.emit(send, lambda got: columns_keep_call(own_pairs, got, "first_keep"), wide)
+    dqkv, low_sums = flow.round((dqkv, low_sums))
+    dqkv, rest = attention_back_call(flag, qkv, do, probs, mixed, 1, dqkv)
+    send, high_sums = columns_send_call([(h1_away, rest, 0, rest.shape[1])], "last_send")
+    flow.emit(send, lambda got: columns_keep_call([(h1_own, rest, 0, rest.shape[1])], got, "last_keep"), wide)
+    dqkv, dx1, high_sums, g = flow.round((dqkv, dx1, high_sums, g))
+    grad_tokens, sums_one = first_back_call(dqkv, w_qkv, x, mod, dx1)
+    result, sum_gate = result_call(g, w_fc2, b_fc2[None], x1, mod, top, keep)
+
+    def in_order(low, high):
+        first, second = low.shape[1] // 3, high.shape[1] // 3
+        return [
+            part
+            for third in range(3)
+            for part in (low[:, third * first : (third + 1) * first], high[:, third * second : (third + 1) * second])
         ]
-        fc2 += scatter_sum(halves[0], halves[1], bits)
-    result, sum_gate = result_call(g, w_fc2, b_fc2[None], x1, mod, top, keep)
-    dx1, da, do, sums_two = middle_back_call(df, w_fc1, x1, mod, top, a, w_proj, head_rows)
-    send, kept, _ = columns_grad_call(om, perm, da, "proj_grad")
-    proj = scatter_sum(send, kept, bits)
-
-    dqkv = attention_back_call(flag, qkv, do, probs, mixed)
-    send, kept, sum_dqkv = columns_grad_call(h1, perm, dqkv, "qkv_grad")
-    wide = scatter_sum(send, kept, bits)
-    grad_tokens, sums_one = first_back_call(dqkv, w_qkv, x, mod, dx1)
-
-    biases = jnp.concatenate(
-        [
-            part.reshape(devices, -1)
-            for part in (
-                sum_df,
-                jnp.sum(sum_dm, axis=(0, 1)),
-                jnp.sum(sums_two[:, 3], axis=0),
-                jnp.concatenate([sum_dqkv[0, :width], sum_dqkv[0, 2 * width :]]),
-            )
-        ],
-        axis=1,
+
+    grad_tokens, sums_one, result, sum_gate = flow.round((grad_tokens, sums_one, result, sum_gate))
+    column_sums = in_order(low_sums, high_sums)
+    spread = flow.spread(
+        jnp.concatenate(
+            [
+                by_item(
+                    sums_one[:, 0], sums_one[:, 1], sums_two[:, 0], sums_two[:, 1], sums_two[:, 2], sum_gate[:, 0]
+                ),
+                cond,
+                in_rows(
+                    sum_df[0],
+                    jnp.sum(sum_dm, axis=(0, 1)),
+                    jnp.sum(sums_two[:, 3], axis=0),
+                    jnp.concatenate(column_sums[:2] + column_sums[4:], axis=1)[0],
+                ),
+            ],
+            axis=1,
+        )
     )
-    biases = biases[own_order]
-    bias = scatter_sum(biases[batch:], biases[:batch], bits, [list(range(bits))])[0][0]
+    result, shards = flow.totals(result)
+    grad_w_ada, mod_sums, grad_table = modulation_back_call(
+        me[None], spread.own, spread.other, used_rows, w_ada, null_class + 1, shard
+    )
+    share = 6 * width // devices
+    grad_b_ada = lax.dynamic_slice_in_dim(mod_sums[0], me * share, share)
     ends = [hidden // devices, width // devices, width // devices, 2 * width // devices]
+    bias = sum(own_part(rows, 7 * width, sum(ends)) for rows in (spread.own, spread.other))
     at = [sum(ends[:n]) for n in range(5)]
     grad_b_fc1, grad_b_fc2, grad_b_proj, grad_b_qv = [bias[at[n] : at[n + 1]] for n in range(4)]
-
-    by_tile = jnp.stack(
-        [sums_one[:, 0], sums_one[:, 1], sums_two[:, 0], sums_two[:, 1], sums_two[:, 2], sum_gate[:, 0]],
-        axis=1,
-    ).reshape(tiles, 6 * width)
-    grad_mod = jnp.sum(jnp.where(chosen[:, :, None], by_tile[:, None], 0.0), axis=0)
-    grad_mod = grad_mod.astype(BF16).astype(F32)
-    gathered = lax.all_gather(
-        jnp.concatenate([grad_mod, cond], axis=1), ("stream", "batch"), axis=0, tiled=True
-    )
-    all_mod = gathered[:, : 6 * width]
-    all_cond = gathered[:, 6 * width :]
-    all_mod16 = all_mod.astype(BF16)
-    me = stream * batch + index
-    all_act = jax.nn.silu(all_cond).astype(BF16)
-    own_act = lax.dynamic_slice_in_dim(all_act, me * shard, shard, axis=1)
-    grad_w_ada = dot(own_act, all_mod16, TN)
-    share = 6 * width // devices
-    grad_b_ada = jnp.sum(lax.dynamic_slice_in_dim(all_mod, me * share, share, axis=1), axis=0)
-    grad_act = dot(all_mod16, w_ada, NT)
-    grad_cond = jax.vjp(jax.nn.silu, all_cond)[1](grad_act)[0]
-    all_labels = jnp.concatenate([labels, jnp.full_like(labels, null_class)])
-    class_index = jnp.arange(null_class + 1, dtype=jnp.int32)
-    label_select = (all_labels[:, None] == class_index[None, :]).astype(F32)
-    grad_table = dot(label_select, grad_cond, TN, HIGHEST)
+    shards = dict(zip(map(id, flow.chunks), shards))
+    grad_w_fc1, grad_w_fc2 = [
+        jnp.concatenate([shards[id(chunk)] for chunk in store], axis=1) for store in (fc1, fc2)
+    ]
+    first_shard, last_shard = [shards[id(chunk)] for chunk in wide]
+    grad_w_proj = first_shard[:, :width]
+    grad_w_qkv = jnp.concatenate(in_order(first_shard[:, width:], last_shard), axis=1)
 
     return (
         result[None],
@@ -728,13 +1147,13 @@
         grad_table,
         grad_w_ada,
         grad_b_ada,
-        jnp.concatenate(wide, axis=1),
+        grad_w_qkv,
         grad_b_qv,
-        jnp.concatenate(proj, axis=1),
+        grad_w_proj,
         grad_b_proj,
-        jnp.concatenate(fc1, axis=1),
+        grad_w_fc1,
         grad_b_fc1,
-        jnp.concatenate(fc2, axis=1),
+        grad_w_fc2,
         grad_b_fc2,
     )
 

time: 923 us -> 650 us (0.70)
  local copies, waits for them, and re-layouts: 175 us -> 34.3 us
  other arithmetic: 113 us -> 16.1 us
  Pallas kernels: 323 us -> 405 us
  starting transfers between devices: 126 us -> 57.6 us
  matrix products: 26.4 us -> 7.72 us
  between operations: 17.3 us -> 2.92 us
  waiting for transfers between devices: 135 us -> 121 us
    pallas_call x6 -> x22, Pallas kernels: 82.4 us -> 168 us  [the longest x5 42.6 us: columns_keep_call(): call(functools.partial(columns_keep_body, starts=starts), name, 2 * token...]
    another operation x66 -> x2, local copies, waits for them, and re-layouts: 72.4 us -> 0.16 us  [in_rows(): part.reshape(devices, -1)]
    ppermute x96 -> x39, starting transfers between devices: 126 us -> 57.6 us  [the longest x28 51.2 us: round(): lax.ppermute(send, ('stream', 'batch'), self.pairs(chunk.stage, chunk.lead))]
    slice x59 -> x0, other arithmetic: 55.5 us -> none  [the longest x58 55.3 us: pick(): term.reshape(before, 2, after, share)[:, which].reshape(count // 2, share)]
    slice x28 -> x4, local copies, waits for them, and re-layouts: 49.9 us -> 2.37 us  [the longest x1 1.67 us: per_device(): grad_w_proj = first_shard[:, :width]]
    add x31 -> x3, other arithmetic: 24.2 us -> 0.15 us  [the longest x2 0.14 us: picked(): order[:, None] * shard + jnp.arange(shard, dtype=jnp.int32)[None, :]]
    dot_general x4 -> x1, matrix products: 26.4 us -> 7.72 us  [dot(): lax.dot_general(left, right, dims, precision=precision, preferred_element...]
    pallas_call x3, Pallas kernels: 62.9 us -> 46.1 us  [hidden_call(): call(hidden_body, 'hidden', 6 * tokens * width * count, 6 * tokens * widt...]
  transfers between devices with their start and end apart: 97 -> 39, of which waited for: 37 -> 11; matrix products, arithmetic and copies ran while one was open for 31% -> 3% of each run, Pallas kernels for 26% -> 32%
where the time goes in v2:
time: 650 us; the launch traced here: 644 us
  Pallas kernels  405 us (62%)
  waiting for transfers between devices  121 us (19%)
  starting transfers between devices  57.6 us (9%)
  local copies, waits for them, and re-layouts  34.3 us (5%)
  other arithmetic  16.1 us (2%)
  matrix products  7.72 us (1%)
    ppermute x28, waiting for transfers between devices, round(): lax.ppermute(send, ('stream', 'batch'), self.pairs(chunk.stage, chunk.lead))  61.7 us
    ppermute x4, waiting for transfers between devices, round(): doubles[number] = lax.ppermute(rows, ('stream', 'batch'), pairs)  59.2 us
    pallas_call x2, Pallas kernels, attention_back_call(): call(functools.partial(attention_back_body, width=width, head_width=head_...  54.5 us
    ppermute x28, starting transfers between devices, round(): lax.ppermute(send, ('stream', 'batch'), self.pairs(chunk.stage, chunk.lead))  51.2 us
    pallas_call x3, Pallas kernels, hidden_call(): call(hidden_body, 'hidden', 6 * tokens * width * count, 6 * tokens * widt...  46.1 us
    pallas_call x5, Pallas kernels, columns_keep_call(): call(functools.partial(columns_keep_body, starts=starts), name, 2 * token...  42.6 us
    pallas_call x10, Pallas kernels, add_call(): call(functools.partial(add_body, plans=plans), 'add', moved // 4, moved,...  41 us
    pallas_call x1, Pallas kernels, attention_call(): call(functools.partial(attention_body, width=width, head_width=head_width...  36.1 us
  transfers between devices with their start and end apart: 39, of which 11 were waited for; matrix products, arithmetic and copies ran while one was open for 3% of the time, Pallas kernels for 32%

profile of v2, /device:TPU:0, one launch (start us, length us, event | category | flops | bytes accessed | tf_op | source)
XLA Modules:
  0.0 644.5 jit_solution(5979710847496580676)
XLA Ops:
  4.5 7.7 %convolution_add_fusion = f32[4,6912]{1,0:T(4,128)S(1)} fusion(bf16[1152,6912]{1,0:T(8,128)(2,1)} %w_ref.9, f32[6912]{0:T(1024)} %param.28, f32[4,1152]{1,0:T(4,128)S(1)} %maximum_add_fusion), kind=kOutput, calls=%fused_computation.3 | convolution fusion | flops 63751680 | bytes 16081920 | tf_op jit(solution)/shard_map/dot_general | solution.py:28
  17.7 1.7 fusion.away_ref
  19.6 1.7 fusion.1.own_ref
  23.5 16.8 %qkv.1 = (bf16[1024,1152]{1,0:T(8,128)(2,1)}, bf16[1024,3456]{1,0:T(8,128)(2,1)}) custom-call(bf16[1024,1152]{1,0:T(8,128)(2,1)} %bitcast.56, f32[4,6,1152]{2,1,0:T(8,128)} %reshape.311.mod_ref, bf16[1152,3456]{1,0:T(8,128)(2,1)} %w_ref.7, f32[1,3456]{1,0:T(1,128)} %broadcast_in_dim.153.b_ref), custom_call_target="tpu_custom_call" | custom-call | flops 1019215872 | bytes 2469888 | tf_op jit(solution)/shard_map/qkv/pallas_call | solution.py:73
  40.3 36.1 %attention.1 = (bf16[16,1024,1024]{2,1,0:T(8,128)(2,1)}, f32[16,72,1024]{2,1,0:T(8,128)}, bf16[1024,1152]{1,0:T(8,128)(2,1)}) custom-call(s32[1]{0:T(128)} %bitcast.1.flag_ref, bf16[1024,3456]{1,0:T(8,128)(2,1)} %get-tuple-element.252.qkv_ref, f32[16,1,1024]{2,1,0:T(1,128)} %reshape_reshape.6.keep_ref), custom_call_target="tpu_custom_call" | custom-call | flops 2147483648 | bytes 5963776 | tf_op jit(solution)/shard_map/attention/pallas_call | solution.py:153
  76.4 15.4 %middle.1 = (f32[1024,1152]{1,0:T(8,128)}, f32[1024,1152]{1,0:T(8,128)}, bf16[1024,1152]{1,0:T(8,128)(2,1)}, bf16[1024,576]{1,0:T(8,128)(2,1)}, bf16[1024,576]{1...) custom-call(bf16[1024,1152]{1,0:T(8,128)(2,1)} %get-tuple-element.253.om_ref.left_ref, ...), custom_call_target="tpu_custom_call" | custom-call | flops 679477248 | bytes 3833856 | tf_op jit(solution)/shard_map/middle/pallas_call | solution.py:310
  91.8 11.7 %hidden.3 = (bf16[1024,4608]{1,0:T(8,128)(2,1)}, bf16[1024,4608]{1,0:T(8,128)(2,1)}, f32[1,4608]{1,0:T(1,128)}, f32[576,1024]{1,0:T(8,128)}) custom-call(bf16[1024,1152]{1,0:T(8,128)(2,1)} %get-tuple-element.281.h_ref, bf16[1024,576]{1,0:T(8,128)(2,1)} %get-tuple-element.255.away_ref, bf16[1024,1152]{1,0:T(8,128)(2,1)} %get-tuple-element.256.dm_ref, ...), custom_call_target="tpu_custom_call" | custom-call | flops 905969664 | bytes 2588672 | tf_op jit(solution)/shard_map/hidden/pallas_call | solution.py:363
  104.0 15.3 %hidden.4 = (bf16[1024,4608]{1,0:T(8,128)(2,1)}, bf16[1024,4608]{1,0:T(8,128)(2,1)}, f32[1,4608]{1,0:T(1,128)}, f32[576,1536]{1,0:T(8,128)}) custom-call(bf16[1024,1152]{1,0:T(8,128)(2,1)} %get-tuple-element.281.h_ref, bf16[1024,576]{1,0:T(8,128)(2,1)} %get-tuple-element.255.away_ref, ...), custom_call_target="tpu_custom_call", output_to_operand_aliasing={{0}: (6, {}), {1}: (7, {}), {2}: (8, {})} | custom-call | flops 1358954496 | bytes 3440640 | tf_op jit(solution)/shard_map/hidden/pallas_call | solution.py:363
  119.4 4.7 hidden_keep.3
  124.1 9.0 %collective-permute-start.2 = (f32[288,1024]{1,0:T(8,128)}, f32[288,1024]{1,0:T(8,128)S(1)}, u32[]{:S(2)}, u32[]{:S(2)}) collective-permute-start(f32[288,1024]{1,0:T(8,128)} %get-tuple-element.289), channel_id=1, source_target_pairs={{0,1},{1,0},{2,3},{3,2},{4,5},{5,4},{6,7},{7,6},{8,9},{9,8},{10,11... | collective-permute-start | bytes 3538952 | tf_op jit(solution)/shard_map/ppermute | solution.py:929
  133.1 19.0 %hidden.5 = (bf16[1024,4608]{1,0:T(8,128)(2,1)}, bf16[1024,4608]{1,0:T(8,128)(2,1)}, f32[1,4608]{1,0:T(1,128)}, f32[576,2048]{1,0:T(8,128)}) custom-call(bf16[1024,1152]{1,0:T(8,128)(2,1)} %get-tuple-element.281.h_ref, bf16[1024,576]{1,0:T(8,128)(2,1)} %get-tuple-element.255.away_ref, ...), custom_call_target="tpu_custom_call", output_to_operand_aliasing={{0}: (6, {}), {1}: (7, {}), {2}: (8, {})} | custom-call | flops 1811939328 | bytes 4292608 | tf_op jit(solution)/shard_map/hidden/pallas_call | solution.py:363
  152.1 7.3 %hidden_keep.4 = (f32[288,1536]{1,0:T(8,128)}, f32[288,1536]{1,0:T(8,128)}) custom-call(bf16[1024,576]{1,0:T(8,128)(2,1)} %get-tuple-element.278.refs_0_, bf16[1024,4608]{1,0:T(8,128)(2,1)} %get-tuple-element.322.refs_1_.df_ref, f32[576,1536]{1,0:T(8,128)} %collective-permute-done.1.refs_2_), custom_call_target="tpu_custom_call" | custom-call | flops 226492416 | bytes 1425408 | tf_op jit(solution)/shard_map/hidden_keep/pallas_call | solution.py:659
  159.4 2.2 add.282
  161.8 1.7 collective-permute-start.4
  163.5 7.3 %moved.2 = (bf16[1024,576]{1,0:T(8,128)(2,1)}, bf16[1024,576]{1,0:T(8,128)(2,1)}) custom-call(bf16[1024,1152]{1,0:T(8,128)(2,1)} %get-tuple-element.253.om_ref.left_ref, bf16[1152,576]{1,0:T(8,128)(2,1)} %fusion.away_ref, bf16[1152,576]{1,0:T(8,128)(2,1)} %fusion.1.own_ref), custom_call_target="tpu_custom_call" | custom-call | flops 339738624 | bytes 921600 | tf_op jit(solution)/shard_map/moved/pallas_call | solution.py:683
  170.8 7.3 %moved.3 = (bf16[1024,576]{1,0:T(8,128)(2,1)}, bf16[1024,576]{1,0:T(8,128)(2,1)}) custom-call(bf16[1024,1152]{1,0:T(8,128)(2,1)} %get-tuple-element.302.left_ref, bf16[1152,576]{1,0:T(8,128)(2,1)} %fusion.away_ref, bf16[1152,576]{1,0:T(8,128)(2,1)} %fusion.1.own_ref), custom_call_target="tpu_custom_call" | custom-call | flops 339738624 | bytes 921600 | tf_op jit(solution)/shard_map/moved/pallas_call | solution.py:683
  178.8 13.1 %rows_send.1 = f32[16,144,1152]{2,1,0:T(8,128)} custom-call(s32[1]{0:T(128)} %bitcast.6.side_ref, s32[3,16]{1,0:T(4,128)} %pad_add_fusion.spot_ref, bf16[1024,4608]{1,0:T(8,128)(2,1)} %get-tuple-element.403.g_ref, bf16[1024,1152]{1,0:T(8,128)(2,1)} %get-tuple-element.256.dm_ref), custom_call_target="tpu_custom_call" | custom-call | flops 679477248 | bytes 2211840 | tf_op jit(solution)/shard_map/rows_send/pallas_call | solution.py:419
  191.9 8.6 %hidden_keep.5 = (f32[288,2048]{1,0:T(8,128)}, f32[288,2048]{1,0:T(8,128)}) custom-call(bf16[1024,576]{1,0:T(8,128)(2,1)} %get-tuple-element.278.refs_0_, bf16[1024,4608]{1,0:T(8,128)(2,1)} %get-tuple-element.322.refs_1_.df_ref, f32[576,2048]{1,0:T(8,128)} %collective-permute-done.3.refs_2_), custom_call_target="tpu_custom_call" | custom-call | flops 301989888 | bytes 1851392 | tf_op jit(solution)/shard_map/hidden_keep/pallas_call | solution.py:659
  200.5 2.6 add.283
  203.6 1.9 collective-permute-start.8
  205.5 1.6 collective-permute-start.7
  208.4 30.7 %middle_back.1 = (f32[1024,1152]{1,0:T(8,128)}, bf16[1024,1152]{1,0:T(8,128)(2,1)}, bf16[1024,1152]{1,0:T(8,128)(2,1)}, f32[4,4,1152]{2,1,0:T(4,128)}) custom-call(bf16[1024,4608]{1,0:T(8,128)(2,1)} %get-tuple-element.322.refs_1_.df_ref, bf16[1152,4608]{1,0:T(8,128)(2,1)} %w1_ref.7, f32[1024,1152]{1,0:T(8,128)} %get-tuple-element.323.x1_ref, ...), custom_call_target="tpu_custom_call" | custom-call | flops 1698693120 | bytes 5160960 | tf_op jit(solution)/shard_map/middle_back/pallas_call | solution.py:555
  239.1 2.4 collective-permute-done.9.refs_8_.refs_5_.refs_1_.refs_11_
  241.6 18.5 %rows_keep.1 = (f32[8,144,768]{2,1,0:T(8,128)}, f32[8,144,768]{2,1,0:T(8,128)}, f32[8,144,384]{2,1,0:T(8,128)}, f32[8,144,384]{2,1,0:T(8,128)}) custom-call(s32[1]{0:T(128)} %bitcast.8.side_ref, s32[3,16]{1,0:T(4,128)} %pad_add_fusion.1.spot_ref, bf16[1024,4608]{1,0:T(8,128)(2,1)} %get-tuple-element.403.g_ref, bf16[1024,1152]{1,0:T(8,128)(2,1)} %get-tuple-element.256.dm_ref, ...), custom_call_target="tpu_custom_call" | custom-call | flops 679477248 | bytes 3538944 | tf_op jit(solution)/shard_map/rows_keep/pallas_call | solution.py:478
  260.0 3.5 add.284
  264.2 2.7 collective-permute-start.14
  267.7 3.0 collective-permute-start.10
  270.7 26.0 %attention_back.2 = (bf16[1024,3456]{1,0:T(8,128)(2,1)}, bf16[1024,1536]{1,0:T(8,128)(2,1)}) custom-call(s32[1]{0:T(128)} %bitcast.1.flag_ref, bf16[1024,3456]{1,0:T(8,128)(2,1)} %get-tuple-element.252.qkv_ref, bf16[1024,1152]{1,0:T(8,128)(2,1)} %get-tuple-element.347.do_ref, bf16[16,1024,1024]{2,1,0:T(8,128)(2,1)} %get-tuple-element.348.p_ref, ...), custom_call_target="tpu_custom_call" | custom-call | flops 2147483648 | bytes 4751360 | tf_op jit(solution)/shard_map/attention_back/pallas_call | solution.py:265
  296.7 10.9 %first_send.1 = (f32[576,2688]{1,0:T(8,128)}, f32[1,2688]{1,0:T(1,128)}) custom-call(bf16[1024,576]{1,0:T(8,128)(2,1)} %get-tuple-element.351.refs_0_, bf16[1024,1152]{1,0:T(8,128)(2,1)} %get-tuple-element.352.refs_1_, bf16[1024,576]{1,0:T(8,128)(2,1)} %get-tuple-element.353.refs_2_.refs_0_, bf16[1024,1536]{1,0:T(8,128)(2,1)} %get-tuple-element.354.refs_3_), custom_call_target="tpu_custom_call" | custom-call | flops 396361728 | bytes 1609728 | tf_op jit(solution)/shard_map/first_send/pallas_call | solution.py:626
  308.4 9.2 %collective-permute-done.10.refs_4_ = f32[36,1024]{1,0:T(8,128)S(1)} collective-permute-done((f32[36,1024]{1,0:T(8,128)}, f32[36,1024]{1,0:T(8,128)S(1)}, u32[]{:S(2)}, u32[]{:S(2)}) %collective-permute-start.10) | collective-permute-done | bytes 147488 | tf_op jit(solution)/shard_map/ppermute | solution.py:929
  320.0 5.4 add.285
  327.7 2.7 collective-permute-start.17
  330.8 28.4 %attention_back.3 = (bf16[1024,3456]{1,0:T(8,128)(2,1)}, bf16[1024,1920]{1,0:T(8,128)(2,1)}) custom-call(s32[1]{0:T(128)} %bitcast.1.flag_ref, bf16[1024,3456]{1,0:T(8,128)(2,1)} %get-tuple-element.252.qkv_ref, bf16[1024,1152]{1,0:T(8,128)(2,1)} %get-tuple-element.347.do_ref, bf16[16,1024,1024]{2,1,0:T(8,128)(2,1)} %get-tuple-element.348.p_ref, ...), custom_call_target="tpu_custom_call" | custom-call | flops 2147483648 | bytes 4751360 | tf_op jit(solution)/shard_map/attention_back/pallas_call | solution.py:265
  359.3 7.0 %last_send.1 = (f32[576,1920]{1,0:T(8,128)}, f32[1,1920]{1,0:T(1,128)}) custom-call(bf16[1024,576]{1,0:T(8,128)(2,1)} %get-tuple-element.353.refs_2_.refs_0_, bf16[1024,1920]{1,0:T(8,128)(2,1)} %get-tuple-element.377.refs_1_), custom_call_target="tpu_custom_call" | custom-call | flops 283115520 | bytes 1191936 | tf_op jit(solution)/shard_map/last_send/pallas_call | solution.py:626
  366.3 13.2 %first_keep.1 = (f32[288,2688]{1,0:T(8,128)}, f32[288,2688]{1,0:T(8,128)}) custom-call(bf16[1024,576]{1,0:T(8,128)(2,1)} %get-tuple-element.395.refs_0_, bf16[1024,1152]{1,0:T(8,128)(2,1)} %get-tuple-element.352.refs_1_, bf16[1024,576]{1,0:T(8,128)(2,1)} %get-tuple-element.396.refs_2_.refs_0_, bf16[1024,1536]{1,0:T(8,128)(2,1)} %get-tuple-element.354.refs_3_, ...), custom_call_target="tpu_custom_call" | custom-call | flops 396361728 | bytes 2383872 | tf_op jit(solution)/shard_map/first_keep/pallas_call | solution.py:659
  379.6 4.1 add.286
  383.7 7.6 %collective-permute-start.24 = (f32[288,2688]{1,0:T(8,128)}, f32[288,2688]{1,0:T(8,128)}, u32[]{:S(2)}, u32[]{:S(2)}) collective-permute-start(f32[288,2688]{1,0:T(8,128)} %get-tuple-element.410), channel_id=1, source_target_pairs={{0,1},{1,0},{2,3},{3,2},{4,5},{5,4},{6,7},{7,6},{8,9},{9,8},{10,11... | collective-permute-start | bytes 9289736 | tf_op jit(solution)/shard_map/ppermute | solution.py:929
  395.4 17.7 %first_back.1 = (f32[1024,1152]{1,0:T(8,128)}, f32[4,2,1152]{2,1,0:T(2,128)}) custom-call(bf16[1024,3456]{1,0:T(8,128)(2,1)} %get-tuple-element.399.dqkv_ref, bf16[1152,3456]{1,0:T(8,128)(2,1)} %w_ref.7, bf16[1024,1152]{1,0:T(8,128)(2,1)} %bitcast.58, f32[4,6,1152]{2,1,0:T(8,128)} %reshape.311.mod_ref, f32[1024,1152]{1,0:T(8,128)} %get-tuple-element.400.dx_ref), custom_call_target="tpu_custom_call" | custom-call | flops 1019215872 | bytes 3354624 | tf_op jit(solution)/shard_map/first_back/pallas_call | solution.py:709
  413.0 19.7 %result.1 = (bf16[1024,1152]{1,0:T(8,128)(2,1)}, f32[4,1,1152]{2,1,0:T(1,128)}) custom-call(bf16[1024,4608]{1,0:T(8,128)(2,1)} %get-tuple-element.403.g_ref, bf16[4608,1152]{1,0:T(8,128)(2,1)} %w_ref.8, f32[1,1152]{1,0:T(1,128)} %broadcast_in_dim.163.b_ref, f32[1024,1152]{1,0:T(8,128)} %get-tuple-element.323.x1_ref, f32[4,6,1152]{2,1,0:T(8,128)} %reshape.311.mod_ref, ...), custom_call_target="tpu_custom_call" | custom-call | flops 1358954496 | bytes 3686400 | tf_op jit(solution)/shard_map/result/pallas_call | solution.py:511
  432.8 8.8 %last_keep.1 = (f32[288,1920]{1,0:T(8,128)}, f32[288,1920]{1,0:T(8,128)}) custom-call(bf16[1024,576]{1,0:T(8,128)(2,1)} %get-tuple-element.396.refs_2_.refs_0_, bf16[1024,1920]{1,0:T(8,128)(2,1)} %get-tuple-element.377.refs_1_, f32[576,1920]{1,0:T(8,128)} %collective-permute-done.20.refs_2_), custom_call_target="tpu_custom_call" | custom-call | flops 283115520 | bytes 1744896 | tf_op jit(solution)/shard_map/last_keep/pallas_call | solution.py:659
  441.7 4.8 add.287
  449.2 2.0 collective-permute-start.25
  452.2 28.3 %collective-permute-done.26.refs_24_ = f32[144,384]{1,0:T(8,128)S(1)} collective-permute-done((f32[144,384]{1,0:T(8,128)}, f32[144,384]{1,0:T(8,128)S(1)}, u32[]{:S(2)}, u32[]{:S(2)}) %collective-permute-start.26) | collective-permute-done | bytes 221216 | tf_op jit(solution)/shard_map/ppermute | solution.py:929
  480.5 3.9 collective-permute-done.27.refs_2_.refs_27_
  484.5 5.5 collective-permute-done.28.refs_4_.refs_5_.refs_1_.refs_31_
  491.3 4.3 add.288
  496.8 1.7 collective-permute-start.29
  499.2 18.7 %collective-permute-done.31 = f32[4,10368]{1,0:T(4,128)S(1)} collective-permute-done((f32[4,10368]{1,0:T(4,128)S(1)}, f32[4,10368]{1,0:T(4,128)S(1)}, u32[]{:S(2)}, u32[]{:S(2)}) %collective-permute-start.31) | collective-permute-done | bytes 165920 | tf_op jit(solution)/shard_map/ppermute | solution.py:936
  519.9 4.0 add.289
  523.9 1.6 collective-permute-start.33
  526.6 2.0 collective-permute-start.34
  528.5 24.3 %collective-permute-done.34 = f32[8,10368]{1,0:T(8,128)S(1)} collective-permute-done((f32[8,10368]{1,0:T(8,128)S(1)}, f32[8,10368]{1,0:T(8,128)S(1)}, u32[]{:S(2)}, u32[]{:S(2)}) %collective-permute-start.34) | collective-permute-done | bytes 331808 | tf_op jit(solution)/shard_map/ppermute | solution.py:936
  553.7 3.2 add.290
  556.8 2.3 collective-permute-start.36
  559.1 2.6 collective-permute-start.35
  561.8 11.0 %collective-permute-done.35.refs_34_ = f32[36,1920]{1,0:T(8,128)S(1)} collective-permute-done((f32[36,1920]{1,0:T(8,128)}, f32[36,1920]{1,0:T(8,128)S(1)}, u32[]{:S(2)}, u32[]{:S(2)}) %collective-permute-start.35) | collective-permute-done | bytes 276512 | tf_op jit(solution)/shard_map/ppermute | solution.py:929
  574.5 16.3 %collective-permute-done.37 = f32[32,10368]{1,0:T(8,128)} collective-permute-done((f32[32,10368]{1,0:T(8,128)S(1)}, f32[32,10368]{1,0:T(8,128)}, u32[]{:S(2)}, u32[]{:S(2)}) %collective-permute-start.37) | collective-permute-done | bytes 1327136 | tf_op jit(solution)/shard_map/ppermute | solution.py:936
  590.8 3.0 pad_maximum_fusion.own_ref.own_cond_ref
  595.4 6.8 %add.291 = (f32[36,1024]{1,0:T(8,128)}, f32[36,1536]{1,0:T(8,128)}, f32[36,2048]{1,0:T(8,128)}, f32[144,768]{1,0:T(8,128)}, f32[144,384]{1,0:T(8,128)}, /*index=5*/f32[36,2688]{1,0:T(8,128)}, f32[36,1920]{1,0:T(8,128)}) custom-call(f32[288,1024]{1,0:T(8,128)} %get-tuple-element.294.refs_0_, f32[288,1024]{1,0:T(8,128)} %copy-done.5, f32[144,1024]{1,0:T(8,128)} %copy-done.12, ...), custom_call_target="tpu_custom_call" | custom-call | flops 373248 | bytes 1492992 | tf_op jit(solution)/shard_map/add/pallas_call | solution.py:832
  602.3 1.7 slice.108
  609.3 2.2 pad_maximum_fusion.4
  612.5 3.2 reshape.322
  616.7 3.2 reshape.323
  622.7 20.2 %modulation_back.1 = (f32[36,6912]{1,0:T(8,128)}, f32[1,6912]{1,0:T(1,128)}, f32[1001,1152]{1,0:T(8,128)}) custom-call(s32[1]{0:T(128)} %bitcast.21.me_ref, f32[64,10368]{1,0:T(8,128)} %pad_maximum_fusion.own_ref.own_cond_ref, f32[64,10368]{1,0:T(8,128)} %collective-permute-done.38.other_ref.other_cond_ref, ...), custom_call_target="tpu_custom_call" | custom-call | flops 254803968 | bytes 1990656 | tf_op jit(solution)/shard_map/modulation_back/pallas_call | solution.py:777
  (242 shorter events, 50.4 us)
Async XLA Ops:
  3.1 10.9 %copy-start.42 = (pred[4,4]{1,0:T(4,128)(4,1)}, pred[4,4]{1,0:T(4,128)(4,1)S(1)}, u32[]{:S(2)}) copy-start(pred[4,4]{1,0:T(4,128)(4,1)S(1)} %iota_compare_fusion.2) | copy-start | bytes 52
  4.5 9.5 %copy-start.47 = (s32[4,16]{1,0:T(4,128)S(1)}, s32[4,16]{1,0:T(4,128)}, u32[]{:S(2)}) copy-start(s32[4,16]{1,0:T(4,128)} %param.24) | copy-start | bytes 772
  12.2 9.0 %copy-start.44 = (s32[1,1024]{1,0:T(1,128)S(1)}, s32[1,1024]{1,0:T(1,128)}, u32[]{:S(2)}) copy-start(s32[1,1024]{1,0:T(1,128)} %param.25) | copy-start | bytes 12292
  12.2 10.0 %copy-start.40 = (f32[1152]{0:T(1024)S(1)}, f32[1152]{0:T(1024)}, u32[]{:S(2)}) copy-start(f32[1152]{0:T(1024)} %param.32) | copy-start | bytes 13828
  12.2 10.6 %copy-start.36 = (f32[4608]{0:T(1024)S(1)}, f32[4608]{0:T(1024)}, u32[]{:S(2)}) copy-start(f32[4608]{0:T(1024)} %param.34) | copy-start | bytes 55300
  103.5 15.8 %collective-permute-start = (f32[576,1024]{1,0:T(8,128)}, f32[576,1024]{1,0:T(8,128)}, u32[]{:S(2)}, u32[]{:S(2)}) collective-permute-start(f32[576,1024]{1,0:T(8,128)} %get-tuple-element.272), channel_id=1, source_target_pairs={{0,16},{16,0},{1,17},{17,1},{2,18},{18,2},{3,19},{19,3},{4,20},{20... | collective-permute-start | bytes 7077896 | tf_op jit(solution)/shard_map/ppermute | solution.py:931
  124.0 28.0 %collective-permute-start.1 = (f32[576,1536]{1,0:T(8,128)}, f32[576,1536]{1,0:T(8,128)}, u32[]{:S(2)}, u32[]{:S(2)}) collective-permute-start(f32[576,1536]{1,0:T(8,128)} %get-tuple-element.288), channel_id=1, source_target_pairs={{0,16},{16,0},{1,17},{17,1},{2,18},{18,2},{3,19},{19,3},{4,20},{20... | collective-permute-start | bytes 10616840 | tf_op jit(solution)/shard_map/ppermute | solution.py:931
  124.1 28.0 %collective-permute-start.2 = (f32[288,1024]{1,0:T(8,128)}, f32[288,1024]{1,0:T(8,128)S(1)}, u32[]{:S(2)}, u32[]{:S(2)}) collective-permute-start(f32[288,1024]{1,0:T(8,128)} %get-tuple-element.289), channel_id=1, source_target_pairs={{0,1},{1,0},{2,3},{3,2},{4,5},{5,4},{6,7},{7,6},{8,9},{9,8},{10,11... | collective-permute-start | bytes 3538952 | tf_op jit(solution)/shard_map/ppermute | solution.py:929
  161.6 30.2 %collective-permute-start.3 = (f32[576,2048]{1,0:T(8,128)}, f32[576,2048]{1,0:T(8,128)}, u32[]{:S(2)}, u32[]{:S(2)}) collective-permute-start(f32[576,2048]{1,0:T(8,128)} %get-tuple-element.305), channel_id=1, source_target_pairs={{0,16},{16,0},{1,17},{17,1},{2,18},{18,2},{3,19},{19,3},{4,20},{20... | collective-permute-start | bytes 14155784 | tf_op jit(solution)/shard_map/ppermute | solution.py:931
  161.7 30.1 %collective-permute-start.5 = (f32[288,1536]{1,0:T(8,128)}, f32[288,1536]{1,0:T(8,128)S(1)}, u32[]{:S(2)}, u32[]{:S(2)}) collective-permute-start(f32[288,1536]{1,0:T(8,128)} %get-tuple-element.307), channel_id=1, source_target_pairs={{0,1},{1,0},{2,3},{3,2},{4,5},{5,4},{6,7},{7,6},{8,9},{9,8},{10,11... | collective-permute-start | bytes 5308424 | tf_op jit(solution)/shard_map/ppermute | solution.py:929
  161.8 30.0 %collective-permute-start.4 = (f32[144,1024]{1,0:T(8,128)}, f32[144,1024]{1,0:T(8,128)S(1)}, u32[]{:S(2)}, u32[]{:S(2)}) collective-permute-start(f32[144,1024]{1,0:T(8,128)} %add.282), channel_id=1, source_target_pairs={{0,2},{1,3},{2,0},{3,1},{4,6},{5,7},{6,4},{7,5},{8,10},{9,11},{10,... | collective-permute-start | bytes 1769480 | tf_op jit(solution)/shard_map/ppermute | solution.py:929
  203.1 38.5 %collective-permute-start.6 = (f32[2304,1152]{1,0:T(8,128)}, f32[2304,1152]{1,0:T(8,128)}, u32[]{:S(2)}, u32[]{:S(2)}) collective-permute-start(f32[2304,1152]{1,0:T(8,128)} %bitcast.59), channel_id=1, source_target_pairs={{0,16},{16,0},{1,17},{17,1},{2,18},{18,2},{3,19},{19,3},{4,20},{20... | collective-permute-start | bytes 31850504 | tf_op jit(solution)/shard_map/ppermute | solution.py:931
  203.1 38.5 %collective-permute-start.9 = (f32[288,2048]{1,0:T(8,128)}, f32[288,2048]{1,0:T(8,128)}, u32[]{:S(2)}, u32[]{:S(2)}) collective-permute-start(f32[288,2048]{1,0:T(8,128)} %get-tuple-element.332), channel_id=1, source_target_pairs={{0,1},{1,0},{2,3},{3,2},{4,5},{5,4},{6,7},{7,6},{8,9},{9,8},{10,11... | collective-permute-start | bytes 7077896 | tf_op jit(solution)/shard_map/ppermute | solution.py:929
  203.6 35.6 %collective-permute-start.8 = (f32[144,1536]{1,0:T(8,128)}, f32[144,1536]{1,0:T(8,128)S(1)}, u32[]{:S(2)}, u32[]{:S(2)}) collective-permute-start(f32[144,1536]{1,0:T(8,128)} %get-tuple-element.331), channel_id=1, source_target_pairs={{0,2},{1,3},{2,0},{3,1},{4,6},{5,7},{6,4},{7,5},{8,10},{9,11},{10,... | collective-permute-start | bytes 2654216 | tf_op jit(solution)/shard_map/ppermute | solution.py:929
  205.5 33.6 %collective-permute-start.7 = (f32[72,1024]{1,0:T(8,128)}, f32[72,1024]{1,0:T(8,128)S(1)}, u32[]{:S(2)}, u32[]{:S(2)}) collective-permute-start(f32[72,1024]{1,0:T(8,128)} %get-tuple-element.330), channel_id=1, source_target_pairs={{0,4},{1,5},{2,6},{3,7},{4,0},{5,1},{6,2},{7,3},{8,12},{9,13},{10,... | collective-permute-start | bytes 884744 | tf_op jit(solution)/shard_map/ppermute | solution.py:929
  239.1 20.9 %copy-start.19 = (f32[72,1024]{1,0:T(8,128)}, f32[72,1024]{1,0:T(8,128)S(1)}, u32[]{:S(2)}) copy-start(f32[72,1024]{1,0:T(8,128)S(1)} %collective-permute-done.7.refs_3_) | copy-start | bytes 884740
  239.1 20.9 %copy-start.10 = (f32[144,1536]{1,0:T(8,128)}, f32[144,1536]{1,0:T(8,128)S(1)}, u32[]{:S(2)}) copy-start(f32[144,1536]{1,0:T(8,128)S(1)} %collective-permute-done.8.refs_6_.refs_2_.refs_7_) | copy-start | bytes 2654212
  263.6 54.6 %collective-permute-start.13 = (f32[1152,768]{1,0:T(8,128)}, f32[1152,768]{1,0:T(8,128)}, u32[]{:S(2)}, u32[]{:S(2)}) collective-permute-start(f32[1152,768]{1,0:T(8,128)} %bitcast.63), channel_id=1, source_target_pairs={{0,1},{1,0},{2,3},{3,2},{4,5},{5,4},{6,7},{7,6},{8,9},{9,8},{10,11... | collective-permute-start | bytes 10616840 | tf_op jit(solution)/shard_map/ppermute | solution.py:929
  264.2 54.0 %collective-permute-start.14 = (f32[1152,384]{1,0:T(8,128)}, f32[1152,384]{1,0:T(8,128)S(1)}, u32[]{:S(2)}, u32[]{:S(2)}) collective-permute-start(f32[1152,384]{1,0:T(8,128)} %bitcast.11), channel_id=1, source_target_pairs={{0,4},{1,5},{2,6},{3,7},{4,0},{5,1},{6,2},{7,3},{8,12},{9,13},{10,... | collective-permute-start | bytes 5308424 | tf_op jit(solution)/shard_map/ppermute | solution.py:929
  266.9 51.3 %collective-permute-start.12 = (f32[144,2048]{1,0:T(8,128)}, f32[144,2048]{1,0:T(8,128)S(1)}, u32[]{:S(2)}, u32[]{:S(2)}) collective-permute-start(f32[144,2048]{1,0:T(8,128)} %get-tuple-element.358), channel_id=1, source_target_pairs={{0,2},{1,3},{2,0},{3,1},{4,6},{5,7},{6,4},{7,5},{8,10},{9,11},{10,... | collective-permute-start | bytes 3538952 | tf_op jit(solution)/shard_map/ppermute | solution.py:929
  267.7 50.5 %collective-permute-start.11 = (f32[72,1536]{1,0:T(8,128)}, f32[72,1536]{1,0:T(8,128)S(1)}, u32[]{:S(2)}, u32[]{:S(2)}) collective-permute-start(f32[72,1536]{1,0:T(8,128)} %get-tuple-element.357), channel_id=1, source_target_pairs={{0,4},{1,5},{2,6},{3,7},{4,0},{5,1},{6,2},{7,3},{8,12},{9,13},{10,... | collective-permute-start | bytes 1327112 | tf_op jit(solution)/shard_map/ppermute | solution.py:929
  267.7 49.9 %collective-permute-start.10 = (f32[36,1024]{1,0:T(8,128)}, f32[36,1024]{1,0:T(8,128)S(1)}, u32[]{:S(2)}, u32[]{:S(2)}) collective-permute-start(f32[36,1024]{1,0:T(8,128)} %get-tuple-element.356), channel_id=1, source_target_pairs={{0,8},{1,9},{2,10},{3,11},{4,12},{5,13},{6,14},{7,15},{8,0},{9,1},... | collective-permute-start | bytes 442376 | tf_op jit(solution)/shard_map/ppermute | solution.py:929
  325.4 41.0 %collective-permute-start.15 = (f32[576,2688]{1,0:T(8,128)}, f32[576,2688]{1,0:T(8,128)}, u32[]{:S(2)}, u32[]{:S(2)}) collective-permute-start(f32[576,2688]{1,0:T(8,128)} %get-tuple-element.379), channel_id=1, source_target_pairs={{0,16},{16,0},{1,17},{17,1},{2,18},{18,2},{3,19},{19,3},{4,20},{20... | collective-permute-start | bytes 18579464 | tf_op jit(solution)/shard_map/ppermute | solution.py:931
  325.4 40.9 %collective-permute-start.18 = (f32[576,768]{1,0:T(8,128)}, f32[576,768]{1,0:T(8,128)S(1)}, u32[]{:S(2)}, u32[]{:S(2)}) collective-permute-start(f32[576,768]{1,0:T(8,128)} %get-tuple-element.382), channel_id=1, source_target_pairs={{0,2},{1,3},{2,0},{3,1},{4,6},{5,7},{6,4},{7,5},{8,10},{9,11},{10,... | collective-permute-start | bytes 5308424 | tf_op jit(solution)/shard_map/ppermute | solution.py:929
  326.2 40.0 %collective-permute-start.19 = (f32[576,384]{1,0:T(8,128)}, f32[576,384]{1,0:T(8,128)S(1)}, u32[]{:S(2)}, u32[]{:S(2)}) collective-permute-start(f32[576,384]{1,0:T(8,128)} %get-tuple-element.383), channel_id=1, source_target_pairs={{0,1},{1,0},{2,3},{3,2},{4,5},{5,4},{6,7},{7,6},{8,9},{9,8},{10,11... | collective-permute-start | bytes 2654216 | tf_op jit(solution)/shard_map/ppermute | solution.py:929
  327.7 38.5 %collective-permute-start.17 = (f32[72,2048]{1,0:T(8,128)}, f32[72,2048]{1,0:T(8,128)S(1)}, u32[]{:S(2)}, u32[]{:S(2)}) collective-permute-start(f32[72,2048]{1,0:T(8,128)} %get-tuple-element.381), channel_id=1, source_target_pairs={{0,4},{1,5},{2,6},{3,7},{4,0},{5,1},{6,2},{7,3},{8,12},{9,13},{10,... | collective-permute-start | bytes 1769480 | tf_op jit(solution)/shard_map/ppermute | solution.py:929
  330.5 35.8 %collective-permute-start.16 = (f32[36,1536]{1,0:T(8,128)}, f32[36,1536]{1,0:T(8,128)S(1)}, u32[]{:S(2)}, u32[]{:S(2)}) collective-permute-start(f32[36,1536]{1,0:T(8,128)} %get-tuple-element.380), channel_id=1, source_target_pairs={{0,8},{1,9},{2,10},{3,11},{4,12},{5,13},{6,14},{7,15},{8,0},{9,1},... | collective-permute-start | bytes 663560 | tf_op jit(solution)/shard_map/ppermute | solution.py:929
  366.2 13.2 %copy-start.25 = (f32[36,1536]{1,0:T(8,128)}, f32[36,1536]{1,0:T(8,128)S(1)}, u32[]{:S(2)}) copy-start(f32[36,1536]{1,0:T(8,128)S(1)} %collective-permute-done.16.refs_9_) | copy-start | bytes 663556
  366.3 13.2 %copy-start.15 = (f32[72,2048]{1,0:T(8,128)}, f32[72,2048]{1,0:T(8,128)S(1)}, u32[]{:S(2)}) copy-start(f32[72,2048]{1,0:T(8,128)S(1)} %collective-permute-done.17.refs_3_.refs_13_) | copy-start | bytes 1769476
  366.3 13.2 %copy-start.11 = (f32[576,384]{1,0:T(8,128)}, f32[576,384]{1,0:T(8,128)S(1)}, u32[]{:S(2)}) copy-start(f32[576,384]{1,0:T(8,128)S(1)} %collective-permute-done.19.refs_9_.refs_6_.refs_22_) | copy-start | bytes 2654212
  366.3 13.2 %copy-start.6 = (f32[576,768]{1,0:T(8,128)}, f32[576,768]{1,0:T(8,128)S(1)}, u32[]{:S(2)}) copy-start(f32[576,768]{1,0:T(8,128)S(1)} %collective-permute-done.18.refs_6_.refs_2_.refs_17_) | copy-start | bytes 5308420
  379.5 11.7 %copy-start.41 = (f32[1152]{0:T(1024)S(1)}, f32[1152]{0:T(1024)}, u32[]{:S(2)}) copy-start(f32[1152]{0:T(1024)} %param.36) | copy-start | bytes 13828
  379.5 12.3 %copy-start.38 = (f32[4,1,1152]{2,1,0:T(1,128)S(1)}, f32[4,1,1152]{2,1,0:T(1,128)}, u32[]{:S(2)}) copy-start(f32[4,1,1152]{2,1,0:T(1,128)} %get-tuple-element.439) | copy-start | bytes 55300
  379.5 12.4 %copy-start.30 = (f32[1,4608]{1,0:T(1,128)S(1)}, f32[1,4608]{1,0:T(1,128)}, u32[]{:S(2)}) copy-start(f32[1,4608]{1,0:T(1,128)} %get-tuple-element.438) | copy-start | bytes 55300
  379.5 12.6 %copy-start.33 = (f32[4,4,1152]{2,1,0:T(4,128)S(1)}, f32[4,4,1152]{2,1,0:T(4,128)}, u32[]{:S(2)}) copy-start(f32[4,4,1152]{2,1,0:T(4,128)} %get-tuple-element.436) | copy-start | bytes 221188
  379.5 15.5 %copy-start.45 = (f32[1,1920]{1,0:T(1,128)S(1)}, f32[1,1920]{1,0:T(1,128)}, u32[]{:S(2)}) copy-start(f32[1,1920]{1,0:T(1,128)} %get-tuple-element.441) | copy-start | bytes 23044
  383.7 49.1 %collective-permute-start.20 = (f32[576,1920]{1,0:T(8,128)}, f32[576,1920]{1,0:T(8,128)}, u32[]{:S(2)}, u32[]{:S(2)}) collective-permute-start(f32[576,1920]{1,0:T(8,128)} %get-tuple-element.406), channel_id=1, source_target_pairs={{0,16},{16,0},{1,17},{17,1},{2,18},{18,2},{3,19},{19,3},{4,20},{20... | collective-permute-start | bytes 13271048 | tf_op jit(solution)/shard_map/ppermute | solution.py:931
  383.7 49.1 %collective-permute-start.24 = (f32[288,2688]{1,0:T(8,128)}, f32[288,2688]{1,0:T(8,128)}, u32[]{:S(2)}, u32[]{:S(2)}) collective-permute-start(f32[288,2688]{1,0:T(8,128)} %get-tuple-element.410), channel_id=1, source_target_pairs={{0,1},{1,0},{2,3},{3,2},{4,5},{5,4},{6,7},{7,6},{8,9},{9,8},{10,11... | collective-permute-start | bytes 9289736 | tf_op jit(solution)/shard_map/ppermute | solution.py:929
  392.2 40.6 %collective-permute-start.22 = (f32[288,768]{1,0:T(8,128)}, f32[288,768]{1,0:T(8,128)S(1)}, u32[]{:S(2)}, u32[]{:S(2)}) collective-permute-start(f32[288,768]{1,0:T(8,128)} %get-tuple-element.408), channel_id=1, source_target_pairs={{0,4},{1,5},{2,6},{3,7},{4,0},{5,1},{6,2},{7,3},{8,12},{9,13},{10,... | collective-permute-start | bytes 2654216 | tf_op jit(solution)/shard_map/ppermute | solution.py:929
  392.8 40.0 %collective-permute-start.23 = (f32[288,384]{1,0:T(8,128)}, f32[288,384]{1,0:T(8,128)S(1)}, u32[]{:S(2)}, u32[]{:S(2)}) collective-permute-start(f32[288,384]{1,0:T(8,128)} %get-tuple-element.409), channel_id=1, source_target_pairs={{0,2},{1,3},{2,0},{3,1},{4,6},{5,7},{6,4},{7,5},{8,10},{9,11},{10,... | collective-permute-start | bytes 1327112 | tf_op jit(solution)/shard_map/ppermute | solution.py:929
  394.0 38.7 %collective-permute-start.21 = (f32[36,2048]{1,0:T(8,128)}, f32[36,2048]{1,0:T(8,128)S(1)}, u32[]{:S(2)}, u32[]{:S(2)}) collective-permute-start(f32[36,2048]{1,0:T(8,128)} %get-tuple-element.407), channel_id=1, source_target_pairs={{0,8},{1,9},{2,10},{3,11},{4,12},{5,13},{6,14},{7,15},{8,0},{9,1},... | collective-permute-start | bytes 884744 | tf_op jit(solution)/shard_map/ppermute | solution.py:929
  441.6 10.6 %copy-start.29 = (f32[4,1152]{1,0:T(4,128)S(1)}, f32[4,1152]{1,0:T(4,128)}, u32[]{:S(2)}) copy-start(f32[4,1152]{1,0:T(4,128)} %copy-done.28) | copy-start | bytes 55300
  446.6 43.4 %collective-permute-start.28 = (f32[288,1920]{1,0:T(8,128)}, f32[288,1920]{1,0:T(8,128)S(1)}, u32[]{:S(2)}, u32[]{:S(2)}) collective-permute-start(f32[288,1920]{1,0:T(8,128)} %get-tuple-element.428), channel_id=1, source_target_pairs={{0,1},{1,0},{2,3},{3,2},{4,5},{5,4},{6,7},{7,6},{8,9},{9,8},{10,11... | collective-permute-start | bytes 6635528 | tf_op jit(solution)/shard_map/ppermute | solution.py:929
  447.4 37.0 %collective-permute-start.27 = (f32[144,2688]{1,0:T(8,128)}, f32[144,2688]{1,0:T(8,128)S(1)}, u32[]{:S(2)}, u32[]{:S(2)}) collective-permute-start(f32[144,2688]{1,0:T(8,128)} %get-tuple-element.427), channel_id=1, source_target_pairs={{0,2},{1,3},{2,0},{3,1},{4,6},{5,7},{6,4},{7,5},{8,10},{9,11},{10,... | collective-permute-start | bytes 4644872 | tf_op jit(solution)/shard_map/ppermute | solution.py:929
  449.2 31.3 %collective-permute-start.25 = (f32[144,768]{1,0:T(8,128)}, f32[144,768]{1,0:T(8,128)S(1)}, u32[]{:S(2)}, u32[]{:S(2)}) collective-permute-start(f32[144,768]{1,0:T(8,128)} %get-tuple-element.425), channel_id=1, source_target_pairs={{0,8},{1,9},{2,10},{3,11},{4,12},{5,13},{6,14},{7,15},{8,0},{9,1},... | collective-permute-start | bytes 1327112 | tf_op jit(solution)/shard_map/ppermute | solution.py:929
  451.2 29.3 %collective-permute-start.26 = (f32[144,384]{1,0:T(8,128)}, f32[144,384]{1,0:T(8,128)S(1)}, u32[]{:S(2)}, u32[]{:S(2)}) collective-permute-start(f32[144,384]{1,0:T(8,128)} %get-tuple-element.426), channel_id=1, source_target_pairs={{0,8},{1,9},{2,10},{3,11},{4,12},{5,13},{6,14},{7,15},{8,0},{9,1},... | collective-permute-start | bytes 663560 | tf_op jit(solution)/shard_map/ppermute | solution.py:929
  480.5 9.4 %copy-start.27 = (f32[144,384]{1,0:T(8,128)}, f32[144,384]{1,0:T(8,128)S(1)}, u32[]{:S(2)}) copy-start(f32[144,384]{1,0:T(8,128)S(1)} %collective-permute-done.26.refs_24_) | copy-start | bytes 663556
  480.5 9.4 %copy-start.20 = (f32[144,768]{1,0:T(8,128)}, f32[144,768]{1,0:T(8,128)S(1)}, u32[]{:S(2)}) copy-start(f32[144,768]{1,0:T(8,128)S(1)} %collective-permute-done.25.refs_19_) | copy-start | bytes 1327108
  495.6 23.1 %collective-permute-start.30 = (f32[144,1920]{1,0:T(8,128)}, f32[144,1920]{1,0:T(8,128)S(1)}, u32[]{:S(2)}, u32[]{:S(2)}) collective-permute-start(f32[144,1920]{1,0:T(8,128)} %get-tuple-element.444), channel_id=1, source_target_pairs={{0,2},{1,3},{2,0},{3,1},{4,6},{5,7},{6,4},{7,5},{8,10},{9,11},{10,... | collective-permute-start | bytes 3317768 | tf_op jit(solution)/shard_map/ppermute | solution.py:929
  496.8 21.8 %collective-permute-start.29 = (f32[72,2688]{1,0:T(8,128)}, f32[72,2688]{1,0:T(8,128)S(1)}, u32[]{:S(2)}, u32[]{:S(2)}) collective-permute-start(f32[72,2688]{1,0:T(8,128)} %get-tuple-element.443), channel_id=1, source_target_pairs={{0,4},{1,5},{2,6},{3,7},{4,0},{5,1},{6,2},{7,3},{8,12},{9,13},{10,... | collective-permute-start | bytes 2322440 | tf_op jit(solution)/shard_map/ppermute | solution.py:929
  498.5 19.4 %collective-permute-start.31 = (f32[4,10368]{1,0:T(4,128)S(1)}, f32[4,10368]{1,0:T(4,128)S(1)}, u32[]{:S(2)}, u32[]{:S(2)}) collective-permute-start(f32[4,10368]{1,0:T(4,128)S(1)} %pad_maximum_fusion.6), channel_id=1, source_target_pairs={{0,8},{1,9},{2,10},{3,11},{4,12},{5,13},{6,14},{7,15},{8,0},{9,1},... | collective-permute-start | bytes 497672 | tf_op jit(solution)/shard_map/ppermute | solution.py:936
  523.9 29.0 %collective-permute-start.33 = (f32[72,1920]{1,0:T(8,128)}, f32[72,1920]{1,0:T(8,128)S(1)}, u32[]{:S(2)}, u32[]{:S(2)}) collective-permute-start(f32[72,1920]{1,0:T(8,128)} %get-tuple-element.454), channel_id=1, source_target_pairs={{0,4},{1,5},{2,6},{3,7},{4,0},{5,1},{6,2},{7,3},{8,12},{9,13},{10,... | collective-permute-start | bytes 1658888 | tf_op jit(solution)/shard_map/ppermute | solution.py:929
  525.5 27.3 %collective-permute-start.32 = (f32[36,2688]{1,0:T(8,128)}, f32[36,2688]{1,0:T(8,128)S(1)}, u32[]{:S(2)}, u32[]{:S(2)}) collective-permute-start(f32[36,2688]{1,0:T(8,128)} %get-tuple-element.453), channel_id=1, source_target_pairs={{0,8},{1,9},{2,10},{3,11},{4,12},{5,13},{6,14},{7,15},{8,0},{9,1},... | collective-permute-start | bytes 1161224 | tf_op jit(solution)/shard_map/ppermute | solution.py:929
  526.6 26.2 %collective-permute-start.34 = (f32[8,10368]{1,0:T(8,128)S(1)}, f32[8,10368]{1,0:T(8,128)S(1)}, u32[]{:S(2)}, u32[]{:S(2)}) collective-permute-start(f32[8,10368]{1,0:T(8,128)S(1)} %pad_maximum_fusion.5), channel_id=1, source_target_pairs={{0,4},{1,5},{2,6},{3,7},{4,0},{5,1},{6,2},{7,3},{8,12},{9,13},{10,... | collective-permute-start | bytes 995336 | tf_op jit(solution)/shard_map/ppermute | solution.py:936
  556.8 16.9 %copy-start.46 = (s32[64]{0:T(128)S(1)}, s32[64]{0:T(128)}, u32[]{:S(2)}) copy-start(s32[64]{0:T(128)} %param.23) | copy-start | bytes 772
  556.8 15.9 %collective-permute-start.36 = (f32[16,10368]{1,0:T(8,128)S(1)}, f32[16,10368]{1,0:T(8,128)S(1)}, u32[]{:S(2)}, u32[]{:S(2)}) collective-permute-start(f32[16,10368]{1,0:T(8,128)S(1)} %pad_maximum_fusion.3), channel_id=1, source_target_pairs={{0,2},{1,3},{2,0},{3,1},{4,6},{5,7},{6,4},{7,5},{8,10},{9,11},{10,... | collective-permute-start | bytes 1990664 | tf_op jit(solution)/shard_map/ppermute | solution.py:936
  559.1 13.6 %collective-permute-start.35 = (f32[36,1920]{1,0:T(8,128)}, f32[36,1920]{1,0:T(8,128)S(1)}, u32[]{:S(2)}, u32[]{:S(2)}) collective-permute-start(f32[36,1920]{1,0:T(8,128)} %add.290), channel_id=1, source_target_pairs={{0,8},{1,9},{2,10},{3,11},{4,12},{5,13},{6,14},{7,15},{8,0},{9,1},... | collective-permute-start | bytes 829448 | tf_op jit(solution)/shard_map/ppermute | solution.py:929
  572.8 21.1 %copy-start.24 = (f32[36,1920]{1,0:T(8,128)}, f32[36,1920]{1,0:T(8,128)S(1)}, u32[]{:S(2)}) copy-start(f32[36,1920]{1,0:T(8,128)S(1)} %collective-permute-done.35.refs_34_) | copy-start | bytes 829444
  572.9 18.0 %collective-permute-start.37 = (f32[32,10368]{1,0:T(8,128)S(1)}, f32[32,10368]{1,0:T(8,128)}, u32[]{:S(2)}, u32[]{:S(2)}) collective-permute-start(f32[32,10368]{1,0:T(8,128)S(1)} %pad_maximum_fusion.1), channel_id=1, source_target_pairs={{0,1},{1,0},{2,3},{3,2},{4,5},{5,4},{6,7},{7,6},{8,9},{9,8},{10,11... | collective-permute-start | bytes 3981320 | tf_op jit(solution)/shard_map/ppermute | solution.py:936
  593.8 22.9 %collective-permute-start.38 = (f32[64,10368]{1,0:T(8,128)}, f32[64,10368]{1,0:T(8,128)}, u32[]{:S(2)}, u32[]{:S(2)}) collective-permute-start(f32[64,10368]{1,0:T(8,128)} %pad_maximum_fusion.own_ref.own_cond_ref), channel_id=1, source_target_pairs={{0,16},{16,0},{1,17},{17,1},{2,18},{18,2},{3,19},{19,3},{4,20},{20... | collective-permute-start | bytes 7962632 | tf_op jit(solution)/shard_map/ppermute | solution.py:938
  602.2 9.3 %copy-start.23 = (f32[36,2048]{1,0:T(8,128)S(1)}, f32[36,2048]{1,0:T(8,128)}, u32[]{:S(2)}) copy-start(f32[36,2048]{1,0:T(8,128)} %get-tuple-element.487) | copy-start | bytes 884740
  602.2 9.3 %copy-start.26 = (f32[36,1536]{1,0:T(8,128)S(1)}, f32[36,1536]{1,0:T(8,128)}, u32[]{:S(2)}) copy-start(f32[36,1536]{1,0:T(8,128)} %get-tuple-element.486) | copy-start | bytes 663556
  602.3 9.3 %copy-start.32 = (f32[36,1024]{1,0:T(8,128)S(1)}, f32[36,1024]{1,0:T(8,128)}, u32[]{:S(2)}) copy-start(f32[36,1024]{1,0:T(8,128)} %get-tuple-element.485) | copy-start | bytes 442372
  622.7 21.6 %copy-start.1 = (bf16[1001,1152]{1,0:T(8,128)(2,1)S(1)}, bf16[1001,1152]{1,0:T(8,128)(2,1)}, u32[]{:S(2)}) copy-start(bf16[1001,1152]{1,0:T(8,128)(2,1)} %param.26) | copy-start | bytes 6918916
  (23 other events, 114.3 us)

commit v3 on v2

--- a/solution.py
+++ b/solution.py
@@ -63,7 +63,7 @@
             normal, _ = normed(x_ref[rows].astype(F32))
             h_ref[rows] = (normal * (1.0 + mod_ref[tile, 1:2]) + mod_ref[tile, 0:1]).astype(BF16)
 
-    out_ref[...] = (dot(h_ref[...], w_ref[...]) + b_ref[...]).astype(BF16)
+    out_ref[...] = (dot(w_ref[...], h_ref[...], TT) + b_ref[...]).astype(BF16)
 
 
 def qkv_call(x, mod, w, bias):
@@ -80,206 +80,155 @@
             pl.BlockSpec((tokens, width), lambda j: (0, 0)),
             pl.BlockSpec(mod.shape, lambda j: (0, 0, 0)),
             pl.BlockSpec((width, block), lambda j: (0, j)),
-            pl.BlockSpec((1, block), lambda j: (0, j)),
+            pl.BlockSpec((block, 1), lambda j: (j, 0)),
         ],
         out_specs=[
             pl.BlockSpec((tokens, width), lambda j: (0, 0)),
-            pl.BlockSpec((tokens, block), lambda j: (0, j)),
-        ],
-        out_shape=[shaped((tokens, width), BF16), shaped((tokens, wide), BF16)],
+            pl.BlockSpec((block, tokens), lambda j: (j, 0)),
+        ],
+        out_shape=[shaped((tokens, width), BF16), shaped((wide, tokens), BF16)],
     )(x, mod, w, bias)
 
 
-def pair_select(offset, head_width):
-    row = lax.broadcasted_iota(jnp.int32, (256, 256), 0)
-    col = lax.broadcasted_iota(jnp.int32, (256, 256), 1)
-    lane = col & 127
-    base = offset + jnp.where(col >= 128, head_width, 0)
-    return jnp.where((lane < head_width) & (row == base + lane), 1.0, 0.0).astype(BF16)
-
-
-def attention_body(flag_ref, qkv_ref, keep_ref, p_ref, ot_ref, om_ref, *, width, head_width):
-    pair = pl.program_id(1)
-    column = pair * (2 * head_width)
-    start = pl.multiple_of(column // 128 * 128, 128)
-    select = pair_select(column - start, head_width)
+def heads_of(ref, head_width):
+    values = ref[...].astype(F32)
+    return [values[head * head_width : (head + 1) * head_width] for head in range(2)]
+
+
+def attention_body(flag_ref, q_ref, k_ref, v_ref, keep_ref, p_ref, ot_ref, om_ref):
+    head_width = ot_ref.shape[1]
     scale = math.log2(math.e) / math.sqrt(head_width)
-    tokens = qkv_ref.shape[0]
-
-    @pl.when(pair == 0)
-    def _():
-        om_ref[...] = jnp.zeros_like(om_ref)
-
-    q = dot(qkv_ref[:, pl.ds(start, 256)], select).astype(BF16)
-    k = dot(qkv_ref[:, pl.ds(width + start, 256)], select).astype(BF16)
-    v = dot(qkv_ref[:, pl.ds(2 * width + start, 256)], select)
-    lane = lax.broadcasted_iota(jnp.int32, v.shape, 1) & 127
-    v = jnp.where(lane == head_width, 1.0, v).astype(BF16)
+    tokens = q_ref.shape[1]
+    q, k = [[part.astype(BF16) for part in heads_of(ref, head_width)] for ref in (q_ref, k_ref)]
+    v = [jnp.concatenate([part, jnp.ones((8, tokens), F32)], axis=0).astype(BF16) for part in heads_of(v_ref, head_width)]
 
     def part(head, first, count):
         rows = slice(first, first + count)
-        lanes = slice(128 * head, 128 * head + 128)
-        scores = dot(k[rows, lanes], q[rows, lanes], NT)
+        scores = dot(k[head][:, rows], q[head][:, rows], TN)
         top = jnp.max(scores, axis=0, keepdims=True)
         expo = jnp.exp2((scores - top) * scale)
         total = jnp.sum(expo, axis=0, keepdims=True)
         probs = (expo * (1.0 / total)).astype(BF16)
         p_ref[head, rows, rows] = probs
-        mixed = dot(v[rows, lanes], probs, TN)
+        mixed = dot(v[head][:, rows], probs)
         ot_ref[head, :, rows] = mixed[:head_width] * (1.0 / mixed[head_width : head_width + 1])
-        return (mixed * keep_ref[head, :, rows]).astype(BF16)
-
-    def finish(parts):
-        mixed = jnp.concatenate([jnp.concatenate(row, axis=1) for row in parts], axis=0)
-        new = dot(mixed, select, TT)
-        om_ref[:, pl.ds(start, 256)] = (om_ref[:, pl.ds(start, 256)].astype(F32) + new).astype(BF16)
+        return mixed[:head_width] * keep_ref[head, :, rows]
+
+    def run(count):
+        made = [
+            jnp.concatenate([part(head, at, count) for at in range(0, tokens, count)], axis=1) for head in range(2)
+        ]
+        om_ref[...] = jnp.concatenate(made, axis=0).astype(BF16)
 
     whole = flag_ref[pl.program_id(0)] == 1
-
-    @pl.when(whole)
-    def _():
-        finish([[part(head, 0, tokens)] for head in range(2)])
-
-    @pl.when(jnp.logical_not(whole))
-    def _():
-        finish([[part(head, at, ROW) for at in range(0, tokens, ROW)] for head in range(2)])
+    pl.when(whole)(lambda: run(tokens))
+    pl.when(jnp.logical_not(whole))(lambda: run(ROW))
 
 
 def attention_call(flag, qkv, keep, heads):
-    tokens, wide = qkv.shape
+    wide, tokens = qkv.shape
     width = wide // 3
     head_width = width // heads
     groups = tokens // GROUP
+    pairs = heads // 2
+    rows = 2 * head_width
+
+    def third(number):
+        return pl.BlockSpec((rows, GROUP), functools.partial(lambda g, h, base: (base + h, g), base=number * pairs))
+
     return call(
-        functools.partial(attention_body, width=width, head_width=head_width),
+        attention_body,
         "attention",
         2 * 2 * heads * tokens * GROUP * 256,
         2 * tokens * wide + 2 * heads * tokens * GROUP + 6 * tokens * width,
-        grid=(groups, heads // 2),
+        grid=(groups, pairs),
         in_specs=[
             pl.BlockSpec(memory_space=pltpu.SMEM),
-            pl.BlockSpec((GROUP, wide), lambda g, h: (g, 0)),
+            third(0),
+            third(1),
+            third(2),
             pl.BlockSpec((2, 1, GROUP), lambda g, h: (h, 0, g)),
         ],
         out_specs=[
             pl.BlockSpec((2, GROUP, GROUP), lambda g, h: (h, 0, g)),
             pl.BlockSpec((2, head_width, GROUP), lambda g, h: (h, 0, g)),
-            pl.BlockSpec((GROUP, width), lambda g, h: (g, 0)),
+            third(0),
         ],
         out_shape=[
             shaped((heads, GROUP, tokens), BF16),
             shaped((heads, head_width, tokens), F32),
-            shaped((tokens, width), BF16),
-        ],
-    )(flag, qkv, keep)
-
-
-def attention_back_body(
-    flag_ref, qkv_ref, do_ref, p_ref, ot_ref, *refs, width, head_width, first_pair, span
-):
-    out_ref, ready_ref, ds_ref = refs[-3:]
-    step = pl.program_id(1)
-    pair = step + first_pair
-    column = pair * (2 * head_width)
-    start = pl.multiple_of(column // 128 * 128, 128)
-    select = pair_select(column - start, head_width)
+            shaped((width, tokens), BF16),
+        ],
+    )(flag, qkv, qkv, qkv, keep)
+
+
+def attention_back_body(flag_ref, q_ref, k_ref, v_ref, do_ref, keep_ref, p_ref, ot_ref, out_ref, ds_ref):
+    head_width = ot_ref.shape[1]
     scale = 1.0 / math.sqrt(head_width)
-    tokens = qkv_ref.shape[0]
-
-    @pl.when(step == 0)
-    def _():
-        out_ref[...] = refs[0][...] if len(refs) > 3 else jnp.zeros_like(out_ref)
-
-    q = dot(qkv_ref[:, pl.ds(start, 256)], select).astype(BF16)
-    k = dot(qkv_ref[:, pl.ds(width + start, 256)], select).astype(BF16)
-    v = dot(qkv_ref[:, pl.ds(2 * width + start, 256)], select).astype(BF16)
-    window = do_ref[:, pl.ds(start, 256)]
-    do = dot(window, select).astype(BF16)
-    do_t = dot(select, window, TT)
-    delta = [
-        jnp.sum(do_t[128 * head : 128 * head + head_width] * ot_ref[head], axis=0, keepdims=True)
-        for head in range(2)
-    ]
-
-    def grad_scores(head, first, count):
-        rows = slice(first, first + count)
-        lanes = slice(128 * head, 128 * head + 128)
-        dp = dot(v[rows, lanes], do[rows, lanes], NT)
-        probs = p_ref[head, rows, rows].astype(F32)
-        return (probs * (dp - delta[head][:, rows])).astype(BF16)
-
-    def add(base, value, dims):
-        new = dot(value, select, dims)
-        spot = pl.ds(base + start, 256)
-        out_ref[:, spot] = (out_ref[:, spot].astype(F32) + new).astype(BF16)
+    tokens = q_ref.shape[1]
+    q, k, v = [[part.astype(BF16) for part in heads_of(ref, head_width)] for ref in (q_ref, k_ref, v_ref)]
+    kept = [part * keep_ref[head] for head, part in enumerate(heads_of(do_ref, head_width))]
+    do = [part.astype(BF16) for part in kept]
+    delta = [jnp.sum(kept[head] * ot_ref[head], axis=0, keepdims=True) for head in range(2)]
 
     def run(count):
-        dq, dk, dv = [], [], []
+        made = [[], [], []]
         for head in range(2):
-            lanes = slice(128 * head, 128 * head + 128)
-            dq_row, dk_col, dv_col = [], [], []
+            row = [[], [], []]
             for first in range(0, tokens, count):
                 rows = slice(first, first + count)
-                ds = grad_scores(head, first, count)
+                dp = dot(v[head][:, rows], do[head][:, rows], TN)
+                probs = p_ref[head, rows, rows].astype(F32)
+                ds = (probs * (dp - delta[head][:, rows])).astype(BF16)
                 if count == tokens:
                     ds_ref[head] = ds
                     ds = ds_ref[head]
-                dq_row.append((dot(k[rows, lanes], ds, TN) * scale).astype(BF16))
-                dk_col.append((dot(ds, q[rows, lanes]) * scale).astype(BF16))
-                dv_col.append(dot(p_ref[head, rows, rows], do[rows, lanes]).astype(BF16))
-            dq.append(jnp.concatenate(dq_row, axis=1))
-            dk.append(jnp.concatenate(dk_col, axis=0))
-            dv.append(jnp.concatenate(dv_col, axis=0))
-        add(0, jnp.concatenate(dq, axis=0), TT)
-        add(width, jnp.concatenate(dk, axis=1), NT)
-        add(2 * width, jnp.concatenate(dv, axis=1), NT)
+                row[0].append(dot(k[head][:, rows], ds) * scale)
+                row[1].append(dot(q[head][:, rows], ds, NT) * scale)
+                row[2].append(dot(do[head][:, rows], p_ref[head, rows, rows], NT))
+            for third in range(3):
+                made[third].append(jnp.concatenate(row[third], axis=1))
+        for third in range(3):
+            out_ref[third] = jnp.concatenate(made[third], axis=0).astype(BF16)
 
     whole = flag_ref[pl.program_id(0)] == 1
-
-    @pl.when(whole)
-    def _():
-        run(tokens)
-
-    @pl.when(jnp.logical_not(whole))
-    def _():
-        run(ROW)
-
-    @pl.when(step == pl.num_programs(1) - 1)
-    def _():
-        first, size = span
-        for third in range(3):
-            at = third * width + first
-            ready_ref[:, third * size : (third + 1) * size] = out_ref[:, at : at + size]
-
-
-def attention_back_call(flag, qkv, do, probs, mixed, part, *before):
-    tokens, wide = qkv.shape
+    pl.when(whole)(lambda: run(tokens))
+    pl.when(jnp.logical_not(whole))(lambda: run(ROW))
+
+
+def attention_back_call(flag, qkv, do, keep, probs, mixed, part):
+    wide, tokens = qkv.shape
     width = wide // 3
     heads, head_width = mixed.shape[:2]
     groups = tokens // GROUP
     pairs = heads // 4
     base = part * pairs
-    cut = width // 2 // 128 * 128
-    span = (cut, width - cut) if part else (0, cut)
-    whole = pl.BlockSpec((GROUP, wide), lambda g, h: (g, 0))
+    rows = 2 * head_width
+
+    def third(number):
+        first = number * heads // 2 + base
+        return pl.BlockSpec((rows, GROUP), functools.partial(lambda g, h, first: (first + h, g), first=first))
+
     return call(
-        functools.partial(attention_back_body, width=width, head_width=head_width, first_pair=base, span=span),
+        attention_back_body,
         "attention_back",
         2 * 2 * heads * tokens * GROUP * 256,
-        4 * tokens * wide + heads * tokens * GROUP + 6 * tokens * width,
+        2 * tokens * wide + heads * tokens * GROUP + 6 * tokens * width,
         grid=(groups, pairs),
         in_specs=[
             pl.BlockSpec(memory_space=pltpu.SMEM),
-            whole,
-            pl.BlockSpec((GROUP, width), lambda g, h: (g, 0)),
+            third(0),
+            third(1),
+            third(2),
+            third(0),
+            pl.BlockSpec((2, 1, GROUP), lambda g, h: (base + h, 0, g)),
             pl.BlockSpec((2, GROUP, GROUP), lambda g, h: (base + h, 0, g)),
             pl.BlockSpec((2, head_width, GROUP), lambda g, h: (base + h, 0, g)),
-        ]
-        + [whole] * len(before),
-        out_specs=[whole, pl.BlockSpec((GROUP, 3 * span[1]), lambda g, h: (g, 0))],
-        out_shape=[shaped((tokens, wide), BF16), shaped((tokens, 3 * span[1]), BF16)],
+        ],
+        out_specs=pl.BlockSpec((3, rows, GROUP), lambda g, h: (0, h, g)),
+        out_shape=shaped((3, width // 2, tokens), BF16),
         scratch_shapes=[pltpu.VMEM((2, GROUP, GROUP), BF16)],
-    )(flag, qkv, do, probs, mixed, *before)
+    )(flag, qkv, qkv, qkv, do, keep, probs, mixed)
 
 
 def middle_body(
@@ -287,7 +236,7 @@
     a_ref, x1_ref, h_ref, h_away_ref, h_own_ref, dm_ref, sum_ref,
 ):
     tile = pl.program_id(0)
-    branch = dot(om_ref[...], w_ref[...]) + b_ref[...]
+    branch = dot(om_ref[...], w_ref[...], TN) + b_ref[...]
     a_ref[...] = branch
     middle = x_ref[...].astype(F32) + mod_ref[tile, 2:3] * branch
     x1_ref[...] = middle
@@ -314,7 +263,7 @@
         26 * tokens * width,
         grid=(tiles,),
         in_specs=[
-            rows,
+            pl.BlockSpec((width, ROW), lambda i: (0, i)),
             fixed,
             pl.BlockSpec((1, width), lambda i: (0, 0)),
             rows,
@@ -529,7 +478,7 @@
 
 
 def middle_back_body(
-    df_ref, w1_ref, x1_ref, mod_ref, top_ref, a_ref, wp_ref, head_ref,
+    df_ref, w1_ref, x1_ref, mod_ref, top_ref, a_ref, wp_ref,
     dx_ref, da_ref, do_ref, sum_ref,
 ):
     tile = pl.program_id(0)
@@ -540,14 +489,14 @@
     dx_ref[...] = dx
     da = (dx * mod_ref[tile, 2:3]).astype(BF16)
     da_ref[...] = da
-    do_ref[...] = (dot(da, wp_ref[...], NT) * head_ref[tile]).astype(BF16)
+    do_ref[...] = dot(wp_ref[...], da, NT).astype(BF16)
     sum_ref[0, 0:1] = jnp.sum(dx * a_ref[...], axis=0, keepdims=True)
     sum_ref[0, 1:2] = jnp.sum(grad, axis=0, keepdims=True)
     sum_ref[0, 2:3] = jnp.sum(grad * normal, axis=0, keepdims=True)
     sum_ref[0, 3:4] = jnp.sum(da.astype(F32), axis=0, keepdims=True)
 
 
-def middle_back_call(df, w1, x1, mod, top, a, wp, head_rows):
+def middle_back_call(df, w1, x1, mod, top, a, wp):
     tokens, width = x1.shape
     hidden = df.shape[1]
     tiles = tokens // ROW
@@ -566,116 +515,163 @@
             rows,
             rows,
             pl.BlockSpec((width, width), lambda i: (0, 0)),
-            pl.BlockSpec(head_rows.shape, lambda i: (0, 0, 0)),
-        ],
-        out_specs=[rows, rows, rows, pl.BlockSpec((1, 4, width), lambda i: (i, 0, 0))],
+        ],
+        out_specs=[
+            rows,
+            rows,
+            pl.BlockSpec((width, ROW), lambda i: (0, i)),
+            pl.BlockSpec((1, 4, width), lambda i: (i, 0, 0)),
+        ],
         out_shape=[
             shaped((tokens, width), F32),
             shaped((tokens, width), BF16),
-            shaped((tokens, width), BF16),
+            shaped((width, tokens), BF16),
             shaped((tiles, 4, width), F32),
         ],
-    )(df, w1, x1, mod, top, a, wp, head_rows)
-
-
-def step_of(counts):
-    return next(size for size in (512, 640, 384, 128) if all(count % size == 0 for count in counts))
-
-
-def operand_specs(pairs, step):
-    specs, starts, at = [], [], 0
-    for left, _, first, count in pairs:
-        base, steps = first // step, count // step
-        specs.append(pl.BlockSpec(left.shape, lambda j: (0, 0)))
-        specs.append(
+    )(df, w1, x1, mod, top, a, wp)
+
+
+class Wide:
+    def __init__(self, *parts):
+        self.parts = parts
+        self.count = sum(rows for _, _, rows in parts)
+        self.steps = 3
+
+    def arrays(self):
+        return [array for array, _, _ in self.parts]
+
+    def specs(self, at):
+        return [
             pl.BlockSpec(
-                (left.shape[0], step),
-                functools.partial(lambda j, at, base, steps: (0, base + jnp.clip(j - at, 0, steps - 1)), at=at, base=base, steps=steps),
+                (1, rows, array.shape[2]),
+                functools.partial(lambda j, at, index: (jnp.clip(j - at, 0, 2), index, 0), at=at, index=first // rows),
             )
+            for array, first, rows in self.parts
+        ]
+
+    def value(self, refs):
+        got = [ref[0] for ref in refs]
+        return jnp.concatenate(got, axis=0) if len(got) > 1 else got[0]
+
+    def product(self, left, right):
+        return dot(left, right, TT)
+
+    def sums(self, right):
+        return dot(jnp.ones((8, right.shape[1]), BF16), right, NT)[:1]
+
+
+class Plain:
+    def __init__(self, array, first, count, steps):
+        self.array, self.first, self.count, self.steps = array, first, count, steps
+
+    def arrays(self):
+        return [self.array]
+
+    def specs(self, at):
+        base, steps = self.first // self.count, self.steps
+        index = functools.partial(
+            lambda j, at, base, steps: (0, base + jnp.clip(j - at, 0, steps - 1)), at=at, base=base, steps=steps
         )
-        starts.append(at)
-        at += steps
-    return specs, starts + [at]
-
-
-def each_pair(starts, body):
-    if len(starts) == 2:
-        body(0)
-        return
-    step = pl.program_id(0)
-    for number in range(len(starts) - 1):
-        pl.when((step >= starts[number]) & (step < starts[number + 1]))(functools.partial(body, number))
-
-
-def columns_send_body(*refs, starts):
-    send_ref, sum_ref = refs[-2:]
-
-    def run(number):
-        grad = refs[2 * number + 1][...]
-        send_ref[...] = dot(refs[2 * number][...], grad, TN)
-        sum_ref[...] = jnp.sum(grad.astype(F32), axis=0, keepdims=True)
-
-    each_pair(starts, run)
-
-
-def columns_send_call(pairs, name):
-    tokens, half = pairs[0][0].shape
-    count = sum(pair[3] for pair in pairs)
-    step = step_of([pair[3] for pair in pairs])
-    specs, starts = operand_specs(pairs, step)
-    return call(
-        functools.partial(columns_send_body, starts=starts),
-        name,
-        2 * tokens * half * count,
-        2 * tokens * (count + half) + 4 * half * count,
-        grid=(count // step,),
-        in_specs=specs,
-        out_specs=[
-            pl.BlockSpec((half, step), lambda j: (0, j)),
-            pl.BlockSpec((1, step), lambda j: (0, j)),
-        ],
-        out_shape=[shaped((half, count), F32), shaped((1, count), F32)],
-    )(*[array for pair in pairs for array in pair[:2]])
-
-
-def columns_keep_body(*refs, starts):
-    got_ref, send_ref, keep_ref = refs[-3:]
-    rows = keep_ref.shape[0]
-
-    def run(number):
-        made = dot(refs[2 * number][...], refs[2 * number + 1][...], TN) + got_ref[...]
+        return [pl.BlockSpec((self.array.shape[0], self.count), index)]
+
+    def value(self, refs):
+        return refs[0][...]
+
+    def product(self, left, right):
+        return dot(left, right, TN)
+
+    def sums(self, right):
+        return jnp.sum(right.astype(F32), axis=0, keepdims=True)
+
+
+def columns_body(*refs, right, both):
+    count = len(right.arrays())
+    left_ref, right_refs, rest = refs[0], refs[1 : 1 + count], refs[1 + count :]
+    value = right.value(right_refs)
+    made = right.product(left_ref[...], value)
+    if both:
+        got_ref, send_ref, keep_ref = rest
+        made = made + got_ref[...]
+        rows = keep_ref.shape[0]
         send_ref[...] = made[rows:]
         keep_ref[...] = made[:rows]
-
-    each_pair(starts, run)
-
-
-def columns_keep_call(pairs, got, name):
-    tokens, half = pairs[0][0].shape
-    count = got.shape[1]
-    step = step_of([pair[3] for pair in pairs])
-    specs, starts = operand_specs(pairs, step)
-    out = pl.BlockSpec((half // 2, step), lambda j: (0, j))
+    else:
+        send_ref, sum_ref = rest
+        send_ref[...] = made
+        sum_ref[...] = right.sums(value)
+
+
+def columns_call(left, right, name, got=None):
+    tokens, half = left.shape
+    count = right.count * right.steps
+    both = got is not None
+    wide = pl.BlockSpec((half, right.count), lambda j: (0, j))
+    narrow = pl.BlockSpec((half // 2, right.count), lambda j: (0, j))
     made = call(
-        functools.partial(columns_keep_body, starts=starts),
+        functools.partial(columns_body, right=right, both=both),
         name,
         2 * tokens * half * count,
         2 * tokens * (count + half) + 8 * half * count,
-        grid=(count // step,),
-        in_specs=specs + [pl.BlockSpec((half, step), lambda j: (0, j))],
-        out_specs=[out, out],
-        out_shape=[shaped((half // 2, count), F32)] * 2,
-    )(*[array for pair in pairs for array in pair[:2]], got)
-    return [tuple(made)]
-
-
-def moved_body(left_ref, away_ref, own_ref, left_away_ref, left_own_ref):
-    left_away_ref[...] = dot(left_ref[...], away_ref[...]).astype(BF16)
-    left_own_ref[...] = dot(left_ref[...], own_ref[...]).astype(BF16)
-
-
-def moved_call(left, away, own):
-    tokens, width = left.shape
+        grid=(right.steps,),
+        in_specs=[pl.BlockSpec(left.shape, lambda j: (0, 0)), *right.specs(0)] + [wide] * both,
+        out_specs=[narrow, narrow] if both else [wide, pl.BlockSpec((1, right.count), lambda j: (0, j))],
+        out_shape=[shaped((half // 2, count), F32)] * 2
+        if both
+        else [shaped((half, count), F32), shaped((1, count), F32)],
+    )(left, *right.arrays(), *([got] if both else []))
+    return [tuple(made)] if both else made
+
+
+def pair_body(*refs, rights, both):
+    counts = [len(right.arrays()) for right in rights]
+    step = pl.program_id(0)
+    at = 0
+    rest = refs[2 + sum(counts) :]
+    for number, (right, count) in enumerate(zip(rights, counts)):
+        mine = (refs[at], *refs[at + 1 : at + 1 + count], *rest)
+        when = step < rights[0].steps if number == 0 else step >= rights[0].steps
+        pl.when(when)(functools.partial(columns_body, *mine, right=right, both=both))
+        at += 1 + count
+
+
+def pair_call(lefts, rights, name, got=None):
+    tokens, half = lefts[0].shape
+    step = rights[0].count
+    steps = sum(right.steps for right in rights)
+    count = step * steps
+    both = got is not None
+    wide = pl.BlockSpec((half, step), lambda j: (0, j))
+    narrow = pl.BlockSpec((half // 2, step), lambda j: (0, j))
+    operands, specs, at = [], [], 0
+    for left, right in zip(lefts, rights):
+        operands += [left, *right.arrays()]
+        specs += [pl.BlockSpec(left.shape, lambda j: (0, 0)), *right.specs(at)]
+        at += right.steps
+    made = call(
+        functools.partial(pair_body, rights=rights, both=both),
+        name,
+        2 * tokens * half * count,
+        2 * tokens * (count + half) + 8 * half * count,
+        grid=(steps,),
+        in_specs=specs + [wide] * both,
+        out_specs=[narrow, narrow] if both else [wide, pl.BlockSpec((1, step), lambda j: (0, j))],
+        out_shape=[shaped((half // 2, count), F32)] * 2
+        if both
+        else [shaped((half, count), F32), shaped((1, count), F32)],
+    )(*operands, *([got] if both else []))
+    return [tuple(made)] if both else made
+
+
+def moved_body(om_ref, h_ref, away_ref, own_ref, *out_refs):
+    om, hidden = om_ref[...], h_ref[...]
+    out_refs[0][...] = dot(om, away_ref[...], TN).astype(BF16)
+    out_refs[1][...] = dot(om, own_ref[...], TN).astype(BF16)
+    out_refs[2][...] = dot(hidden, away_ref[...]).astype(BF16)
+    out_refs[3][...] = dot(hidden, own_ref[...]).astype(BF16)
+
+
+def moved_call(om, hidden, away, own):
+    tokens, width = hidden.shape
     half = width // 2
     block = tokens // 2
     fixed = pl.BlockSpec((width, half), lambda i: (0, 0))
@@ -683,27 +679,38 @@
     return call(
         moved_body,
         "moved",
-        2 * tokens * width * width,
-        4 * tokens * width + 2 * width * width,
+        4 * tokens * width * width,
+        8 * tokens * width + 2 * width * width,
         grid=(2,),
-        in_specs=[pl.BlockSpec((block, width), lambda i: (i, 0)), fixed, fixed],
-        out_specs=[out, out],
-        out_shape=[shaped((tokens, half), BF16)] * 2,
-    )(left, away, own)
-
-
-def first_back_body(dqkv_ref, w_ref, x_ref, mod_ref, dx_ref, out_ref, sum_ref):
+        in_specs=[
+            pl.BlockSpec((width, block), lambda i: (0, i)),
+            pl.BlockSpec((block, width), lambda i: (i, 0)),
+            fixed,
+            fixed,
+        ],
+        out_specs=[out] * 4,
+        out_shape=[shaped((tokens, half), BF16)] * 4,
+    )(om, hidden, away, own)
+
+
+def first_back_body(low_ref, high_ref, w_ref, x_ref, mod_ref, dx_ref, out_ref, sum_ref):
     tile = pl.program_id(0)
-    grad = dot(dqkv_ref[...], w_ref[...], NT)
+    width = x_ref.shape[1]
+    grad = None
+    for third in range(3):
+        rows = jnp.concatenate([low_ref[third], high_ref[third]], axis=0)
+        part = dot(rows, w_ref[:, third * width : (third + 1) * width], TT)
+        grad = part if grad is None else grad + part
     normal, inverse = normed(x_ref[...].astype(F32))
     out_ref[...] = dx_ref[...] + normed_back(grad * (1.0 + mod_ref[tile, 1:2]), normal, inverse)
     sum_ref[0, 0:1] = jnp.sum(grad, axis=0, keepdims=True)
     sum_ref[0, 1:2] = jnp.sum(grad * normal, axis=0, keepdims=True)
 
 
-def first_back_call(dqkv, w, x, mod, dx):
-    tokens, wide = dqkv.shape
-    width = x.shape[1]
+def first_back_call(low, high, w, x, mod, dx):
+    tokens, width = x.shape
+    wide = w.shape[1]
+    half = pl.BlockSpec((3, width // 2, ROW), lambda i: (0, 0, i))
     tiles = tokens // ROW
     rows = pl.BlockSpec((ROW, width), lambda i: (i, 0))
     return call(
@@ -713,7 +720,8 @@
         2 * tokens * wide + 2 * width * wide + 10 * tokens * width,
         grid=(tiles,),
         in_specs=[
-            pl.BlockSpec((ROW, wide), lambda i: (i, 0)),
+            half,
+            half,
             pl.BlockSpec((width, wide), lambda i: (0, 0)),
             rows,
             pl.BlockSpec(mod.shape, lambda i: (0, 0, 0)),
@@ -721,71 +729,72 @@
         ],
         out_specs=[rows, pl.BlockSpec((1, 2, width), lambda i: (i, 0, 0))],
         out_shape=[shaped((tokens, width), F32), shaped((tiles, 2, width), F32)],
-    )(dqkv, w, x, mod, dx)
-
-
-def modulation_back_body(
-    me_ref, own_ref, other_ref, own_cond_ref, other_cond_ref, label_ref, w_ref,
-    grad_ref, sum_ref, table_ref, act_ref, total_ref,
-):
+    )(low, high, w, x, mod, dx)
+
+
+def modulation_back_body(me_ref, *refs, count):
+    part_refs, cond_refs, sum_refs = refs[:count], refs[count : 2 * count], refs[2 * count : 3 * count]
+    label_ref, w_ref, grad_ref, bias_ref, table_ref, own_sums_ref, act_ref, own_ref, total_ref = refs[3 * count :]
     step = pl.program_id(0)
-    half = own_ref.shape[0]
     width = act_ref.shape[1]
+    shard = grad_ref.shape[0]
+    items = own_sums_ref.shape[0]
 
     @pl.when(step == 0)
     def _():
-        for at, cond_ref in ((0, own_cond_ref), (half, other_cond_ref)):
+        at = 0
+        for cond_ref in cond_refs:
             cond = cond_ref[...]
-            act_ref[at : at + half] = (cond / (1.0 + jnp.exp(-cond))).astype(BF16)
-
-    mod = jnp.concatenate([own_ref[...], other_ref[...]], axis=0)
-    sum_ref[...] = jnp.sum(mod, axis=0, keepdims=True)
+            act_ref[at : at + cond.shape[0]] = (cond / (1.0 + jnp.exp(-cond))).astype(BF16)
+            at += cond.shape[0]
+        row = lax.broadcasted_iota(jnp.int32, (width, 128), 0)
+        column = lax.broadcasted_iota(jnp.int32, (width, 128), 1)
+        picked = jnp.where((column < shard) & (row == me_ref[0] * shard + column), 1.0, 0.0).astype(BF16)
+        own_ref[...] = dot(act_ref[...], picked).astype(BF16)
+        total_ref[...] = jnp.zeros_like(total_ref)
+        sums = None
+        for sum_ref in sum_refs:
+            rows = sum_ref.shape[0]
+            item = lax.broadcasted_iota(jnp.int32, (items, rows), 0)
+            source = lax.broadcasted_iota(jnp.int32, (items, rows), 1)
+            select = (lax.rem(source, jnp.full_like(source, items)) == item).astype(F32)
+            part = dot(select, sum_ref[...], NN, HIGHEST)
+            sums = part if sums is None else sums + part
+        own_sums_ref[...] = sums
+
+    mod = jnp.concatenate([part_ref[...] for part_ref in part_refs], axis=0)
+    bias_ref[...] = jnp.sum(mod, axis=0, keepdims=True)
     mod = mod.astype(BF16)
-    shard = grad_ref.shape[0]
-    row = lax.broadcasted_iota(jnp.int32, (width, 128), 0)
-    column = lax.broadcasted_iota(jnp.int32, (width, 128), 1)
-    picked = jnp.where((column < shard) & (row == me_ref[0] * shard + column), 1.0, 0.0).astype(BF16)
-    own_act = dot(act_ref[...], picked).astype(BF16)
-    grad_ref[...] = dot(own_act, mod, TN)[:shard]
-    part = dot(mod, w_ref[...], NT)
-
-    @pl.when(step == 0)
-    def _():
-        total_ref[...] = part
-
-    @pl.when(step > 0)
-    def _():
-        total_ref[...] += part
+    grad_ref[...] = dot(own_ref[...], mod, TN)[:shard]
+    total_ref[...] += dot(w_ref[...], mod, NT)
 
     @pl.when(step == pl.num_programs(0) - 1)
     def _():
-        cond = jnp.concatenate([own_cond_ref[...], other_cond_ref[...]], axis=0)
+        cond = jnp.concatenate([cond_ref[...] for cond_ref in cond_refs], axis=0)
         gate = 1.0 / (1.0 + jnp.exp(-cond))
-        grad = total_ref[...] * (gate * (1.0 + cond * (1.0 - gate)))
+        grad = total_ref[...].T * (gate * (1.0 + cond * (1.0 - gate)))
         classes = table_ref.shape[0]
-        select = (label_ref[...] == lax.broadcasted_iota(jnp.int32, (2 * half, classes), 1)).astype(F32)
+        select = (label_ref[...] == lax.broadcasted_iota(jnp.int32, (grad.shape[0], classes), 1)).astype(F32)
         table_ref[...] = dot(select, grad, TN, HIGHEST)
 
 
-def modulation_back_call(me, own, other, used, w, classes, shard):
-    rows = own.shape[0]
+def modulation_back_call(me, parts, used, w, classes, shard, items):
     width, wide = w.shape
-    block = 768
-    at = wide // width
-    part = pl.BlockSpec((rows, block), lambda j: (0, j))
-    cond = pl.BlockSpec((rows, width), lambda j: (0, at))
+    block = 1152
+    rows = sum(part.shape[0] for part in parts)
+    extra = parts[0].shape[1] - wide - width
+    at = (wide + extra) // width
     return call(
-        modulation_back_body,
+        functools.partial(modulation_back_body, count=len(parts)),
         "modulation_back",
         4 * rows * width * wide,
         2 * width * wide,
         grid=(wide // block,),
         in_specs=[
             pl.BlockSpec(memory_space=pltpu.SMEM),
-            part,
-            part,
-            cond,
-            cond,
+            *[pl.BlockSpec((part.shape[0], block), lambda j: (0, j)) for part in parts],
+            *[pl.BlockSpec((part.shape[0], width), lambda j: (0, at)) for part in parts],
+            *[pl.BlockSpec((part.shape[0], extra), lambda j: (0, wide // extra)) for part in parts],
             pl.BlockSpec(used.shape, lambda j: (0, 0)),
             pl.BlockSpec((width, block), lambda j: (0, j)),
         ],
@@ -793,10 +802,20 @@
             pl.BlockSpec((shard, block), lambda j: (0, j)),
             pl.BlockSpec((1, block), lambda j: (0, j)),
             pl.BlockSpec((classes, width), lambda j: (0, 0)),
-        ],
-        out_shape=[shaped((shard, wide), F32), shaped((1, wide), F32), shaped((classes, width), F32)],
-        scratch_shapes=[pltpu.VMEM((2 * rows, width), BF16), pltpu.VMEM((2 * rows, width), F32)],
-    )(me, own, other, own, other, used, w)
+            pl.BlockSpec((items, extra), lambda j: (0, 0)),
+        ],
+        out_shape=[
+            shaped((shard, wide), F32),
+            shaped((1, wide), F32),
+            shaped((classes, width), F32),
+            shaped((items, extra), F32),
+        ],
+        scratch_shapes=[
+            pltpu.VMEM((rows, width), BF16),
+            pltpu.VMEM((rows, 128), BF16),
+            pltpu.VMEM((width, rows), F32),
+        ],
+    )(me, *parts, *parts, *parts, used, w)
 
 
 def add_body(*refs, plans):
@@ -841,6 +860,46 @@
     )(*operands)
 
 
+def assemble_body(*refs, plans):
+    outs = refs[-len(plans) :]
+    for out_ref, (rows, blocks) in zip(outs, plans):
+        for terms, source, target, count in blocks:
+            value = refs[terms[0]][:rows, source : source + count]
+            for term in terms[1:]:
+                value = value + refs[term][:rows, source : source + count]
+            out_ref[:, target : target + count] = value
+
+
+def assemble_call(outputs):
+    operands, specs, known, plans, shapes = [], [], {}, [], []
+    for blocks in outputs:
+        rows, target, made = blocks[0][0].rows, 0, []
+        for chunk, source, count in blocks:
+            if id(chunk) not in known:
+                known[id(chunk)] = []
+                for term in chunk.terms:
+                    size = rows
+                    while size % 8 and size < term.shape[0]:
+                        size *= 2
+                    known[id(chunk)].append(len(operands))
+                    operands.append(term)
+                    specs.append(pl.BlockSpec((size, term.shape[1]), lambda j: (0, 0)))
+            made.append((known[id(chunk)], source, target, count))
+            target += count
+        plans.append((rows, made))
+        shapes.append(shaped((rows, target), F32))
+    return call(
+        functools.partial(assemble_body, plans=plans),
+        "assemble",
+        0,
+        sum(8 * 4 * shape.shape[0] * shape.shape[1] for shape in shapes),
+        grid=(1,),
+        in_specs=specs,
+        out_specs=[pl.BlockSpec(shape.shape, lambda j: (0, 0)) for shape in shapes],
+        out_shape=shapes,
+    )(*operands)
+
+
 def bit_order(bits, core, lead):
     order = list(range(bits))
     if bits >= 2 and core:
@@ -860,7 +919,7 @@
 
 class Spread:
     def __init__(self, rows):
-        self.own, self.other = rows, None
+        self.own, self.other = [rows], None
         self.stage = 0
 
 
@@ -892,8 +951,10 @@
         for spread, block in zip([spread for spread in self.spreads if spread.other is None and spread.stage], doubles):
             if spread.stage > self.bits:
                 spread.other = block
+            elif spread.stage == self.bits:
+                spread.own += block
             else:
-                spread.own = jnp.concatenate([spread.own, block], axis=0)
+                spread.own = [jnp.concatenate(spread.own + block, axis=0)]
         jobs, waiting = [], []
         for chunk, block in zip(self.last, blocks):
             chunk.terms.append(block)
@@ -933,18 +994,12 @@
             spread.own = rows
             if spread.stage < self.bits:
                 pairs = self.pairs(self.bits - 1 - spread.stage, 0)
-                doubles[number] = lax.ppermute(rows, ("stream", "batch"), pairs)
+                doubles[number] = [lax.ppermute(piece, ("stream", "batch"), pairs) for piece in rows]
             else:
-                doubles[number] = lax.ppermute(rows, "stream", [(0, 1), (1, 0)])
+                doubles[number] = [lax.ppermute(piece, "stream", [(0, 1), (1, 0)]) for piece in rows]
             spread.stage += 1
         self.crossing, self.last, self.blocks = crossing, moving, (cores, blocks, doubles)
         return live
-
-    def totals(self, live):
-        while self.busy():
-            live = self.round(live)
-        live = self.received(live)
-        return live, add_call([(chunk.terms, 0, chunk.rows) for chunk in self.chunks])
 
 
 def offsets_of(bits, side, lead):
@@ -983,7 +1038,6 @@
     count, width = x.shape
     hidden = w_fc1.shape[1]
     heads = head_keep.shape[1]
-    head_width = width // heads
     items = timesteps.shape[0]
     tiles = count // ROW
     groups = count // GROUP
@@ -1003,7 +1057,6 @@
     mod = jnp.sum(jnp.where(chosen[:, :, None], modulation[None], 0.0), axis=1)
     mod = mod.reshape(tiles, 6, width)
     tile_heads = jnp.sum(jnp.where(chosen[:, :, None], head_keep[None], 0), axis=1).astype(F32)
-    head_rows = jnp.repeat(tile_heads, head_width, axis=1).reshape(tiles, 1, width)
     head_columns = jnp.repeat(tile_heads.T, ROW, axis=1).reshape(heads, 1, count)
     keep = token_keep[0].astype(F32)[:, None]
     grouped = segments.reshape(groups, GROUP)
@@ -1022,7 +1075,7 @@
     other = 1 - stream
     away, own = picked(other), picked(stream)
 
-    bias_full = jnp.concatenate([b_qv[:width], jnp.zeros((width,), F32), b_qv[width:]])[None]
+    bias_full = jnp.concatenate([b_qv[:width], jnp.zeros((width,), F32), b_qv[width:]])[:, None]
     h1, qkv = qkv_call(x, mod, w_qkv, bias_full)
     probs, mixed, om = attention_call(flag, qkv, head_columns, heads)
     a, x1, h2, h2_away, h2_own, dm, sum_dm = middle_call(om, w_proj, b_proj[None], x, mod, top, keep, away, own)
@@ -1036,7 +1089,7 @@
         latest["df"] = filled[1]
 
         def hidden_keep(got, low=low, count=high - low):
-            return columns_keep_call([(h2_own, latest["df"], low, count)], got, "hidden_keep")
+            return columns_call(h2_own, Plain(latest["df"], low, UNITS, count // UNITS), "hidden_keep", got)
 
         flow.emit(send, hidden_keep, fc1)
         h2, filled = flow.round((h2, filled))
@@ -1053,10 +1106,9 @@
         [0] * len(ROW_PARTS),
         [lead for _, lead in ROW_PARTS],
     )
-    om_away, om_own = moved_call(om, away, own)
-    h1_away, h1_own = moved_call(h1, away, own)
+    om_away, om_own, h1_away, h1_own = moved_call(om, h1, away, own)
     df, x1, om_away, om_own, h1_away, h1_own = flow.round((df, x1, om_away, om_own, h1_away, h1_own))
-    dx1, da, do, sums_two = middle_back_call(df, w_fc1, x1, mod, top, a, w_proj, head_rows)
+    dx1, da, do, sums_two = middle_back_call(df, w_fc1, x1, mod, top, a, w_proj)
 
     def by_item(*sums):
         by_tile = jnp.concatenate(sums, axis=1)
@@ -1065,11 +1117,6 @@
     def in_rows(*sums):
         made = jnp.concatenate([part.reshape(devices, -1) for part in sums], axis=1).reshape(items, -1)
         return jnp.pad(made, ((0, 0), (0, -made.shape[1] % 128)))
-
-    def own_part(gathered, first, count):
-        each = devices // items
-        rows = lax.dynamic_index_in_dim(gathered.reshape(batch, items, -1), me // each, axis=1, keepdims=False)
-        return jnp.sum(lax.dynamic_slice_in_dim(rows, first + me % each * count, count, axis=1), axis=0)
 
     me = stream * batch + index
 
@@ -1082,18 +1129,18 @@
 
     used_rows = jnp.concatenate([used_labels(stream), used_labels(other)])[:, None]
     dx1, da, do, sums_two = flow.round((dx1, da, do, sums_two))
-    dqkv, ready = attention_back_call(flag, qkv, do, probs, mixed, 0)
-    first_pairs = [(om_away, da, 0, width), (h1_away, ready, 0, ready.shape[1])]
-    own_pairs = [(om_own, da, 0, width), (h1_own, ready, 0, ready.shape[1])]
-    send, first_sums = columns_send_call(first_pairs, "first_send")
-    low_sums = first_sums[:, width:]
-    flow.emit(send, lambda got: columns_keep_call(own_pairs, got, "first_keep"), wide)
-    dqkv, low_sums = flow.round((dqkv, low_sums))
-    dqkv, rest = attention_back_call(flag, qkv, do, probs, mixed, 1, dqkv)
-    send, high_sums = columns_send_call([(h1_away, rest, 0, rest.shape[1])], "last_send")
-    flow.emit(send, lambda got: columns_keep_call([(h1_own, rest, 0, rest.shape[1])], got, "last_keep"), wide)
-    dqkv, dx1, high_sums, g = flow.round((dqkv, dx1, high_sums, g))
-    grad_tokens, sums_one = first_back_call(dqkv, w_qkv, x, mod, dx1)
+    half = width // 2
+    low = attention_back_call(flag, qkv, do, head_columns, probs, mixed, 0)
+    rights = [Plain(da, 0, COLUMNS, width // COLUMNS), Wide((low, 0, COLUMNS))]
+    send, first_sums = pair_call([om_away, h1_away], rights, "first_send")
+    flow.emit(send, lambda got: pair_call([om_own, h1_own], rights, "first_keep", got), wide)
+    low, first_sums = flow.round((low, first_sums))
+    high = attention_back_call(flag, qkv, do, head_columns, probs, mixed, 1)
+    rest = Wide((low, COLUMNS, half - COLUMNS), (high, 0, half))
+    send, high_sums = columns_call(h1_away, rest, "last_send")
+    flow.emit(send, lambda got: columns_call(h1_own, rest, "last_keep", got), wide)
+    low, high, dx1, high_sums, g = flow.round((low, high, dx1, high_sums, g))
+    grad_tokens, sums_one = first_back_call(low, high, w_qkv, x, mod, dx1)
     result, sum_gate = result_call(g, w_fc2, b_fc2[None], x1, mod, top, keep)
 
     def in_order(low, high):
@@ -1105,41 +1152,55 @@
         ]
 
     grad_tokens, sums_one, result, sum_gate = flow.round((grad_tokens, sums_one, result, sum_gate))
-    column_sums = in_order(low_sums, high_sums)
+    column_sums = in_order(first_sums[:, width:], high_sums)
     spread = flow.spread(
         jnp.concatenate(
             [
                 by_item(
                     sums_one[:, 0], sums_one[:, 1], sums_two[:, 0], sums_two[:, 1], sums_two[:, 2], sum_gate[:, 0]
                 ),
-                cond,
                 in_rows(
                     sum_df[0],
                     jnp.sum(sum_dm, axis=(0, 1)),
                     jnp.sum(sums_two[:, 3], axis=0),
                     jnp.concatenate(column_sums[:2] + column_sums[4:], axis=1)[0],
                 ),
+                cond,
             ],
             axis=1,
         )
     )
-    result, shards = flow.totals(result)
-    grad_w_ada, mod_sums, grad_table = modulation_back_call(
-        me[None], spread.own, spread.other, used_rows, w_ada, null_class + 1, shard
+    while any(chunk.stage < bits for chunk in fc1 + fc2):
+        result = flow.round(result)
+    result = flow.round(result)
+    grad_w_fc1, grad_w_fc2 = assemble_call(
+        [[(chunk, 0, chunk.terms[0].shape[1]) for chunk in store] for store in (fc1, fc2)]
+    )
+    result, grad_w_fc1, grad_w_fc2 = flow.round((result, grad_w_fc1, grad_w_fc2))
+    while any(chunk.stage < bits for chunk in wide):
+        result = flow.round(result)
+    result = flow.round(result) if flow.busy() else flow.received(result)
+    first, last = wide
+    each = COLUMNS, width - COLUMNS
+    blocks = [
+        block
+        for third in range(3)
+        for block in ((first, width + third * each[0], each[0]), (last, third * each[1], each[1]))
+    ]
+    grad_w_proj, grad_w_qkv = assemble_call([[(first, 0, width)], blocks])
+    while flow.busy():
+        result = flow.round(result)
+    result, grad_w_proj = flow.received((result, grad_w_proj))
+    grad_w_ada, mod_sums, grad_table, own_sums = modulation_back_call(
+        me[None], spread.own + spread.other, used_rows, w_ada, null_class + 1, shard, items
     )
     share = 6 * width // devices
     grad_b_ada = lax.dynamic_slice_in_dim(mod_sums[0], me * share, share)
     ends = [hidden // devices, width // devices, width // devices, 2 * width // devices]
-    bias = sum(own_part(rows, 7 * width, sum(ends)) for rows in (spread.own, spread.other))
+    each = devices // items
+    bias = lax.dynamic_slice(own_sums, (me // each, me % each * sum(ends)), (1, sum(ends)))[0]
     at = [sum(ends[:n]) for n in range(5)]
     grad_b_fc1, grad_b_fc2, grad_b_proj, grad_b_qv = [bias[at[n] : at[n + 1]] for n in range(4)]
-    shards = dict(zip(map(id, flow.chunks), shards))
-    grad_w_fc1, grad_w_fc2 = [
-        jnp.concatenate([shards[id(chunk)] for chunk in store], axis=1) for store in (fc1, fc2)
-    ]
-    first_shard, last_shard = [shards[id(chunk)] for chunk in wide]
-    grad_w_proj = first_shard[:, :width]
-    grad_w_qkv = jnp.concatenate(in_order(first_shard[:, width:], last_shard), axis=1)
 
     return (
         result[None],

time: 650 us -> 615 us (0.946)
  Pallas kernels: 405 us -> 364 us
  waiting for transfers between devices: 121 us -> 148 us
  local copies, waits for them, and re-layouts: 34.3 us -> 24.1 us
  other arithmetic: 16.1 us -> 9.39 us
    pallas_call x13 -> x14, Pallas kernels: 186 us -> 152 us  [the longest x5 38.6 us: columns_call(): call(functools.partial(columns_body, right=right, both=both), name, 2 * t...]
    ppermute x28, waiting for transfers between devices: 61.7 us -> 91.9 us  [round(): lax.ppermute(send, ('stream', 'batch'), self.pairs(chunk.stage, chunk.lead))]
    pallas_call x10 -> x9, Pallas kernels: 41 us -> 34 us  [add_call(): call(functools.partial(add_body, plans=plans), 'add', moved // 4, moved,...]
    ppermute x5 -> x6, waiting for transfers between devices: 59.2 us -> 56 us  [the longest x4 56 us: round(): lax.ppermute(piece, ('stream', 'batch'), pairs)]
  transfers between devices with their start and end apart: 39 -> 40, of which waited for: 11 -> 14; matrix products, arithmetic and copies ran while one was open for 3% -> 1% of each run, Pallas kernels for 32% -> 30%
where the time goes in v3:
time: 615 us; the launch traced here: 610 us
  Pallas kernels  364 us (59%)
  waiting for transfers between devices  148 us (24%)
  starting transfers between devices  53.9 us (9%)
  local copies, waits for them, and re-layouts  24.1 us (4%)
  other arithmetic  9.39 us (2%)
  matrix products  7.69 us (1%)
    ppermute x28, waiting for transfers between devices, round(): lax.ppermute(send, ('stream', 'batch'), self.pairs(chunk.stage, chunk.lead))  91.9 us
    ppermute x4, waiting for transfers between devices, round(): lax.ppermute(piece, ('stream', 'batch'), pairs)  56 us
    ppermute x28, starting transfers between devices, round(): lax.ppermute(send, ('stream', 'batch'), self.pairs(chunk.stage, chunk.lead))  49.5 us
    pallas_call x3, Pallas kernels, hidden_call(): call(hidden_body, 'hidden', 6 * tokens * width * count, 6 * tokens * widt...  46.3 us
    pallas_call x5, Pallas kernels, columns_call(): call(functools.partial(columns_body, right=right, both=both), name, 2 * t...  38.6 us
    pallas_call x9, Pallas kernels, add_call(): call(functools.partial(add_body, plans=plans), 'add', moved // 4, moved,...  34 us
    pallas_call x1, Pallas kernels, middle_back_call(): call(middle_back_body, 'middle_back', 2 * tokens * width * (hidden + widt...  30.2 us
    pallas_call x2, Pallas kernels, attention_back_call(): call(attention_back_body, 'attention_back', 2 * 2 * heads * tokens * GROU...  27.2 us
  transfers between devices with their start and end apart: 40, of which 14 were waited for; matrix products, arithmetic and copies ran while one was open for 1% of the time, Pallas kernels for 30%

profile of v3, /device:TPU:0, one launch (start us, length us, event | category | flops | bytes accessed | tf_op | source)
XLA Modules:
  0.0 609.7 jit_solution(674311391203910094)
XLA Ops:
  9.6 1.3 broadcast_in_dim.156.b1_ref
  13.2 7.7 %convolution_add_fusion = f32[4,6912]{1,0:T(4,128)S(1)} fusion(bf16[1152,6912]{1,0:T(8,128)(2,1)} %refs_13_.1, f32[6912]{0:T(1024)} %param.28, f32[4,1152]{1,0:T(4,128)S(1)} %maximum_add_fusion), kind=kOutput, calls=%fused_computation.3 | convolution fusion | flops 63751680 | bytes 16081920 | tf_op jit(solution)/shard_map/dot_general | solution.py:28
  23.0 1.7 fusion.away_ref
  24.6 1.7 fusion.1.own_ref
  26.3 1.7 broadcast_in_dim.173.b_ref
  28.1 16.3 %qkv.1 = (bf16[1024,1152]{1,0:T(8,128)(2,1)}, bf16[3456,1024]{1,0:T(8,128)(2,1)}) custom-call(bf16[1024,1152]{1,0:T(8,128)(2,1)} %bitcast.63, f32[4,6,1152]{2,1,0:T(8,128)} %reshape.307.mod_ref, bf16[1152,3456]{1,0:T(8,128)(2,1)} %w_ref.6, f32[3456,1]{1,0:T(8,128)} %broadcast_in_dim.173.b_ref), custom_call_target="tpu_custom_call" | custom-call | flops 1019215872 | bytes 2469888 | tf_op jit(solution)/shard_map/qkv/pallas_call | solution.py:73
  44.3 26.4 %attention.1 = (bf16[16,1024,1024]{2,1,0:T(8,128)(2,1)}, f32[16,72,1024]{2,1,0:T(8,128)}, bf16[1152,1024]{1,0:T(8,128)(2,1)}) custom-call(s32[1]{0:T(128)} %bitcast.1.flag_ref, bf16[3456,1024]{1,0:T(8,128)(2,1)} %get-tuple-element.255.q_ref.k_ref.v_ref, bf16[3456,1024]{1,0:T(8,128)(2,1)} %get-tuple-element.255.q_ref.k_ref.v_ref, ...), custom_call_target="tpu_custom_call" | custom-call | flops 2147483648 | bytes 5963776 | tf_op jit(solution)/shard_map/attention/pallas_call | solution.py:139
  70.7 15.1 %middle.1 = (f32[1024,1152]{1,0:T(8,128)}, f32[1024,1152]{1,0:T(8,128)}, bf16[1024,1152]{1,0:T(8,128)(2,1)}, bf16[1024,576]{1,0:T(8,128)(2,1)}, bf16[1024,576]{1...) custom-call(bf16[1152,1024]{1,0:T(8,128)(2,1)} %get-tuple-element.256.om_ref, ...), custom_call_target="tpu_custom_call" | custom-call | flops 679477248 | bytes 3833856 | tf_op jit(solution)/shard_map/middle/pallas_call | solution.py:259
  85.8 11.9 %hidden.3 = (bf16[1024,4608]{1,0:T(8,128)(2,1)}, bf16[1024,4608]{1,0:T(8,128)(2,1)}, f32[1,4608]{1,0:T(1,128)}, f32[576,1024]{1,0:T(8,128)}) custom-call(bf16[1024,1152]{1,0:T(8,128)(2,1)} %get-tuple-element.284.h_ref, bf16[1024,576]{1,0:T(8,128)(2,1)} %get-tuple-element.258.away_ref, bf16[1024,1152]{1,0:T(8,128)(2,1)} %get-tuple-element.259.dm_ref, ...), custom_call_target="tpu_custom_call" | custom-call | flops 905969664 | bytes 2588672 | tf_op jit(solution)/shard_map/hidden/pallas_call | solution.py:312
  98.1 15.3 %hidden.4 = (bf16[1024,4608]{1,0:T(8,128)(2,1)}, bf16[1024,4608]{1,0:T(8,128)(2,1)}, f32[1,4608]{1,0:T(1,128)}, f32[576,1536]{1,0:T(8,128)}) custom-call(bf16[1024,1152]{1,0:T(8,128)(2,1)} %get-tuple-element.284.h_ref, bf16[1024,576]{1,0:T(8,128)(2,1)} %get-tuple-element.258.away_ref, ...), custom_call_target="tpu_custom_call", output_to_operand_aliasing={{0}: (6, {}), {1}: (7, {}), {2}: (8, {})} | custom-call | flops 1358954496 | bytes 3440640 | tf_op jit(solution)/shard_map/hidden/pallas_call | solution.py:312
  113.5 4.7 hidden_keep.3
  118.2 9.3 %collective-permute-start.2 = (f32[288,1024]{1,0:T(8,128)}, f32[288,1024]{1,0:T(8,128)S(1)}, u32[]{:S(2)}, u32[]{:S(2)}) collective-permute-start(f32[288,1024]{1,0:T(8,128)} %get-tuple-element.292), channel_id=1, source_target_pairs={{0,1},{1,0},{2,3},{3,2},{4,5},{5,4},{6,7},{7,6},{8,9},{9,8},{10,11... | collective-permute-start | bytes 3538952 | tf_op jit(solution)/shard_map/ppermute | solution.py:990
  127.6 19.1 %hidden.5 = (bf16[1024,4608]{1,0:T(8,128)(2,1)}, bf16[1024,4608]{1,0:T(8,128)(2,1)}, f32[1,4608]{1,0:T(1,128)}, f32[576,2048]{1,0:T(8,128)}) custom-call(bf16[1024,1152]{1,0:T(8,128)(2,1)} %get-tuple-element.284.h_ref, bf16[1024,576]{1,0:T(8,128)(2,1)} %get-tuple-element.258.away_ref, ...), custom_call_target="tpu_custom_call", output_to_operand_aliasing={{0}: (6, {}), {1}: (7, {}), {2}: (8, {})} | custom-call | flops 1811939328 | bytes 4292608 | tf_op jit(solution)/shard_map/hidden/pallas_call | solution.py:312
  146.6 7.3 %hidden_keep.4 = (f32[288,1536]{1,0:T(8,128)}, f32[288,1536]{1,0:T(8,128)}) custom-call(bf16[1024,576]{1,0:T(8,128)(2,1)} %get-tuple-element.281.refs_0_, bf16[1024,4608]{1,0:T(8,128)(2,1)} %get-tuple-element.325.refs_1_.df_ref, f32[576,1536]{1,0:T(8,128)} %collective-permute-done.1.refs_2_), custom_call_target="tpu_custom_call" | custom-call | flops 226492416 | bytes 1425408 | tf_op jit(solution)/shard_map/hidden_keep/pallas_call | solution.py:610
  154.0 2.0 add.263
  158.0 11.9 %moved.1 = (bf16[1024,576]{1,0:T(8,128)(2,1)}, bf16[1024,576]{1,0:T(8,128)(2,1)}, bf16[1024,576]{1,0:T(8,128)(2,1)}, bf16[1024,576]{1,0:T(8,128)(2,1)}) custom-call(bf16[1152,1024]{1,0:T(8,128)(2,1)} %get-tuple-element.256.om_ref, bf16[1024,1152]{1,0:T(8,128)(2,1)} %get-tuple-element.303.h_ref, bf16[1152,576]{1,0:T(8,128)(2,1)} %fusion.away_ref, ...), custom_call_target="tpu_custom_call" | custom-call | flops 679477248 | bytes 1511424 | tf_op jit(solution)/shard_map/moved/pallas_call | solution.py:679
  170.6 13.2 %rows_send.1 = f32[16,144,1152]{2,1,0:T(8,128)} custom-call(s32[1]{0:T(128)} %bitcast.6.side_ref, s32[3,16]{1,0:T(4,128)} %pad_add_fusion.spot_ref, bf16[1024,4608]{1,0:T(8,128)(2,1)} %get-tuple-element.404.g_ref, bf16[1024,1152]{1,0:T(8,128)(2,1)} %get-tuple-element.259.dm_ref), custom_call_target="tpu_custom_call" | custom-call | flops 679477248 | bytes 2211840 | tf_op jit(solution)/shard_map/rows_send/pallas_call | solution.py:368
  185.0 8.4 %hidden_keep.5 = (f32[288,2048]{1,0:T(8,128)}, f32[288,2048]{1,0:T(8,128)}) custom-call(bf16[1024,576]{1,0:T(8,128)(2,1)} %get-tuple-element.281.refs_0_, bf16[1024,4608]{1,0:T(8,128)(2,1)} %get-tuple-element.325.refs_1_.df_ref, f32[576,2048]{1,0:T(8,128)} %collective-permute-done.3.refs_2_), custom_call_target="tpu_custom_call" | custom-call | flops 301989888 | bytes 1851392 | tf_op jit(solution)/shard_map/hidden_keep/pallas_call | solution.py:610
  193.5 2.6 add.264
  196.1 1.4 collective-permute-start.9
  198.2 1.3 collective-permute-start.7
  200.2 30.2 %middle_back.1 = (f32[1024,1152]{1,0:T(8,128)}, bf16[1024,1152]{1,0:T(8,128)(2,1)}, bf16[1152,1024]{1,0:T(8,128)(2,1)}, f32[4,4,1152]{2,1,0:T(4,128)}) custom-call(bf16[1024,4608]{1,0:T(8,128)(2,1)} %get-tuple-element.325.refs_1_.df_ref, bf16[1152,4608]{1,0:T(8,128)(2,1)} %w1_ref.7, f32[1024,1152]{1,0:T(8,128)} %get-tuple-element.326.x1_ref, ...), custom_call_target="tpu_custom_call" | custom-call | flops 1698693120 | bytes 5160960 | tf_op jit(solution)/shard_map/middle_back/pallas_call | solution.py:504
  230.4 4.4 collective-permute-done.9.refs_8_.refs_5_.refs_1_.refs_11_
  234.8 18.5 %rows_keep.1 = (f32[8,144,768]{2,1,0:T(8,128)}, f32[8,144,768]{2,1,0:T(8,128)}, f32[8,144,384]{2,1,0:T(8,128)}, f32[8,144,384]{2,1,0:T(8,128)}) custom-call(s32[1]{0:T(128)} %bitcast.8.side_ref, s32[3,16]{1,0:T(4,128)} %pad_add_fusion.1.spot_ref, bf16[1024,4608]{1,0:T(8,128)(2,1)} %get-tuple-element.404.g_ref, bf16[1024,1152]{1,0:T(8,128)(2,1)} %get-tuple-element.259.dm_ref, ...), custom_call_target="tpu_custom_call" | custom-call | flops 679477248 | bytes 3538944 | tf_op jit(solution)/shard_map/rows_keep/pallas_call | solution.py:427
  253.3 3.6 add.265
  258.1 1.4 collective-permute-start.14
  260.9 2.3 collective-permute-start.10
  263.2 13.6 %attention_back.2.refs_3_.refs_1_.low_ref = bf16[3,576,1024]{2,1,0:T(8,128)(2,1)} custom-call(s32[1]{0:T(128)} %bitcast.1.flag_ref, bf16[3456,1024]{1,0:T(8,128)(2,1)} %get-tuple-element.255.q_ref.k_ref.v_ref, bf16[3456,1024]{1,0:T(8,128)(2,1)} %get-tuple-element.255.q_ref.k_ref.v_ref, bf16[3456,1024]{1,0:T(8,128)(2,1)} %get-tuple-element.255.q_ref.k_ref.v_ref, ...), custom_call_target="tpu_custom_call" | custom-call | flops 2147483648 | bytes 3866624 | tf_op jit(solution)/shard_map/attention_back/pallas_call | solution.py:212
  276.9 10.0 %first_send.1 = (f32[576,2304]{1,0:T(8,128)}, f32[1,2304]{1,0:T(1,128)}) custom-call(bf16[1024,576]{1,0:T(8,128)(2,1)} %get-tuple-element.353.refs_0_, bf16[1024,1152]{1,0:T(8,128)(2,1)} %get-tuple-element.354.refs_1_, bf16[1024,576]{1,0:T(8,128)(2,1)} %get-tuple-element.355.refs_2_.refs_0_, bf16[3,576,1024]{2,1,0:T(8,128)(2,1)} %attention_back.2.refs_3_.refs_1_.low_ref), custom_call_target="tpu_custom_call" | custom-call | flops 339738624 | bytes 2064384 | tf_op jit(solution)/shard_map/first_send/pallas_call | solution.py:650
  286.8 23.5 %collective-permute-done.10.refs_4_ = f32[36,1024]{1,0:T(8,128)S(1)} collective-permute-done((f32[36,1024]{1,0:T(8,128)}, f32[36,1024]{1,0:T(8,128)S(1)}, u32[]{:S(2)}, u32[]{:S(2)}) %collective-permute-start.10) | collective-permute-done | bytes 147488 | tf_op jit(solution)/shard_map/ppermute | solution.py:990
  312.9 5.4 add.266
  319.1 1.3 collective-permute-start.19
  320.5 2.3 collective-permute-start.17
  323.8 13.6 %attention_back.3.refs_2_.high_ref = bf16[3,576,1024]{2,1,0:T(8,128)(2,1)} custom-call(s32[1]{0:T(128)} %bitcast.1.flag_ref, bf16[3456,1024]{1,0:T(8,128)(2,1)} %get-tuple-element.255.q_ref.k_ref.v_ref, bf16[3456,1024]{1,0:T(8,128)(2,1)} %get-tuple-element.255.q_ref.k_ref.v_ref, bf16[3456,1024]{1,0:T(8,128)(2,1)} %get-tuple-element.255.q_ref.k_ref.v_ref, ...), custom_call_target="tpu_custom_call" | custom-call | flops 2147483648 | bytes 3866624 | tf_op jit(solution)/shard_map/attention_back/pallas_call | solution.py:212
  337.4 8.2 %last_send.1 = (f32[576,2304]{1,0:T(8,128)}, f32[1,2304]{1,0:T(1,128)}) custom-call(bf16[1024,576]{1,0:T(8,128)(2,1)} %get-tuple-element.355.refs_2_.refs_0_, bf16[3,576,1024]{2,1,0:T(8,128)(2,1)} %attention_back.2.refs_3_.refs_1_.low_ref, bf16[3,576,1024]{2,1,0:T(8,128)(2,1)} %attention_back.3.refs_2_.high_ref), custom_call_target="tpu_custom_call" | custom-call | flops 339738624 | bytes 2064384 | tf_op jit(solution)/shard_map/last_send/pallas_call | solution.py:610
  345.6 4.9 collective-permute-done.18.refs_6_.refs_2_.refs_17_
  350.6 11.0 %first_keep.1 = (f32[288,2304]{1,0:T(8,128)}, f32[288,2304]{1,0:T(8,128)}) custom-call(bf16[1024,576]{1,0:T(8,128)(2,1)} %get-tuple-element.395.refs_0_, bf16[1024,1152]{1,0:T(8,128)(2,1)} %get-tuple-element.354.refs_1_, bf16[1024,576]{1,0:T(8,128)(2,1)} %get-tuple-element.396.refs_2_.refs_0_, bf16[3,576,1024]{2,1,0:T(8,128)(2,1)} %attention_back.2.refs_3_.refs_1_.low_ref, ...), custom_call_target="tpu_custom_call" | custom-call | flops 339738624 | bytes 2064384 | tf_op jit(solution)/shard_map/first_keep/pallas_call | solution.py:650
  361.6 4.1 add.267
  365.7 5.5 collective-permute-start.24
  376.6 18.4 %first_back.1 = (f32[1024,1152]{1,0:T(8,128)}, f32[4,2,1152]{2,1,0:T(2,128)}) custom-call(bf16[3,576,1024]{2,1,0:T(8,128)(2,1)} %attention_back.2.refs_3_.refs_1_.low_ref, bf16[3,576,1024]{2,1,0:T(8,128)(2,1)} %attention_back.3.refs_2_.high_ref, bf16[1152,3456]{1,0:T(8,128)(2,1)} %w_ref.6, bf16[1024,1152]{1,0:T(8,128)(2,1)} %bitcast.65, ...), custom_call_target="tpu_custom_call" | custom-call | flops 1019215872 | bytes 3354624 | tf_op jit(solution)/shard_map/first_back/pallas_call | solution.py:716
  395.0 19.7 %result.1 = (bf16[1024,1152]{1,0:T(8,128)(2,1)}, f32[4,1,1152]{2,1,0:T(1,128)}) custom-call(bf16[1024,4608]{1,0:T(8,128)(2,1)} %get-tuple-element.404.g_ref, bf16[4608,1152]{1,0:T(8,128)(2,1)} %w_ref.7, f32[1,1152]{1,0:T(1,128)} %broadcast_in_dim.159.b_ref, f32[1024,1152]{1,0:T(8,128)} %get-tuple-element.326.x1_ref, f32[4,6,1152]{2,1,0:T(8,128)} %reshape.307.mod_ref, ...), custom_call_target="tpu_custom_call" | custom-call | flops 1358954496 | bytes 3686400 | tf_op jit(solution)/shard_map/result/pallas_call | solution.py:460
  414.8 10.0 %last_keep.1 = (f32[288,2304]{1,0:T(8,128)}, f32[288,2304]{1,0:T(8,128)}) custom-call(bf16[1024,576]{1,0:T(8,128)(2,1)} %get-tuple-element.396.refs_2_.refs_0_, bf16[3,576,1024]{2,1,0:T(8,128)(2,1)} %attention_back.2.refs_3_.refs_1_.low_ref, bf16[3,576,1024]{2,1,0:T(8,128)(2,1)} %attention_back.3.refs_2_.high_ref, f32[576,2304]{1,0:T(8,128)} %collective-permute-done.20.refs_3_), custom_call_target="tpu_custom_call" | custom-call | flops 339738624 | bytes 2064384 | tf_op jit(solution)/shard_map/last_keep/pallas_call | solution.py:610
  424.8 4.6 add.268
  431.6 2.0 collective-permute-start.26
  434.6 19.4 %collective-permute-done.26.refs_24_ = f32[144,384]{1,0:T(8,128)S(1)} collective-permute-done((f32[144,384]{1,0:T(8,128)}, f32[144,384]{1,0:T(8,128)S(1)}, u32[]{:S(2)}, u32[]{:S(2)}) %collective-permute-start.26) | collective-permute-done | bytes 221216 | tf_op jit(solution)/shard_map/ppermute | solution.py:990
  454.0 8.6 %collective-permute-done.25.refs_19_ = f32[144,768]{1,0:T(8,128)S(1)} collective-permute-done((f32[144,768]{1,0:T(8,128)}, f32[144,768]{1,0:T(8,128)S(1)}, u32[]{:S(2)}, u32[]{:S(2)}) %collective-permute-start.25) | collective-permute-done | bytes 442400 | tf_op jit(solution)/shard_map/ppermute | solution.py:990
  462.6 12.1 %collective-permute-done.28.refs_4_.refs_5_.refs_1_.refs_6_ = f32[288,2304]{1,0:T(8,128)} collective-permute-done((f32[288,2304]{1,0:T(8,128)}, f32[288,2304]{1,0:T(8,128)}, u32[]{:S(2)}, u32[]{:S(2)}) %collective-permute-start.28) | collective-permute-done | bytes 2654240 | tf_op jit(solution)/shard_map/ppermute | solution.py:990
  474.8 4.4 add.269
  479.9 1.7 collective-permute-start.29
  482.7 4.9 assemble.2
  487.6 12.5 %collective-permute-done.31 = f32[4,10368]{1,0:T(4,128)S(1)} collective-permute-done((f32[4,10368]{1,0:T(4,128)S(1)}, f32[4,10368]{1,0:T(4,128)S(1)}, u32[]{:S(2)}, u32[]{:S(2)}) %collective-permute-start.31) | collective-permute-done | bytes 165920 | tf_op jit(solution)/shard_map/ppermute | solution.py:997
  502.3 4.0 add.270
  506.3 1.7 collective-permute-start.33
  508.3 2.5 collective-permute-start.32
  510.8 27.3 %collective-permute-done.34 = f32[8,10368]{1,0:T(8,128)S(1)} collective-permute-done((f32[8,10368]{1,0:T(8,128)S(1)}, f32[8,10368]{1,0:T(8,128)S(1)}, u32[]{:S(2)}, u32[]{:S(2)}) %collective-permute-start.34) | collective-permute-done | bytes 331808 | tf_op jit(solution)/shard_map/ppermute | solution.py:997
  539.0 3.3 add.271
  542.4 2.6 collective-permute-start.35
  545.0 15.8 %collective-permute-done.35.refs_9_ = f32[36,2304]{1,0:T(8,128)S(1)} collective-permute-done((f32[36,2304]{1,0:T(8,128)}, f32[36,2304]{1,0:T(8,128)S(1)}, u32[]{:S(2)}, u32[]{:S(2)}) %collective-permute-start.35) | collective-permute-done | bytes 331808 | tf_op jit(solution)/shard_map/ppermute | solution.py:990
  561.0 1.7 collective-permute-start.37
  562.7 16.2 %collective-permute-done.37.refs_1_.refs_5_.refs_9_ = f32[32,10368]{1,0:T(8,128)} collective-permute-done((f32[32,10368]{1,0:T(8,128)S(1)}, f32[32,10368]{1,0:T(8,128)}, u32[]{:S(2)}, u32[]{:S(2)}) %collective-permute-start.37) | collective-permute-done | bytes 1327136 | tf_op jit(solution)/shard_map/ppermute | solution.py:997
  581.9 3.7 assemble.3
  585.5 18.6 %modulation_back.1 = (f32[36,6912]{1,0:T(8,128)}, f32[1,6912]{1,0:T(1,128)}, f32[1001,1152]{1,0:T(8,128)}, f32[4,2304]{1,0:T(4,128)}) custom-call(s32[1]{0:T(128)} %bitcast.21.me_ref, f32[32,10368]{1,0:T(8,128)} %copy-done.4, f32[32,10368]{1,0:T(8,128)} %collective-permute-done.37.refs_1_.refs_5_.refs_9_, ...), custom_call_target="tpu_custom_call" | custom-call | flops 509607936 | bytes 1990656 | tf_op jit(solution)/shard_map/modulation_back/pallas_call | solution.py:787
  604.2 1.3 dynamic-slice.3
  606.8 1.3 dynamic-slice_bitcast_fusion
  (206 shorter events, 44.2 us)
Async XLA Ops:
  0.6 11.1 %copy-start = (bf16[1001,1152]{1,0:T(8,128)(2,1)S(1)}, bf16[1001,1152]{1,0:T(8,128)(2,1)}, u32[]{:S(2)}) copy-start(bf16[1001,1152]{1,0:T(8,128)(2,1)} %param.26) | copy-start | bytes 6918916
  2.4 18.5 %copy-start.34 = (pred[4,4]{1,0:T(4,128)(4,1)}, pred[4,4]{1,0:T(4,128)(4,1)S(1)}, u32[]{:S(2)}) copy-start(pred[4,4]{1,0:T(4,128)(4,1)S(1)} %iota_compare_fusion.2) | copy-start | bytes 52
  97.7 15.8 %collective-permute-start = (f32[576,1024]{1,0:T(8,128)}, f32[576,1024]{1,0:T(8,128)}, u32[]{:S(2)}, u32[]{:S(2)}) collective-permute-start(f32[576,1024]{1,0:T(8,128)} %get-tuple-element.275), channel_id=1, source_target_pairs={{0,16},{16,0},{1,17},{17,1},{2,18},{18,2},{3,19},{19,3},{4,20},{20... | collective-permute-start | bytes 7077896 | tf_op jit(solution)/shard_map/ppermute | solution.py:992
  118.2 28.5 %collective-permute-start.1 = (f32[576,1536]{1,0:T(8,128)}, f32[576,1536]{1,0:T(8,128)}, u32[]{:S(2)}, u32[]{:S(2)}) collective-permute-start(f32[576,1536]{1,0:T(8,128)} %get-tuple-element.291), channel_id=1, source_target_pairs={{0,16},{16,0},{1,17},{17,1},{2,18},{18,2},{3,19},{19,3},{4,20},{20... | collective-permute-start | bytes 10616840 | tf_op jit(solution)/shard_map/ppermute | solution.py:992
  118.2 28.4 %collective-permute-start.2 = (f32[288,1024]{1,0:T(8,128)}, f32[288,1024]{1,0:T(8,128)S(1)}, u32[]{:S(2)}, u32[]{:S(2)}) collective-permute-start(f32[288,1024]{1,0:T(8,128)} %get-tuple-element.292), channel_id=1, source_target_pairs={{0,1},{1,0},{2,3},{3,2},{4,5},{5,4},{6,7},{7,6},{8,9},{9,8},{10,11... | collective-permute-start | bytes 3538952 | tf_op jit(solution)/shard_map/ppermute | solution.py:990
  156.0 29.1 %collective-permute-start.3 = (f32[576,2048]{1,0:T(8,128)}, f32[576,2048]{1,0:T(8,128)}, u32[]{:S(2)}, u32[]{:S(2)}) collective-permute-start(f32[576,2048]{1,0:T(8,128)} %get-tuple-element.308), channel_id=1, source_target_pairs={{0,16},{16,0},{1,17},{17,1},{2,18},{18,2},{3,19},{19,3},{4,20},{20... | collective-permute-start | bytes 14155784 | tf_op jit(solution)/shard_map/ppermute | solution.py:992
  156.0 29.1 %collective-permute-start.5 = (f32[288,1536]{1,0:T(8,128)}, f32[288,1536]{1,0:T(8,128)S(1)}, u32[]{:S(2)}, u32[]{:S(2)}) collective-permute-start(f32[288,1536]{1,0:T(8,128)} %get-tuple-element.310), channel_id=1, source_target_pairs={{0,1},{1,0},{2,3},{3,2},{4,5},{5,4},{6,7},{7,6},{8,9},{9,8},{10,11... | collective-permute-start | bytes 5308424 | tf_op jit(solution)/shard_map/ppermute | solution.py:990
  157.3 26.5 %collective-permute-start.4 = (f32[144,1024]{1,0:T(8,128)}, f32[144,1024]{1,0:T(8,128)S(1)}, u32[]{:S(2)}, u32[]{:S(2)}) collective-permute-start(f32[144,1024]{1,0:T(8,128)} %add.263), channel_id=1, source_target_pairs={{0,2},{1,3},{2,0},{3,1},{4,6},{5,7},{6,4},{7,5},{8,10},{9,11},{10,... | collective-permute-start | bytes 1769480 | tf_op jit(solution)/shard_map/ppermute | solution.py:990
  183.8 9.7 %copy-start.12 = (f32[144,1024]{1,0:T(8,128)}, f32[144,1024]{1,0:T(8,128)S(1)}, u32[]{:S(2)}) copy-start(f32[144,1024]{1,0:T(8,128)S(1)} %collective-permute-done.4.refs_2_) | copy-start | bytes 1769476
  196.1 38.7 %collective-permute-start.6 = (f32[2304,1152]{1,0:T(8,128)}, f32[2304,1152]{1,0:T(8,128)}, u32[]{:S(2)}, u32[]{:S(2)}) collective-permute-start(f32[2304,1152]{1,0:T(8,128)} %bitcast.66), channel_id=1, source_target_pairs={{0,16},{16,0},{1,17},{17,1},{2,18},{18,2},{3,19},{19,3},{4,20},{20... | collective-permute-start | bytes 31850504 | tf_op jit(solution)/shard_map/ppermute | solution.py:992
  196.1 38.7 %collective-permute-start.9 = (f32[288,2048]{1,0:T(8,128)}, f32[288,2048]{1,0:T(8,128)}, u32[]{:S(2)}, u32[]{:S(2)}) collective-permute-start(f32[288,2048]{1,0:T(8,128)} %get-tuple-element.335), channel_id=1, source_target_pairs={{0,1},{1,0},{2,3},{3,2},{4,5},{5,4},{6,7},{7,6},{8,9},{9,8},{10,11... | collective-permute-start | bytes 7077896 | tf_op jit(solution)/shard_map/ppermute | solution.py:990
  197.5 32.9 %collective-permute-start.8 = (f32[144,1536]{1,0:T(8,128)}, f32[144,1536]{1,0:T(8,128)S(1)}, u32[]{:S(2)}, u32[]{:S(2)}) collective-permute-start(f32[144,1536]{1,0:T(8,128)} %get-tuple-element.334), channel_id=1, source_target_pairs={{0,2},{1,3},{2,0},{3,1},{4,6},{5,7},{6,4},{7,5},{8,10},{9,11},{10,... | collective-permute-start | bytes 2654216 | tf_op jit(solution)/shard_map/ppermute | solution.py:990
  198.2 32.1 %collective-permute-start.7 = (f32[72,1024]{1,0:T(8,128)}, f32[72,1024]{1,0:T(8,128)S(1)}, u32[]{:S(2)}, u32[]{:S(2)}) collective-permute-start(f32[72,1024]{1,0:T(8,128)} %get-tuple-element.333), channel_id=1, source_target_pairs={{0,4},{1,5},{2,6},{3,7},{4,0},{5,1},{6,2},{7,3},{8,12},{9,13},{10,... | collective-permute-start | bytes 884744 | tf_op jit(solution)/shard_map/ppermute | solution.py:990
  230.3 22.9 %copy-start.18 = (f32[72,1024]{1,0:T(8,128)}, f32[72,1024]{1,0:T(8,128)S(1)}, u32[]{:S(2)}) copy-start(f32[72,1024]{1,0:T(8,128)S(1)} %collective-permute-done.7.refs_3_) | copy-start | bytes 884740
  230.3 22.9 %copy-start.10 = (f32[144,1536]{1,0:T(8,128)}, f32[144,1536]{1,0:T(8,128)S(1)}, u32[]{:S(2)}) copy-start(f32[144,1536]{1,0:T(8,128)S(1)} %collective-permute-done.8.refs_6_.refs_2_.refs_7_) | copy-start | bytes 2654212
  256.8 54.4 %collective-permute-start.13 = (f32[1152,768]{1,0:T(8,128)}, f32[1152,768]{1,0:T(8,128)}, u32[]{:S(2)}, u32[]{:S(2)}) collective-permute-start(f32[1152,768]{1,0:T(8,128)} %bitcast.71), channel_id=1, source_target_pairs={{0,1},{1,0},{2,3},{3,2},{4,5},{5,4},{6,7},{7,6},{8,9},{9,8},{10,11... | collective-permute-start | bytes 10616840 | tf_op jit(solution)/shard_map/ppermute | solution.py:990
  258.1 53.1 %collective-permute-start.14 = (f32[1152,384]{1,0:T(8,128)}, f32[1152,384]{1,0:T(8,128)S(1)}, u32[]{:S(2)}, u32[]{:S(2)}) collective-permute-start(f32[1152,384]{1,0:T(8,128)} %bitcast.11), channel_id=1, source_target_pairs={{0,4},{1,5},{2,6},{3,7},{4,0},{5,1},{6,2},{7,3},{8,12},{9,13},{10,... | collective-permute-start | bytes 5308424 | tf_op jit(solution)/shard_map/ppermute | solution.py:990
  259.5 51.7 %collective-permute-start.12 = (f32[144,2048]{1,0:T(8,128)}, f32[144,2048]{1,0:T(8,128)S(1)}, u32[]{:S(2)}, u32[]{:S(2)}) collective-permute-start(f32[144,2048]{1,0:T(8,128)} %get-tuple-element.359), channel_id=1, source_target_pairs={{0,2},{1,3},{2,0},{3,1},{4,6},{5,7},{6,4},{7,5},{8,10},{9,11},{10,... | collective-permute-start | bytes 3538952 | tf_op jit(solution)/shard_map/ppermute | solution.py:990
  260.3 50.9 %collective-permute-start.11 = (f32[72,1536]{1,0:T(8,128)}, f32[72,1536]{1,0:T(8,128)S(1)}, u32[]{:S(2)}, u32[]{:S(2)}) collective-permute-start(f32[72,1536]{1,0:T(8,128)} %get-tuple-element.358), channel_id=1, source_target_pairs={{0,4},{1,5},{2,6},{3,7},{4,0},{5,1},{6,2},{7,3},{8,12},{9,13},{10,... | collective-permute-start | bytes 1327112 | tf_op jit(solution)/shard_map/ppermute | solution.py:990
  260.9 49.5 %collective-permute-start.10 = (f32[36,1024]{1,0:T(8,128)}, f32[36,1024]{1,0:T(8,128)S(1)}, u32[]{:S(2)}, u32[]{:S(2)}) collective-permute-start(f32[36,1024]{1,0:T(8,128)} %get-tuple-element.357), channel_id=1, source_target_pairs={{0,8},{1,9},{2,10},{3,11},{4,12},{5,13},{6,14},{7,15},{8,0},{9,1},... | collective-permute-start | bytes 442376 | tf_op jit(solution)/shard_map/ppermute | solution.py:990
  318.3 32.2 %collective-permute-start.15 = (f32[576,2304]{1,0:T(8,128)}, f32[576,2304]{1,0:T(8,128)}, u32[]{:S(2)}, u32[]{:S(2)}) collective-permute-start(f32[576,2304]{1,0:T(8,128)} %get-tuple-element.378), channel_id=1, source_target_pairs={{0,16},{16,0},{1,17},{17,1},{2,18},{18,2},{3,19},{19,3},{4,20},{20... | collective-permute-start | bytes 15925256 | tf_op jit(solution)/shard_map/ppermute | solution.py:992
  318.3 32.2 %collective-permute-start.18 = (f32[576,768]{1,0:T(8,128)}, f32[576,768]{1,0:T(8,128)S(1)}, u32[]{:S(2)}, u32[]{:S(2)}) collective-permute-start(f32[576,768]{1,0:T(8,128)} %get-tuple-element.381), channel_id=1, source_target_pairs={{0,2},{1,3},{2,0},{3,1},{4,6},{5,7},{6,4},{7,5},{8,10},{9,11},{10,... | collective-permute-start | bytes 5308424 | tf_op jit(solution)/shard_map/ppermute | solution.py:990
  319.1 26.5 %collective-permute-start.19 = (f32[576,384]{1,0:T(8,128)}, f32[576,384]{1,0:T(8,128)S(1)}, u32[]{:S(2)}, u32[]{:S(2)}) collective-permute-start(f32[576,384]{1,0:T(8,128)} %get-tuple-element.382), channel_id=1, source_target_pairs={{0,1},{1,0},{2,3},{3,2},{4,5},{5,4},{6,7},{7,6},{8,9},{9,8},{10,11... | collective-permute-start | bytes 2654216 | tf_op jit(solution)/shard_map/ppermute | solution.py:990
  320.5 25.1 %collective-permute-start.17 = (f32[72,2048]{1,0:T(8,128)}, f32[72,2048]{1,0:T(8,128)}, u32[]{:S(2)}, u32[]{:S(2)}) collective-permute-start(f32[72,2048]{1,0:T(8,128)} %get-tuple-element.380), channel_id=1, source_target_pairs={{0,4},{1,5},{2,6},{3,7},{4,0},{5,1},{6,2},{7,3},{8,12},{9,13},{10,... | collective-permute-start | bytes 1769480 | tf_op jit(solution)/shard_map/ppermute | solution.py:990
  322.8 22.8 %collective-permute-start.16 = (f32[36,1536]{1,0:T(8,128)}, f32[36,1536]{1,0:T(8,128)S(1)}, u32[]{:S(2)}, u32[]{:S(2)}) collective-permute-start(f32[36,1536]{1,0:T(8,128)} %get-tuple-element.379), channel_id=1, source_target_pairs={{0,8},{1,9},{2,10},{3,11},{4,12},{5,13},{6,14},{7,15},{8,0},{9,1},... | collective-permute-start | bytes 663560 | tf_op jit(solution)/shard_map/ppermute | solution.py:990
  345.6 16.0 %copy-start.23 = (f32[36,1536]{1,0:T(8,128)}, f32[36,1536]{1,0:T(8,128)S(1)}, u32[]{:S(2)}) copy-start(f32[36,1536]{1,0:T(8,128)S(1)} %collective-permute-done.16.refs_9_) | copy-start | bytes 663556
  345.6 15.9 %copy-start.11 = (f32[576,384]{1,0:T(8,128)}, f32[576,384]{1,0:T(8,128)S(1)}, u32[]{:S(2)}) copy-start(f32[576,384]{1,0:T(8,128)S(1)} %collective-permute-done.19.refs_9_.refs_6_.refs_22_) | copy-start | bytes 2654212
  350.6 11.0 %copy-start.6 = (f32[576,768]{1,0:T(8,128)}, f32[576,768]{1,0:T(8,128)S(1)}, u32[]{:S(2)}) copy-start(f32[576,768]{1,0:T(8,128)S(1)} %collective-permute-done.18.refs_6_.refs_2_.refs_17_) | copy-start | bytes 5308420
  361.6 9.7 %copy-start.33 = (f32[1152]{0:T(1024)S(1)}, f32[1152]{0:T(1024)}, u32[]{:S(2)}) copy-start(f32[1152]{0:T(1024)} %param.36) | copy-start | bytes 13828
  361.6 10.3 %copy-start.32 = (f32[4,1,1152]{2,1,0:T(1,128)S(1)}, f32[4,1,1152]{2,1,0:T(1,128)}, u32[]{:S(2)}) copy-start(f32[4,1,1152]{2,1,0:T(1,128)} %get-tuple-element.440) | copy-start | bytes 55300
  361.6 10.4 %copy-start.27 = (f32[1,4608]{1,0:T(1,128)S(1)}, f32[1,4608]{1,0:T(1,128)}, u32[]{:S(2)}) copy-start(f32[1,4608]{1,0:T(1,128)} %get-tuple-element.439) | copy-start | bytes 55300
  361.6 10.6 %copy-start.29 = (f32[4,4,1152]{2,1,0:T(4,128)S(1)}, f32[4,4,1152]{2,1,0:T(4,128)}, u32[]{:S(2)}) copy-start(f32[4,4,1152]{2,1,0:T(4,128)} %get-tuple-element.437) | copy-start | bytes 221188
  361.6 13.6 %copy-start.36 = (f32[1,2304]{1,0:T(1,128)S(1)}, f32[1,2304]{1,0:T(1,128)}, u32[]{:S(2)}) copy-start(f32[1,2304]{1,0:T(1,128)} %get-tuple-element.442) | copy-start | bytes 27652
  365.7 49.0 %collective-permute-start.20 = (f32[576,2304]{1,0:T(8,128)}, f32[576,2304]{1,0:T(8,128)}, u32[]{:S(2)}, u32[]{:S(2)}) collective-permute-start(f32[576,2304]{1,0:T(8,128)} %get-tuple-element.407), channel_id=1, source_target_pairs={{0,16},{16,0},{1,17},{17,1},{2,18},{18,2},{3,19},{19,3},{4,20},{20... | collective-permute-start | bytes 15925256 | tf_op jit(solution)/shard_map/ppermute | solution.py:992
  365.7 49.0 %collective-permute-start.24 = (f32[288,2304]{1,0:T(8,128)}, f32[288,2304]{1,0:T(8,128)}, u32[]{:S(2)}, u32[]{:S(2)}) collective-permute-start(f32[288,2304]{1,0:T(8,128)} %get-tuple-element.411), channel_id=1, source_target_pairs={{0,1},{1,0},{2,3},{3,2},{4,5},{5,4},{6,7},{7,6},{8,9},{9,8},{10,11... | collective-permute-start | bytes 7962632 | tf_op jit(solution)/shard_map/ppermute | solution.py:990
  372.2 42.5 %collective-permute-start.22 = (f32[288,768]{1,0:T(8,128)}, f32[288,768]{1,0:T(8,128)S(1)}, u32[]{:S(2)}, u32[]{:S(2)}) collective-permute-start(f32[288,768]{1,0:T(8,128)} %get-tuple-element.409), channel_id=1, source_target_pairs={{0,4},{1,5},{2,6},{3,7},{4,0},{5,1},{6,2},{7,3},{8,12},{9,13},{10,... | collective-permute-start | bytes 2654216 | tf_op jit(solution)/shard_map/ppermute | solution.py:990
  373.9 40.8 %collective-permute-start.23 = (f32[288,384]{1,0:T(8,128)}, f32[288,384]{1,0:T(8,128)S(1)}, u32[]{:S(2)}, u32[]{:S(2)}) collective-permute-start(f32[288,384]{1,0:T(8,128)} %get-tuple-element.410), channel_id=1, source_target_pairs={{0,2},{1,3},{2,0},{3,1},{4,6},{5,7},{6,4},{7,5},{8,10},{9,11},{10,... | collective-permute-start | bytes 1327112 | tf_op jit(solution)/shard_map/ppermute | solution.py:990
  375.3 39.4 %collective-permute-start.21 = (f32[36,2048]{1,0:T(8,128)}, f32[36,2048]{1,0:T(8,128)S(1)}, u32[]{:S(2)}, u32[]{:S(2)}) collective-permute-start(f32[36,2048]{1,0:T(8,128)} %get-tuple-element.408), channel_id=1, source_target_pairs={{0,8},{1,9},{2,10},{3,11},{4,12},{5,13},{6,14},{7,15},{8,0},{9,1},... | collective-permute-start | bytes 884744 | tf_op jit(solution)/shard_map/ppermute | solution.py:990
  414.7 10.0 %copy-start.22 = (f32[36,2048]{1,0:T(8,128)}, f32[36,2048]{1,0:T(8,128)S(1)}, u32[]{:S(2)}) copy-start(f32[36,2048]{1,0:T(8,128)S(1)} %collective-permute-done.21.refs_14_) | copy-start | bytes 884740
  414.7 10.0 %copy-start.17 = (f32[288,384]{1,0:T(8,128)}, f32[288,384]{1,0:T(8,128)S(1)}, u32[]{:S(2)}) copy-start(f32[288,384]{1,0:T(8,128)S(1)} %collective-permute-done.23.refs_7_.refs_23_) | copy-start | bytes 1327108
  414.7 10.0 %copy-start.13 = (f32[288,768]{1,0:T(8,128)}, f32[288,768]{1,0:T(8,128)S(1)}, u32[]{:S(2)}) copy-start(f32[288,768]{1,0:T(8,128)S(1)} %collective-permute-done.22.refs_3_.refs_18_) | copy-start | bytes 2654212
  424.8 9.8 %copy-start.26 = (f32[4,1152]{1,0:T(4,128)S(1)}, f32[4,1152]{1,0:T(4,128)}, u32[]{:S(2)}) copy-start(f32[4,1152]{1,0:T(4,128)} %copy-done.25) | copy-start | bytes 55300
  429.5 33.2 %collective-permute-start.27 = (f32[144,2304]{1,0:T(8,128)}, f32[144,2304]{1,0:T(8,128)S(1)}, u32[]{:S(2)}, u32[]{:S(2)}) collective-permute-start(f32[144,2304]{1,0:T(8,128)} %get-tuple-element.428), channel_id=1, source_target_pairs={{0,2},{1,3},{2,0},{3,1},{4,6},{5,7},{6,4},{7,5},{8,10},{9,11},{10,... | collective-permute-start | bytes 3981320 | tf_op jit(solution)/shard_map/ppermute | solution.py:990
  430.2 44.5 %collective-permute-start.28 = (f32[288,2304]{1,0:T(8,128)}, f32[288,2304]{1,0:T(8,128)}, u32[]{:S(2)}, u32[]{:S(2)}) collective-permute-start(f32[288,2304]{1,0:T(8,128)} %get-tuple-element.429), channel_id=1, source_target_pairs={{0,1},{1,0},{2,3},{3,2},{4,5},{5,4},{6,7},{7,6},{8,9},{9,8},{10,11... | collective-permute-start | bytes 7962632 | tf_op jit(solution)/shard_map/ppermute | solution.py:990
  431.6 22.5 %collective-permute-start.26 = (f32[144,384]{1,0:T(8,128)}, f32[144,384]{1,0:T(8,128)S(1)}, u32[]{:S(2)}, u32[]{:S(2)}) collective-permute-start(f32[144,384]{1,0:T(8,128)} %get-tuple-element.427), channel_id=1, source_target_pairs={{0,8},{1,9},{2,10},{3,11},{4,12},{5,13},{6,14},{7,15},{8,0},{9,1},... | collective-permute-start | bytes 663560 | tf_op jit(solution)/shard_map/ppermute | solution.py:990
  433.6 29.0 %collective-permute-start.25 = (f32[144,768]{1,0:T(8,128)}, f32[144,768]{1,0:T(8,128)S(1)}, u32[]{:S(2)}, u32[]{:S(2)}) collective-permute-start(f32[144,768]{1,0:T(8,128)} %get-tuple-element.426), channel_id=1, source_target_pairs={{0,8},{1,9},{2,10},{3,11},{4,12},{5,13},{6,14},{7,15},{8,0},{9,1},... | collective-permute-start | bytes 1327112 | tf_op jit(solution)/shard_map/ppermute | solution.py:990
  454.0 28.7 %copy-start.24 = (f32[144,384]{1,0:T(8,128)}, f32[144,384]{1,0:T(8,128)S(1)}, u32[]{:S(2)}) copy-start(f32[144,384]{1,0:T(8,128)S(1)} %collective-permute-done.26.refs_24_) | copy-start | bytes 663556
  462.6 20.1 %copy-start.19 = (f32[144,768]{1,0:T(8,128)}, f32[144,768]{1,0:T(8,128)S(1)}, u32[]{:S(2)}) copy-start(f32[144,768]{1,0:T(8,128)S(1)} %collective-permute-done.25.refs_19_) | copy-start | bytes 1327108
  462.6 12.1 %copy-start.7 = (f32[144,2304]{1,0:T(8,128)}, f32[144,2304]{1,0:T(8,128)S(1)}, u32[]{:S(2)}) copy-start(f32[144,2304]{1,0:T(8,128)S(1)} %collective-permute-done.27.refs_2_) | copy-start | bytes 3981316
  479.1 21.9 %collective-permute-start.30 = (f32[144,2304]{1,0:T(8,128)}, f32[144,2304]{1,0:T(8,128)S(1)}, u32[]{:S(2)}, u32[]{:S(2)}) collective-permute-start(f32[144,2304]{1,0:T(8,128)} %get-tuple-element.452), channel_id=1, source_target_pairs={{0,2},{1,3},{2,0},{3,1},{4,6},{5,7},{6,4},{7,5},{8,10},{9,11},{10,... | collective-permute-start | bytes 3981320 | tf_op jit(solution)/shard_map/ppermute | solution.py:990
  479.9 21.1 %collective-permute-start.29 = (f32[72,2304]{1,0:T(8,128)}, f32[72,2304]{1,0:T(8,128)S(1)}, u32[]{:S(2)}, u32[]{:S(2)}) collective-permute-start(f32[72,2304]{1,0:T(8,128)} %get-tuple-element.451), channel_id=1, source_target_pairs={{0,4},{1,5},{2,6},{3,7},{4,0},{5,1},{6,2},{7,3},{8,12},{9,13},{10,... | collective-permute-start | bytes 1990664 | tf_op jit(solution)/shard_map/ppermute | solution.py:990
  481.6 18.5 %collective-permute-start.31 = (f32[4,10368]{1,0:T(4,128)S(1)}, f32[4,10368]{1,0:T(4,128)S(1)}, u32[]{:S(2)}, u32[]{:S(2)}) collective-permute-start(f32[4,10368]{1,0:T(4,128)S(1)} %pad_maximum_fusion.3), channel_id=1, source_target_pairs={{0,8},{1,9},{2,10},{3,11},{4,12},{5,13},{6,14},{7,15},{8,0},{9,1},... | collective-permute-start | bytes 497672 | tf_op jit(solution)/shard_map/ppermute | solution.py:997
  506.3 31.8 %collective-permute-start.33 = (f32[72,2304]{1,0:T(8,128)}, f32[72,2304]{1,0:T(8,128)S(1)}, u32[]{:S(2)}, u32[]{:S(2)}) collective-permute-start(f32[72,2304]{1,0:T(8,128)} %get-tuple-element.464), channel_id=1, source_target_pairs={{0,4},{1,5},{2,6},{3,7},{4,0},{5,1},{6,2},{7,3},{8,12},{9,13},{10,... | collective-permute-start | bytes 1990664 | tf_op jit(solution)/shard_map/ppermute | solution.py:990
  508.0 30.2 %collective-permute-start.34 = (f32[8,10368]{1,0:T(8,128)S(1)}, f32[8,10368]{1,0:T(8,128)S(1)}, u32[]{:S(2)}, u32[]{:S(2)}) collective-permute-start(f32[8,10368]{1,0:T(8,128)S(1)} %pad_maximum_fusion.2), channel_id=1, source_target_pairs={{0,4},{1,5},{2,6},{3,7},{4,0},{5,1},{6,2},{7,3},{8,12},{9,13},{10,... | collective-permute-start | bytes 995336 | tf_op jit(solution)/shard_map/ppermute | solution.py:997
  508.3 29.8 %collective-permute-start.32 = (f32[36,2304]{1,0:T(8,128)}, f32[36,2304]{1,0:T(8,128)S(1)}, u32[]{:S(2)}, u32[]{:S(2)}) collective-permute-start(f32[36,2304]{1,0:T(8,128)} %get-tuple-element.463), channel_id=1, source_target_pairs={{0,8},{1,9},{2,10},{3,11},{4,12},{5,13},{6,14},{7,15},{8,0},{9,1},... | collective-permute-start | bytes 995336 | tf_op jit(solution)/shard_map/ppermute | solution.py:990
  542.3 37.2 %copy-start.37 = (s32[64]{0:T(128)S(1)}, s32[64]{0:T(128)}, u32[]{:S(2)}) copy-start(s32[64]{0:T(128)} %param.23) | copy-start | bytes 772
  542.3 18.6 %collective-permute-start.36 = (f32[16,10368]{1,0:T(8,128)S(1)}, f32[16,10368]{1,0:T(8,128)S(1)}, u32[]{:S(2)}, u32[]{:S(2)}) collective-permute-start(f32[16,10368]{1,0:T(8,128)S(1)} %pad_maximum_fusion.1), channel_id=1, source_target_pairs={{0,2},{1,3},{2,0},{3,1},{4,6},{5,7},{6,4},{7,5},{8,10},{9,11},{10,... | collective-permute-start | bytes 1990664 | tf_op jit(solution)/shard_map/ppermute | solution.py:997
  542.4 18.4 %collective-permute-start.35 = (f32[36,2304]{1,0:T(8,128)}, f32[36,2304]{1,0:T(8,128)S(1)}, u32[]{:S(2)}, u32[]{:S(2)}) collective-permute-start(f32[36,2304]{1,0:T(8,128)} %add.271), channel_id=1, source_target_pairs={{0,8},{1,9},{2,10},{3,11},{4,12},{5,13},{6,14},{7,15},{8,0},{9,1},... | collective-permute-start | bytes 995336 | tf_op jit(solution)/shard_map/ppermute | solution.py:990
  560.8 21.0 %copy-start.21 = (f32[36,2304]{1,0:T(8,128)}, f32[36,2304]{1,0:T(8,128)S(1)}, u32[]{:S(2)}) copy-start(f32[36,2304]{1,0:T(8,128)S(1)} %collective-permute-done.35.refs_9_) | copy-start | bytes 995332
  561.0 24.6 %copy-start.4 = (f32[32,10368]{1,0:T(8,128)}, f32[32,10368]{1,0:T(8,128)S(1)}, u32[]{:S(2)}) copy-start(f32[32,10368]{1,0:T(8,128)S(1)} %pad_maximum_fusion.refs_0_.refs_4_.refs_8_) | copy-start | bytes 3981316
  561.0 18.0 %collective-permute-start.37 = (f32[32,10368]{1,0:T(8,128)S(1)}, f32[32,10368]{1,0:T(8,128)}, u32[]{:S(2)}, u32[]{:S(2)}) collective-permute-start(f32[32,10368]{1,0:T(8,128)S(1)} %pad_maximum_fusion.refs_0_.refs_4_.refs_8_), channel_id=1, source_target_pairs={{0,1},{1,0},{2,3},{3,2},{4,5},{5,4},{6,7},{7,6},{8,9},{9,8},{10,11... | collective-permute-start | bytes 3981320 | tf_op jit(solution)/shard_map/ppermute | solution.py:997
  578.9 6.6 %collective-permute-start.38 = (f32[32,10368]{1,0:T(8,128)S(1)}, f32[32,10368]{1,0:T(8,128)}, u32[]{:S(2)}, u32[]{:S(2)}) collective-permute-start(f32[32,10368]{1,0:T(8,128)S(1)} %pad_maximum_fusion.refs_0_.refs_4_.refs_8_), channel_id=1, source_target_pairs={{0,16},{16,0},{1,17},{17,1},{2,18},{18,2},{3,19},{19,3},{4,20},{20... | collective-permute-start | bytes 3981320 | tf_op jit(solution)/shard_map/ppermute | solution.py:999
  578.9 6.6 %collective-permute-start.39 = (f32[32,10368]{1,0:T(8,128)}, f32[32,10368]{1,0:T(8,128)}, u32[]{:S(2)}, u32[]{:S(2)}) collective-permute-start(f32[32,10368]{1,0:T(8,128)} %collective-permute-done.37.refs_1_.refs_5_.refs_9_), channel_id=1, source_target_pairs={{0,16},{16,0},{1,17},{17,1},{2,18},{18,2},{3,19},{19,3},{4,20},{20... | collective-permute-start | bytes 3981320 | tf_op jit(solution)/shard_map/ppermute | solution.py:999
  585.5 23.9 %copy-start.1 = (bf16[1001,1152]{1,0:T(8,128)(2,1)S(1)}, bf16[1001,1152]{1,0:T(8,128)(2,1)}, u32[]{:S(2)}) copy-start(bf16[1001,1152]{1,0:T(8,128)(2,1)} %param.26) | copy-start | bytes 6918916
  (14 other events, 53.0 us)

commit v4 on v3

--- a/solution.py
+++ b/solution.py
@@ -732,6 +732,46 @@
     )(low, high, w, x, mod, dx)
 
 
+def payload_body(item_ref, one_ref, two_ref, gate_ref, dm_ref, df_ref, first_ref, last_ref, cond_ref, out_ref):
+    tiles, _, width = one_ref.shape
+    items = out_ref.shape[0]
+    parts = [(one_ref, 0), (one_ref, 1), (two_ref, 0), (two_ref, 1), (two_ref, 2), (gate_ref, 0)]
+    for number, (ref, row) in enumerate(parts):
+        for item in range(items):
+            total = jnp.zeros((1, width), F32)
+            for tile in range(tiles):
+                total = total + jnp.where(item_ref[tile] == item, ref[tile, row : row + 1], 0.0)
+            out_ref[item : item + 1, number * width : (number + 1) * width] = total.astype(BF16).astype(F32)
+    at = 6 * width
+    hidden = df_ref.shape[1]
+    out_ref[0:1, at : at + hidden // 2] = df_ref[:, : hidden // 2]
+    out_ref[1:2, at : at + hidden // 2] = df_ref[:, hidden // 2 :]
+    out_ref[2:3, at : at + width] = jnp.sum(dm_ref[:, 0], axis=0, keepdims=True)
+    out_ref[2:3, at + width : at + 2 * width] = jnp.sum(two_ref[:, 3], axis=0, keepdims=True)
+    rest = width - COLUMNS
+    for number, third in enumerate((0, 2)):
+        spot = at + number * width
+        out_ref[3:4, spot : spot + COLUMNS] = first_ref[:, width + third * COLUMNS : width + (third + 1) * COLUMNS]
+        out_ref[3:4, spot + COLUMNS : spot + width] = last_ref[:, third * rest : (third + 1) * rest]
+    out_ref[:, at + 2 * width :] = cond_ref[...]
+
+
+def payload_call(tile_item, *sums):
+    items, width = sums[-1].shape
+    out = shaped((items, 9 * width), F32)
+    return call(
+        payload_body,
+        "payload",
+        0,
+        0,
+        grid=(1,),
+        in_specs=[pl.BlockSpec(memory_space=pltpu.SMEM)]
+        + [pl.BlockSpec(part.shape, functools.partial(lambda j, rank: (0,) * rank, rank=part.ndim)) for part in sums],
+        out_specs=pl.BlockSpec(out.shape, lambda j: (0, 0)),
+        out_shape=out,
+    )(tile_item, *sums)
+
+
 def modulation_back_body(me_ref, *refs, count):
     part_refs, cond_refs, sum_refs = refs[:count], refs[count : 2 * count], refs[2 * count : 3 * count]
     label_ref, w_ref, grad_ref, bias_ref, table_ref, own_sums_ref, act_ref, own_ref, total_ref = refs[3 * count :]
@@ -1110,14 +1150,6 @@
     df, x1, om_away, om_own, h1_away, h1_own = flow.round((df, x1, om_away, om_own, h1_away, h1_own))
     dx1, da, do, sums_two = middle_back_call(df, w_fc1, x1, mod, top, a, w_proj)
 
-    def by_item(*sums):
-        by_tile = jnp.concatenate(sums, axis=1)
-        return jnp.sum(jnp.where(chosen[:, :, None], by_tile[:, None], 0.0), axis=0).astype(BF16).astype(F32)
-
-    def in_rows(*sums):
-        made = jnp.concatenate([part.reshape(devices, -1) for part in sums], axis=1).reshape(items, -1)
-        return jnp.pad(made, ((0, 0), (0, -made.shape[1] % 128)))
-
     me = stream * batch + index
 
     def used_labels(side):
@@ -1128,47 +1160,23 @@
         return jnp.where(side == 0, jnp.take(labels.reshape(batch, items), from_device, axis=0).reshape(-1), null_class)
 
     used_rows = jnp.concatenate([used_labels(stream), used_labels(other)])[:, None]
-    dx1, da, do, sums_two = flow.round((dx1, da, do, sums_two))
+    dx1, da, do, sums_two, g = flow.round((dx1, da, do, sums_two, g))
     half = width // 2
     low = attention_back_call(flag, qkv, do, head_columns, probs, mixed, 0)
     rights = [Plain(da, 0, COLUMNS, width // COLUMNS), Wide((low, 0, COLUMNS))]
     send, first_sums = pair_call([om_away, h1_away], rights, "first_send")
     flow.emit(send, lambda got: pair_call([om_own, h1_own], rights, "first_keep", got), wide)
-    low, first_sums = flow.round((low, first_sums))
+    result, sum_gate = result_call(g, w_fc2, b_fc2[None], x1, mod, top, keep)
+    low, first_sums, result, sum_gate = flow.round((low, first_sums, result, sum_gate))
     high = attention_back_call(flag, qkv, do, head_columns, probs, mixed, 1)
     rest = Wide((low, COLUMNS, half - COLUMNS), (high, 0, half))
     send, high_sums = columns_call(h1_away, rest, "last_send")
     flow.emit(send, lambda got: columns_call(h1_own, rest, "last_keep", got), wide)
-    low, high, dx1, high_sums, g = flow.round((low, high, dx1, high_sums, g))
+    low, high, dx1, high_sums = flow.round((low, high, dx1, high_sums))
     grad_tokens, sums_one = first_back_call(low, high, w_qkv, x, mod, dx1)
-    result, sum_gate = result_call(g, w_fc2, b_fc2[None], x1, mod, top, keep)
-
-    def in_order(low, high):
-        first, second = low.shape[1] // 3, high.shape[1] // 3
-        return [
-            part
-            for third in range(3)
-            for part in (low[:, third * first : (third + 1) * first], high[:, third * second : (third + 1) * second])
-        ]
-
-    grad_tokens, sums_one, result, sum_gate = flow.round((grad_tokens, sums_one, result, sum_gate))
-    column_sums = in_order(first_sums[:, width:], high_sums)
+
     spread = flow.spread(
-        jnp.concatenate(
-            [
-                by_item(
-                    sums_one[:, 0], sums_one[:, 1], sums_two[:, 0], sums_two[:, 1], sums_two[:, 2], sum_gate[:, 0]
-                ),
-                in_rows(
-                    sum_df[0],
-                    jnp.sum(sum_dm, axis=(0, 1)),
-                    jnp.sum(sums_two[:, 3], axis=0),
-                    jnp.concatenate(column_sums[:2] + column_sums[4:], axis=1)[0],
-                ),
-                cond,
-            ],
-            axis=1,
-        )
+        payload_call(tile_item, sums_one, sums_two, sum_gate, sum_dm, sum_df, first_sums, high_sums, cond)
     )
     while any(chunk.stage < bits for chunk in fc1 + fc2):
         result = flow.round(result)
@@ -1179,7 +1187,7 @@
     result, grad_w_fc1, grad_w_fc2 = flow.round((result, grad_w_fc1, grad_w_fc2))
     while any(chunk.stage < bits for chunk in wide):
         result = flow.round(result)
-    result = flow.round(result) if flow.busy() else flow.received(result)
+    result = flow.round(result)
     first, last = wide
     each = COLUMNS, width - COLUMNS
     blocks = [
@@ -1196,11 +1204,14 @@
     )
     share = 6 * width // devices
     grad_b_ada = lax.dynamic_slice_in_dim(mod_sums[0], me * share, share)
-    ends = [hidden // devices, width // devices, width // devices, 2 * width // devices]
-    each = devices // items
-    bias = lax.dynamic_slice(own_sums, (me // each, me % each * sum(ends)), (1, sum(ends)))[0]
-    at = [sum(ends[:n]) for n in range(5)]
-    grad_b_fc1, grad_b_fc2, grad_b_proj, grad_b_qv = [bias[at[n] : at[n + 1]] for n in range(4)]
+    def own_sums_of(row, first, count):
+        return lax.dynamic_slice(own_sums, (row, first), (1, count))[0]
+
+    each = hidden // devices
+    grad_b_fc1 = own_sums_of(me // (devices // 2), me % (devices // 2) * each, each)
+    grad_b_fc2 = own_sums_of(2, me * shard, shard)
+    grad_b_proj = own_sums_of(2, width + me * shard, shard)
+    grad_b_qv = own_sums_of(3, me * 2 * shard, 2 * shard)
 
     return (
         result[None],

time: 615 us -> 588 us (0.956)
  waiting for transfers between devices: 148 us -> 121 us
    ppermute x28, waiting for transfers between devices: 91.9 us -> 71.1 us  [round(): lax.ppermute(send, ('stream', 'batch'), self.pairs(chunk.stage, chunk.lead))]
  transfers between devices with their start and end apart: 40 -> 40, of which waited for: 14 -> 15; matrix products, arithmetic and copies ran while one was open for 1% -> 1% of each run, Pallas kernels for 30% -> 31%
where the time goes in v4:
time: 588 us; the launch traced here: 584 us
  Pallas kernels  365 us (62%)
  waiting for transfers between devices  121 us (21%)
  starting transfers between devices  54.7 us (9%)
  local copies, waits for them, and re-layouts  23.6 us (4%)
  other arithmetic  8.94 us (2%)
  matrix products  7.69 us (1%)
    ppermute x28, waiting for transfers between devices, round(): lax.ppermute(send, ('stream', 'batch'), self.pairs(chunk.stage, chunk.lead))  71.1 us
    ppermute x4, waiting for transfers between devices, round(): lax.ppermute(piece, ('stream', 'batch'), pairs)  50.1 us
    ppermute x28, starting transfers between devices, round(): lax.ppermute(send, ('stream', 'batch'), self.pairs(chunk.stage, chunk.lead))  49.1 us
    pallas_call x3, Pallas kernels, hidden_call(): call(hidden_body, 'hidden', 6 * tokens * width * count, 6 * tokens * widt...  46.3 us
    pallas_call x5, Pallas kernels, columns_call(): call(functools.partial(columns_body, right=right, both=both), name, 2 * t...  37.9 us
    pallas_call x9, Pallas kernels, add_call(): call(functools.partial(add_body, plans=plans), 'add', moved // 4, moved,...  34 us
    pallas_call x1, Pallas kernels, middle_back_call(): call(middle_back_body, 'middle_back', 2 * tokens * width * (hidden + widt...  30.2 us
    pallas_call x2, Pallas kernels, attention_back_call(): call(attention_back_body, 'attention_back', 2 * 2 * heads * tokens * GROU...  27.2 us
  transfers between devices with their start and end apart: 40, of which 15 were waited for; matrix products, arithmetic and copies ran while one was open for 1% of the time, Pallas kernels for 31%

profile of v4, /device:TPU:0, one launch (start us, length us, event | category | flops | bytes accessed | tf_op | source)
XLA Modules:
  0.0 583.7 jit_solution(7266299684788642831)
XLA Ops:
  9.6 1.3 broadcast_in_dim.138.b1_ref
  13.2 7.7 %convolution_add_fusion = f32[4,6912]{1,0:T(4,128)S(1)} fusion(bf16[1152,6912]{1,0:T(8,128)(2,1)} %refs_13_.1, f32[6912]{0:T(1024)} %param.28, f32[4,1152]{1,0:T(4,128)S(1)} %maximum_add_fusion.cond_ref), kind=kOutput, calls=%fused_computation.3 | convolution fusion | flops 63751680 | bytes 16081920 | tf_op jit(solution)/shard_map/dot_general | solution.py:28
  23.0 1.7 fusion.away_ref
  24.7 1.7 fusion.1.own_ref
  26.4 1.7 broadcast_in_dim.154.b_ref
  28.1 16.3 %qkv.1 = (bf16[1024,1152]{1,0:T(8,128)(2,1)}, bf16[3456,1024]{1,0:T(8,128)(2,1)}) custom-call(bf16[1024,1152]{1,0:T(8,128)(2,1)} %bitcast.41, f32[4,6,1152]{2,1,0:T(8,128)} %reshape.293.mod_ref, bf16[1152,3456]{1,0:T(8,128)(2,1)} %w_ref.7, f32[3456,1]{1,0:T(8,128)} %broadcast_in_dim.154.b_ref), custom_call_target="tpu_custom_call" | custom-call | flops 1019215872 | bytes 2469888 | tf_op jit(solution)/shard_map/qkv/pallas_call | solution.py:73
  44.4 26.4 %attention.1 = (bf16[16,1024,1024]{2,1,0:T(8,128)(2,1)}, f32[16,72,1024]{2,1,0:T(8,128)}, bf16[1152,1024]{1,0:T(8,128)(2,1)}) custom-call(s32[1]{0:T(128)} %bitcast.1.flag_ref, bf16[3456,1024]{1,0:T(8,128)(2,1)} %get-tuple-element.251.q_ref.k_ref.v_ref, bf16[3456,1024]{1,0:T(8,128)(2,1)} %get-tuple-element.251.q_ref.k_ref.v_ref, ...), custom_call_target="tpu_custom_call" | custom-call | flops 2147483648 | bytes 5963776 | tf_op jit(solution)/shard_map/attention/pallas_call | solution.py:139
  70.7 15.1 %middle.1 = (f32[1024,1152]{1,0:T(8,128)}, f32[1024,1152]{1,0:T(8,128)}, bf16[1024,1152]{1,0:T(8,128)(2,1)}, bf16[1024,576]{1,0:T(8,128)(2,1)}, bf16[1024,576]{1...) custom-call(bf16[1152,1024]{1,0:T(8,128)(2,1)} %get-tuple-element.252.om_ref, ...), custom_call_target="tpu_custom_call" | custom-call | flops 679477248 | bytes 3833856 | tf_op jit(solution)/shard_map/middle/pallas_call | solution.py:259
  85.9 11.9 %hidden.3 = (bf16[1024,4608]{1,0:T(8,128)(2,1)}, bf16[1024,4608]{1,0:T(8,128)(2,1)}, f32[1,4608]{1,0:T(1,128)}, f32[576,1024]{1,0:T(8,128)}) custom-call(bf16[1024,1152]{1,0:T(8,128)(2,1)} %get-tuple-element.280.h_ref, bf16[1024,576]{1,0:T(8,128)(2,1)} %get-tuple-element.254.away_ref, bf16[1024,1152]{1,0:T(8,128)(2,1)} %get-tuple-element.255.dm_ref, ...), custom_call_target="tpu_custom_call" | custom-call | flops 905969664 | bytes 2588672 | tf_op jit(solution)/shard_map/hidden/pallas_call | solution.py:312
  98.2 15.3 %hidden.4 = (bf16[1024,4608]{1,0:T(8,128)(2,1)}, bf16[1024,4608]{1,0:T(8,128)(2,1)}, f32[1,4608]{1,0:T(1,128)}, f32[576,1536]{1,0:T(8,128)}) custom-call(bf16[1024,1152]{1,0:T(8,128)(2,1)} %get-tuple-element.280.h_ref, bf16[1024,576]{1,0:T(8,128)(2,1)} %get-tuple-element.254.away_ref, ...), custom_call_target="tpu_custom_call", output_to_operand_aliasing={{0}: (6, {}), {1}: (7, {}), {2}: (8, {})} | custom-call | flops 1358954496 | bytes 3440640 | tf_op jit(solution)/shard_map/hidden/pallas_call | solution.py:312
  113.6 4.7 hidden_keep.3
  118.3 9.3 %collective-permute-start.2 = (f32[288,1024]{1,0:T(8,128)}, f32[288,1024]{1,0:T(8,128)S(1)}, u32[]{:S(2)}, u32[]{:S(2)}) collective-permute-start(f32[288,1024]{1,0:T(8,128)} %get-tuple-element.288), channel_id=1, source_target_pairs={{0,1},{1,0},{2,3},{3,2},{4,5},{5,4},{6,7},{7,6},{8,9},{9,8},{10,11... | collective-permute-start | bytes 3538952 | tf_op jit(solution)/shard_map/ppermute | solution.py:1030
  127.6 19.0 %hidden.5 = (bf16[1024,4608]{1,0:T(8,128)(2,1)}, bf16[1024,4608]{1,0:T(8,128)(2,1)}, f32[1,4608]{1,0:T(1,128)}, f32[576,2048]{1,0:T(8,128)}) custom-call(bf16[1024,1152]{1,0:T(8,128)(2,1)} %get-tuple-element.280.h_ref, bf16[1024,576]{1,0:T(8,128)(2,1)} %get-tuple-element.254.away_ref, ...), custom_call_target="tpu_custom_call", output_to_operand_aliasing={{0}: (6, {}), {1}: (7, {}), {2}: (8, {})} | custom-call | flops 1811939328 | bytes 4292608 | tf_op jit(solution)/shard_map/hidden/pallas_call | solution.py:312
  146.7 7.3 %hidden_keep.4 = (f32[288,1536]{1,0:T(8,128)}, f32[288,1536]{1,0:T(8,128)}) custom-call(bf16[1024,576]{1,0:T(8,128)(2,1)} %get-tuple-element.277.refs_0_, bf16[1024,4608]{1,0:T(8,128)(2,1)} %get-tuple-element.321.refs_1_.df_ref, f32[576,1536]{1,0:T(8,128)} %collective-permute-done.1.refs_2_), custom_call_target="tpu_custom_call" | custom-call | flops 226492416 | bytes 1425408 | tf_op jit(solution)/shard_map/hidden_keep/pallas_call | solution.py:610
  154.0 2.0 add.272
  158.1 11.9 %moved.1 = (bf16[1024,576]{1,0:T(8,128)(2,1)}, bf16[1024,576]{1,0:T(8,128)(2,1)}, bf16[1024,576]{1,0:T(8,128)(2,1)}, bf16[1024,576]{1,0:T(8,128)(2,1)}) custom-call(bf16[1152,1024]{1,0:T(8,128)(2,1)} %get-tuple-element.252.om_ref, bf16[1024,1152]{1,0:T(8,128)(2,1)} %get-tuple-element.299.h_ref, bf16[1152,576]{1,0:T(8,128)(2,1)} %fusion.away_ref, ...), custom_call_target="tpu_custom_call" | custom-call | flops 679477248 | bytes 1511424 | tf_op jit(solution)/shard_map/moved/pallas_call | solution.py:679
  170.6 13.1 %rows_send.1 = f32[16,144,1152]{2,1,0:T(8,128)} custom-call(s32[1]{0:T(128)} %bitcast.6.side_ref, s32[3,16]{1,0:T(4,128)} %pad_add_fusion.spot_ref, bf16[1024,4608]{1,0:T(8,128)(2,1)} %get-tuple-element.354.g_ref, bf16[1024,1152]{1,0:T(8,128)(2,1)} %get-tuple-element.255.dm_ref), custom_call_target="tpu_custom_call" | custom-call | flops 679477248 | bytes 2211840 | tf_op jit(solution)/shard_map/rows_send/pallas_call | solution.py:368
  183.7 1.4 collective-permute-done.5.refs_4_.refs_5_.refs_1_.refs_6_
  185.1 8.4 %hidden_keep.5 = (f32[288,2048]{1,0:T(8,128)}, f32[288,2048]{1,0:T(8,128)}) custom-call(bf16[1024,576]{1,0:T(8,128)(2,1)} %get-tuple-element.277.refs_0_, bf16[1024,4608]{1,0:T(8,128)(2,1)} %get-tuple-element.321.refs_1_.df_ref, f32[576,2048]{1,0:T(8,128)} %collective-permute-done.3.refs_2_), custom_call_target="tpu_custom_call" | custom-call | flops 301989888 | bytes 1851392 | tf_op jit(solution)/shard_map/hidden_keep/pallas_call | solution.py:610
  193.5 2.6 add.273
  196.1 1.4 collective-permute-start.9
  198.2 1.6 collective-permute-start.7
  200.4 30.2 %middle_back.1 = (f32[1024,1152]{1,0:T(8,128)}, bf16[1024,1152]{1,0:T(8,128)(2,1)}, bf16[1152,1024]{1,0:T(8,128)(2,1)}, f32[4,4,1152]{2,1,0:T(4,128)}) custom-call(bf16[1024,4608]{1,0:T(8,128)(2,1)} %get-tuple-element.321.refs_1_.df_ref, bf16[1152,4608]{1,0:T(8,128)(2,1)} %w1_ref.7, f32[1024,1152]{1,0:T(8,128)} %get-tuple-element.322.x1_ref, ...), custom_call_target="tpu_custom_call" | custom-call | flops 1698693120 | bytes 5160960 | tf_op jit(solution)/shard_map/middle_back/pallas_call | solution.py:504
  230.6 4.2 collective-permute-done.9.refs_8_.refs_5_.refs_1_.refs_11_
  234.8 18.4 %rows_keep.1 = (f32[8,144,768]{2,1,0:T(8,128)}, f32[8,144,768]{2,1,0:T(8,128)}, f32[8,144,384]{2,1,0:T(8,128)}, f32[8,144,384]{2,1,0:T(8,128)}) custom-call(s32[1]{0:T(128)} %bitcast.8.side_ref, s32[3,16]{1,0:T(4,128)} %pad_add_fusion.1.spot_ref, bf16[1024,4608]{1,0:T(8,128)(2,1)} %get-tuple-element.354.g_ref, bf16[1024,1152]{1,0:T(8,128)(2,1)} %get-tuple-element.255.dm_ref, ...), custom_call_target="tpu_custom_call" | custom-call | flops 679477248 | bytes 3538944 | tf_op jit(solution)/shard_map/rows_keep/pallas_call | solution.py:427
  253.2 3.5 add.274
  258.0 1.6 collective-permute-start.14
  261.5 2.6 collective-permute-start.10
  264.0 13.6 %attention_back.2.refs_3_.refs_1_.low_ref = bf16[3,576,1024]{2,1,0:T(8,128)(2,1)} custom-call(s32[1]{0:T(128)} %bitcast.1.flag_ref, bf16[3456,1024]{1,0:T(8,128)(2,1)} %get-tuple-element.251.q_ref.k_ref.v_ref, bf16[3456,1024]{1,0:T(8,128)(2,1)} %get-tuple-element.251.q_ref.k_ref.v_ref, bf16[3456,1024]{1,0:T(8,128)(2,1)} %get-tuple-element.251.q_ref.k_ref.v_ref, ...), custom_call_target="tpu_custom_call" | custom-call | flops 2147483648 | bytes 3866624 | tf_op jit(solution)/shard_map/attention_back/pallas_call | solution.py:212
  277.6 10.0 %first_send.1 = (f32[576,2304]{1,0:T(8,128)}, f32[1,2304]{1,0:T(1,128)}) custom-call(bf16[1024,576]{1,0:T(8,128)(2,1)} %get-tuple-element.350.refs_0_, bf16[1024,1152]{1,0:T(8,128)(2,1)} %get-tuple-element.351.refs_1_, bf16[1024,576]{1,0:T(8,128)(2,1)} %get-tuple-element.352.refs_2_.refs_0_, bf16[3,576,1024]{2,1,0:T(8,128)(2,1)} %attention_back.2.refs_3_.refs_1_.low_ref), custom_call_target="tpu_custom_call" | custom-call | flops 339738624 | bytes 2064384 | tf_op jit(solution)/shard_map/first_send/pallas_call | solution.py:650
  287.7 19.7 %result.1 = (bf16[1024,1152]{1,0:T(8,128)(2,1)}, f32[4,1,1152]{2,1,0:T(1,128)}) custom-call(bf16[1024,4608]{1,0:T(8,128)(2,1)} %get-tuple-element.354.g_ref, bf16[4608,1152]{1,0:T(8,128)(2,1)} %w_ref.6, f32[1,1152]{1,0:T(1,128)} %broadcast_in_dim.141.b_ref, f32[1024,1152]{1,0:T(8,128)} %get-tuple-element.322.x1_ref, f32[4,6,1152]{2,1,0:T(8,128)} %reshape.293.mod_ref, ...), custom_call_target="tpu_custom_call" | custom-call | flops 1358954496 | bytes 3686400 | tf_op jit(solution)/shard_map/result/pallas_call | solution.py:460
  307.4 2.9 collective-permute-done.10.refs_4_
  312.8 5.4 add.275
  318.3 6.7 %collective-permute-start.18 = (f32[576,768]{1,0:T(8,128)}, f32[576,768]{1,0:T(8,128)S(1)}, u32[]{:S(2)}, u32[]{:S(2)}) collective-permute-start(f32[576,768]{1,0:T(8,128)} %get-tuple-element.384), channel_id=1, source_target_pairs={{0,2},{1,3},{2,0},{3,1},{4,6},{5,7},{6,4},{7,5},{8,10},{9,11},{10,... | collective-permute-start | bytes 5308424 | tf_op jit(solution)/shard_map/ppermute | solution.py:1030
  326.9 13.6 %attention_back.3.refs_2_.high_ref = bf16[3,576,1024]{2,1,0:T(8,128)(2,1)} custom-call(s32[1]{0:T(128)} %bitcast.1.flag_ref, bf16[3456,1024]{1,0:T(8,128)(2,1)} %get-tuple-element.251.q_ref.k_ref.v_ref, bf16[3456,1024]{1,0:T(8,128)(2,1)} %get-tuple-element.251.q_ref.k_ref.v_ref, bf16[3456,1024]{1,0:T(8,128)(2,1)} %get-tuple-element.251.q_ref.k_ref.v_ref, ...), custom_call_target="tpu_custom_call" | custom-call | flops 2147483648 | bytes 3866624 | tf_op jit(solution)/shard_map/attention_back/pallas_call | solution.py:212
  340.6 8.1 %last_send.1 = (f32[576,2304]{1,0:T(8,128)}, f32[1,2304]{1,0:T(1,128)}) custom-call(bf16[1024,576]{1,0:T(8,128)(2,1)} %get-tuple-element.352.refs_2_.refs_0_, bf16[3,576,1024]{2,1,0:T(8,128)(2,1)} %attention_back.2.refs_3_.refs_1_.low_ref, bf16[3,576,1024]{2,1,0:T(8,128)(2,1)} %attention_back.3.refs_2_.high_ref), custom_call_target="tpu_custom_call" | custom-call | flops 339738624 | bytes 2064384 | tf_op jit(solution)/shard_map/last_send/pallas_call | solution.py:610
  348.7 6.4 %collective-permute-done.18.refs_6_.refs_2_.refs_17_ = f32[576,768]{1,0:T(8,128)S(1)} collective-permute-done((f32[576,768]{1,0:T(8,128)}, f32[576,768]{1,0:T(8,128)S(1)}, u32[]{:S(2)}, u32[]{:S(2)}) %collective-permute-start.18) | collective-permute-done | bytes 1769504 | tf_op jit(solution)/shard_map/ppermute | solution.py:1030
  355.1 11.2 %first_keep.1 = (f32[288,2304]{1,0:T(8,128)}, f32[288,2304]{1,0:T(8,128)}) custom-call(bf16[1024,576]{1,0:T(8,128)(2,1)} %get-tuple-element.397.refs_0_, bf16[1024,1152]{1,0:T(8,128)(2,1)} %get-tuple-element.351.refs_1_, bf16[1024,576]{1,0:T(8,128)(2,1)} %get-tuple-element.398.refs_2_.refs_0_, bf16[3,576,1024]{2,1,0:T(8,128)(2,1)} %attention_back.2.refs_3_.refs_1_.low_ref, ...), custom_call_target="tpu_custom_call" | custom-call | flops 339738624 | bytes 2064384 | tf_op jit(solution)/shard_map/first_keep/pallas_call | solution.py:650
  366.4 4.1 add.276
  370.5 5.2 collective-permute-start.24
  376.9 1.8 collective-permute-start.21
  378.6 18.2 %first_back.1 = (f32[1024,1152]{1,0:T(8,128)}, f32[4,2,1152]{2,1,0:T(2,128)}) custom-call(bf16[3,576,1024]{2,1,0:T(8,128)(2,1)} %attention_back.2.refs_3_.refs_1_.low_ref, bf16[3,576,1024]{2,1,0:T(8,128)(2,1)} %attention_back.3.refs_2_.high_ref, bf16[1152,3456]{1,0:T(8,128)(2,1)} %w_ref.7, bf16[1024,1152]{1,0:T(8,128)(2,1)} %bitcast.43, ...), custom_call_target="tpu_custom_call" | custom-call | flops 1019215872 | bytes 3354624 | tf_op jit(solution)/shard_map/first_back/pallas_call | solution.py:716
  396.8 1.8 payload.1
  398.6 3.9 collective-permute-done.21.refs_14_
  402.5 2.1 collective-permute-done.22.refs_3_.refs_18_
  404.6 6.0 %collective-permute-done.24.refs_9_.refs_1_ = f32[288,2304]{1,0:T(8,128)} collective-permute-done((f32[288,2304]{1,0:T(8,128)}, f32[288,2304]{1,0:T(8,128)}, u32[]{:S(2)}, u32[]{:S(2)}) %collective-permute-start.24) | collective-permute-done | bytes 2654240 | tf_op jit(solution)/shard_map/ppermute | solution.py:1030
  410.7 9.4 %last_keep.1 = (f32[288,2304]{1,0:T(8,128)}, f32[288,2304]{1,0:T(8,128)}) custom-call(bf16[1024,576]{1,0:T(8,128)(2,1)} %get-tuple-element.398.refs_2_.refs_0_, bf16[3,576,1024]{2,1,0:T(8,128)(2,1)} %attention_back.2.refs_3_.refs_1_.low_ref, bf16[3,576,1024]{2,1,0:T(8,128)(2,1)} %attention_back.3.refs_2_.high_ref, f32[576,2304]{1,0:T(8,128)} %collective-permute-done.20.refs_3_), custom_call_target="tpu_custom_call" | custom-call | flops 339738624 | bytes 2064384 | tf_op jit(solution)/shard_map/last_keep/pallas_call | solution.py:610
  420.1 4.6 add.277
  424.7 2.1 collective-permute-start.28
  426.9 2.5 collective-permute-start.25
  429.8 2.5 collective-permute-start.29
  432.4 33.1 %collective-permute-done.29 = f32[4,10368]{1,0:T(4,128)S(1)} collective-permute-done((f32[4,10368]{1,0:T(4,128)S(1)}, f32[4,10368]{1,0:T(4,128)S(1)}, u32[]{:S(2)}, u32[]{:S(2)}) %collective-permute-start.29) | collective-permute-done | bytes 165920 | tf_op jit(solution)/shard_map/ppermute | solution.py:1037
  465.5 5.8 collective-permute-done.28.refs_4_.refs_5_.refs_1_.refs_6_
  471.4 4.4 add.278
  478.6 4.9 assemble.2
  483.6 17.0 %collective-permute-done.32 = f32[8,10368]{1,0:T(8,128)S(1)} collective-permute-done((f32[8,10368]{1,0:T(8,128)S(1)}, f32[8,10368]{1,0:T(8,128)S(1)}, u32[]{:S(2)}, u32[]{:S(2)}) %collective-permute-start.32) | collective-permute-done | bytes 331808 | tf_op jit(solution)/shard_map/ppermute | solution.py:1037
  501.9 4.0 add.279
  507.1 2.0 collective-permute-start.33
  509.2 18.4 %collective-permute-done.33.refs_4_ = f32[36,2304]{1,0:T(8,128)S(1)} collective-permute-done((f32[36,2304]{1,0:T(8,128)}, f32[36,2304]{1,0:T(8,128)S(1)}, u32[]{:S(2)}, u32[]{:S(2)}) %collective-permute-start.33) | collective-permute-done | bytes 331808 | tf_op jit(solution)/shard_map/ppermute | solution.py:1030
  527.6 2.1 collective-permute-done.34.refs_3_.refs_8_
  530.6 3.3 add.280
  536.0 16.9 %collective-permute-done.36.refs_9_ = f32[36,2304]{1,0:T(8,128)S(1)} collective-permute-done((f32[36,2304]{1,0:T(8,128)S(1)}, f32[36,2304]{1,0:T(8,128)S(1)}, u32[]{:S(2)}, u32[]{:S(2)}) %collective-permute-start.36) | collective-permute-done | bytes 331808 | tf_op jit(solution)/shard_map/ppermute | solution.py:1030
  555.9 3.7 assemble.3
  559.7 18.6 %modulation_back.1 = (f32[36,6912]{1,0:T(8,128)}, f32[1,6912]{1,0:T(1,128)}, f32[1001,1152]{1,0:T(8,128)}, f32[4,2304]{1,0:T(4,128)}) custom-call(s32[1]{0:T(128)} %bitcast.16.me_ref, f32[32,10368]{1,0:T(8,128)} %copy-done.4, f32[32,10368]{1,0:T(8,128)} %collective-permute-done.37.refs_1_.refs_5_.refs_9_, ...), custom_call_target="tpu_custom_call" | custom-call | flops 509607936 | bytes 1990656 | tf_op jit(solution)/shard_map/modulation_back/pallas_call | solution.py:827
  (174 shorter events, 42.5 us)
Async XLA Ops:
  0.6 11.1 %copy-start = (bf16[1001,1152]{1,0:T(8,128)(2,1)S(1)}, bf16[1001,1152]{1,0:T(8,128)(2,1)}, u32[]{:S(2)}) copy-start(bf16[1001,1152]{1,0:T(8,128)(2,1)} %param.26) | copy-start | bytes 6918916
  2.3 4.2 copy-start.32
  97.7 15.8 %collective-permute-start = (f32[576,1024]{1,0:T(8,128)}, f32[576,1024]{1,0:T(8,128)}, u32[]{:S(2)}, u32[]{:S(2)}) collective-permute-start(f32[576,1024]{1,0:T(8,128)} %get-tuple-element.271), channel_id=1, source_target_pairs={{0,16},{16,0},{1,17},{17,1},{2,18},{18,2},{3,19},{19,3},{4,20},{20... | collective-permute-start | bytes 7077896 | tf_op jit(solution)/shard_map/ppermute | solution.py:1032
  118.2 28.4 %collective-permute-start.1 = (f32[576,1536]{1,0:T(8,128)}, f32[576,1536]{1,0:T(8,128)}, u32[]{:S(2)}, u32[]{:S(2)}) collective-permute-start(f32[576,1536]{1,0:T(8,128)} %get-tuple-element.287), channel_id=1, source_target_pairs={{0,16},{16,0},{1,17},{17,1},{2,18},{18,2},{3,19},{19,3},{4,20},{20... | collective-permute-start | bytes 10616840 | tf_op jit(solution)/shard_map/ppermute | solution.py:1032
  118.3 28.4 %collective-permute-start.2 = (f32[288,1024]{1,0:T(8,128)}, f32[288,1024]{1,0:T(8,128)S(1)}, u32[]{:S(2)}, u32[]{:S(2)}) collective-permute-start(f32[288,1024]{1,0:T(8,128)} %get-tuple-element.288), channel_id=1, source_target_pairs={{0,1},{1,0},{2,3},{3,2},{4,5},{5,4},{6,7},{7,6},{8,9},{9,8},{10,11... | collective-permute-start | bytes 3538952 | tf_op jit(solution)/shard_map/ppermute | solution.py:1030
  146.6 7.4 %copy-start.5 = (f32[288,1024]{1,0:T(8,128)}, f32[288,1024]{1,0:T(8,128)S(1)}, u32[]{:S(2)}) copy-start(f32[288,1024]{1,0:T(8,128)S(1)} %collective-permute-done.2.refs_1_) | copy-start | bytes 3538948
  156.0 29.1 %collective-permute-start.3 = (f32[576,2048]{1,0:T(8,128)}, f32[576,2048]{1,0:T(8,128)}, u32[]{:S(2)}, u32[]{:S(2)}) collective-permute-start(f32[576,2048]{1,0:T(8,128)} %get-tuple-element.304), channel_id=1, source_target_pairs={{0,16},{16,0},{1,17},{17,1},{2,18},{18,2},{3,19},{19,3},{4,20},{20... | collective-permute-start | bytes 14155784 | tf_op jit(solution)/shard_map/ppermute | solution.py:1032
  156.0 29.1 %collective-permute-start.5 = (f32[288,1536]{1,0:T(8,128)}, f32[288,1536]{1,0:T(8,128)S(1)}, u32[]{:S(2)}, u32[]{:S(2)}) collective-permute-start(f32[288,1536]{1,0:T(8,128)} %get-tuple-element.306), channel_id=1, source_target_pairs={{0,1},{1,0},{2,3},{3,2},{4,5},{5,4},{6,7},{7,6},{8,9},{9,8},{10,11... | collective-permute-start | bytes 5308424 | tf_op jit(solution)/shard_map/ppermute | solution.py:1030
  157.3 26.4 %collective-permute-start.4 = (f32[144,1024]{1,0:T(8,128)}, f32[144,1024]{1,0:T(8,128)S(1)}, u32[]{:S(2)}, u32[]{:S(2)}) collective-permute-start(f32[144,1024]{1,0:T(8,128)} %add.272), channel_id=1, source_target_pairs={{0,2},{1,3},{2,0},{3,1},{4,6},{5,7},{6,4},{7,5},{8,10},{9,11},{10,... | collective-permute-start | bytes 1769480 | tf_op jit(solution)/shard_map/ppermute | solution.py:1030
  183.7 9.8 %copy-start.12 = (f32[144,1024]{1,0:T(8,128)}, f32[144,1024]{1,0:T(8,128)S(1)}, u32[]{:S(2)}) copy-start(f32[144,1024]{1,0:T(8,128)S(1)} %collective-permute-done.4.refs_2_) | copy-start | bytes 1769476
  185.1 8.4 %copy-start.2 = (f32[288,1536]{1,0:T(8,128)}, f32[288,1536]{1,0:T(8,128)S(1)}, u32[]{:S(2)}) copy-start(f32[288,1536]{1,0:T(8,128)S(1)} %collective-permute-done.5.refs_4_.refs_5_.refs_1_.refs_6_) | copy-start | bytes 5308420
  196.1 38.7 %collective-permute-start.6 = (f32[2304,1152]{1,0:T(8,128)}, f32[2304,1152]{1,0:T(8,128)}, u32[]{:S(2)}, u32[]{:S(2)}) collective-permute-start(f32[2304,1152]{1,0:T(8,128)} %bitcast.44), channel_id=1, source_target_pairs={{0,16},{16,0},{1,17},{17,1},{2,18},{18,2},{3,19},{19,3},{4,20},{20... | collective-permute-start | bytes 31850504 | tf_op jit(solution)/shard_map/ppermute | solution.py:1032
  196.1 38.7 %collective-permute-start.9 = (f32[288,2048]{1,0:T(8,128)}, f32[288,2048]{1,0:T(8,128)}, u32[]{:S(2)}, u32[]{:S(2)}) collective-permute-start(f32[288,2048]{1,0:T(8,128)} %get-tuple-element.331), channel_id=1, source_target_pairs={{0,1},{1,0},{2,3},{3,2},{4,5},{5,4},{6,7},{7,6},{8,9},{9,8},{10,11... | collective-permute-start | bytes 7077896 | tf_op jit(solution)/shard_map/ppermute | solution.py:1030
  197.5 33.1 %collective-permute-start.8 = (f32[144,1536]{1,0:T(8,128)}, f32[144,1536]{1,0:T(8,128)S(1)}, u32[]{:S(2)}, u32[]{:S(2)}) collective-permute-start(f32[144,1536]{1,0:T(8,128)} %get-tuple-element.330), channel_id=1, source_target_pairs={{0,2},{1,3},{2,0},{3,1},{4,6},{5,7},{6,4},{7,5},{8,10},{9,11},{10,... | collective-permute-start | bytes 2654216 | tf_op jit(solution)/shard_map/ppermute | solution.py:1030
  198.2 32.4 %collective-permute-start.7 = (f32[72,1024]{1,0:T(8,128)}, f32[72,1024]{1,0:T(8,128)S(1)}, u32[]{:S(2)}, u32[]{:S(2)}) collective-permute-start(f32[72,1024]{1,0:T(8,128)} %get-tuple-element.329), channel_id=1, source_target_pairs={{0,4},{1,5},{2,6},{3,7},{4,0},{5,1},{6,2},{7,3},{8,12},{9,13},{10,... | collective-permute-start | bytes 884744 | tf_op jit(solution)/shard_map/ppermute | solution.py:1030
  230.6 22.6 %copy-start.19 = (f32[72,1024]{1,0:T(8,128)}, f32[72,1024]{1,0:T(8,128)S(1)}, u32[]{:S(2)}) copy-start(f32[72,1024]{1,0:T(8,128)S(1)} %collective-permute-done.7.refs_3_) | copy-start | bytes 884740
  230.6 22.6 %copy-start.10 = (f32[144,1536]{1,0:T(8,128)}, f32[144,1536]{1,0:T(8,128)S(1)}, u32[]{:S(2)}) copy-start(f32[144,1536]{1,0:T(8,128)S(1)} %collective-permute-done.8.refs_6_.refs_2_.refs_7_) | copy-start | bytes 2654212
  253.2 7.6 %copy-start.30 = (f32[1152]{0:T(1024)S(1)}, f32[1152]{0:T(1024)}, u32[]{:S(2)}) copy-start(f32[1152]{0:T(1024)} %param.36) | copy-start | bytes 13828
  256.8 54.4 %collective-permute-start.13 = (f32[1152,768]{1,0:T(8,128)}, f32[1152,768]{1,0:T(8,128)}, u32[]{:S(2)}, u32[]{:S(2)}) collective-permute-start(f32[1152,768]{1,0:T(8,128)} %bitcast.49), channel_id=1, source_target_pairs={{0,1},{1,0},{2,3},{3,2},{4,5},{5,4},{6,7},{7,6},{8,9},{9,8},{10,11... | collective-permute-start | bytes 10616840 | tf_op jit(solution)/shard_map/ppermute | solution.py:1030
  258.0 53.1 %collective-permute-start.14 = (f32[1152,384]{1,0:T(8,128)}, f32[1152,384]{1,0:T(8,128)S(1)}, u32[]{:S(2)}, u32[]{:S(2)}) collective-permute-start(f32[1152,384]{1,0:T(8,128)} %bitcast.11), channel_id=1, source_target_pairs={{0,4},{1,5},{2,6},{3,7},{4,0},{5,1},{6,2},{7,3},{8,12},{9,13},{10,... | collective-permute-start | bytes 5308424 | tf_op jit(solution)/shard_map/ppermute | solution.py:1030
  259.6 51.5 %collective-permute-start.12 = (f32[144,2048]{1,0:T(8,128)}, f32[144,2048]{1,0:T(8,128)S(1)}, u32[]{:S(2)}, u32[]{:S(2)}) collective-permute-start(f32[144,2048]{1,0:T(8,128)} %get-tuple-element.359), channel_id=1, source_target_pairs={{0,2},{1,3},{2,0},{3,1},{4,6},{5,7},{6,4},{7,5},{8,10},{9,11},{10,... | collective-permute-start | bytes 3538952 | tf_op jit(solution)/shard_map/ppermute | solution.py:1030
  260.4 50.7 %collective-permute-start.11 = (f32[72,1536]{1,0:T(8,128)}, f32[72,1536]{1,0:T(8,128)S(1)}, u32[]{:S(2)}, u32[]{:S(2)}) collective-permute-start(f32[72,1536]{1,0:T(8,128)} %get-tuple-element.358), channel_id=1, source_target_pairs={{0,4},{1,5},{2,6},{3,7},{4,0},{5,1},{6,2},{7,3},{8,12},{9,13},{10,... | collective-permute-start | bytes 1327112 | tf_op jit(solution)/shard_map/ppermute | solution.py:1030
  261.5 48.8 %collective-permute-start.10 = (f32[36,1024]{1,0:T(8,128)}, f32[36,1024]{1,0:T(8,128)S(1)}, u32[]{:S(2)}, u32[]{:S(2)}) collective-permute-start(f32[36,1024]{1,0:T(8,128)} %get-tuple-element.357), channel_id=1, source_target_pairs={{0,8},{1,9},{2,10},{3,11},{4,12},{5,13},{6,14},{7,15},{8,0},{9,1},... | collective-permute-start | bytes 442376 | tf_op jit(solution)/shard_map/ppermute | solution.py:1030
  310.3 8.0 %copy-start.29 = (f32[36,1024]{1,0:T(8,128)}, f32[36,1024]{1,0:T(8,128)S(1)}, u32[]{:S(2)}) copy-start(f32[36,1024]{1,0:T(8,128)S(1)} %collective-permute-done.10.refs_4_) | copy-start | bytes 442372
  318.3 36.9 %collective-permute-start.15 = (f32[576,2304]{1,0:T(8,128)}, f32[576,2304]{1,0:T(8,128)}, u32[]{:S(2)}, u32[]{:S(2)}) collective-permute-start(f32[576,2304]{1,0:T(8,128)} %get-tuple-element.381), channel_id=1, source_target_pairs={{0,16},{16,0},{1,17},{17,1},{2,18},{18,2},{3,19},{19,3},{4,20},{20... | collective-permute-start | bytes 15925256 | tf_op jit(solution)/shard_map/ppermute | solution.py:1032
  318.3 36.9 %collective-permute-start.18 = (f32[576,768]{1,0:T(8,128)}, f32[576,768]{1,0:T(8,128)S(1)}, u32[]{:S(2)}, u32[]{:S(2)}) collective-permute-start(f32[576,768]{1,0:T(8,128)} %get-tuple-element.384), channel_id=1, source_target_pairs={{0,2},{1,3},{2,0},{3,1},{4,6},{5,7},{6,4},{7,5},{8,10},{9,11},{10,... | collective-permute-start | bytes 5308424 | tf_op jit(solution)/shard_map/ppermute | solution.py:1030
  324.9 23.8 %collective-permute-start.19 = (f32[576,384]{1,0:T(8,128)}, f32[576,384]{1,0:T(8,128)S(1)}, u32[]{:S(2)}, u32[]{:S(2)}) collective-permute-start(f32[576,384]{1,0:T(8,128)} %get-tuple-element.385), channel_id=1, source_target_pairs={{0,1},{1,0},{2,3},{3,2},{4,5},{5,4},{6,7},{7,6},{8,9},{9,8},{10,11... | collective-permute-start | bytes 2654216 | tf_op jit(solution)/shard_map/ppermute | solution.py:1030
  325.5 23.2 %collective-permute-start.17 = (f32[72,2048]{1,0:T(8,128)}, f32[72,2048]{1,0:T(8,128)S(1)}, u32[]{:S(2)}, u32[]{:S(2)}) collective-permute-start(f32[72,2048]{1,0:T(8,128)} %get-tuple-element.383), channel_id=1, source_target_pairs={{0,4},{1,5},{2,6},{3,7},{4,0},{5,1},{6,2},{7,3},{8,12},{9,13},{10,... | collective-permute-start | bytes 1769480 | tf_op jit(solution)/shard_map/ppermute | solution.py:1030
  326.6 22.1 %collective-permute-start.16 = (f32[36,1536]{1,0:T(8,128)}, f32[36,1536]{1,0:T(8,128)S(1)}, u32[]{:S(2)}, u32[]{:S(2)}) collective-permute-start(f32[36,1536]{1,0:T(8,128)} %get-tuple-element.382), channel_id=1, source_target_pairs={{0,8},{1,9},{2,10},{3,11},{4,12},{5,13},{6,14},{7,15},{8,0},{9,1},... | collective-permute-start | bytes 663560 | tf_op jit(solution)/shard_map/ppermute | solution.py:1030
  348.7 17.7 %copy-start.26 = (f32[36,1536]{1,0:T(8,128)}, f32[36,1536]{1,0:T(8,128)S(1)}, u32[]{:S(2)}) copy-start(f32[36,1536]{1,0:T(8,128)S(1)} %collective-permute-done.16.refs_9_) | copy-start | bytes 663556
  348.7 17.7 %copy-start.16 = (f32[72,2048]{1,0:T(8,128)}, f32[72,2048]{1,0:T(8,128)S(1)}, u32[]{:S(2)}) copy-start(f32[72,2048]{1,0:T(8,128)S(1)} %collective-permute-done.17.refs_3_.refs_13_) | copy-start | bytes 1769476
  348.7 17.6 %copy-start.11 = (f32[576,384]{1,0:T(8,128)}, f32[576,384]{1,0:T(8,128)S(1)}, u32[]{:S(2)}) copy-start(f32[576,384]{1,0:T(8,128)S(1)} %collective-permute-done.19.refs_9_.refs_6_.refs_22_) | copy-start | bytes 2654212
  355.1 11.2 %copy-start.6 = (f32[576,768]{1,0:T(8,128)}, f32[576,768]{1,0:T(8,128)S(1)}, u32[]{:S(2)}) copy-start(f32[576,768]{1,0:T(8,128)S(1)} %collective-permute-done.18.refs_6_.refs_2_.refs_17_) | copy-start | bytes 5308420
  370.5 40.2 %collective-permute-start.20 = (f32[576,2304]{1,0:T(8,128)}, f32[576,2304]{1,0:T(8,128)}, u32[]{:S(2)}, u32[]{:S(2)}) collective-permute-start(f32[576,2304]{1,0:T(8,128)} %get-tuple-element.401), channel_id=1, source_target_pairs={{0,16},{16,0},{1,17},{17,1},{2,18},{18,2},{3,19},{19,3},{4,20},{20... | collective-permute-start | bytes 15925256 | tf_op jit(solution)/shard_map/ppermute | solution.py:1032
  370.5 40.2 %collective-permute-start.24 = (f32[288,2304]{1,0:T(8,128)}, f32[288,2304]{1,0:T(8,128)}, u32[]{:S(2)}, u32[]{:S(2)}) collective-permute-start(f32[288,2304]{1,0:T(8,128)} %get-tuple-element.405), channel_id=1, source_target_pairs={{0,1},{1,0},{2,3},{3,2},{4,5},{5,4},{6,7},{7,6},{8,9},{9,8},{10,11... | collective-permute-start | bytes 7962632 | tf_op jit(solution)/shard_map/ppermute | solution.py:1030
  375.6 29.0 %collective-permute-start.22 = (f32[288,768]{1,0:T(8,128)}, f32[288,768]{1,0:T(8,128)S(1)}, u32[]{:S(2)}, u32[]{:S(2)}) collective-permute-start(f32[288,768]{1,0:T(8,128)} %get-tuple-element.403), channel_id=1, source_target_pairs={{0,4},{1,5},{2,6},{3,7},{4,0},{5,1},{6,2},{7,3},{8,12},{9,13},{10,... | collective-permute-start | bytes 2654216 | tf_op jit(solution)/shard_map/ppermute | solution.py:1030
  376.1 26.5 %collective-permute-start.23 = (f32[288,384]{1,0:T(8,128)}, f32[288,384]{1,0:T(8,128)S(1)}, u32[]{:S(2)}, u32[]{:S(2)}) collective-permute-start(f32[288,384]{1,0:T(8,128)} %get-tuple-element.404), channel_id=1, source_target_pairs={{0,2},{1,3},{2,0},{3,1},{4,6},{5,7},{6,4},{7,5},{8,10},{9,11},{10,... | collective-permute-start | bytes 1327112 | tf_op jit(solution)/shard_map/ppermute | solution.py:1030
  376.9 25.7 %collective-permute-start.21 = (f32[36,2048]{1,0:T(8,128)}, f32[36,2048]{1,0:T(8,128)S(1)}, u32[]{:S(2)}, u32[]{:S(2)}) collective-permute-start(f32[36,2048]{1,0:T(8,128)} %get-tuple-element.402), channel_id=1, source_target_pairs={{0,8},{1,9},{2,10},{3,11},{4,12},{5,13},{6,14},{7,15},{8,0},{9,1},... | collective-permute-start | bytes 884744 | tf_op jit(solution)/shard_map/ppermute | solution.py:1030
  402.5 17.5 %copy-start.25 = (f32[36,2048]{1,0:T(8,128)}, f32[36,2048]{1,0:T(8,128)S(1)}, u32[]{:S(2)}) copy-start(f32[36,2048]{1,0:T(8,128)S(1)} %collective-permute-done.21.refs_14_) | copy-start | bytes 884740
  402.5 17.5 %copy-start.18 = (f32[288,384]{1,0:T(8,128)}, f32[288,384]{1,0:T(8,128)S(1)}, u32[]{:S(2)}) copy-start(f32[288,384]{1,0:T(8,128)S(1)} %collective-permute-done.23.refs_7_.refs_23_) | copy-start | bytes 1327108
  404.6 15.4 %copy-start.13 = (f32[288,768]{1,0:T(8,128)}, f32[288,768]{1,0:T(8,128)S(1)}, u32[]{:S(2)}) copy-start(f32[288,768]{1,0:T(8,128)S(1)} %collective-permute-done.22.refs_3_.refs_18_) | copy-start | bytes 2654212
  420.0 9.8 %copy-start.20 = (f32[4,10368]{1,0:T(4,128)S(1)}, f32[4,10368]{1,0:T(4,128)}, u32[]{:S(2)}) copy-start(f32[4,10368]{1,0:T(4,128)} %payload.1) | copy-start | bytes 497668
  424.7 46.6 %collective-permute-start.28 = (f32[288,2304]{1,0:T(8,128)}, f32[288,2304]{1,0:T(8,128)}, u32[]{:S(2)}, u32[]{:S(2)}) collective-permute-start(f32[288,2304]{1,0:T(8,128)} %get-tuple-element.430), channel_id=1, source_target_pairs={{0,1},{1,0},{2,3},{3,2},{4,5},{5,4},{6,7},{7,6},{8,9},{9,8},{10,11... | collective-permute-start | bytes 7962632 | tf_op jit(solution)/shard_map/ppermute | solution.py:1030
  426.8 38.7 %collective-permute-start.27 = (f32[144,2304]{1,0:T(8,128)}, f32[144,2304]{1,0:T(8,128)S(1)}, u32[]{:S(2)}, u32[]{:S(2)}) collective-permute-start(f32[144,2304]{1,0:T(8,128)} %get-tuple-element.429), channel_id=1, source_target_pairs={{0,2},{1,3},{2,0},{3,1},{4,6},{5,7},{6,4},{7,5},{8,10},{9,11},{10,... | collective-permute-start | bytes 3981320 | tf_op jit(solution)/shard_map/ppermute | solution.py:1030
  426.9 38.6 %collective-permute-start.25 = (f32[144,768]{1,0:T(8,128)}, f32[144,768]{1,0:T(8,128)S(1)}, u32[]{:S(2)}, u32[]{:S(2)}) collective-permute-start(f32[144,768]{1,0:T(8,128)} %get-tuple-element.427), channel_id=1, source_target_pairs={{0,8},{1,9},{2,10},{3,11},{4,12},{5,13},{6,14},{7,15},{8,0},{9,1},... | collective-permute-start | bytes 1327112 | tf_op jit(solution)/shard_map/ppermute | solution.py:1030
  429.4 36.1 %collective-permute-start.26 = (f32[144,384]{1,0:T(8,128)}, f32[144,384]{1,0:T(8,128)S(1)}, u32[]{:S(2)}, u32[]{:S(2)}) collective-permute-start(f32[144,384]{1,0:T(8,128)} %get-tuple-element.428), channel_id=1, source_target_pairs={{0,8},{1,9},{2,10},{3,11},{4,12},{5,13},{6,14},{7,15},{8,0},{9,1},... | collective-permute-start | bytes 663560 | tf_op jit(solution)/shard_map/ppermute | solution.py:1030
  429.8 35.7 %collective-permute-start.29 = (f32[4,10368]{1,0:T(4,128)S(1)}, f32[4,10368]{1,0:T(4,128)S(1)}, u32[]{:S(2)}, u32[]{:S(2)}) collective-permute-start(f32[4,10368]{1,0:T(4,128)S(1)} %copy-done.20), channel_id=1, source_target_pairs={{0,8},{1,9},{2,10},{3,11},{4,12},{5,13},{6,14},{7,15},{8,0},{9,1},... | collective-permute-start | bytes 497672 | tf_op jit(solution)/shard_map/ppermute | solution.py:1037
  465.5 10.3 %copy-start.27 = (f32[144,384]{1,0:T(8,128)}, f32[144,384]{1,0:T(8,128)S(1)}, u32[]{:S(2)}) copy-start(f32[144,384]{1,0:T(8,128)S(1)} %collective-permute-done.26.refs_24_) | copy-start | bytes 663556
  465.5 10.3 %copy-start.21 = (f32[144,768]{1,0:T(8,128)}, f32[144,768]{1,0:T(8,128)S(1)}, u32[]{:S(2)}) copy-start(f32[144,768]{1,0:T(8,128)S(1)} %collective-permute-done.25.refs_19_) | copy-start | bytes 1327108
  465.5 5.9 %copy-start.7 = (f32[144,2304]{1,0:T(8,128)}, f32[144,2304]{1,0:T(8,128)S(1)}, u32[]{:S(2)}) copy-start(f32[144,2304]{1,0:T(8,128)S(1)} %collective-permute-done.27.refs_2_) | copy-start | bytes 3981316
  475.8 24.7 %collective-permute-start.31 = (f32[144,2304]{1,0:T(8,128)}, f32[144,2304]{1,0:T(8,128)S(1)}, u32[]{:S(2)}, u32[]{:S(2)}) collective-permute-start(f32[144,2304]{1,0:T(8,128)} %get-tuple-element.448), channel_id=1, source_target_pairs={{0,2},{1,3},{2,0},{3,1},{4,6},{5,7},{6,4},{7,5},{8,10},{9,11},{10,... | collective-permute-start | bytes 3981320 | tf_op jit(solution)/shard_map/ppermute | solution.py:1030
  476.6 23.9 %collective-permute-start.30 = (f32[72,2304]{1,0:T(8,128)}, f32[72,2304]{1,0:T(8,128)S(1)}, u32[]{:S(2)}, u32[]{:S(2)}) collective-permute-start(f32[72,2304]{1,0:T(8,128)} %get-tuple-element.447), channel_id=1, source_target_pairs={{0,4},{1,5},{2,6},{3,7},{4,0},{5,1},{6,2},{7,3},{8,12},{9,13},{10,... | collective-permute-start | bytes 1990664 | tf_op jit(solution)/shard_map/ppermute | solution.py:1030
  477.5 23.0 %collective-permute-start.32 = (f32[8,10368]{1,0:T(8,128)S(1)}, f32[8,10368]{1,0:T(8,128)S(1)}, u32[]{:S(2)}, u32[]{:S(2)}) collective-permute-start(f32[8,10368]{1,0:T(8,128)S(1)} %pad_maximum_fusion.2), channel_id=1, source_target_pairs={{0,4},{1,5},{2,6},{3,7},{4,0},{5,1},{6,2},{7,3},{8,12},{9,13},{10,... | collective-permute-start | bytes 995336 | tf_op jit(solution)/shard_map/ppermute | solution.py:1037
  505.9 23.8 %collective-permute-start.34 = (f32[72,2304]{1,0:T(8,128)}, f32[72,2304]{1,0:T(8,128)S(1)}, u32[]{:S(2)}, u32[]{:S(2)}) collective-permute-start(f32[72,2304]{1,0:T(8,128)} %get-tuple-element.460), channel_id=1, source_target_pairs={{0,4},{1,5},{2,6},{3,7},{4,0},{5,1},{6,2},{7,3},{8,12},{9,13},{10,... | collective-permute-start | bytes 1990664 | tf_op jit(solution)/shard_map/ppermute | solution.py:1030
  506.3 23.4 %collective-permute-start.35 = (f32[16,10368]{1,0:T(8,128)S(1)}, f32[16,10368]{1,0:T(8,128)S(1)}, u32[]{:S(2)}, u32[]{:S(2)}) collective-permute-start(f32[16,10368]{1,0:T(8,128)S(1)} %pad_maximum_fusion.1), channel_id=1, source_target_pairs={{0,2},{1,3},{2,0},{3,1},{4,6},{5,7},{6,4},{7,5},{8,10},{9,11},{10,... | collective-permute-start | bytes 1990664 | tf_op jit(solution)/shard_map/ppermute | solution.py:1037
  507.1 20.5 %collective-permute-start.33 = (f32[36,2304]{1,0:T(8,128)}, f32[36,2304]{1,0:T(8,128)S(1)}, u32[]{:S(2)}, u32[]{:S(2)}) collective-permute-start(f32[36,2304]{1,0:T(8,128)} %get-tuple-element.459), channel_id=1, source_target_pairs={{0,8},{1,9},{2,10},{3,11},{4,12},{5,13},{6,14},{7,15},{8,0},{9,1},... | collective-permute-start | bytes 995336 | tf_op jit(solution)/shard_map/ppermute | solution.py:1030
  527.6 28.3 %copy-start.22 = (f32[36,2304]{1,0:T(8,128)}, f32[36,2304]{1,0:T(8,128)S(1)}, u32[]{:S(2)}) copy-start(f32[36,2304]{1,0:T(8,128)S(1)} %collective-permute-done.33.refs_4_) | copy-start | bytes 995332
  533.8 19.6 %copy-start.31 = (s32[64]{0:T(128)S(1)}, s32[64]{0:T(128)}, u32[]{:S(2)}) copy-start(s32[64]{0:T(128)} %param.23) | copy-start | bytes 772
  533.9 25.7 %copy-start.4 = (f32[32,10368]{1,0:T(8,128)}, f32[32,10368]{1,0:T(8,128)S(1)}, u32[]{:S(2)}) copy-start(f32[32,10368]{1,0:T(8,128)S(1)} %pad_maximum_fusion.refs_0_.refs_4_.refs_8_) | copy-start | bytes 3981316
  533.9 19.0 %collective-permute-start.37 = (f32[32,10368]{1,0:T(8,128)S(1)}, f32[32,10368]{1,0:T(8,128)}, u32[]{:S(2)}, u32[]{:S(2)}) collective-permute-start(f32[32,10368]{1,0:T(8,128)S(1)} %pad_maximum_fusion.refs_0_.refs_4_.refs_8_), channel_id=1, source_target_pairs={{0,1},{1,0},{2,3},{3,2},{4,5},{5,4},{6,7},{7,6},{8,9},{9,8},{10,11... | collective-permute-start | bytes 3981320 | tf_op jit(solution)/shard_map/ppermute | solution.py:1037
  534.8 18.1 %collective-permute-start.36 = (f32[36,2304]{1,0:T(8,128)S(1)}, f32[36,2304]{1,0:T(8,128)S(1)}, u32[]{:S(2)}, u32[]{:S(2)}) collective-permute-start(f32[36,2304]{1,0:T(8,128)S(1)} %copy-done.24), channel_id=1, source_target_pairs={{0,8},{1,9},{2,10},{3,11},{4,12},{5,13},{6,14},{7,15},{8,0},{9,1},... | collective-permute-start | bytes 995336 | tf_op jit(solution)/shard_map/ppermute | solution.py:1030
  553.0 6.7 %collective-permute-start.38 = (f32[32,10368]{1,0:T(8,128)S(1)}, f32[32,10368]{1,0:T(8,128)}, u32[]{:S(2)}, u32[]{:S(2)}) collective-permute-start(f32[32,10368]{1,0:T(8,128)S(1)} %pad_maximum_fusion.refs_0_.refs_4_.refs_8_), channel_id=1, source_target_pairs={{0,16},{16,0},{1,17},{17,1},{2,18},{18,2},{3,19},{19,3},{4,20},{20... | collective-permute-start | bytes 3981320 | tf_op jit(solution)/shard_map/ppermute | solution.py:1039
  553.0 6.7 %collective-permute-start.39 = (f32[32,10368]{1,0:T(8,128)}, f32[32,10368]{1,0:T(8,128)}, u32[]{:S(2)}, u32[]{:S(2)}) collective-permute-start(f32[32,10368]{1,0:T(8,128)} %collective-permute-done.37.refs_1_.refs_5_.refs_9_), channel_id=1, source_target_pairs={{0,16},{16,0},{1,17},{17,1},{2,18},{18,2},{3,19},{19,3},{4,20},{20... | collective-permute-start | bytes 3981320 | tf_op jit(solution)/shard_map/ppermute | solution.py:1039
  559.6 23.8 %copy-start.1 = (bf16[1001,1152]{1,0:T(8,128)(2,1)S(1)}, bf16[1001,1152]{1,0:T(8,128)(2,1)}, u32[]{:S(2)}) copy-start(bf16[1001,1152]{1,0:T(8,128)(2,1)} %param.26) | copy-start | bytes 6918916
  (9 other events, 11.2 us)

commit v5 on v4

--- a/solution.py
+++ b/solution.py
@@ -63,7 +63,7 @@
             normal, _ = normed(x_ref[rows].astype(F32))
             h_ref[rows] = (normal * (1.0 + mod_ref[tile, 1:2]) + mod_ref[tile, 0:1]).astype(BF16)
 
-    out_ref[...] = (dot(w_ref[...], h_ref[...], TT) + b_ref[...]).astype(BF16)
+    out_ref[...] = (dot(w_ref[...], h_ref[...], TT) + b_ref[...].T).astype(BF16)
 
 
 def qkv_call(x, mod, w, bias):
@@ -80,7 +80,7 @@
             pl.BlockSpec((tokens, width), lambda j: (0, 0)),
             pl.BlockSpec(mod.shape, lambda j: (0, 0, 0)),
             pl.BlockSpec((width, block), lambda j: (0, j)),
-            pl.BlockSpec((block, 1), lambda j: (j, 0)),
+            pl.BlockSpec((1, block), lambda j: (0, j)),
         ],
         out_specs=[
             pl.BlockSpec((tokens, width), lambda j: (0, 0)),
@@ -340,24 +340,26 @@
     )(h, away, dm, w1, b1, w2, *before)
 
 
-def shard_rows(spot_ref, g_ref, grad, put):
+def shard_rows(spot_ref, g_ref, grad, made_ref):
     shards = spot_ref.shape[1]
     rows = g_ref.shape[1] // 2
     shard = g_ref.shape[1] // shards
     part = pl.program_id(0)
-    place = 0
     for piece in range(2):
         made = dot(g_ref[:, piece * rows : (piece + 1) * rows], grad, TN)
-        for at in range(0, rows, shard):
-            put(spot_ref[part, place], made[at : at + shard])
-            place += 1
-
-
-def rows_send_body(side_ref, spot_ref, g_ref, dm_ref, out_ref):
-    def put(spot, value):
-        out_ref[spot] = value
-
-    shard_rows(spot_ref, g_ref, dm_ref[...], put)
+        for number in range(shards // 2):
+            made_ref[piece * (shards // 2) + number] = made[number * shard : (number + 1) * shard]
+
+    def rows_of(place):
+        return made_ref[spot_ref[part, place]]
+
+    return rows_of
+
+
+def rows_send_body(side_ref, spot_ref, g_ref, dm_ref, out_ref, made_ref):
+    rows_of = shard_rows(spot_ref, g_ref, dm_ref[...], made_ref)
+    for place in range(out_ref.shape[0]):
+        out_ref[place] = rows_of(place)
 
 
 def rows_send_call(side, spots, g, dm):
@@ -378,30 +380,24 @@
                 pl.BlockSpec((tokens, COLUMNS), lambda j, side, spots: (0, j)),
             ],
             out_specs=pl.BlockSpec((shards, half // shards, COLUMNS), lambda j, side, spots: (0, 0, j)),
+            scratch_shapes=[pltpu.VMEM((shards, half // shards, COLUMNS), F32)],
         ),
         out_shape=shaped((shards, half // shards, width), F32),
     )(side, spots, g, dm)
 
 
 def rows_keep_body(side_ref, spot_ref, g_ref, dm_ref, got_ref, *outs, bounds):
+    *outs, made_ref = outs
     half = spot_ref.shape[1] // 2
     step = pl.program_id(0)
+    rows_of = shard_rows(spot_ref, g_ref, dm_ref[...], made_ref)
     for part in range(len(bounds) - 1):
 
         @pl.when((step >= bounds[part]) & (step < bounds[part + 1]))
         def _():
-            def put(spot, value):
-                value = value + got_ref[spot]
-
-                @pl.when(spot < half)
-                def _():
-                    outs[2 * part + 1][jnp.minimum(spot, half - 1)] = value
-
-                @pl.when(spot >= half)
-                def _():
-                    outs[2 * part][jnp.maximum(spot - half, 0)] = value
-
-            shard_rows(spot_ref, g_ref, dm_ref[...], put)
+            for place in range(half):
+                outs[2 * part + 1][place] = rows_of(place) + got_ref[place]
+                outs[2 * part][place] = rows_of(half + place) + got_ref[half + place]
 
 
 def rows_keep_call(side, spots, g, dm, got, counts):
@@ -438,6 +434,7 @@
                 pl.BlockSpec((shards, half // shards, COLUMNS), lambda j, side, spots: (0, 0, j)),
             ],
             out_specs=specs,
+            scratch_shapes=[pltpu.VMEM((shards, half // shards, COLUMNS), F32)],
         ),
         out_shape=shapes,
     )(side, spots, g, dm, got)
@@ -662,35 +659,29 @@
     return [tuple(made)] if both else made
 
 
-def moved_body(om_ref, h_ref, away_ref, own_ref, *out_refs):
-    om, hidden = om_ref[...], h_ref[...]
-    out_refs[0][...] = dot(om, away_ref[...], TN).astype(BF16)
-    out_refs[1][...] = dot(om, own_ref[...], TN).astype(BF16)
-    out_refs[2][...] = dot(hidden, away_ref[...]).astype(BF16)
-    out_refs[3][...] = dot(hidden, own_ref[...]).astype(BF16)
-
-
-def moved_call(om, hidden, away, own):
-    tokens, width = hidden.shape
-    half = width // 2
+def moved_body(left_ref, away_ref, own_ref, left_away_ref, left_own_ref, *, dims):
+    left = left_ref[...]
+    left_away_ref[...] = dot(left, away_ref[...], dims).astype(BF16)
+    left_own_ref[...] = dot(left, own_ref[...], dims).astype(BF16)
+
+
+def moved_call(left, away, own, turned):
+    width, half = away.shape
+    tokens = left.shape[1] if turned else left.shape[0]
     block = tokens // 2
     fixed = pl.BlockSpec((width, half), lambda i: (0, 0))
     out = pl.BlockSpec((block, half), lambda i: (i, 0))
-    return call(
-        moved_body,
+    side = pl.BlockSpec((width, block), lambda i: (0, i)) if turned else pl.BlockSpec((block, width), lambda i: (i, 0))
+    return call(
+        functools.partial(moved_body, dims=TN if turned else NN),
         "moved",
-        4 * tokens * width * width,
-        8 * tokens * width + 2 * width * width,
+        2 * tokens * width * width,
+        4 * tokens * width + 2 * width * width,
         grid=(2,),
-        in_specs=[
-            pl.BlockSpec((width, block), lambda i: (0, i)),
-            pl.BlockSpec((block, width), lambda i: (i, 0)),
-            fixed,
-            fixed,
-        ],
-        out_specs=[out] * 4,
-        out_shape=[shaped((tokens, half), BF16)] * 4,
-    )(om, hidden, away, own)
+        in_specs=[side, fixed, fixed],
+        out_specs=[out] * 2,
+        out_shape=[shaped((tokens, half), BF16)] * 2,
+    )(left, away, own)
 
 
 def first_back_body(low_ref, high_ref, w_ref, x_ref, mod_ref, dx_ref, out_ref, sum_ref):
@@ -870,9 +861,7 @@
 
 
 def add_call(jobs):
-    steps = 3 if all(terms[0].shape[1] % 384 == 0 for terms, _, _ in jobs) else 2
-    if any(terms[0].shape[1] % (128 * steps) for terms, _, _ in jobs):
-        steps = 1
+    steps = 1
     operands, specs, outs, shapes, plans = [], [], [], [], []
     moved = 0
     for terms, first, rows in jobs:
@@ -1110,12 +1099,12 @@
         return (jnp.arange(width, dtype=jnp.int32)[:, None] == source[None, :]).astype(BF16)
 
     def spots(side):
-        return jnp.stack([places_of(bits, side, lead, jnp.arange(batch, dtype=jnp.int32) ^ index) for steps, lead in ROW_PARTS for _ in range(steps)])
+        return jnp.stack([index ^ offsets_of(bits, side, lead) for steps, lead in ROW_PARTS for _ in range(steps)])
 
     other = 1 - stream
     away, own = picked(other), picked(stream)
 
-    bias_full = jnp.concatenate([b_qv[:width], jnp.zeros((width,), F32), b_qv[width:]])[:, None]
+    bias_full = jnp.concatenate([b_qv[:width], jnp.zeros((width,), F32), b_qv[width:]])[None]
     h1, qkv = qkv_call(x, mod, w_qkv, bias_full)
     probs, mixed, om = attention_call(flag, qkv, head_columns, heads)
     a, x1, h2, h2_away, h2_own, dm, sum_dm = middle_call(om, w_proj, b_proj[None], x, mod, top, keep, away, own)
@@ -1146,8 +1135,9 @@
         [0] * len(ROW_PARTS),
         [lead for _, lead in ROW_PARTS],
     )
-    om_away, om_own, h1_away, h1_own = moved_call(om, h1, away, own)
-    df, x1, om_away, om_own, h1_away, h1_own = flow.round((df, x1, om_away, om_own, h1_away, h1_own))
+    om_away, om_own = moved_call(om, away, own, True)
+    df, x1, om_away, om_own, h1 = flow.round((df, x1, om_away, om_own, h1))
+    h1_away, h1_own = moved_call(h1, away, own, False)
     dx1, da, do, sums_two = middle_back_call(df, w_fc1, x1, mod, top, a, w_proj)
 
     me = stream * batch + index
@@ -1160,7 +1150,7 @@
         return jnp.where(side == 0, jnp.take(labels.reshape(batch, items), from_device, axis=0).reshape(-1), null_class)
 
     used_rows = jnp.concatenate([used_labels(stream), used_labels(other)])[:, None]
-    dx1, da, do, sums_two, g = flow.round((dx1, da, do, sums_two, g))
+    dx1, da, do, sums_two, g, h1_away, h1_own = flow.round((dx1, da, do, sums_two, g, h1_away, h1_own))
     half = width // 2
     low = attention_back_call(flag, qkv, do, head_columns, probs, mixed, 0)
     rights = [Plain(da, 0, COLUMNS, width // COLUMNS), Wide((low, 0, COLUMNS))]

time: 588 us -> 582 us (0.990)
    pallas_call x1 -> x2, Pallas kernels: 11.9 us -> 14.7 us  [moved_call(): call(functools.partial(moved_body, dims=TN if turned else NN), 'moved', 2...]
  transfers between devices with their start and end apart: 40 -> 40, of which waited for: 15 -> 14; matrix products, arithmetic and copies ran while one was open for 1% -> 1% of each run, Pallas kernels for 31% -> 32%
where the time goes in v5:
time: 582 us; the launch traced here: 577 us
  Pallas kernels  365 us (63%)
  waiting for transfers between devices  117 us (20%)
  starting transfers between devices  55.9 us (10%)
  local copies, waits for them, and re-layouts  20 us (3%)
  matrix products  7.72 us (1%)
  other arithmetic  7.6 us (1%)
    ppermute x28, waiting for transfers between devices, round(): lax.ppermute(send, ('stream', 'batch'), self.pairs(chunk.stage, chunk.lead))  67.3 us
    ppermute x28, starting transfers between devices, round(): lax.ppermute(send, ('stream', 'batch'), self.pairs(chunk.stage, chunk.lead))  51.5 us
    ppermute x4, waiting for transfers between devices, round(): lax.ppermute(piece, ('stream', 'batch'), pairs)  50.1 us
    pallas_call x3, Pallas kernels, hidden_call(): call(hidden_body, 'hidden', 6 * tokens * width * count, 6 * tokens * widt...  46.4 us
    pallas_call x5, Pallas kernels, columns_call(): call(functools.partial(columns_body, right=right, both=both), name, 2 * t...  38.3 us
    pallas_call x9, Pallas kernels, add_call(): call(functools.partial(add_body, plans=plans), 'add', moved // 4, moved,...  32 us
    pallas_call x1, Pallas kernels, middle_back_call(): call(middle_back_body, 'middle_back', 2 * tokens * width * (hidden + widt...  30.2 us
    pallas_call x2, Pallas kernels, attention_back_call(): call(attention_back_body, 'attention_back', 2 * 2 * heads * tokens * GROU...  27.6 us
  transfers between devices with their start and end apart: 40, of which 14 were waited for; matrix products, arithmetic and copies ran while one was open for 1% of the time, Pallas kernels for 32%

profile of v5, /device:TPU:0, one launch (start us, length us, event | category | flops | bytes accessed | tf_op | source)
XLA Modules:
  0.0 576.8 jit_solution(16978298679028998359)
XLA Ops:
  5.0 7.7 %convolution_add_fusion = f32[4,6912]{1,0:T(4,128)S(1)} fusion(bf16[1152,6912]{1,0:T(8,128)(2,1)} %refs_13_.1, f32[6912]{0:T(1024)} %param.28, f32[4,1152]{1,0:T(4,128)S(1)} %maximum_add_fusion.cond_ref), kind=kOutput, calls=%fused_computation.3 | convolution fusion | flops 63751680 | bytes 16081920 | tf_op jit(solution)/shard_map/dot_general | solution.py:28
  18.2 1.7 fusion.away_ref
  20.0 1.7 fusion.1.own_ref
  24.0 15.9 %qkv.1 = (bf16[1024,1152]{1,0:T(8,128)(2,1)}, bf16[3456,1024]{1,0:T(8,128)(2,1)}) custom-call(bf16[1024,1152]{1,0:T(8,128)(2,1)} %bitcast.41, f32[4,6,1152]{2,1,0:T(8,128)} %reshape.311.mod_ref, bf16[1152,3456]{1,0:T(8,128)(2,1)} %w_ref.7, f32[1,3456]{1,0:T(1,128)} %broadcast_in_dim.132.b_ref), custom_call_target="tpu_custom_call" | custom-call | flops 1019215872 | bytes 2469888 | tf_op jit(solution)/shard_map/qkv/pallas_call | solution.py:73
  39.9 26.4 %attention.1 = (bf16[16,1024,1024]{2,1,0:T(8,128)(2,1)}, f32[16,72,1024]{2,1,0:T(8,128)}, bf16[1152,1024]{1,0:T(8,128)(2,1)}) custom-call(s32[1]{0:T(128)} %bitcast.1.flag_ref, bf16[3456,1024]{1,0:T(8,128)(2,1)} %get-tuple-element.253.q_ref.k_ref.v_ref, bf16[3456,1024]{1,0:T(8,128)(2,1)} %get-tuple-element.253.q_ref.k_ref.v_ref, ...), custom_call_target="tpu_custom_call" | custom-call | flops 2147483648 | bytes 5963776 | tf_op jit(solution)/shard_map/attention/pallas_call | solution.py:139
  66.3 15.1 %middle.1 = (f32[1024,1152]{1,0:T(8,128)}, f32[1024,1152]{1,0:T(8,128)}, bf16[1024,1152]{1,0:T(8,128)(2,1)}, bf16[1024,576]{1,0:T(8,128)(2,1)}, bf16[1024,576]{1...) custom-call(bf16[1152,1024]{1,0:T(8,128)(2,1)} %get-tuple-element.254.om_ref.left_ref, ...), custom_call_target="tpu_custom_call" | custom-call | flops 679477248 | bytes 3833856 | tf_op jit(solution)/shard_map/middle/pallas_call | solution.py:259
  81.4 12.0 %hidden.3 = (bf16[1024,4608]{1,0:T(8,128)(2,1)}, bf16[1024,4608]{1,0:T(8,128)(2,1)}, f32[1,4608]{1,0:T(1,128)}, f32[576,1024]{1,0:T(8,128)}) custom-call(bf16[1024,1152]{1,0:T(8,128)(2,1)} %get-tuple-element.282.h_ref, bf16[1024,576]{1,0:T(8,128)(2,1)} %get-tuple-element.256.away_ref, bf16[1024,1152]{1,0:T(8,128)(2,1)} %get-tuple-element.257.dm_ref, ...), custom_call_target="tpu_custom_call" | custom-call | flops 905969664 | bytes 2588672 | tf_op jit(solution)/shard_map/hidden/pallas_call | solution.py:312
  93.8 15.3 %hidden.4 = (bf16[1024,4608]{1,0:T(8,128)(2,1)}, bf16[1024,4608]{1,0:T(8,128)(2,1)}, f32[1,4608]{1,0:T(1,128)}, f32[576,1536]{1,0:T(8,128)}) custom-call(bf16[1024,1152]{1,0:T(8,128)(2,1)} %get-tuple-element.282.h_ref, bf16[1024,576]{1,0:T(8,128)(2,1)} %get-tuple-element.256.away_ref, ...), custom_call_target="tpu_custom_call", output_to_operand_aliasing={{0}: (6, {}), {1}: (7, {}), {2}: (8, {})} | custom-call | flops 1358954496 | bytes 3440640 | tf_op jit(solution)/shard_map/hidden/pallas_call | solution.py:312
  109.2 4.7 hidden_keep.3
  114.0 9.3 %collective-permute-start.2 = (f32[288,1024]{1,0:T(8,128)}, f32[288,1024]{1,0:T(8,128)S(1)}, u32[]{:S(2)}, u32[]{:S(2)}) collective-permute-start(f32[288,1024]{1,0:T(8,128)} %get-tuple-element.290), channel_id=1, source_target_pairs={{0,1},{1,0},{2,3},{3,2},{4,5},{5,4},{6,7},{7,6},{8,9},{9,8},{10,11... | collective-permute-start | bytes 3538952 | tf_op jit(solution)/shard_map/ppermute | solution.py:1019
  123.3 19.0 %hidden.5 = (bf16[1024,4608]{1,0:T(8,128)(2,1)}, bf16[1024,4608]{1,0:T(8,128)(2,1)}, f32[1,4608]{1,0:T(1,128)}, f32[576,2048]{1,0:T(8,128)}) custom-call(bf16[1024,1152]{1,0:T(8,128)(2,1)} %get-tuple-element.282.h_ref, bf16[1024,576]{1,0:T(8,128)(2,1)} %get-tuple-element.256.away_ref, ...), custom_call_target="tpu_custom_call", output_to_operand_aliasing={{0}: (6, {}), {1}: (7, {}), {2}: (8, {})} | custom-call | flops 1811939328 | bytes 4292608 | tf_op jit(solution)/shard_map/hidden/pallas_call | solution.py:312
  142.3 7.4 %hidden_keep.4 = (f32[288,1536]{1,0:T(8,128)}, f32[288,1536]{1,0:T(8,128)}) custom-call(bf16[1024,576]{1,0:T(8,128)(2,1)} %get-tuple-element.279.refs_0_, bf16[1024,4608]{1,0:T(8,128)(2,1)} %get-tuple-element.320.refs_1_.df_ref, f32[576,1536]{1,0:T(8,128)} %collective-permute-done.1.refs_2_), custom_call_target="tpu_custom_call" | custom-call | flops 226492416 | bytes 1425408 | tf_op jit(solution)/shard_map/hidden_keep/pallas_call | solution.py:607
  149.7 2.1 add.272
  153.9 7.4 %moved.2 = (bf16[1024,576]{1,0:T(8,128)(2,1)}, bf16[1024,576]{1,0:T(8,128)(2,1)}) custom-call(bf16[1152,1024]{1,0:T(8,128)(2,1)} %get-tuple-element.254.om_ref.left_ref, bf16[1152,576]{1,0:T(8,128)(2,1)} %fusion.away_ref, bf16[1152,576]{1,0:T(8,128)(2,1)} %fusion.1.own_ref), custom_call_target="tpu_custom_call" | custom-call | flops 339738624 | bytes 921600 | tf_op jit(solution)/shard_map/moved/pallas_call | solution.py:675
  161.9 14.3 %rows_send.1 = f32[16,144,1152]{2,1,0:T(8,128)} custom-call(s32[1]{0:T(128)} %bitcast.6.side_ref, s32[3,16]{1,0:T(4,128)} %pad_add_fusion.spot_ref, bf16[1024,4608]{1,0:T(8,128)(2,1)} %get-tuple-element.358.g_ref, bf16[1024,1152]{1,0:T(8,128)(2,1)} %get-tuple-element.257.dm_ref), custom_call_target="tpu_custom_call" | custom-call | flops 679477248 | bytes 2211840 | tf_op jit(solution)/shard_map/rows_send/pallas_call | solution.py:370
  176.2 4.7 collective-permute-done.5.refs_4_.refs_5_.refs_1_.refs_6_
  180.9 8.4 %hidden_keep.5 = (f32[288,2048]{1,0:T(8,128)}, f32[288,2048]{1,0:T(8,128)}) custom-call(bf16[1024,576]{1,0:T(8,128)(2,1)} %get-tuple-element.279.refs_0_, bf16[1024,4608]{1,0:T(8,128)(2,1)} %get-tuple-element.320.refs_1_.df_ref, f32[576,2048]{1,0:T(8,128)} %collective-permute-done.3.refs_2_), custom_call_target="tpu_custom_call" | custom-call | flops 301989888 | bytes 1851392 | tf_op jit(solution)/shard_map/hidden_keep/pallas_call | solution.py:607
  189.3 2.8 add.273
  194.2 1.6 collective-permute-start.7
  196.4 7.3 %moved.3 = (bf16[1024,576]{1,0:T(8,128)(2,1)}, bf16[1024,576]{1,0:T(8,128)(2,1)}) custom-call(bf16[1024,1152]{1,0:T(8,128)(2,1)} %get-tuple-element.327.left_ref, bf16[1152,576]{1,0:T(8,128)(2,1)} %fusion.away_ref, bf16[1152,576]{1,0:T(8,128)(2,1)} %fusion.1.own_ref), custom_call_target="tpu_custom_call" | custom-call | flops 339738624 | bytes 921600 | tf_op jit(solution)/shard_map/moved/pallas_call | solution.py:675
  203.7 30.2 %middle_back.1 = (f32[1024,1152]{1,0:T(8,128)}, bf16[1024,1152]{1,0:T(8,128)(2,1)}, bf16[1152,1024]{1,0:T(8,128)(2,1)}, f32[4,4,1152]{2,1,0:T(4,128)}) custom-call(bf16[1024,4608]{1,0:T(8,128)(2,1)} %get-tuple-element.320.refs_1_.df_ref, bf16[1152,4608]{1,0:T(8,128)(2,1)} %w1_ref.7, f32[1024,1152]{1,0:T(8,128)} %get-tuple-element.321.x1_ref, ...), custom_call_target="tpu_custom_call" | custom-call | flops 1698693120 | bytes 5160960 | tf_op jit(solution)/shard_map/middle_back/pallas_call | solution.py:501
  233.9 17.0 %rows_keep.1 = (f32[8,144,768]{2,1,0:T(8,128)}, f32[8,144,768]{2,1,0:T(8,128)}, f32[8,144,384]{2,1,0:T(8,128)}, f32[8,144,384]{2,1,0:T(8,128)}) custom-call(s32[1]{0:T(128)} %bitcast.8.side_ref, s32[3,16]{1,0:T(4,128)} %pad_add_fusion.1.spot_ref, bf16[1024,4608]{1,0:T(8,128)(2,1)} %get-tuple-element.358.g_ref, bf16[1024,1152]{1,0:T(8,128)(2,1)} %get-tuple-element.257.dm_ref, ...), custom_call_target="tpu_custom_call" | custom-call | flops 679477248 | bytes 3538944 | tf_op jit(solution)/shard_map/rows_keep/pallas_call | solution.py:423
  250.9 3.7 add.274
  257.1 1.6 collective-permute-start.11
  259.3 2.2 collective-permute-start.10
  261.5 13.8 %attention_back.2.refs_3_.refs_1_.low_ref = bf16[3,576,1024]{2,1,0:T(8,128)(2,1)} custom-call(s32[1]{0:T(128)} %bitcast.1.flag_ref, bf16[3456,1024]{1,0:T(8,128)(2,1)} %get-tuple-element.253.q_ref.k_ref.v_ref, bf16[3456,1024]{1,0:T(8,128)(2,1)} %get-tuple-element.253.q_ref.k_ref.v_ref, bf16[3456,1024]{1,0:T(8,128)(2,1)} %get-tuple-element.253.q_ref.k_ref.v_ref, ...), custom_call_target="tpu_custom_call" | custom-call | flops 2147483648 | bytes 3866624 | tf_op jit(solution)/shard_map/attention_back/pallas_call | solution.py:212
  275.3 9.8 %first_send.1 = (f32[576,2304]{1,0:T(8,128)}, f32[1,2304]{1,0:T(1,128)}) custom-call(bf16[1024,576]{1,0:T(8,128)(2,1)} %get-tuple-element.354.refs_0_, bf16[1024,1152]{1,0:T(8,128)(2,1)} %get-tuple-element.355.refs_1_, bf16[1024,576]{1,0:T(8,128)(2,1)} %get-tuple-element.356.refs_2_.refs_0_, bf16[3,576,1024]{2,1,0:T(8,128)(2,1)} %attention_back.2.refs_3_.refs_1_.low_ref), custom_call_target="tpu_custom_call" | custom-call | flops 339738624 | bytes 2064384 | tf_op jit(solution)/shard_map/first_send/pallas_call | solution.py:647
  285.1 19.7 %result.1 = (bf16[1024,1152]{1,0:T(8,128)(2,1)}, f32[4,1,1152]{2,1,0:T(1,128)}) custom-call(bf16[1024,4608]{1,0:T(8,128)(2,1)} %get-tuple-element.358.g_ref, bf16[4608,1152]{1,0:T(8,128)(2,1)} %w_ref.6, f32[1,1152]{1,0:T(1,128)} %broadcast_in_dim.141.b_ref, f32[1024,1152]{1,0:T(8,128)} %get-tuple-element.321.x1_ref, f32[4,6,1152]{2,1,0:T(8,128)} %reshape.311.mod_ref, ...), custom_call_target="tpu_custom_call" | custom-call | flops 1358954496 | bytes 3686400 | tf_op jit(solution)/shard_map/result/pallas_call | solution.py:457
  304.8 2.3 collective-permute-done.10.refs_4_
  307.1 1.9 collective-permute-done.11.refs_3_.refs_8_
  310.8 5.4 add.275
  316.2 5.6 collective-permute-start.18
  321.8 1.5 collective-permute-start.19
  324.0 13.8 %attention_back.3.refs_2_.high_ref = bf16[3,576,1024]{2,1,0:T(8,128)(2,1)} custom-call(s32[1]{0:T(128)} %bitcast.1.flag_ref, bf16[3456,1024]{1,0:T(8,128)(2,1)} %get-tuple-element.253.q_ref.k_ref.v_ref, bf16[3456,1024]{1,0:T(8,128)(2,1)} %get-tuple-element.253.q_ref.k_ref.v_ref, bf16[3456,1024]{1,0:T(8,128)(2,1)} %get-tuple-element.253.q_ref.k_ref.v_ref, ...), custom_call_target="tpu_custom_call" | custom-call | flops 2147483648 | bytes 3866624 | tf_op jit(solution)/shard_map/attention_back/pallas_call | solution.py:212
  337.8 8.2 %last_send.1 = (f32[576,2304]{1,0:T(8,128)}, f32[1,2304]{1,0:T(1,128)}) custom-call(bf16[1024,576]{1,0:T(8,128)(2,1)} %get-tuple-element.356.refs_2_.refs_0_, bf16[3,576,1024]{2,1,0:T(8,128)(2,1)} %attention_back.2.refs_3_.refs_1_.low_ref, bf16[3,576,1024]{2,1,0:T(8,128)(2,1)} %attention_back.3.refs_2_.high_ref), custom_call_target="tpu_custom_call" | custom-call | flops 339738624 | bytes 2064384 | tf_op jit(solution)/shard_map/last_send/pallas_call | solution.py:607
  346.1 5.9 %collective-permute-done.18.refs_6_.refs_2_.refs_17_ = f32[576,768]{1,0:T(8,128)S(1)} collective-permute-done((f32[576,768]{1,0:T(8,128)}, f32[576,768]{1,0:T(8,128)S(1)}, u32[]{:S(2)}, u32[]{:S(2)}) %collective-permute-start.18) | collective-permute-done | bytes 1769504 | tf_op jit(solution)/shard_map/ppermute | solution.py:1019
  352.0 11.0 %first_keep.1 = (f32[288,2304]{1,0:T(8,128)}, f32[288,2304]{1,0:T(8,128)}) custom-call(bf16[1024,576]{1,0:T(8,128)(2,1)} %get-tuple-element.401.refs_0_, bf16[1024,1152]{1,0:T(8,128)(2,1)} %get-tuple-element.355.refs_1_, bf16[1024,576]{1,0:T(8,128)(2,1)} %get-tuple-element.402.refs_2_.refs_0_, bf16[3,576,1024]{2,1,0:T(8,128)(2,1)} %attention_back.2.refs_3_.refs_1_.low_ref, ...), custom_call_target="tpu_custom_call" | custom-call | flops 339738624 | bytes 2064384 | tf_op jit(solution)/shard_map/first_keep/pallas_call | solution.py:647
  363.1 4.1 add.276
  367.2 5.2 collective-permute-start.24
  372.4 1.6 collective-permute-start.22
  375.8 18.2 %first_back.1 = (f32[1024,1152]{1,0:T(8,128)}, f32[4,2,1152]{2,1,0:T(2,128)}) custom-call(bf16[3,576,1024]{2,1,0:T(8,128)(2,1)} %attention_back.2.refs_3_.refs_1_.low_ref, bf16[3,576,1024]{2,1,0:T(8,128)(2,1)} %attention_back.3.refs_2_.high_ref, bf16[1152,3456]{1,0:T(8,128)(2,1)} %w_ref.7, bf16[1024,1152]{1,0:T(8,128)(2,1)} %bitcast.43, ...), custom_call_target="tpu_custom_call" | custom-call | flops 1019215872 | bytes 3354624 | tf_op jit(solution)/shard_map/first_back/pallas_call | solution.py:707
  394.0 1.8 payload.1
  395.8 4.8 collective-permute-done.21.refs_14_
  401.4 6.0 %collective-permute-done.24.refs_9_.refs_1_ = f32[288,2304]{1,0:T(8,128)} collective-permute-done((f32[288,2304]{1,0:T(8,128)}, f32[288,2304]{1,0:T(8,128)}, u32[]{:S(2)}, u32[]{:S(2)}) %collective-permute-start.24) | collective-permute-done | bytes 2654240 | tf_op jit(solution)/shard_map/ppermute | solution.py:1019
  407.4 9.7 %last_keep.1 = (f32[288,2304]{1,0:T(8,128)}, f32[288,2304]{1,0:T(8,128)}) custom-call(bf16[1024,576]{1,0:T(8,128)(2,1)} %get-tuple-element.402.refs_2_.refs_0_, bf16[3,576,1024]{2,1,0:T(8,128)(2,1)} %attention_back.2.refs_3_.refs_1_.low_ref, bf16[3,576,1024]{2,1,0:T(8,128)(2,1)} %attention_back.3.refs_2_.high_ref, f32[576,2304]{1,0:T(8,128)} %collective-permute-done.20.refs_3_), custom_call_target="tpu_custom_call" | custom-call | flops 339738624 | bytes 2064384 | tf_op jit(solution)/shard_map/last_keep/pallas_call | solution.py:607
  417.2 3.9 add.277
  421.1 2.0 collective-permute-start.28
  423.8 2.6 collective-permute-start.25
  426.8 2.6 collective-permute-start.29
  429.3 32.8 %collective-permute-done.29 = f32[4,10368]{1,0:T(4,128)S(1)} collective-permute-done((f32[4,10368]{1,0:T(4,128)S(1)}, f32[4,10368]{1,0:T(4,128)S(1)}, u32[]{:S(2)}, u32[]{:S(2)}) %collective-permute-start.29) | collective-permute-done | bytes 165920 | tf_op jit(solution)/shard_map/ppermute | solution.py:1026
  462.2 5.4 collective-permute-done.28.refs_4_.refs_5_.refs_1_.refs_6_
  467.7 3.7 add.278
  472.1 2.0 collective-permute-start.30
  474.1 5.0 assemble.2
  479.1 16.9 %collective-permute-done.32 = f32[8,10368]{1,0:T(8,128)S(1)} collective-permute-done((f32[8,10368]{1,0:T(8,128)S(1)}, f32[8,10368]{1,0:T(8,128)S(1)}, u32[]{:S(2)}, u32[]{:S(2)}) %collective-permute-start.32) | collective-permute-done | bytes 331808 | tf_op jit(solution)/shard_map/ppermute | solution.py:1026
  497.4 3.3 add.279
  500.7 1.6 collective-permute-start.34
  503.0 1.4 collective-permute-start.33
  504.4 18.9 %collective-permute-done.33.refs_4_ = f32[36,2304]{1,0:T(8,128)S(1)} collective-permute-done((f32[36,2304]{1,0:T(8,128)}, f32[36,2304]{1,0:T(8,128)S(1)}, u32[]{:S(2)}, u32[]{:S(2)}) %collective-permute-start.33) | collective-permute-done | bytes 331808 | tf_op jit(solution)/shard_map/ppermute | solution.py:1019
  525.4 3.0 add.280
  528.4 2.3 collective-permute-start.36
  530.7 15.3 %collective-permute-done.36.refs_9_ = f32[36,2304]{1,0:T(8,128)S(1)} collective-permute-done((f32[36,2304]{1,0:T(8,128)}, f32[36,2304]{1,0:T(8,128)S(1)}, u32[]{:S(2)}, u32[]{:S(2)}) %collective-permute-start.36) | collective-permute-done | bytes 331808 | tf_op jit(solution)/shard_map/ppermute | solution.py:1019
  549.3 3.7 assemble.3
  552.9 18.4 %modulation_back.1 = (f32[36,6912]{1,0:T(8,128)}, f32[1,6912]{1,0:T(1,128)}, f32[1001,1152]{1,0:T(8,128)}, f32[4,2304]{1,0:T(4,128)}) custom-call(s32[1]{0:T(128)} %bitcast.16.me_ref, f32[32,10368]{1,0:T(8,128)} %copy-done.4, f32[32,10368]{1,0:T(8,128)} %collective-permute-done.37.refs_1_.refs_5_.refs_9_, ...), custom_call_target="tpu_custom_call" | custom-call | flops 509607936 | bytes 1990656 | tf_op jit(solution)/shard_map/modulation_back/pallas_call | solution.py:818
  (183 shorter events, 39.5 us)
Async XLA Ops:
  5.0 8.8 %copy-start.29 = (f32[2304]{0:T(1024)S(1)}, f32[2304]{0:T(1024)}, u32[]{:S(2)}) copy-start(f32[2304]{0:T(1024)} %param.30) | copy-start | bytes 27652
  5.0 9.4 %copy-start.35 = (s32[4,16]{1,0:T(4,128)S(1)}, s32[4,16]{1,0:T(4,128)}, u32[]{:S(2)}) copy-start(s32[4,16]{1,0:T(4,128)} %param.24) | copy-start | bytes 772
  12.7 9.0 %copy-start.33 = (s32[1,1024]{1,0:T(1,128)S(1)}, s32[1,1024]{1,0:T(1,128)}, u32[]{:S(2)}) copy-start(s32[1,1024]{1,0:T(1,128)} %param.25) | copy-start | bytes 12292
  12.7 10.0 %copy-start.31 = (f32[1152]{0:T(1024)S(1)}, f32[1152]{0:T(1024)}, u32[]{:S(2)}) copy-start(f32[1152]{0:T(1024)} %param.32) | copy-start | bytes 13828
  12.8 10.6 %copy-start.30 = (f32[4608]{0:T(1024)S(1)}, f32[4608]{0:T(1024)}, u32[]{:S(2)}) copy-start(f32[4608]{0:T(1024)} %param.34) | copy-start | bytes 55300
  93.4 15.8 %collective-permute-start = (f32[576,1024]{1,0:T(8,128)}, f32[576,1024]{1,0:T(8,128)}, u32[]{:S(2)}, u32[]{:S(2)}) collective-permute-start(f32[576,1024]{1,0:T(8,128)} %get-tuple-element.273), channel_id=1, source_target_pairs={{0,16},{16,0},{1,17},{17,1},{2,18},{18,2},{3,19},{19,3},{4,20},{20... | collective-permute-start | bytes 7077896 | tf_op jit(solution)/shard_map/ppermute | solution.py:1021
  113.9 28.5 %collective-permute-start.1 = (f32[576,1536]{1,0:T(8,128)}, f32[576,1536]{1,0:T(8,128)}, u32[]{:S(2)}, u32[]{:S(2)}) collective-permute-start(f32[576,1536]{1,0:T(8,128)} %get-tuple-element.289), channel_id=1, source_target_pairs={{0,16},{16,0},{1,17},{17,1},{2,18},{18,2},{3,19},{19,3},{4,20},{20... | collective-permute-start | bytes 10616840 | tf_op jit(solution)/shard_map/ppermute | solution.py:1021
  114.0 28.4 %collective-permute-start.2 = (f32[288,1024]{1,0:T(8,128)}, f32[288,1024]{1,0:T(8,128)S(1)}, u32[]{:S(2)}, u32[]{:S(2)}) collective-permute-start(f32[288,1024]{1,0:T(8,128)} %get-tuple-element.290), channel_id=1, source_target_pairs={{0,1},{1,0},{2,3},{3,2},{4,5},{5,4},{6,7},{7,6},{8,9},{9,8},{10,11... | collective-permute-start | bytes 3538952 | tf_op jit(solution)/shard_map/ppermute | solution.py:1019
  151.8 29.1 %collective-permute-start.3 = (f32[576,2048]{1,0:T(8,128)}, f32[576,2048]{1,0:T(8,128)}, u32[]{:S(2)}, u32[]{:S(2)}) collective-permute-start(f32[576,2048]{1,0:T(8,128)} %get-tuple-element.304), channel_id=1, source_target_pairs={{0,16},{16,0},{1,17},{17,1},{2,18},{18,2},{3,19},{19,3},{4,20},{20... | collective-permute-start | bytes 14155784 | tf_op jit(solution)/shard_map/ppermute | solution.py:1021
  151.8 29.1 %collective-permute-start.5 = (f32[288,1536]{1,0:T(8,128)}, f32[288,1536]{1,0:T(8,128)S(1)}, u32[]{:S(2)}, u32[]{:S(2)}) collective-permute-start(f32[288,1536]{1,0:T(8,128)} %get-tuple-element.306), channel_id=1, source_target_pairs={{0,1},{1,0},{2,3},{3,2},{4,5},{5,4},{6,7},{7,6},{8,9},{9,8},{10,11... | collective-permute-start | bytes 5308424 | tf_op jit(solution)/shard_map/ppermute | solution.py:1019
  153.1 23.1 %collective-permute-start.4 = (f32[144,1024]{1,0:T(8,128)}, f32[144,1024]{1,0:T(8,128)S(1)}, u32[]{:S(2)}, u32[]{:S(2)}) collective-permute-start(f32[144,1024]{1,0:T(8,128)} %add.272), channel_id=1, source_target_pairs={{0,2},{1,3},{2,0},{3,1},{4,6},{5,7},{6,4},{7,5},{8,10},{9,11},{10,... | collective-permute-start | bytes 1769480 | tf_op jit(solution)/shard_map/ppermute | solution.py:1019
  176.2 13.1 %copy-start.12 = (f32[144,1024]{1,0:T(8,128)}, f32[144,1024]{1,0:T(8,128)S(1)}, u32[]{:S(2)}) copy-start(f32[144,1024]{1,0:T(8,128)S(1)} %collective-permute-done.4.refs_2_) | copy-start | bytes 1769476
  180.9 8.4 %copy-start.2 = (f32[288,1536]{1,0:T(8,128)}, f32[288,1536]{1,0:T(8,128)S(1)}, u32[]{:S(2)}) copy-start(f32[288,1536]{1,0:T(8,128)S(1)} %collective-permute-done.5.refs_4_.refs_5_.refs_1_.refs_6_) | copy-start | bytes 5308420
  192.1 41.8 %collective-permute-start.6 = (f32[2304,1152]{1,0:T(8,128)}, f32[2304,1152]{1,0:T(8,128)}, u32[]{:S(2)}, u32[]{:S(2)}) collective-permute-start(f32[2304,1152]{1,0:T(8,128)} %bitcast.44), channel_id=1, source_target_pairs={{0,16},{16,0},{1,17},{17,1},{2,18},{18,2},{3,19},{19,3},{4,20},{20... | collective-permute-start | bytes 31850504 | tf_op jit(solution)/shard_map/ppermute | solution.py:1021
  192.1 41.8 %collective-permute-start.9 = (f32[288,2048]{1,0:T(8,128)}, f32[288,2048]{1,0:T(8,128)}, u32[]{:S(2)}, u32[]{:S(2)}) collective-permute-start(f32[288,2048]{1,0:T(8,128)} %get-tuple-element.333), channel_id=1, source_target_pairs={{0,1},{1,0},{2,3},{3,2},{4,5},{5,4},{6,7},{7,6},{8,9},{9,8},{10,11... | collective-permute-start | bytes 7077896 | tf_op jit(solution)/shard_map/ppermute | solution.py:1019
  193.4 40.5 %collective-permute-start.8 = (f32[144,1536]{1,0:T(8,128)}, f32[144,1536]{1,0:T(8,128)S(1)}, u32[]{:S(2)}, u32[]{:S(2)}) collective-permute-start(f32[144,1536]{1,0:T(8,128)} %get-tuple-element.332), channel_id=1, source_target_pairs={{0,2},{1,3},{2,0},{3,1},{4,6},{5,7},{6,4},{7,5},{8,10},{9,11},{10,... | collective-permute-start | bytes 2654216 | tf_op jit(solution)/shard_map/ppermute | solution.py:1019
  194.2 39.7 %collective-permute-start.7 = (f32[72,1024]{1,0:T(8,128)}, f32[72,1024]{1,0:T(8,128)S(1)}, u32[]{:S(2)}, u32[]{:S(2)}) collective-permute-start(f32[72,1024]{1,0:T(8,128)} %get-tuple-element.331), channel_id=1, source_target_pairs={{0,4},{1,5},{2,6},{3,7},{4,0},{5,1},{6,2},{7,3},{8,12},{9,13},{10,... | collective-permute-start | bytes 884744 | tf_op jit(solution)/shard_map/ppermute | solution.py:1019
  233.8 17.0 %copy-start.19 = (f32[72,1024]{1,0:T(8,128)}, f32[72,1024]{1,0:T(8,128)S(1)}, u32[]{:S(2)}) copy-start(f32[72,1024]{1,0:T(8,128)S(1)} %collective-permute-done.7.refs_3_) | copy-start | bytes 884740
  233.9 17.0 %copy-start.10 = (f32[144,1536]{1,0:T(8,128)}, f32[144,1536]{1,0:T(8,128)S(1)}, u32[]{:S(2)}) copy-start(f32[144,1536]{1,0:T(8,128)S(1)} %collective-permute-done.8.refs_6_.refs_2_.refs_7_) | copy-start | bytes 2654212
  250.9 7.8 %copy-start.32 = (f32[1152]{0:T(1024)S(1)}, f32[1152]{0:T(1024)}, u32[]{:S(2)}) copy-start(f32[1152]{0:T(1024)} %param.36) | copy-start | bytes 13828
  254.6 54.4 %collective-permute-start.13 = (f32[1152,768]{1,0:T(8,128)}, f32[1152,768]{1,0:T(8,128)}, u32[]{:S(2)}, u32[]{:S(2)}) collective-permute-start(f32[1152,768]{1,0:T(8,128)} %bitcast.49), channel_id=1, source_target_pairs={{0,1},{1,0},{2,3},{3,2},{4,5},{5,4},{6,7},{7,6},{8,9},{9,8},{10,11... | collective-permute-start | bytes 10616840 | tf_op jit(solution)/shard_map/ppermute | solution.py:1019
  255.9 53.1 %collective-permute-start.14 = (f32[1152,384]{1,0:T(8,128)}, f32[1152,384]{1,0:T(8,128)S(1)}, u32[]{:S(2)}, u32[]{:S(2)}) collective-permute-start(f32[1152,384]{1,0:T(8,128)} %bitcast.11), channel_id=1, source_target_pairs={{0,4},{1,5},{2,6},{3,7},{4,0},{5,1},{6,2},{7,3},{8,12},{9,13},{10,... | collective-permute-start | bytes 5308424 | tf_op jit(solution)/shard_map/ppermute | solution.py:1019
  256.4 52.6 %collective-permute-start.12 = (f32[144,2048]{1,0:T(8,128)}, f32[144,2048]{1,0:T(8,128)S(1)}, u32[]{:S(2)}, u32[]{:S(2)}) collective-permute-start(f32[144,2048]{1,0:T(8,128)} %get-tuple-element.363), channel_id=1, source_target_pairs={{0,2},{1,3},{2,0},{3,1},{4,6},{5,7},{6,4},{7,5},{8,10},{9,11},{10,... | collective-permute-start | bytes 3538952 | tf_op jit(solution)/shard_map/ppermute | solution.py:1019
  257.1 51.9 %collective-permute-start.11 = (f32[72,1536]{1,0:T(8,128)}, f32[72,1536]{1,0:T(8,128)S(1)}, u32[]{:S(2)}, u32[]{:S(2)}) collective-permute-start(f32[72,1536]{1,0:T(8,128)} %get-tuple-element.362), channel_id=1, source_target_pairs={{0,4},{1,5},{2,6},{3,7},{4,0},{5,1},{6,2},{7,3},{8,12},{9,13},{10,... | collective-permute-start | bytes 1327112 | tf_op jit(solution)/shard_map/ppermute | solution.py:1019
  259.3 47.8 %collective-permute-start.10 = (f32[36,1024]{1,0:T(8,128)}, f32[36,1024]{1,0:T(8,128)S(1)}, u32[]{:S(2)}, u32[]{:S(2)}) collective-permute-start(f32[36,1024]{1,0:T(8,128)} %get-tuple-element.361), channel_id=1, source_target_pairs={{0,8},{1,9},{2,10},{3,11},{4,12},{5,13},{6,14},{7,15},{8,0},{9,1},... | collective-permute-start | bytes 442376 | tf_op jit(solution)/shard_map/ppermute | solution.py:1019
  307.1 9.1 %copy-start.28 = (f32[36,1024]{1,0:T(8,128)}, f32[36,1024]{1,0:T(8,128)S(1)}, u32[]{:S(2)}) copy-start(f32[36,1024]{1,0:T(8,128)S(1)} %collective-permute-done.10.refs_4_) | copy-start | bytes 442372
  316.2 35.8 %collective-permute-start.15 = (f32[576,2304]{1,0:T(8,128)}, f32[576,2304]{1,0:T(8,128)}, u32[]{:S(2)}, u32[]{:S(2)}) collective-permute-start(f32[576,2304]{1,0:T(8,128)} %get-tuple-element.385), channel_id=1, source_target_pairs={{0,16},{16,0},{1,17},{17,1},{2,18},{18,2},{3,19},{19,3},{4,20},{20... | collective-permute-start | bytes 15925256 | tf_op jit(solution)/shard_map/ppermute | solution.py:1021
  316.2 35.8 %collective-permute-start.18 = (f32[576,768]{1,0:T(8,128)}, f32[576,768]{1,0:T(8,128)S(1)}, u32[]{:S(2)}, u32[]{:S(2)}) collective-permute-start(f32[576,768]{1,0:T(8,128)} %get-tuple-element.388), channel_id=1, source_target_pairs={{0,2},{1,3},{2,0},{3,1},{4,6},{5,7},{6,4},{7,5},{8,10},{9,11},{10,... | collective-permute-start | bytes 5308424 | tf_op jit(solution)/shard_map/ppermute | solution.py:1019
  321.8 24.2 %collective-permute-start.19 = (f32[576,384]{1,0:T(8,128)}, f32[576,384]{1,0:T(8,128)S(1)}, u32[]{:S(2)}, u32[]{:S(2)}) collective-permute-start(f32[576,384]{1,0:T(8,128)} %get-tuple-element.389), channel_id=1, source_target_pairs={{0,1},{1,0},{2,3},{3,2},{4,5},{5,4},{6,7},{7,6},{8,9},{9,8},{10,11... | collective-permute-start | bytes 2654216 | tf_op jit(solution)/shard_map/ppermute | solution.py:1019
  323.3 22.7 %collective-permute-start.17 = (f32[72,2048]{1,0:T(8,128)}, f32[72,2048]{1,0:T(8,128)S(1)}, u32[]{:S(2)}, u32[]{:S(2)}) collective-permute-start(f32[72,2048]{1,0:T(8,128)} %get-tuple-element.387), channel_id=1, source_target_pairs={{0,4},{1,5},{2,6},{3,7},{4,0},{5,1},{6,2},{7,3},{8,12},{9,13},{10,... | collective-permute-start | bytes 1769480 | tf_op jit(solution)/shard_map/ppermute | solution.py:1019
  324.0 22.0 %collective-permute-start.16 = (f32[36,1536]{1,0:T(8,128)}, f32[36,1536]{1,0:T(8,128)S(1)}, u32[]{:S(2)}, u32[]{:S(2)}) collective-permute-start(f32[36,1536]{1,0:T(8,128)} %get-tuple-element.386), channel_id=1, source_target_pairs={{0,8},{1,9},{2,10},{3,11},{4,12},{5,13},{6,14},{7,15},{8,0},{9,1},... | collective-permute-start | bytes 663560 | tf_op jit(solution)/shard_map/ppermute | solution.py:1019
  346.0 17.0 %copy-start.25 = (f32[36,1536]{1,0:T(8,128)}, f32[36,1536]{1,0:T(8,128)S(1)}, u32[]{:S(2)}) copy-start(f32[36,1536]{1,0:T(8,128)S(1)} %collective-permute-done.16.refs_9_) | copy-start | bytes 663556
  346.1 17.0 %copy-start.16 = (f32[72,2048]{1,0:T(8,128)}, f32[72,2048]{1,0:T(8,128)S(1)}, u32[]{:S(2)}) copy-start(f32[72,2048]{1,0:T(8,128)S(1)} %collective-permute-done.17.refs_3_.refs_13_) | copy-start | bytes 1769476
  346.1 17.0 %copy-start.11 = (f32[576,384]{1,0:T(8,128)}, f32[576,384]{1,0:T(8,128)S(1)}, u32[]{:S(2)}) copy-start(f32[576,384]{1,0:T(8,128)S(1)} %collective-permute-done.19.refs_9_.refs_6_.refs_22_) | copy-start | bytes 2654212
  352.0 11.0 %copy-start.6 = (f32[576,768]{1,0:T(8,128)}, f32[576,768]{1,0:T(8,128)S(1)}, u32[]{:S(2)}) copy-start(f32[576,768]{1,0:T(8,128)S(1)} %collective-permute-done.18.refs_6_.refs_2_.refs_17_) | copy-start | bytes 5308420
  367.1 40.3 %collective-permute-start.20 = (f32[576,2304]{1,0:T(8,128)}, f32[576,2304]{1,0:T(8,128)}, u32[]{:S(2)}, u32[]{:S(2)}) collective-permute-start(f32[576,2304]{1,0:T(8,128)} %get-tuple-element.405), channel_id=1, source_target_pairs={{0,16},{16,0},{1,17},{17,1},{2,18},{18,2},{3,19},{19,3},{4,20},{20... | collective-permute-start | bytes 15925256 | tf_op jit(solution)/shard_map/ppermute | solution.py:1021
  367.2 40.3 %collective-permute-start.24 = (f32[288,2304]{1,0:T(8,128)}, f32[288,2304]{1,0:T(8,128)}, u32[]{:S(2)}, u32[]{:S(2)}) collective-permute-start(f32[288,2304]{1,0:T(8,128)} %get-tuple-element.409), channel_id=1, source_target_pairs={{0,1},{1,0},{2,3},{3,2},{4,5},{5,4},{6,7},{7,6},{8,9},{9,8},{10,11... | collective-permute-start | bytes 7962632 | tf_op jit(solution)/shard_map/ppermute | solution.py:1019
  372.4 29.0 %collective-permute-start.22 = (f32[288,768]{1,0:T(8,128)}, f32[288,768]{1,0:T(8,128)S(1)}, u32[]{:S(2)}, u32[]{:S(2)}) collective-permute-start(f32[288,768]{1,0:T(8,128)} %get-tuple-element.407), channel_id=1, source_target_pairs={{0,4},{1,5},{2,6},{3,7},{4,0},{5,1},{6,2},{7,3},{8,12},{9,13},{10,... | collective-permute-start | bytes 2654216 | tf_op jit(solution)/shard_map/ppermute | solution.py:1019
  374.0 26.6 %collective-permute-start.23 = (f32[288,384]{1,0:T(8,128)}, f32[288,384]{1,0:T(8,128)S(1)}, u32[]{:S(2)}, u32[]{:S(2)}) collective-permute-start(f32[288,384]{1,0:T(8,128)} %get-tuple-element.408), channel_id=1, source_target_pairs={{0,2},{1,3},{2,0},{3,1},{4,6},{5,7},{6,4},{7,5},{8,10},{9,11},{10,... | collective-permute-start | bytes 1327112 | tf_op jit(solution)/shard_map/ppermute | solution.py:1019
  374.7 25.9 %collective-permute-start.21 = (f32[36,2048]{1,0:T(8,128)}, f32[36,2048]{1,0:T(8,128)S(1)}, u32[]{:S(2)}, u32[]{:S(2)}) collective-permute-start(f32[36,2048]{1,0:T(8,128)} %get-tuple-element.406), channel_id=1, source_target_pairs={{0,8},{1,9},{2,10},{3,11},{4,12},{5,13},{6,14},{7,15},{8,0},{9,1},... | collective-permute-start | bytes 884744 | tf_op jit(solution)/shard_map/ppermute | solution.py:1019
  400.6 16.5 %copy-start.24 = (f32[36,2048]{1,0:T(8,128)}, f32[36,2048]{1,0:T(8,128)S(1)}, u32[]{:S(2)}) copy-start(f32[36,2048]{1,0:T(8,128)S(1)} %collective-permute-done.21.refs_14_) | copy-start | bytes 884740
  400.6 16.5 %copy-start.18 = (f32[288,384]{1,0:T(8,128)}, f32[288,384]{1,0:T(8,128)S(1)}, u32[]{:S(2)}) copy-start(f32[288,384]{1,0:T(8,128)S(1)} %collective-permute-done.23.refs_7_.refs_23_) | copy-start | bytes 1327108
  401.4 15.8 %copy-start.13 = (f32[288,768]{1,0:T(8,128)}, f32[288,768]{1,0:T(8,128)S(1)}, u32[]{:S(2)}) copy-start(f32[288,768]{1,0:T(8,128)S(1)} %collective-permute-done.22.refs_3_.refs_18_) | copy-start | bytes 2654212
  417.2 9.6 %copy-start.20 = (f32[4,10368]{1,0:T(4,128)S(1)}, f32[4,10368]{1,0:T(4,128)}, u32[]{:S(2)}) copy-start(f32[4,10368]{1,0:T(4,128)} %payload.1) | copy-start | bytes 497668
  421.1 46.5 %collective-permute-start.28 = (f32[288,2304]{1,0:T(8,128)}, f32[288,2304]{1,0:T(8,128)}, u32[]{:S(2)}, u32[]{:S(2)}) collective-permute-start(f32[288,2304]{1,0:T(8,128)} %get-tuple-element.434), channel_id=1, source_target_pairs={{0,1},{1,0},{2,3},{3,2},{4,5},{5,4},{6,7},{7,6},{8,9},{9,8},{10,11... | collective-permute-start | bytes 7962632 | tf_op jit(solution)/shard_map/ppermute | solution.py:1019
  423.1 39.1 %collective-permute-start.27 = (f32[144,2304]{1,0:T(8,128)}, f32[144,2304]{1,0:T(8,128)S(1)}, u32[]{:S(2)}, u32[]{:S(2)}) collective-permute-start(f32[144,2304]{1,0:T(8,128)} %get-tuple-element.433), channel_id=1, source_target_pairs={{0,2},{1,3},{2,0},{3,1},{4,6},{5,7},{6,4},{7,5},{8,10},{9,11},{10,... | collective-permute-start | bytes 3981320 | tf_op jit(solution)/shard_map/ppermute | solution.py:1019
  423.8 38.3 %collective-permute-start.25 = (f32[144,768]{1,0:T(8,128)}, f32[144,768]{1,0:T(8,128)S(1)}, u32[]{:S(2)}, u32[]{:S(2)}) collective-permute-start(f32[144,768]{1,0:T(8,128)} %get-tuple-element.431), channel_id=1, source_target_pairs={{0,8},{1,9},{2,10},{3,11},{4,12},{5,13},{6,14},{7,15},{8,0},{9,1},... | collective-permute-start | bytes 1327112 | tf_op jit(solution)/shard_map/ppermute | solution.py:1019
  426.4 35.8 %collective-permute-start.26 = (f32[144,384]{1,0:T(8,128)}, f32[144,384]{1,0:T(8,128)S(1)}, u32[]{:S(2)}, u32[]{:S(2)}) collective-permute-start(f32[144,384]{1,0:T(8,128)} %get-tuple-element.432), channel_id=1, source_target_pairs={{0,8},{1,9},{2,10},{3,11},{4,12},{5,13},{6,14},{7,15},{8,0},{9,1},... | collective-permute-start | bytes 663560 | tf_op jit(solution)/shard_map/ppermute | solution.py:1019
  426.8 35.4 %collective-permute-start.29 = (f32[4,10368]{1,0:T(4,128)S(1)}, f32[4,10368]{1,0:T(4,128)S(1)}, u32[]{:S(2)}, u32[]{:S(2)}) collective-permute-start(f32[4,10368]{1,0:T(4,128)S(1)} %copy-done.20), channel_id=1, source_target_pairs={{0,8},{1,9},{2,10},{3,11},{4,12},{5,13},{6,14},{7,15},{8,0},{9,1},... | collective-permute-start | bytes 497672 | tf_op jit(solution)/shard_map/ppermute | solution.py:1026
  462.2 9.2 %copy-start.26 = (f32[144,384]{1,0:T(8,128)}, f32[144,384]{1,0:T(8,128)S(1)}, u32[]{:S(2)}) copy-start(f32[144,384]{1,0:T(8,128)S(1)} %collective-permute-done.26.refs_24_) | copy-start | bytes 663556
  462.2 9.2 %copy-start.21 = (f32[144,768]{1,0:T(8,128)}, f32[144,768]{1,0:T(8,128)S(1)}, u32[]{:S(2)}) copy-start(f32[144,768]{1,0:T(8,128)S(1)} %collective-permute-done.25.refs_19_) | copy-start | bytes 1327108
  471.4 24.7 %collective-permute-start.31 = (f32[144,2304]{1,0:T(8,128)}, f32[144,2304]{1,0:T(8,128)S(1)}, u32[]{:S(2)}, u32[]{:S(2)}) collective-permute-start(f32[144,2304]{1,0:T(8,128)} %get-tuple-element.452), channel_id=1, source_target_pairs={{0,2},{1,3},{2,0},{3,1},{4,6},{5,7},{6,4},{7,5},{8,10},{9,11},{10,... | collective-permute-start | bytes 3981320 | tf_op jit(solution)/shard_map/ppermute | solution.py:1019
  472.1 24.0 %collective-permute-start.30 = (f32[72,2304]{1,0:T(8,128)}, f32[72,2304]{1,0:T(8,128)S(1)}, u32[]{:S(2)}, u32[]{:S(2)}) collective-permute-start(f32[72,2304]{1,0:T(8,128)} %get-tuple-element.451), channel_id=1, source_target_pairs={{0,4},{1,5},{2,6},{3,7},{4,0},{5,1},{6,2},{7,3},{8,12},{9,13},{10,... | collective-permute-start | bytes 1990664 | tf_op jit(solution)/shard_map/ppermute | solution.py:1019
  474.1 21.9 %collective-permute-start.32 = (f32[8,10368]{1,0:T(8,128)S(1)}, f32[8,10368]{1,0:T(8,128)S(1)}, u32[]{:S(2)}, u32[]{:S(2)}) collective-permute-start(f32[8,10368]{1,0:T(8,128)S(1)} %pad_maximum_fusion.2), channel_id=1, source_target_pairs={{0,4},{1,5},{2,6},{3,7},{4,0},{5,1},{6,2},{7,3},{8,12},{9,13},{10,... | collective-permute-start | bytes 995336 | tf_op jit(solution)/shard_map/ppermute | solution.py:1026
  500.7 23.9 %collective-permute-start.34 = (f32[72,2304]{1,0:T(8,128)}, f32[72,2304]{1,0:T(8,128)S(1)}, u32[]{:S(2)}, u32[]{:S(2)}) collective-permute-start(f32[72,2304]{1,0:T(8,128)} %get-tuple-element.464), channel_id=1, source_target_pairs={{0,4},{1,5},{2,6},{3,7},{4,0},{5,1},{6,2},{7,3},{8,12},{9,13},{10,... | collective-permute-start | bytes 1990664 | tf_op jit(solution)/shard_map/ppermute | solution.py:1019
  502.3 22.3 %collective-permute-start.35 = (f32[16,10368]{1,0:T(8,128)S(1)}, f32[16,10368]{1,0:T(8,128)S(1)}, u32[]{:S(2)}, u32[]{:S(2)}) collective-permute-start(f32[16,10368]{1,0:T(8,128)S(1)} %pad_maximum_fusion.1), channel_id=1, source_target_pairs={{0,2},{1,3},{2,0},{3,1},{4,6},{5,7},{6,4},{7,5},{8,10},{9,11},{10,... | collective-permute-start | bytes 1990664 | tf_op jit(solution)/shard_map/ppermute | solution.py:1026
  503.0 20.3 %collective-permute-start.33 = (f32[36,2304]{1,0:T(8,128)}, f32[36,2304]{1,0:T(8,128)S(1)}, u32[]{:S(2)}, u32[]{:S(2)}) collective-permute-start(f32[36,2304]{1,0:T(8,128)} %get-tuple-element.463), channel_id=1, source_target_pairs={{0,8},{1,9},{2,10},{3,11},{4,12},{5,13},{6,14},{7,15},{8,0},{9,1},... | collective-permute-start | bytes 995336 | tf_op jit(solution)/shard_map/ppermute | solution.py:1019
  525.4 20.9 %copy-start.4 = (f32[32,10368]{1,0:T(8,128)}, f32[32,10368]{1,0:T(8,128)S(1)}, u32[]{:S(2)}) copy-start(f32[32,10368]{1,0:T(8,128)S(1)} %pad_maximum_fusion.refs_0_.refs_4_.refs_8_) | copy-start | bytes 3981316
  525.4 21.4 %copy-start.34 = (s32[64]{0:T(128)S(1)}, s32[64]{0:T(128)}, u32[]{:S(2)}) copy-start(s32[64]{0:T(128)} %param.23) | copy-start | bytes 772
  528.4 17.9 %collective-permute-start.37 = (f32[32,10368]{1,0:T(8,128)S(1)}, f32[32,10368]{1,0:T(8,128)}, u32[]{:S(2)}, u32[]{:S(2)}) collective-permute-start(f32[32,10368]{1,0:T(8,128)S(1)} %pad_maximum_fusion.refs_0_.refs_4_.refs_8_), channel_id=1, source_target_pairs={{0,1},{1,0},{2,3},{3,2},{4,5},{5,4},{6,7},{7,6},{8,9},{9,8},{10,11... | collective-permute-start | bytes 3981320 | tf_op jit(solution)/shard_map/ppermute | solution.py:1026
  528.4 17.5 %collective-permute-start.36 = (f32[36,2304]{1,0:T(8,128)}, f32[36,2304]{1,0:T(8,128)S(1)}, u32[]{:S(2)}, u32[]{:S(2)}) collective-permute-start(f32[36,2304]{1,0:T(8,128)} %add.280), channel_id=1, source_target_pairs={{0,8},{1,9},{2,10},{3,11},{4,12},{5,13},{6,14},{7,15},{8,0},{9,1},... | collective-permute-start | bytes 995336 | tf_op jit(solution)/shard_map/ppermute | solution.py:1019
  546.3 6.6 %collective-permute-start.38 = (f32[32,10368]{1,0:T(8,128)S(1)}, f32[32,10368]{1,0:T(8,128)}, u32[]{:S(2)}, u32[]{:S(2)}) collective-permute-start(f32[32,10368]{1,0:T(8,128)S(1)} %pad_maximum_fusion.refs_0_.refs_4_.refs_8_), channel_id=1, source_target_pairs={{0,16},{16,0},{1,17},{17,1},{2,18},{18,2},{3,19},{19,3},{4,20},{20... | collective-permute-start | bytes 3981320 | tf_op jit(solution)/shard_map/ppermute | solution.py:1028
  546.3 6.6 %collective-permute-start.39 = (f32[32,10368]{1,0:T(8,128)}, f32[32,10368]{1,0:T(8,128)}, u32[]{:S(2)}, u32[]{:S(2)}) collective-permute-start(f32[32,10368]{1,0:T(8,128)} %collective-permute-done.37.refs_1_.refs_5_.refs_9_), channel_id=1, source_target_pairs={{0,16},{16,0},{1,17},{17,1},{2,18},{18,2},{3,19},{19,3},{4,20},{20... | collective-permute-start | bytes 3981320 | tf_op jit(solution)/shard_map/ppermute | solution.py:1028
  552.9 23.6 %copy-start.1 = (bf16[1001,1152]{1,0:T(8,128)(2,1)S(1)}, bf16[1001,1152]{1,0:T(8,128)(2,1)}, u32[]{:S(2)}) copy-start(bf16[1001,1152]{1,0:T(8,128)(2,1)} %param.26) | copy-start | bytes 6918916
  (13 other events, 32.0 us)

commit v6 on v5

--- a/solution.py
+++ b/solution.py
@@ -805,13 +805,17 @@
         gate = 1.0 / (1.0 + jnp.exp(-cond))
         grad = total_ref[...].T * (gate * (1.0 + cond * (1.0 - gate)))
         classes = table_ref.shape[0]
-        select = (label_ref[...] == lax.broadcasted_iota(jnp.int32, (grad.shape[0], classes), 1)).astype(F32)
-        table_ref[...] = dot(select, grad, TN, HIGHEST)
+        select = (label_ref[...] == lax.broadcasted_iota(jnp.int32, (grad.shape[0], classes), 1)).astype(F32).astype(BF16)
+        high = grad.astype(BF16)
+        rest = grad - high.astype(F32)
+        middle = rest.astype(BF16)
+        low = (rest - middle.astype(F32)).astype(BF16)
+        table_ref[...] = dot(select, high, TN) + (dot(select, middle, TN) + dot(select, low, TN))
 
 
 def modulation_back_call(me, parts, used, w, classes, shard, items):
     width, wide = w.shape
-    block = 1152
+    block = 2 * width
     rows = sum(part.shape[0] for part in parts)
     extra = parts[0].shape[1] - wide - width
     at = (wide + extra) // width
@@ -1174,7 +1178,7 @@
     grad_w_fc1, grad_w_fc2 = assemble_call(
         [[(chunk, 0, chunk.terms[0].shape[1]) for chunk in store] for store in (fc1, fc2)]
     )
-    result, grad_w_fc1, grad_w_fc2 = flow.round((result, grad_w_fc1, grad_w_fc2))
+    result, grad_w_fc1, grad_w_fc2, used_rows = flow.round((result, grad_w_fc1, grad_w_fc2, used_rows))
     while any(chunk.stage < bits for chunk in wide):
         result = flow.round(result)
     result = flow.round(result)

time: 582 us -> 578 us (level)
  transfers between devices with their start and end apart: 40 -> 40, of which waited for: 14 -> 16; matrix products, arithmetic and copies ran while one was open for 1% -> 1% of each run, Pallas kernels for 32% -> 33%
where the time goes in v6:
time: 578 us; the launch traced here: 573 us
  Pallas kernels  363 us (63%)
  waiting for transfers between devices  117 us (20%)
  starting transfers between devices  55.4 us (10%)
  local copies, waits for them, and re-layouts  20 us (3%)
  matrix products  7.72 us (1%)
  other arithmetic  7.58 us (1%)
    ppermute x28, waiting for transfers between devices, round(): lax.ppermute(send, ('stream', 'batch'), self.pairs(chunk.stage, chunk.lead))  66.6 us
    ppermute x28, starting transfers between devices, round(): lax.ppermute(send, ('stream', 'batch'), self.pairs(chunk.stage, chunk.lead))  51.9 us
    ppermute x4, waiting for transfers between devices, round(): lax.ppermute(piece, ('stream', 'batch'), pairs)  50.5 us
    pallas_call x3, Pallas kernels, hidden_call(): call(hidden_body, 'hidden', 6 * tokens * width * count, 6 * tokens * widt...  46.6 us
    pallas_call x5, Pallas kernels, columns_call(): call(functools.partial(columns_body, right=right, both=both), name, 2 * t...  38.1 us
    pallas_call x9, Pallas kernels, add_call(): call(functools.partial(add_body, plans=plans), 'add', moved // 4, moved,...  32 us
    pallas_call x1, Pallas kernels, middle_back_call(): call(middle_back_body, 'middle_back', 2 * tokens * width * (hidden + widt...  30.2 us
    pallas_call x2, Pallas kernels, attention_back_call(): call(attention_back_body, 'attention_back', 2 * 2 * heads * tokens * GROU...  27.9 us
  transfers between devices with their start and end apart: 40, of which 16 were waited for; matrix products, arithmetic and copies ran while one was open for 1% of the time, Pallas kernels for 33%

profile of v6, /device:TPU:0, one launch (start us, length us, event | category | flops | bytes accessed | tf_op | source)
XLA Modules:
  0.0 573.4 jit_solution(15928951942173415319)
XLA Ops:
  5.0 7.7 %convolution_add_fusion = f32[4,6912]{1,0:T(4,128)S(1)} fusion(bf16[1152,6912]{1,0:T(8,128)(2,1)} %refs_13_.1, f32[6912]{0:T(1024)} %param.28, f32[4,1152]{1,0:T(4,128)S(1)} %maximum_add_fusion.cond_ref), kind=kOutput, calls=%fused_computation.3 | convolution fusion | flops 63751680 | bytes 16081920 | tf_op jit(solution)/shard_map/dot_general | solution.py:28
  18.2 1.7 fusion.away_ref
  20.0 1.7 fusion.1.own_ref
  24.0 16.0 %qkv.1 = (bf16[1024,1152]{1,0:T(8,128)(2,1)}, bf16[3456,1024]{1,0:T(8,128)(2,1)}) custom-call(bf16[1024,1152]{1,0:T(8,128)(2,1)} %bitcast.41, f32[4,6,1152]{2,1,0:T(8,128)} %reshape.311.mod_ref, bf16[1152,3456]{1,0:T(8,128)(2,1)} %w_ref.7, f32[1,3456]{1,0:T(1,128)} %broadcast_in_dim.132.b_ref), custom_call_target="tpu_custom_call" | custom-call | flops 1019215872 | bytes 2469888 | tf_op jit(solution)/shard_map/qkv/pallas_call | solution.py:73
  40.0 26.4 %attention.1 = (bf16[16,1024,1024]{2,1,0:T(8,128)(2,1)}, f32[16,72,1024]{2,1,0:T(8,128)}, bf16[1152,1024]{1,0:T(8,128)(2,1)}) custom-call(s32[1]{0:T(128)} %bitcast.1.flag_ref, bf16[3456,1024]{1,0:T(8,128)(2,1)} %get-tuple-element.255.q_ref.k_ref.v_ref, bf16[3456,1024]{1,0:T(8,128)(2,1)} %get-tuple-element.255.q_ref.k_ref.v_ref, ...), custom_call_target="tpu_custom_call" | custom-call | flops 2147483648 | bytes 5963776 | tf_op jit(solution)/shard_map/attention/pallas_call | solution.py:139
  66.4 15.1 %middle.1 = (f32[1024,1152]{1,0:T(8,128)}, f32[1024,1152]{1,0:T(8,128)}, bf16[1024,1152]{1,0:T(8,128)(2,1)}, bf16[1024,576]{1,0:T(8,128)(2,1)}, bf16[1024,576]{1...) custom-call(bf16[1152,1024]{1,0:T(8,128)(2,1)} %get-tuple-element.256.om_ref.left_ref, ...), custom_call_target="tpu_custom_call" | custom-call | flops 679477248 | bytes 3833856 | tf_op jit(solution)/shard_map/middle/pallas_call | solution.py:259
  81.5 12.2 %hidden.3 = (bf16[1024,4608]{1,0:T(8,128)(2,1)}, bf16[1024,4608]{1,0:T(8,128)(2,1)}, f32[1,4608]{1,0:T(1,128)}, f32[576,1024]{1,0:T(8,128)}) custom-call(bf16[1024,1152]{1,0:T(8,128)(2,1)} %get-tuple-element.284.h_ref, bf16[1024,576]{1,0:T(8,128)(2,1)} %get-tuple-element.258.away_ref, bf16[1024,1152]{1,0:T(8,128)(2,1)} %get-tuple-element.259.dm_ref, ...), custom_call_target="tpu_custom_call" | custom-call | flops 905969664 | bytes 2588672 | tf_op jit(solution)/shard_map/hidden/pallas_call | solution.py:312
  94.2 15.3 %hidden.4 = (bf16[1024,4608]{1,0:T(8,128)(2,1)}, bf16[1024,4608]{1,0:T(8,128)(2,1)}, f32[1,4608]{1,0:T(1,128)}, f32[576,1536]{1,0:T(8,128)}) custom-call(bf16[1024,1152]{1,0:T(8,128)(2,1)} %get-tuple-element.284.h_ref, bf16[1024,576]{1,0:T(8,128)(2,1)} %get-tuple-element.258.away_ref, ...), custom_call_target="tpu_custom_call", output_to_operand_aliasing={{0}: (6, {}), {1}: (7, {}), {2}: (8, {})} | custom-call | flops 1358954496 | bytes 3440640 | tf_op jit(solution)/shard_map/hidden/pallas_call | solution.py:312
  109.5 4.7 hidden_keep.3
  114.2 9.3 %collective-permute-start.2 = (f32[288,1024]{1,0:T(8,128)}, f32[288,1024]{1,0:T(8,128)S(1)}, u32[]{:S(2)}, u32[]{:S(2)}) collective-permute-start(f32[288,1024]{1,0:T(8,128)} %get-tuple-element.292), channel_id=1, source_target_pairs={{0,1},{1,0},{2,3},{3,2},{4,5},{5,4},{6,7},{7,6},{8,9},{9,8},{10,11... | collective-permute-start | bytes 3538952 | tf_op jit(solution)/shard_map/ppermute | solution.py:1023
  123.5 19.0 %hidden.5 = (bf16[1024,4608]{1,0:T(8,128)(2,1)}, bf16[1024,4608]{1,0:T(8,128)(2,1)}, f32[1,4608]{1,0:T(1,128)}, f32[576,2048]{1,0:T(8,128)}) custom-call(bf16[1024,1152]{1,0:T(8,128)(2,1)} %get-tuple-element.284.h_ref, bf16[1024,576]{1,0:T(8,128)(2,1)} %get-tuple-element.258.away_ref, ...), custom_call_target="tpu_custom_call", output_to_operand_aliasing={{0}: (6, {}), {1}: (7, {}), {2}: (8, {})} | custom-call | flops 1811939328 | bytes 4292608 | tf_op jit(solution)/shard_map/hidden/pallas_call | solution.py:312
  142.6 7.4 %hidden_keep.4 = (f32[288,1536]{1,0:T(8,128)}, f32[288,1536]{1,0:T(8,128)}) custom-call(bf16[1024,576]{1,0:T(8,128)(2,1)} %get-tuple-element.281.refs_0_, bf16[1024,4608]{1,0:T(8,128)(2,1)} %get-tuple-element.322.refs_1_.df_ref, f32[576,1536]{1,0:T(8,128)} %collective-permute-done.1.refs_2_), custom_call_target="tpu_custom_call" | custom-call | flops 226492416 | bytes 1425408 | tf_op jit(solution)/shard_map/hidden_keep/pallas_call | solution.py:607
  150.0 2.1 add.272
  154.1 7.4 %moved.2 = (bf16[1024,576]{1,0:T(8,128)(2,1)}, bf16[1024,576]{1,0:T(8,128)(2,1)}) custom-call(bf16[1152,1024]{1,0:T(8,128)(2,1)} %get-tuple-element.256.om_ref.left_ref, bf16[1152,576]{1,0:T(8,128)(2,1)} %fusion.away_ref, bf16[1152,576]{1,0:T(8,128)(2,1)} %fusion.1.own_ref), custom_call_target="tpu_custom_call" | custom-call | flops 339738624 | bytes 921600 | tf_op jit(solution)/shard_map/moved/pallas_call | solution.py:675
  162.1 14.0 %rows_send.1 = f32[16,144,1152]{2,1,0:T(8,128)} custom-call(s32[1]{0:T(128)} %bitcast.6.side_ref, s32[3,16]{1,0:T(4,128)} %pad_add_fusion.spot_ref, bf16[1024,4608]{1,0:T(8,128)(2,1)} %get-tuple-element.360.g_ref, bf16[1024,1152]{1,0:T(8,128)(2,1)} %get-tuple-element.259.dm_ref), custom_call_target="tpu_custom_call" | custom-call | flops 679477248 | bytes 2211840 | tf_op jit(solution)/shard_map/rows_send/pallas_call | solution.py:370
  176.1 5.0 collective-permute-done.5.refs_4_.refs_5_.refs_1_.refs_6_
  181.1 8.4 %hidden_keep.5 = (f32[288,2048]{1,0:T(8,128)}, f32[288,2048]{1,0:T(8,128)}) custom-call(bf16[1024,576]{1,0:T(8,128)(2,1)} %get-tuple-element.281.refs_0_, bf16[1024,4608]{1,0:T(8,128)(2,1)} %get-tuple-element.322.refs_1_.df_ref, f32[576,2048]{1,0:T(8,128)} %collective-permute-done.3.refs_2_), custom_call_target="tpu_custom_call" | custom-call | flops 301989888 | bytes 1851392 | tf_op jit(solution)/shard_map/hidden_keep/pallas_call | solution.py:607
  189.6 2.8 add.273
  192.3 1.3 collective-permute-start.9
  194.4 1.7 collective-permute-start.7
  196.6 7.3 %moved.3 = (bf16[1024,576]{1,0:T(8,128)(2,1)}, bf16[1024,576]{1,0:T(8,128)(2,1)}) custom-call(bf16[1024,1152]{1,0:T(8,128)(2,1)} %get-tuple-element.329.left_ref, bf16[1152,576]{1,0:T(8,128)(2,1)} %fusion.away_ref, bf16[1152,576]{1,0:T(8,128)(2,1)} %fusion.1.own_ref), custom_call_target="tpu_custom_call" | custom-call | flops 339738624 | bytes 921600 | tf_op jit(solution)/shard_map/moved/pallas_call | solution.py:675
  204.0 30.2 %middle_back.1 = (f32[1024,1152]{1,0:T(8,128)}, bf16[1024,1152]{1,0:T(8,128)(2,1)}, bf16[1152,1024]{1,0:T(8,128)(2,1)}, f32[4,4,1152]{2,1,0:T(4,128)}) custom-call(bf16[1024,4608]{1,0:T(8,128)(2,1)} %get-tuple-element.322.refs_1_.df_ref, bf16[1152,4608]{1,0:T(8,128)(2,1)} %w1_ref.7, f32[1024,1152]{1,0:T(8,128)} %get-tuple-element.323.x1_ref, ...), custom_call_target="tpu_custom_call" | custom-call | flops 1698693120 | bytes 5160960 | tf_op jit(solution)/shard_map/middle_back/pallas_call | solution.py:501
  234.2 17.1 %rows_keep.1 = (f32[8,144,768]{2,1,0:T(8,128)}, f32[8,144,768]{2,1,0:T(8,128)}, f32[8,144,384]{2,1,0:T(8,128)}, f32[8,144,384]{2,1,0:T(8,128)}) custom-call(s32[1]{0:T(128)} %bitcast.8.side_ref, s32[3,16]{1,0:T(4,128)} %pad_add_fusion.1.spot_ref, bf16[1024,4608]{1,0:T(8,128)(2,1)} %get-tuple-element.360.g_ref, bf16[1024,1152]{1,0:T(8,128)(2,1)} %get-tuple-element.259.dm_ref, ...), custom_call_target="tpu_custom_call" | custom-call | flops 679477248 | bytes 3538944 | tf_op jit(solution)/shard_map/rows_keep/pallas_call | solution.py:423
  251.3 3.7 add.274
  257.5 1.6 collective-permute-start.11
  259.7 2.3 collective-permute-start.10
  261.9 13.8 %attention_back.2.refs_3_.refs_1_.low_ref = bf16[3,576,1024]{2,1,0:T(8,128)(2,1)} custom-call(s32[1]{0:T(128)} %bitcast.1.flag_ref, bf16[3456,1024]{1,0:T(8,128)(2,1)} %get-tuple-element.255.q_ref.k_ref.v_ref, bf16[3456,1024]{1,0:T(8,128)(2,1)} %get-tuple-element.255.q_ref.k_ref.v_ref, bf16[3456,1024]{1,0:T(8,128)(2,1)} %get-tuple-element.255.q_ref.k_ref.v_ref, ...), custom_call_target="tpu_custom_call" | custom-call | flops 2147483648 | bytes 3866624 | tf_op jit(solution)/shard_map/attention_back/pallas_call | solution.py:212
  275.7 9.8 %first_send.1 = (f32[576,2304]{1,0:T(8,128)}, f32[1,2304]{1,0:T(1,128)}) custom-call(bf16[1024,576]{1,0:T(8,128)(2,1)} %get-tuple-element.356.refs_0_, bf16[1024,1152]{1,0:T(8,128)(2,1)} %get-tuple-element.357.refs_1_, bf16[1024,576]{1,0:T(8,128)(2,1)} %get-tuple-element.358.refs_2_.refs_0_, bf16[3,576,1024]{2,1,0:T(8,128)(2,1)} %attention_back.2.refs_3_.refs_1_.low_ref), custom_call_target="tpu_custom_call" | custom-call | flops 339738624 | bytes 2064384 | tf_op jit(solution)/shard_map/first_send/pallas_call | solution.py:647
  285.5 19.7 %result.1 = (bf16[1024,1152]{1,0:T(8,128)(2,1)}, f32[4,1,1152]{2,1,0:T(1,128)}) custom-call(bf16[1024,4608]{1,0:T(8,128)(2,1)} %get-tuple-element.360.g_ref, bf16[4608,1152]{1,0:T(8,128)(2,1)} %w_ref.6, f32[1,1152]{1,0:T(1,128)} %broadcast_in_dim.141.b_ref, f32[1024,1152]{1,0:T(8,128)} %get-tuple-element.323.x1_ref, f32[4,6,1152]{2,1,0:T(8,128)} %reshape.311.mod_ref, ...), custom_call_target="tpu_custom_call" | custom-call | flops 1358954496 | bytes 3686400 | tf_op jit(solution)/shard_map/result/pallas_call | solution.py:457
  305.2 2.3 collective-permute-done.10.refs_4_
  307.5 1.9 collective-permute-done.11.refs_3_.refs_8_
  311.1 5.4 add.275
  316.6 5.7 collective-permute-start.18
  322.2 1.5 collective-permute-start.19
  324.1 14.1 %attention_back.3.refs_2_.high_ref = bf16[3,576,1024]{2,1,0:T(8,128)(2,1)} custom-call(s32[1]{0:T(128)} %bitcast.1.flag_ref, bf16[3456,1024]{1,0:T(8,128)(2,1)} %get-tuple-element.255.q_ref.k_ref.v_ref, bf16[3456,1024]{1,0:T(8,128)(2,1)} %get-tuple-element.255.q_ref.k_ref.v_ref, bf16[3456,1024]{1,0:T(8,128)(2,1)} %get-tuple-element.255.q_ref.k_ref.v_ref, ...), custom_call_target="tpu_custom_call" | custom-call | flops 2147483648 | bytes 3866624 | tf_op jit(solution)/shard_map/attention_back/pallas_call | solution.py:212
  338.2 8.1 %last_send.1 = (f32[576,2304]{1,0:T(8,128)}, f32[1,2304]{1,0:T(1,128)}) custom-call(bf16[1024,576]{1,0:T(8,128)(2,1)} %get-tuple-element.358.refs_2_.refs_0_, bf16[3,576,1024]{2,1,0:T(8,128)(2,1)} %attention_back.2.refs_3_.refs_1_.low_ref, bf16[3,576,1024]{2,1,0:T(8,128)(2,1)} %attention_back.3.refs_2_.high_ref), custom_call_target="tpu_custom_call" | custom-call | flops 339738624 | bytes 2064384 | tf_op jit(solution)/shard_map/last_send/pallas_call | solution.py:607
  346.4 6.1 %collective-permute-done.18.refs_6_.refs_2_.refs_17_ = f32[576,768]{1,0:T(8,128)S(1)} collective-permute-done((f32[576,768]{1,0:T(8,128)}, f32[576,768]{1,0:T(8,128)S(1)}, u32[]{:S(2)}, u32[]{:S(2)}) %collective-permute-start.18) | collective-permute-done | bytes 1769504 | tf_op jit(solution)/shard_map/ppermute | solution.py:1023
  352.4 11.0 %first_keep.1 = (f32[288,2304]{1,0:T(8,128)}, f32[288,2304]{1,0:T(8,128)}) custom-call(bf16[1024,576]{1,0:T(8,128)(2,1)} %get-tuple-element.403.refs_0_, bf16[1024,1152]{1,0:T(8,128)(2,1)} %get-tuple-element.357.refs_1_, bf16[1024,576]{1,0:T(8,128)(2,1)} %get-tuple-element.404.refs_2_.refs_0_, bf16[3,576,1024]{2,1,0:T(8,128)(2,1)} %attention_back.2.refs_3_.refs_1_.low_ref, ...), custom_call_target="tpu_custom_call" | custom-call | flops 339738624 | bytes 2064384 | tf_op jit(solution)/shard_map/first_keep/pallas_call | solution.py:647
  363.4 4.1 add.276
  367.5 4.7 collective-permute-start.24
  372.2 2.0 collective-permute-start.22
  375.9 18.2 %first_back.1 = (f32[1024,1152]{1,0:T(8,128)}, f32[4,2,1152]{2,1,0:T(2,128)}) custom-call(bf16[3,576,1024]{2,1,0:T(8,128)(2,1)} %attention_back.2.refs_3_.refs_1_.low_ref, bf16[3,576,1024]{2,1,0:T(8,128)(2,1)} %attention_back.3.refs_2_.high_ref, bf16[1152,3456]{1,0:T(8,128)(2,1)} %w_ref.7, bf16[1024,1152]{1,0:T(8,128)(2,1)} %bitcast.43, ...), custom_call_target="tpu_custom_call" | custom-call | flops 1019215872 | bytes 3354624 | tf_op jit(solution)/shard_map/first_back/pallas_call | solution.py:707
  394.1 1.8 payload.1
  395.9 5.0 collective-permute-done.21.refs_14_
  401.7 5.6 collective-permute-done.24.refs_9_.refs_1_
  407.3 9.5 %last_keep.1 = (f32[288,2304]{1,0:T(8,128)}, f32[288,2304]{1,0:T(8,128)}) custom-call(bf16[1024,576]{1,0:T(8,128)(2,1)} %get-tuple-element.404.refs_2_.refs_0_, bf16[3,576,1024]{2,1,0:T(8,128)(2,1)} %attention_back.2.refs_3_.refs_1_.low_ref, bf16[3,576,1024]{2,1,0:T(8,128)(2,1)} %attention_back.3.refs_2_.high_ref, f32[576,2304]{1,0:T(8,128)} %collective-permute-done.20.refs_3_), custom_call_target="tpu_custom_call" | custom-call | flops 339738624 | bytes 2064384 | tf_op jit(solution)/shard_map/last_keep/pallas_call | solution.py:607
  416.9 3.9 add.277
  420.8 2.0 collective-permute-start.28
  425.0 1.9 collective-permute-start.26
  428.0 34.3 %collective-permute-done.29 = f32[4,10368]{1,0:T(4,128)S(1)} collective-permute-done((f32[4,10368]{1,0:T(4,128)S(1)}, f32[4,10368]{1,0:T(4,128)S(1)}, u32[]{:S(2)}, u32[]{:S(2)}) %collective-permute-start.29) | collective-permute-done | bytes 165920 | tf_op jit(solution)/shard_map/ppermute | solution.py:1030
  462.4 4.9 collective-permute-done.28.refs_4_.refs_5_.refs_1_.refs_6_
  467.4 3.7 add.278
  472.9 1.6 collective-permute-start.30
  476.1 4.9 assemble.2
  481.0 15.8 %collective-permute-done.32 = f32[8,10368]{1,0:T(8,128)S(1)} collective-permute-done((f32[8,10368]{1,0:T(8,128)S(1)}, f32[8,10368]{1,0:T(8,128)S(1)}, u32[]{:S(2)}, u32[]{:S(2)}) %collective-permute-start.32) | collective-permute-done | bytes 331808 | tf_op jit(solution)/shard_map/ppermute | solution.py:1030
  498.1 3.3 add.279
  501.5 1.7 collective-permute-start.34
  504.8 19.9 %collective-permute-done.33.refs_4_ = f32[36,2304]{1,0:T(8,128)S(1)} collective-permute-done((f32[36,2304]{1,0:T(8,128)}, f32[36,2304]{1,0:T(8,128)S(1)}, u32[]{:S(2)}, u32[]{:S(2)}) %collective-permute-start.33) | collective-permute-done | bytes 331808 | tf_op jit(solution)/shard_map/ppermute | solution.py:1023
  526.2 3.0 add.280
  529.1 3.0 collective-permute-start.36
  532.2 14.5 %collective-permute-done.36.refs_9_ = f32[36,2304]{1,0:T(8,128)S(1)} collective-permute-done((f32[36,2304]{1,0:T(8,128)}, f32[36,2304]{1,0:T(8,128)S(1)}, u32[]{:S(2)}, u32[]{:S(2)}) %collective-permute-start.36) | collective-permute-done | bytes 331808 | tf_op jit(solution)/shard_map/ppermute | solution.py:1023
  548.3 3.7 assemble.3
  552.3 15.7 %modulation_back.1 = (f32[36,6912]{1,0:T(8,128)}, f32[1,6912]{1,0:T(1,128)}, f32[1001,1152]{1,0:T(8,128)}, f32[4,2304]{1,0:T(4,128)}) custom-call(s32[1]{0:T(128)} %bitcast.17.me_ref, f32[32,10368]{1,0:T(8,128)} %copy-done.4, f32[32,10368]{1,0:T(8,128)} %collective-permute-done.37.refs_1_.refs_5_.refs_9_, ...), custom_call_target="tpu_custom_call" | custom-call | flops 509607936 | bytes 1990656 | tf_op jit(solution)/shard_map/modulation_back/pallas_call | solution.py:822
  569.3 1.3 dynamic_slice.25
  (181 shorter events, 40.1 us)
Async XLA Ops:
  5.0 8.8 %copy-start.28 = (f32[2304]{0:T(1024)S(1)}, f32[2304]{0:T(1024)}, u32[]{:S(2)}) copy-start(f32[2304]{0:T(1024)} %param.30) | copy-start | bytes 27652
  5.0 9.4 %copy-start.34 = (s32[4,16]{1,0:T(4,128)S(1)}, s32[4,16]{1,0:T(4,128)}, u32[]{:S(2)}) copy-start(s32[4,16]{1,0:T(4,128)} %param.24) | copy-start | bytes 772
  12.7 9.0 %copy-start.32 = (s32[1,1024]{1,0:T(1,128)S(1)}, s32[1,1024]{1,0:T(1,128)}, u32[]{:S(2)}) copy-start(s32[1,1024]{1,0:T(1,128)} %param.25) | copy-start | bytes 12292
  12.7 10.0 %copy-start.30 = (f32[1152]{0:T(1024)S(1)}, f32[1152]{0:T(1024)}, u32[]{:S(2)}) copy-start(f32[1152]{0:T(1024)} %param.32) | copy-start | bytes 13828
  12.7 10.6 %copy-start.29 = (f32[4608]{0:T(1024)S(1)}, f32[4608]{0:T(1024)}, u32[]{:S(2)}) copy-start(f32[4608]{0:T(1024)} %param.34) | copy-start | bytes 55300
  93.7 15.8 %collective-permute-start = (f32[576,1024]{1,0:T(8,128)}, f32[576,1024]{1,0:T(8,128)}, u32[]{:S(2)}, u32[]{:S(2)}) collective-permute-start(f32[576,1024]{1,0:T(8,128)} %get-tuple-element.275), channel_id=1, source_target_pairs={{0,16},{16,0},{1,17},{17,1},{2,18},{18,2},{3,19},{19,3},{4,20},{20... | collective-permute-start | bytes 7077896 | tf_op jit(solution)/shard_map/ppermute | solution.py:1025
  114.2 28.4 %collective-permute-start.1 = (f32[576,1536]{1,0:T(8,128)}, f32[576,1536]{1,0:T(8,128)}, u32[]{:S(2)}, u32[]{:S(2)}) collective-permute-start(f32[576,1536]{1,0:T(8,128)} %get-tuple-element.291), channel_id=1, source_target_pairs={{0,16},{16,0},{1,17},{17,1},{2,18},{18,2},{3,19},{19,3},{4,20},{20... | collective-permute-start | bytes 10616840 | tf_op jit(solution)/shard_map/ppermute | solution.py:1025
  114.2 28.4 %collective-permute-start.2 = (f32[288,1024]{1,0:T(8,128)}, f32[288,1024]{1,0:T(8,128)S(1)}, u32[]{:S(2)}, u32[]{:S(2)}) collective-permute-start(f32[288,1024]{1,0:T(8,128)} %get-tuple-element.292), channel_id=1, source_target_pairs={{0,1},{1,0},{2,3},{3,2},{4,5},{5,4},{6,7},{7,6},{8,9},{9,8},{10,11... | collective-permute-start | bytes 3538952 | tf_op jit(solution)/shard_map/ppermute | solution.py:1023
  142.6 7.4 %copy-start.5 = (f32[288,1024]{1,0:T(8,128)}, f32[288,1024]{1,0:T(8,128)S(1)}, u32[]{:S(2)}) copy-start(f32[288,1024]{1,0:T(8,128)S(1)} %collective-permute-done.2.refs_1_) | copy-start | bytes 3538948
  152.1 29.1 %collective-permute-start.3 = (f32[576,2048]{1,0:T(8,128)}, f32[576,2048]{1,0:T(8,128)}, u32[]{:S(2)}, u32[]{:S(2)}) collective-permute-start(f32[576,2048]{1,0:T(8,128)} %get-tuple-element.306), channel_id=1, source_target_pairs={{0,16},{16,0},{1,17},{17,1},{2,18},{18,2},{3,19},{19,3},{4,20},{20... | collective-permute-start | bytes 14155784 | tf_op jit(solution)/shard_map/ppermute | solution.py:1025
  152.1 29.1 %collective-permute-start.5 = (f32[288,1536]{1,0:T(8,128)}, f32[288,1536]{1,0:T(8,128)S(1)}, u32[]{:S(2)}, u32[]{:S(2)}) collective-permute-start(f32[288,1536]{1,0:T(8,128)} %get-tuple-element.308), channel_id=1, source_target_pairs={{0,1},{1,0},{2,3},{3,2},{4,5},{5,4},{6,7},{7,6},{8,9},{9,8},{10,11... | collective-permute-start | bytes 5308424 | tf_op jit(solution)/shard_map/ppermute | solution.py:1023
  153.4 22.7 %collective-permute-start.4 = (f32[144,1024]{1,0:T(8,128)}, f32[144,1024]{1,0:T(8,128)S(1)}, u32[]{:S(2)}, u32[]{:S(2)}) collective-permute-start(f32[144,1024]{1,0:T(8,128)} %add.272), channel_id=1, source_target_pairs={{0,2},{1,3},{2,0},{3,1},{4,6},{5,7},{6,4},{7,5},{8,10},{9,11},{10,... | collective-permute-start | bytes 1769480 | tf_op jit(solution)/shard_map/ppermute | solution.py:1023
  176.1 13.4 %copy-start.12 = (f32[144,1024]{1,0:T(8,128)}, f32[144,1024]{1,0:T(8,128)S(1)}, u32[]{:S(2)}) copy-start(f32[144,1024]{1,0:T(8,128)S(1)} %collective-permute-done.4.refs_2_) | copy-start | bytes 1769476
  181.1 8.4 %copy-start.2 = (f32[288,1536]{1,0:T(8,128)}, f32[288,1536]{1,0:T(8,128)S(1)}, u32[]{:S(2)}) copy-start(f32[288,1536]{1,0:T(8,128)S(1)} %collective-permute-done.5.refs_4_.refs_5_.refs_1_.refs_6_) | copy-start | bytes 5308420
  192.3 41.9 %collective-permute-start.6 = (f32[2304,1152]{1,0:T(8,128)}, f32[2304,1152]{1,0:T(8,128)}, u32[]{:S(2)}, u32[]{:S(2)}) collective-permute-start(f32[2304,1152]{1,0:T(8,128)} %bitcast.44), channel_id=1, source_target_pairs={{0,16},{16,0},{1,17},{17,1},{2,18},{18,2},{3,19},{19,3},{4,20},{20... | collective-permute-start | bytes 31850504 | tf_op jit(solution)/shard_map/ppermute | solution.py:1025
  192.3 41.9 %collective-permute-start.9 = (f32[288,2048]{1,0:T(8,128)}, f32[288,2048]{1,0:T(8,128)}, u32[]{:S(2)}, u32[]{:S(2)}) collective-permute-start(f32[288,2048]{1,0:T(8,128)} %get-tuple-element.335), channel_id=1, source_target_pairs={{0,1},{1,0},{2,3},{3,2},{4,5},{5,4},{6,7},{7,6},{8,9},{9,8},{10,11... | collective-permute-start | bytes 7077896 | tf_op jit(solution)/shard_map/ppermute | solution.py:1023
  193.7 40.5 %collective-permute-start.8 = (f32[144,1536]{1,0:T(8,128)}, f32[144,1536]{1,0:T(8,128)S(1)}, u32[]{:S(2)}, u32[]{:S(2)}) collective-permute-start(f32[144,1536]{1,0:T(8,128)} %get-tuple-element.334), channel_id=1, source_target_pairs={{0,2},{1,3},{2,0},{3,1},{4,6},{5,7},{6,4},{7,5},{8,10},{9,11},{10,... | collective-permute-start | bytes 2654216 | tf_op jit(solution)/shard_map/ppermute | solution.py:1023
  194.4 39.8 %collective-permute-start.7 = (f32[72,1024]{1,0:T(8,128)}, f32[72,1024]{1,0:T(8,128)S(1)}, u32[]{:S(2)}, u32[]{:S(2)}) collective-permute-start(f32[72,1024]{1,0:T(8,128)} %get-tuple-element.333), channel_id=1, source_target_pairs={{0,4},{1,5},{2,6},{3,7},{4,0},{5,1},{6,2},{7,3},{8,12},{9,13},{10,... | collective-permute-start | bytes 884744 | tf_op jit(solution)/shard_map/ppermute | solution.py:1023
  234.2 17.1 %copy-start.18 = (f32[72,1024]{1,0:T(8,128)}, f32[72,1024]{1,0:T(8,128)S(1)}, u32[]{:S(2)}) copy-start(f32[72,1024]{1,0:T(8,128)S(1)} %collective-permute-done.7.refs_3_) | copy-start | bytes 884740
  234.2 17.1 %copy-start.10 = (f32[144,1536]{1,0:T(8,128)}, f32[144,1536]{1,0:T(8,128)S(1)}, u32[]{:S(2)}) copy-start(f32[144,1536]{1,0:T(8,128)S(1)} %collective-permute-done.8.refs_6_.refs_2_.refs_7_) | copy-start | bytes 2654212
  251.3 7.8 %copy-start.31 = (f32[1152]{0:T(1024)S(1)}, f32[1152]{0:T(1024)}, u32[]{:S(2)}) copy-start(f32[1152]{0:T(1024)} %param.36) | copy-start | bytes 13828
  255.0 54.4 %collective-permute-start.13 = (f32[1152,768]{1,0:T(8,128)}, f32[1152,768]{1,0:T(8,128)}, u32[]{:S(2)}, u32[]{:S(2)}) collective-permute-start(f32[1152,768]{1,0:T(8,128)} %bitcast.49), channel_id=1, source_target_pairs={{0,1},{1,0},{2,3},{3,2},{4,5},{5,4},{6,7},{7,6},{8,9},{9,8},{10,11... | collective-permute-start | bytes 10616840 | tf_op jit(solution)/shard_map/ppermute | solution.py:1023
  256.3 53.1 %collective-permute-start.14 = (f32[1152,384]{1,0:T(8,128)}, f32[1152,384]{1,0:T(8,128)S(1)}, u32[]{:S(2)}, u32[]{:S(2)}) collective-permute-start(f32[1152,384]{1,0:T(8,128)} %bitcast.11), channel_id=1, source_target_pairs={{0,4},{1,5},{2,6},{3,7},{4,0},{5,1},{6,2},{7,3},{8,12},{9,13},{10,... | collective-permute-start | bytes 5308424 | tf_op jit(solution)/shard_map/ppermute | solution.py:1023
  256.7 52.7 %collective-permute-start.12 = (f32[144,2048]{1,0:T(8,128)}, f32[144,2048]{1,0:T(8,128)S(1)}, u32[]{:S(2)}, u32[]{:S(2)}) collective-permute-start(f32[144,2048]{1,0:T(8,128)} %get-tuple-element.365), channel_id=1, source_target_pairs={{0,2},{1,3},{2,0},{3,1},{4,6},{5,7},{6,4},{7,5},{8,10},{9,11},{10,... | collective-permute-start | bytes 3538952 | tf_op jit(solution)/shard_map/ppermute | solution.py:1023
  257.5 51.9 %collective-permute-start.11 = (f32[72,1536]{1,0:T(8,128)}, f32[72,1536]{1,0:T(8,128)S(1)}, u32[]{:S(2)}, u32[]{:S(2)}) collective-permute-start(f32[72,1536]{1,0:T(8,128)} %get-tuple-element.364), channel_id=1, source_target_pairs={{0,4},{1,5},{2,6},{3,7},{4,0},{5,1},{6,2},{7,3},{8,12},{9,13},{10,... | collective-permute-start | bytes 1327112 | tf_op jit(solution)/shard_map/ppermute | solution.py:1023
  259.7 47.8 %collective-permute-start.10 = (f32[36,1024]{1,0:T(8,128)}, f32[36,1024]{1,0:T(8,128)S(1)}, u32[]{:S(2)}, u32[]{:S(2)}) collective-permute-start(f32[36,1024]{1,0:T(8,128)} %get-tuple-element.363), channel_id=1, source_target_pairs={{0,8},{1,9},{2,10},{3,11},{4,12},{5,13},{6,14},{7,15},{8,0},{9,1},... | collective-permute-start | bytes 442376 | tf_op jit(solution)/shard_map/ppermute | solution.py:1023
  307.5 9.1 %copy-start.27 = (f32[36,1024]{1,0:T(8,128)}, f32[36,1024]{1,0:T(8,128)S(1)}, u32[]{:S(2)}) copy-start(f32[36,1024]{1,0:T(8,128)S(1)} %collective-permute-done.10.refs_4_) | copy-start | bytes 442372
  316.6 35.9 %collective-permute-start.15 = (f32[576,2304]{1,0:T(8,128)}, f32[576,2304]{1,0:T(8,128)}, u32[]{:S(2)}, u32[]{:S(2)}) collective-permute-start(f32[576,2304]{1,0:T(8,128)} %get-tuple-element.387), channel_id=1, source_target_pairs={{0,16},{16,0},{1,17},{17,1},{2,18},{18,2},{3,19},{19,3},{4,20},{20... | collective-permute-start | bytes 15925256 | tf_op jit(solution)/shard_map/ppermute | solution.py:1025
  316.6 35.9 %collective-permute-start.18 = (f32[576,768]{1,0:T(8,128)}, f32[576,768]{1,0:T(8,128)S(1)}, u32[]{:S(2)}, u32[]{:S(2)}) collective-permute-start(f32[576,768]{1,0:T(8,128)} %get-tuple-element.390), channel_id=1, source_target_pairs={{0,2},{1,3},{2,0},{3,1},{4,6},{5,7},{6,4},{7,5},{8,10},{9,11},{10,... | collective-permute-start | bytes 5308424 | tf_op jit(solution)/shard_map/ppermute | solution.py:1023
  322.2 24.1 %collective-permute-start.19 = (f32[576,384]{1,0:T(8,128)}, f32[576,384]{1,0:T(8,128)S(1)}, u32[]{:S(2)}, u32[]{:S(2)}) collective-permute-start(f32[576,384]{1,0:T(8,128)} %get-tuple-element.391), channel_id=1, source_target_pairs={{0,1},{1,0},{2,3},{3,2},{4,5},{5,4},{6,7},{7,6},{8,9},{9,8},{10,11... | collective-permute-start | bytes 2654216 | tf_op jit(solution)/shard_map/ppermute | solution.py:1023
  323.7 22.7 %collective-permute-start.17 = (f32[72,2048]{1,0:T(8,128)}, f32[72,2048]{1,0:T(8,128)}, u32[]{:S(2)}, u32[]{:S(2)}) collective-permute-start(f32[72,2048]{1,0:T(8,128)} %get-tuple-element.389), channel_id=1, source_target_pairs={{0,4},{1,5},{2,6},{3,7},{4,0},{5,1},{6,2},{7,3},{8,12},{9,13},{10,... | collective-permute-start | bytes 1769480 | tf_op jit(solution)/shard_map/ppermute | solution.py:1023
  324.1 22.2 %collective-permute-start.16 = (f32[36,1536]{1,0:T(8,128)}, f32[36,1536]{1,0:T(8,128)S(1)}, u32[]{:S(2)}, u32[]{:S(2)}) collective-permute-start(f32[36,1536]{1,0:T(8,128)} %get-tuple-element.388), channel_id=1, source_target_pairs={{0,8},{1,9},{2,10},{3,11},{4,12},{5,13},{6,14},{7,15},{8,0},{9,1},... | collective-permute-start | bytes 663560 | tf_op jit(solution)/shard_map/ppermute | solution.py:1023
  346.3 17.1 %copy-start.24 = (f32[36,1536]{1,0:T(8,128)}, f32[36,1536]{1,0:T(8,128)S(1)}, u32[]{:S(2)}) copy-start(f32[36,1536]{1,0:T(8,128)S(1)} %collective-permute-done.16.refs_9_) | copy-start | bytes 663556
  346.4 17.0 %copy-start.11 = (f32[576,384]{1,0:T(8,128)}, f32[576,384]{1,0:T(8,128)S(1)}, u32[]{:S(2)}) copy-start(f32[576,384]{1,0:T(8,128)S(1)} %collective-permute-done.19.refs_9_.refs_6_.refs_22_) | copy-start | bytes 2654212
  352.4 11.0 %copy-start.6 = (f32[576,768]{1,0:T(8,128)}, f32[576,768]{1,0:T(8,128)S(1)}, u32[]{:S(2)}) copy-start(f32[576,768]{1,0:T(8,128)S(1)} %collective-permute-done.18.refs_6_.refs_2_.refs_17_) | copy-start | bytes 5308420
  367.5 39.8 %collective-permute-start.20 = (f32[576,2304]{1,0:T(8,128)}, f32[576,2304]{1,0:T(8,128)}, u32[]{:S(2)}, u32[]{:S(2)}) collective-permute-start(f32[576,2304]{1,0:T(8,128)} %get-tuple-element.407), channel_id=1, source_target_pairs={{0,16},{16,0},{1,17},{17,1},{2,18},{18,2},{3,19},{19,3},{4,20},{20... | collective-permute-start | bytes 15925256 | tf_op jit(solution)/shard_map/ppermute | solution.py:1025
  367.5 39.7 %collective-permute-start.24 = (f32[288,2304]{1,0:T(8,128)}, f32[288,2304]{1,0:T(8,128)}, u32[]{:S(2)}, u32[]{:S(2)}) collective-permute-start(f32[288,2304]{1,0:T(8,128)} %get-tuple-element.411), channel_id=1, source_target_pairs={{0,1},{1,0},{2,3},{3,2},{4,5},{5,4},{6,7},{7,6},{8,9},{9,8},{10,11... | collective-permute-start | bytes 7962632 | tf_op jit(solution)/shard_map/ppermute | solution.py:1023
  372.2 29.5 %collective-permute-start.22 = (f32[288,768]{1,0:T(8,128)}, f32[288,768]{1,0:T(8,128)S(1)}, u32[]{:S(2)}, u32[]{:S(2)}) collective-permute-start(f32[288,768]{1,0:T(8,128)} %get-tuple-element.409), channel_id=1, source_target_pairs={{0,4},{1,5},{2,6},{3,7},{4,0},{5,1},{6,2},{7,3},{8,12},{9,13},{10,... | collective-permute-start | bytes 2654216 | tf_op jit(solution)/shard_map/ppermute | solution.py:1023
  374.2 26.6 %collective-permute-start.23 = (f32[288,384]{1,0:T(8,128)}, f32[288,384]{1,0:T(8,128)S(1)}, u32[]{:S(2)}, u32[]{:S(2)}) collective-permute-start(f32[288,384]{1,0:T(8,128)} %get-tuple-element.410), channel_id=1, source_target_pairs={{0,2},{1,3},{2,0},{3,1},{4,6},{5,7},{6,4},{7,5},{8,10},{9,11},{10,... | collective-permute-start | bytes 1327112 | tf_op jit(solution)/shard_map/ppermute | solution.py:1023
  375.0 25.9 %collective-permute-start.21 = (f32[36,2048]{1,0:T(8,128)}, f32[36,2048]{1,0:T(8,128)S(1)}, u32[]{:S(2)}, u32[]{:S(2)}) collective-permute-start(f32[36,2048]{1,0:T(8,128)} %get-tuple-element.408), channel_id=1, source_target_pairs={{0,8},{1,9},{2,10},{3,11},{4,12},{5,13},{6,14},{7,15},{8,0},{9,1},... | collective-permute-start | bytes 884744 | tf_op jit(solution)/shard_map/ppermute | solution.py:1023
  400.9 15.9 %copy-start.23 = (f32[36,2048]{1,0:T(8,128)}, f32[36,2048]{1,0:T(8,128)S(1)}, u32[]{:S(2)}) copy-start(f32[36,2048]{1,0:T(8,128)S(1)} %collective-permute-done.21.refs_14_) | copy-start | bytes 884740
  400.9 15.9 %copy-start.17 = (f32[288,384]{1,0:T(8,128)}, f32[288,384]{1,0:T(8,128)S(1)}, u32[]{:S(2)}) copy-start(f32[288,384]{1,0:T(8,128)S(1)} %collective-permute-done.23.refs_7_.refs_23_) | copy-start | bytes 1327108
  401.7 15.1 %copy-start.13 = (f32[288,768]{1,0:T(8,128)}, f32[288,768]{1,0:T(8,128)S(1)}, u32[]{:S(2)}) copy-start(f32[288,768]{1,0:T(8,128)S(1)} %collective-permute-done.22.refs_3_.refs_18_) | copy-start | bytes 2654212
  416.8 10.1 %copy-start.19 = (f32[4,10368]{1,0:T(4,128)S(1)}, f32[4,10368]{1,0:T(4,128)}, u32[]{:S(2)}) copy-start(f32[4,10368]{1,0:T(4,128)} %payload.1) | copy-start | bytes 497668
  420.8 46.5 %collective-permute-start.28 = (f32[288,2304]{1,0:T(8,128)}, f32[288,2304]{1,0:T(8,128)}, u32[]{:S(2)}, u32[]{:S(2)}) collective-permute-start(f32[288,2304]{1,0:T(8,128)} %get-tuple-element.436), channel_id=1, source_target_pairs={{0,1},{1,0},{2,3},{3,2},{4,5},{5,4},{6,7},{7,6},{8,9},{9,8},{10,11... | collective-permute-start | bytes 7962632 | tf_op jit(solution)/shard_map/ppermute | solution.py:1023
  422.8 39.5 %collective-permute-start.27 = (f32[144,2304]{1,0:T(8,128)}, f32[144,2304]{1,0:T(8,128)S(1)}, u32[]{:S(2)}, u32[]{:S(2)}) collective-permute-start(f32[144,2304]{1,0:T(8,128)} %get-tuple-element.435), channel_id=1, source_target_pairs={{0,2},{1,3},{2,0},{3,1},{4,6},{5,7},{6,4},{7,5},{8,10},{9,11},{10,... | collective-permute-start | bytes 3981320 | tf_op jit(solution)/shard_map/ppermute | solution.py:1023
  424.0 38.4 %collective-permute-start.25 = (f32[144,768]{1,0:T(8,128)}, f32[144,768]{1,0:T(8,128)S(1)}, u32[]{:S(2)}, u32[]{:S(2)}) collective-permute-start(f32[144,768]{1,0:T(8,128)} %get-tuple-element.433), channel_id=1, source_target_pairs={{0,8},{1,9},{2,10},{3,11},{4,12},{5,13},{6,14},{7,15},{8,0},{9,1},... | collective-permute-start | bytes 1327112 | tf_op jit(solution)/shard_map/ppermute | solution.py:1023
  425.0 37.3 %collective-permute-start.26 = (f32[144,384]{1,0:T(8,128)}, f32[144,384]{1,0:T(8,128)S(1)}, u32[]{:S(2)}, u32[]{:S(2)}) collective-permute-start(f32[144,384]{1,0:T(8,128)} %get-tuple-element.434), channel_id=1, source_target_pairs={{0,8},{1,9},{2,10},{3,11},{4,12},{5,13},{6,14},{7,15},{8,0},{9,1},... | collective-permute-start | bytes 663560 | tf_op jit(solution)/shard_map/ppermute | solution.py:1023
  426.9 35.4 %collective-permute-start.29 = (f32[4,10368]{1,0:T(4,128)S(1)}, f32[4,10368]{1,0:T(4,128)S(1)}, u32[]{:S(2)}, u32[]{:S(2)}) collective-permute-start(f32[4,10368]{1,0:T(4,128)S(1)} %copy-done.19), channel_id=1, source_target_pairs={{0,8},{1,9},{2,10},{3,11},{4,12},{5,13},{6,14},{7,15},{8,0},{9,1},... | collective-permute-start | bytes 497672 | tf_op jit(solution)/shard_map/ppermute | solution.py:1030
  462.3 8.8 %copy-start.25 = (f32[144,384]{1,0:T(8,128)}, f32[144,384]{1,0:T(8,128)S(1)}, u32[]{:S(2)}) copy-start(f32[144,384]{1,0:T(8,128)S(1)} %collective-permute-done.26.refs_24_) | copy-start | bytes 663556
  462.3 8.8 %copy-start.20 = (f32[144,768]{1,0:T(8,128)}, f32[144,768]{1,0:T(8,128)S(1)}, u32[]{:S(2)}) copy-start(f32[144,768]{1,0:T(8,128)S(1)} %collective-permute-done.25.refs_19_) | copy-start | bytes 1327108
  462.3 5.0 copy-start.7
  471.1 25.7 %collective-permute-start.31 = (f32[144,2304]{1,0:T(8,128)}, f32[144,2304]{1,0:T(8,128)S(1)}, u32[]{:S(2)}, u32[]{:S(2)}) collective-permute-start(f32[144,2304]{1,0:T(8,128)} %get-tuple-element.454), channel_id=1, source_target_pairs={{0,2},{1,3},{2,0},{3,1},{4,6},{5,7},{6,4},{7,5},{8,10},{9,11},{10,... | collective-permute-start | bytes 3981320 | tf_op jit(solution)/shard_map/ppermute | solution.py:1023
  472.9 23.9 %collective-permute-start.30 = (f32[72,2304]{1,0:T(8,128)}, f32[72,2304]{1,0:T(8,128)S(1)}, u32[]{:S(2)}, u32[]{:S(2)}) collective-permute-start(f32[72,2304]{1,0:T(8,128)} %get-tuple-element.453), channel_id=1, source_target_pairs={{0,4},{1,5},{2,6},{3,7},{4,0},{5,1},{6,2},{7,3},{8,12},{9,13},{10,... | collective-permute-start | bytes 1990664 | tf_op jit(solution)/shard_map/ppermute | solution.py:1023
  475.3 21.5 %collective-permute-start.32 = (f32[8,10368]{1,0:T(8,128)S(1)}, f32[8,10368]{1,0:T(8,128)S(1)}, u32[]{:S(2)}, u32[]{:S(2)}) collective-permute-start(f32[8,10368]{1,0:T(8,128)S(1)} %pad_maximum_fusion.2), channel_id=1, source_target_pairs={{0,4},{1,5},{2,6},{3,7},{4,0},{5,1},{6,2},{7,3},{8,12},{9,13},{10,... | collective-permute-start | bytes 995336 | tf_op jit(solution)/shard_map/ppermute | solution.py:1030
  501.5 23.9 %collective-permute-start.34 = (f32[72,2304]{1,0:T(8,128)}, f32[72,2304]{1,0:T(8,128)S(1)}, u32[]{:S(2)}, u32[]{:S(2)}) collective-permute-start(f32[72,2304]{1,0:T(8,128)} %get-tuple-element.467), channel_id=1, source_target_pairs={{0,4},{1,5},{2,6},{3,7},{4,0},{5,1},{6,2},{7,3},{8,12},{9,13},{10,... | collective-permute-start | bytes 1990664 | tf_op jit(solution)/shard_map/ppermute | solution.py:1023
  503.2 22.1 %collective-permute-start.35 = (f32[16,10368]{1,0:T(8,128)S(1)}, f32[16,10368]{1,0:T(8,128)S(1)}, u32[]{:S(2)}, u32[]{:S(2)}) collective-permute-start(f32[16,10368]{1,0:T(8,128)S(1)} %pad_maximum_fusion.1), channel_id=1, source_target_pairs={{0,2},{1,3},{2,0},{3,1},{4,6},{5,7},{6,4},{7,5},{8,10},{9,11},{10,... | collective-permute-start | bytes 1990664 | tf_op jit(solution)/shard_map/ppermute | solution.py:1030
  503.9 20.8 %collective-permute-start.33 = (f32[36,2304]{1,0:T(8,128)}, f32[36,2304]{1,0:T(8,128)S(1)}, u32[]{:S(2)}, u32[]{:S(2)}) collective-permute-start(f32[36,2304]{1,0:T(8,128)} %get-tuple-element.466), channel_id=1, source_target_pairs={{0,8},{1,9},{2,10},{3,11},{4,12},{5,13},{6,14},{7,15},{8,0},{9,1},... | collective-permute-start | bytes 995336 | tf_op jit(solution)/shard_map/ppermute | solution.py:1023
  526.2 20.9 %copy-start.4 = (f32[32,10368]{1,0:T(8,128)}, f32[32,10368]{1,0:T(8,128)S(1)}, u32[]{:S(2)}) copy-start(f32[32,10368]{1,0:T(8,128)S(1)} %pad_maximum_fusion.refs_0_.refs_4_.refs_8_) | copy-start | bytes 3981316
  529.1 17.9 %collective-permute-start.37 = (f32[32,10368]{1,0:T(8,128)S(1)}, f32[32,10368]{1,0:T(8,128)}, u32[]{:S(2)}, u32[]{:S(2)}) collective-permute-start(f32[32,10368]{1,0:T(8,128)S(1)} %pad_maximum_fusion.refs_0_.refs_4_.refs_8_), channel_id=1, source_target_pairs={{0,1},{1,0},{2,3},{3,2},{4,5},{5,4},{6,7},{7,6},{8,9},{9,8},{10,11... | collective-permute-start | bytes 3981320 | tf_op jit(solution)/shard_map/ppermute | solution.py:1030
  529.1 17.6 %collective-permute-start.36 = (f32[36,2304]{1,0:T(8,128)}, f32[36,2304]{1,0:T(8,128)S(1)}, u32[]{:S(2)}, u32[]{:S(2)}) collective-permute-start(f32[36,2304]{1,0:T(8,128)} %add.280), channel_id=1, source_target_pairs={{0,8},{1,9},{2,10},{3,11},{4,12},{5,13},{6,14},{7,15},{8,0},{9,1},... | collective-permute-start | bytes 995336 | tf_op jit(solution)/shard_map/ppermute | solution.py:1023
  547.0 5.1 collective-permute-start.38
  547.0 5.3 collective-permute-start.39
  552.3 20.9 %copy-start.1 = (bf16[1001,1152]{1,0:T(8,128)(2,1)S(1)}, bf16[1001,1152]{1,0:T(8,128)(2,1)}, u32[]{:S(2)}) copy-start(bf16[1001,1152]{1,0:T(8,128)(2,1)} %param.26) | copy-start | bytes 6918916
  (12 other events, 21.6 us)

commit v7 on v6

--- a/solution.py
+++ b/solution.py
@@ -763,6 +763,14 @@
     )(tile_item, *sums)
 
 
+def chosen_sums(select, values, dims):
+    high = values.astype(BF16)
+    rest = values - high.astype(F32)
+    middle = rest.astype(BF16)
+    low = (rest - middle.astype(F32)).astype(BF16)
+    return dot(select, high, dims) + (dot(select, middle, dims) + dot(select, low, dims))
+
+
 def modulation_back_body(me_ref, *refs, count):
     part_refs, cond_refs, sum_refs = refs[:count], refs[count : 2 * count], refs[2 * count : 3 * count]
     label_ref, w_ref, grad_ref, bias_ref, table_ref, own_sums_ref, act_ref, own_ref, total_ref = refs[3 * count :]
@@ -789,7 +797,7 @@
             item = lax.broadcasted_iota(jnp.int32, (items, rows), 0)
             source = lax.broadcasted_iota(jnp.int32, (items, rows), 1)
             select = (lax.rem(source, jnp.full_like(source, items)) == item).astype(F32)
-            part = dot(select, sum_ref[...], NN, HIGHEST)
+            part = chosen_sums(select.astype(BF16), sum_ref[...], NN)
             sums = part if sums is None else sums + part
         own_sums_ref[...] = sums
 
@@ -806,11 +814,7 @@
         grad = total_ref[...].T * (gate * (1.0 + cond * (1.0 - gate)))
         classes = table_ref.shape[0]
         select = (label_ref[...] == lax.broadcasted_iota(jnp.int32, (grad.shape[0], classes), 1)).astype(F32).astype(BF16)
-        high = grad.astype(BF16)
-        rest = grad - high.astype(F32)
-        middle = rest.astype(BF16)
-        low = (rest - middle.astype(F32)).astype(BF16)
-        table_ref[...] = dot(select, high, TN) + (dot(select, middle, TN) + dot(select, low, TN))
+        table_ref[...] = chosen_sums(select, grad, TN)
 
 
 def modulation_back_call(me, parts, used, w, classes, shard, items):

time: 578 us -> 578 us (level)
  transfers between devices with their start and end apart: 40 -> 40, of which waited for: 16 -> 14; matrix products, arithmetic and copies ran while one was open for 1% -> 1% of each run, Pallas kernels for 33% -> 33%
where the time goes in v7:
time: 578 us; the launch traced here: 574 us
  Pallas kernels  362 us (63%)
  waiting for transfers between devices  115 us (20%)
  starting transfers between devices  58.4 us (10%)
  local copies, waits for them, and re-layouts  20 us (3%)
  matrix products  7.72 us (1%)
  other arithmetic  7.58 us (1%)
    ppermute x28, waiting for transfers between devices, round(): lax.ppermute(send, ('stream', 'batch'), self.pairs(chunk.stage, chunk.lead))  64.2 us
    ppermute x4, waiting for transfers between devices, round(): lax.ppermute(piece, ('stream', 'batch'), pairs)  50.7 us
    ppermute x28, starting transfers between devices, round(): lax.ppermute(send, ('stream', 'batch'), self.pairs(chunk.stage, chunk.lead))  50.5 us
    pallas_call x3, Pallas kernels, hidden_call(): call(hidden_body, 'hidden', 6 * tokens * width * count, 6 * tokens * widt...  46.6 us
    pallas_call x5, Pallas kernels, columns_call(): call(functools.partial(columns_body, right=right, both=both), name, 2 * t...  38.1 us
    pallas_call x9, Pallas kernels, add_call(): call(functools.partial(add_body, plans=plans), 'add', moved // 4, moved,...  32 us
    pallas_call x1, Pallas kernels, middle_back_call(): call(middle_back_body, 'middle_back', 2 * tokens * width * (hidden + widt...  30.2 us
    pallas_call x2, Pallas kernels, attention_back_call(): call(attention_back_body, 'attention_back', 2 * 2 * heads * tokens * GROU...  27.9 us
  transfers between devices with their start and end apart: 40, of which 14 were waited for; matrix products, arithmetic and copies ran while one was open for 1% of the time, Pallas kernels for 33%

profile of v7, /device:TPU:0, one launch (start us, length us, event | category | flops | bytes accessed | tf_op | source)
XLA Modules:
  0.0 573.9 jit_solution(14983538105229849375)
XLA Ops:
  5.0 7.7 %convolution_add_fusion = f32[4,6912]{1,0:T(4,128)S(1)} fusion(bf16[1152,6912]{1,0:T(8,128)(2,1)} %refs_13_.1, f32[6912]{0:T(1024)} %param.28, f32[4,1152]{1,0:T(4,128)S(1)} %maximum_add_fusion.cond_ref), kind=kOutput, calls=%fused_computation.3 | convolution fusion | flops 63751680 | bytes 16081920 | tf_op jit(solution)/shard_map/dot_general | solution.py:28
  18.2 1.7 fusion.away_ref
  20.0 1.7 fusion.1.own_ref
  24.0 16.0 %qkv.1 = (bf16[1024,1152]{1,0:T(8,128)(2,1)}, bf16[3456,1024]{1,0:T(8,128)(2,1)}) custom-call(bf16[1024,1152]{1,0:T(8,128)(2,1)} %bitcast.41, f32[4,6,1152]{2,1,0:T(8,128)} %reshape.311.mod_ref, bf16[1152,3456]{1,0:T(8,128)(2,1)} %w_ref.7, f32[1,3456]{1,0:T(1,128)} %broadcast_in_dim.132.b_ref), custom_call_target="tpu_custom_call" | custom-call | flops 1019215872 | bytes 2469888 | tf_op jit(solution)/shard_map/qkv/pallas_call | solution.py:73
  40.0 26.4 %attention.1 = (bf16[16,1024,1024]{2,1,0:T(8,128)(2,1)}, f32[16,72,1024]{2,1,0:T(8,128)}, bf16[1152,1024]{1,0:T(8,128)(2,1)}) custom-call(s32[1]{0:T(128)} %bitcast.1.flag_ref, bf16[3456,1024]{1,0:T(8,128)(2,1)} %get-tuple-element.255.q_ref.k_ref.v_ref, bf16[3456,1024]{1,0:T(8,128)(2,1)} %get-tuple-element.255.q_ref.k_ref.v_ref, ...), custom_call_target="tpu_custom_call" | custom-call | flops 2147483648 | bytes 5963776 | tf_op jit(solution)/shard_map/attention/pallas_call | solution.py:139
  66.4 15.1 %middle.1 = (f32[1024,1152]{1,0:T(8,128)}, f32[1024,1152]{1,0:T(8,128)}, bf16[1024,1152]{1,0:T(8,128)(2,1)}, bf16[1024,576]{1,0:T(8,128)(2,1)}, bf16[1024,576]{1...) custom-call(bf16[1152,1024]{1,0:T(8,128)(2,1)} %get-tuple-element.256.om_ref.left_ref, ...), custom_call_target="tpu_custom_call" | custom-call | flops 679477248 | bytes 3833856 | tf_op jit(solution)/shard_map/middle/pallas_call | solution.py:259
  81.5 12.2 %hidden.3 = (bf16[1024,4608]{1,0:T(8,128)(2,1)}, bf16[1024,4608]{1,0:T(8,128)(2,1)}, f32[1,4608]{1,0:T(1,128)}, f32[576,1024]{1,0:T(8,128)}) custom-call(bf16[1024,1152]{1,0:T(8,128)(2,1)} %get-tuple-element.284.h_ref, bf16[1024,576]{1,0:T(8,128)(2,1)} %get-tuple-element.258.away_ref, bf16[1024,1152]{1,0:T(8,128)(2,1)} %get-tuple-element.259.dm_ref, ...), custom_call_target="tpu_custom_call" | custom-call | flops 905969664 | bytes 2588672 | tf_op jit(solution)/shard_map/hidden/pallas_call | solution.py:312
  94.2 15.3 %hidden.4 = (bf16[1024,4608]{1,0:T(8,128)(2,1)}, bf16[1024,4608]{1,0:T(8,128)(2,1)}, f32[1,4608]{1,0:T(1,128)}, f32[576,1536]{1,0:T(8,128)}) custom-call(bf16[1024,1152]{1,0:T(8,128)(2,1)} %get-tuple-element.284.h_ref, bf16[1024,576]{1,0:T(8,128)(2,1)} %get-tuple-element.258.away_ref, ...), custom_call_target="tpu_custom_call", output_to_operand_aliasing={{0}: (6, {}), {1}: (7, {}), {2}: (8, {})} | custom-call | flops 1358954496 | bytes 3440640 | tf_op jit(solution)/shard_map/hidden/pallas_call | solution.py:312
  109.5 4.7 hidden_keep.3
  114.2 9.3 %collective-permute-start.2 = (f32[288,1024]{1,0:T(8,128)}, f32[288,1024]{1,0:T(8,128)S(1)}, u32[]{:S(2)}, u32[]{:S(2)}) collective-permute-start(f32[288,1024]{1,0:T(8,128)} %get-tuple-element.292), channel_id=1, source_target_pairs={{0,1},{1,0},{2,3},{3,2},{4,5},{5,4},{6,7},{7,6},{8,9},{9,8},{10,11... | collective-permute-start | bytes 3538952 | tf_op jit(solution)/shard_map/ppermute | solution.py:1027
  123.5 19.0 %hidden.5 = (bf16[1024,4608]{1,0:T(8,128)(2,1)}, bf16[1024,4608]{1,0:T(8,128)(2,1)}, f32[1,4608]{1,0:T(1,128)}, f32[576,2048]{1,0:T(8,128)}) custom-call(bf16[1024,1152]{1,0:T(8,128)(2,1)} %get-tuple-element.284.h_ref, bf16[1024,576]{1,0:T(8,128)(2,1)} %get-tuple-element.258.away_ref, ...), custom_call_target="tpu_custom_call", output_to_operand_aliasing={{0}: (6, {}), {1}: (7, {}), {2}: (8, {})} | custom-call | flops 1811939328 | bytes 4292608 | tf_op jit(solution)/shard_map/hidden/pallas_call | solution.py:312
  142.6 7.4 %hidden_keep.4 = (f32[288,1536]{1,0:T(8,128)}, f32[288,1536]{1,0:T(8,128)}) custom-call(bf16[1024,576]{1,0:T(8,128)(2,1)} %get-tuple-element.281.refs_0_, bf16[1024,4608]{1,0:T(8,128)(2,1)} %get-tuple-element.322.refs_1_.df_ref, f32[576,1536]{1,0:T(8,128)} %collective-permute-done.1.refs_2_), custom_call_target="tpu_custom_call" | custom-call | flops 226492416 | bytes 1425408 | tf_op jit(solution)/shard_map/hidden_keep/pallas_call | solution.py:607
  150.0 2.1 add.272
  152.2 1.7 collective-permute-start.4
  153.9 7.4 %moved.2 = (bf16[1024,576]{1,0:T(8,128)(2,1)}, bf16[1024,576]{1,0:T(8,128)(2,1)}) custom-call(bf16[1152,1024]{1,0:T(8,128)(2,1)} %get-tuple-element.256.om_ref.left_ref, bf16[1152,576]{1,0:T(8,128)(2,1)} %fusion.away_ref, bf16[1152,576]{1,0:T(8,128)(2,1)} %fusion.1.own_ref), custom_call_target="tpu_custom_call" | custom-call | flops 339738624 | bytes 921600 | tf_op jit(solution)/shard_map/moved/pallas_call | solution.py:675
  161.9 14.0 %rows_send.1 = f32[16,144,1152]{2,1,0:T(8,128)} custom-call(s32[1]{0:T(128)} %bitcast.6.side_ref, s32[3,16]{1,0:T(4,128)} %pad_add_fusion.spot_ref, bf16[1024,4608]{1,0:T(8,128)(2,1)} %get-tuple-element.360.g_ref, bf16[1024,1152]{1,0:T(8,128)(2,1)} %get-tuple-element.259.dm_ref), custom_call_target="tpu_custom_call" | custom-call | flops 679477248 | bytes 2211840 | tf_op jit(solution)/shard_map/rows_send/pallas_call | solution.py:370
  175.9 4.8 collective-permute-done.5.refs_4_.refs_5_.refs_1_.refs_6_
  180.7 8.4 %hidden_keep.5 = (f32[288,2048]{1,0:T(8,128)}, f32[288,2048]{1,0:T(8,128)}) custom-call(bf16[1024,576]{1,0:T(8,128)(2,1)} %get-tuple-element.281.refs_0_, bf16[1024,4608]{1,0:T(8,128)(2,1)} %get-tuple-element.322.refs_1_.df_ref, f32[576,2048]{1,0:T(8,128)} %collective-permute-done.3.refs_2_), custom_call_target="tpu_custom_call" | custom-call | flops 301989888 | bytes 1851392 | tf_op jit(solution)/shard_map/hidden_keep/pallas_call | solution.py:607
  189.1 2.8 add.273
  193.9 1.7 collective-permute-start.7
  196.2 7.3 %moved.3 = (bf16[1024,576]{1,0:T(8,128)(2,1)}, bf16[1024,576]{1,0:T(8,128)(2,1)}) custom-call(bf16[1024,1152]{1,0:T(8,128)(2,1)} %get-tuple-element.329.left_ref, bf16[1152,576]{1,0:T(8,128)(2,1)} %fusion.away_ref, bf16[1152,576]{1,0:T(8,128)(2,1)} %fusion.1.own_ref), custom_call_target="tpu_custom_call" | custom-call | flops 339738624 | bytes 921600 | tf_op jit(solution)/shard_map/moved/pallas_call | solution.py:675
  203.6 30.2 %middle_back.1 = (f32[1024,1152]{1,0:T(8,128)}, bf16[1024,1152]{1,0:T(8,128)(2,1)}, bf16[1152,1024]{1,0:T(8,128)(2,1)}, f32[4,4,1152]{2,1,0:T(4,128)}) custom-call(bf16[1024,4608]{1,0:T(8,128)(2,1)} %get-tuple-element.322.refs_1_.df_ref, bf16[1152,4608]{1,0:T(8,128)(2,1)} %w1_ref.7, f32[1024,1152]{1,0:T(8,128)} %get-tuple-element.323.x1_ref, ...), custom_call_target="tpu_custom_call" | custom-call | flops 1698693120 | bytes 5160960 | tf_op jit(solution)/shard_map/middle_back/pallas_call | solution.py:501
  233.8 17.1 %rows_keep.1 = (f32[8,144,768]{2,1,0:T(8,128)}, f32[8,144,768]{2,1,0:T(8,128)}, f32[8,144,384]{2,1,0:T(8,128)}, f32[8,144,384]{2,1,0:T(8,128)}) custom-call(s32[1]{0:T(128)} %bitcast.8.side_ref, s32[3,16]{1,0:T(4,128)} %pad_add_fusion.1.spot_ref, bf16[1024,4608]{1,0:T(8,128)(2,1)} %get-tuple-element.360.g_ref, bf16[1024,1152]{1,0:T(8,128)(2,1)} %get-tuple-element.259.dm_ref, ...), custom_call_target="tpu_custom_call" | custom-call | flops 679477248 | bytes 3538944 | tf_op jit(solution)/shard_map/rows_keep/pallas_call | solution.py:423
  250.9 3.7 add.274
  259.1 2.9 collective-permute-start.10
  261.9 13.8 %attention_back.2.refs_3_.refs_1_.low_ref = bf16[3,576,1024]{2,1,0:T(8,128)(2,1)} custom-call(s32[1]{0:T(128)} %bitcast.1.flag_ref, bf16[3456,1024]{1,0:T(8,128)(2,1)} %get-tuple-element.255.q_ref.k_ref.v_ref, bf16[3456,1024]{1,0:T(8,128)(2,1)} %get-tuple-element.255.q_ref.k_ref.v_ref, bf16[3456,1024]{1,0:T(8,128)(2,1)} %get-tuple-element.255.q_ref.k_ref.v_ref, ...), custom_call_target="tpu_custom_call" | custom-call | flops 2147483648 | bytes 3866624 | tf_op jit(solution)/shard_map/attention_back/pallas_call | solution.py:212
  275.7 9.8 %first_send.1 = (f32[576,2304]{1,0:T(8,128)}, f32[1,2304]{1,0:T(1,128)}) custom-call(bf16[1024,576]{1,0:T(8,128)(2,1)} %get-tuple-element.356.refs_0_, bf16[1024,1152]{1,0:T(8,128)(2,1)} %get-tuple-element.357.refs_1_, bf16[1024,576]{1,0:T(8,128)(2,1)} %get-tuple-element.358.refs_2_.refs_0_, bf16[3,576,1024]{2,1,0:T(8,128)(2,1)} %attention_back.2.refs_3_.refs_1_.low_ref), custom_call_target="tpu_custom_call" | custom-call | flops 339738624 | bytes 2064384 | tf_op jit(solution)/shard_map/first_send/pallas_call | solution.py:647
  285.5 19.7 %result.1 = (bf16[1024,1152]{1,0:T(8,128)(2,1)}, f32[4,1,1152]{2,1,0:T(1,128)}) custom-call(bf16[1024,4608]{1,0:T(8,128)(2,1)} %get-tuple-element.360.g_ref, bf16[4608,1152]{1,0:T(8,128)(2,1)} %w_ref.6, f32[1,1152]{1,0:T(1,128)} %broadcast_in_dim.141.b_ref, f32[1024,1152]{1,0:T(8,128)} %get-tuple-element.323.x1_ref, f32[4,6,1152]{2,1,0:T(8,128)} %reshape.311.mod_ref, ...), custom_call_target="tpu_custom_call" | custom-call | flops 1358954496 | bytes 3686400 | tf_op jit(solution)/shard_map/result/pallas_call | solution.py:457
  305.2 1.9 collective-permute-done.10.refs_4_
  307.1 2.1 collective-permute-done.11.refs_3_.refs_8_
  310.9 5.4 add.275
  317.0 5.1 collective-permute-start.19
  322.1 1.9 collective-permute-start.17
  324.1 14.1 %attention_back.3.refs_2_.high_ref = bf16[3,576,1024]{2,1,0:T(8,128)(2,1)} custom-call(s32[1]{0:T(128)} %bitcast.1.flag_ref, bf16[3456,1024]{1,0:T(8,128)(2,1)} %get-tuple-element.255.q_ref.k_ref.v_ref, bf16[3456,1024]{1,0:T(8,128)(2,1)} %get-tuple-element.255.q_ref.k_ref.v_ref, bf16[3456,1024]{1,0:T(8,128)(2,1)} %get-tuple-element.255.q_ref.k_ref.v_ref, ...), custom_call_target="tpu_custom_call" | custom-call | flops 2147483648 | bytes 3866624 | tf_op jit(solution)/shard_map/attention_back/pallas_call | solution.py:212
  338.1 8.1 %last_send.1 = (f32[576,2304]{1,0:T(8,128)}, f32[1,2304]{1,0:T(1,128)}) custom-call(bf16[1024,576]{1,0:T(8,128)(2,1)} %get-tuple-element.358.refs_2_.refs_0_, bf16[3,576,1024]{2,1,0:T(8,128)(2,1)} %attention_back.2.refs_3_.refs_1_.low_ref, bf16[3,576,1024]{2,1,0:T(8,128)(2,1)} %attention_back.3.refs_2_.high_ref), custom_call_target="tpu_custom_call" | custom-call | flops 339738624 | bytes 2064384 | tf_op jit(solution)/shard_map/last_send/pallas_call | solution.py:607
  346.3 2.3 collective-permute-done.18.refs_6_.refs_2_.refs_17_
  348.6 11.0 %first_keep.1 = (f32[288,2304]{1,0:T(8,128)}, f32[288,2304]{1,0:T(8,128)}) custom-call(bf16[1024,576]{1,0:T(8,128)(2,1)} %get-tuple-element.403.refs_0_, bf16[1024,1152]{1,0:T(8,128)(2,1)} %get-tuple-element.357.refs_1_, bf16[1024,576]{1,0:T(8,128)(2,1)} %get-tuple-element.404.refs_2_.refs_0_, bf16[3,576,1024]{2,1,0:T(8,128)(2,1)} %attention_back.2.refs_3_.refs_1_.low_ref, ...), custom_call_target="tpu_custom_call" | custom-call | flops 339738624 | bytes 2064384 | tf_op jit(solution)/shard_map/first_keep/pallas_call | solution.py:647
  359.6 4.1 add.276
  363.7 3.2 collective-permute-start.20
  366.9 5.3 collective-permute-start.24
  372.2 2.0 collective-permute-start.23
  375.8 18.2 %first_back.1 = (f32[1024,1152]{1,0:T(8,128)}, f32[4,2,1152]{2,1,0:T(2,128)}) custom-call(bf16[3,576,1024]{2,1,0:T(8,128)(2,1)} %attention_back.2.refs_3_.refs_1_.low_ref, bf16[3,576,1024]{2,1,0:T(8,128)(2,1)} %attention_back.3.refs_2_.high_ref, bf16[1152,3456]{1,0:T(8,128)(2,1)} %w_ref.7, bf16[1024,1152]{1,0:T(8,128)(2,1)} %bitcast.43, ...), custom_call_target="tpu_custom_call" | custom-call | flops 1019215872 | bytes 3354624 | tf_op jit(solution)/shard_map/first_back/pallas_call | solution.py:707
  393.9 1.8 payload.1
  395.8 3.3 collective-permute-done.21.refs_14_
  399.7 7.5 %collective-permute-done.24.refs_9_.refs_1_ = f32[288,2304]{1,0:T(8,128)} collective-permute-done((f32[288,2304]{1,0:T(8,128)}, f32[288,2304]{1,0:T(8,128)}, u32[]{:S(2)}, u32[]{:S(2)}) %collective-permute-start.24) | collective-permute-done | bytes 2654240 | tf_op jit(solution)/shard_map/ppermute | solution.py:1027
  407.2 9.5 %last_keep.1 = (f32[288,2304]{1,0:T(8,128)}, f32[288,2304]{1,0:T(8,128)}) custom-call(bf16[1024,576]{1,0:T(8,128)(2,1)} %get-tuple-element.404.refs_2_.refs_0_, bf16[3,576,1024]{2,1,0:T(8,128)(2,1)} %attention_back.2.refs_3_.refs_1_.low_ref, bf16[3,576,1024]{2,1,0:T(8,128)(2,1)} %attention_back.3.refs_2_.high_ref, f32[576,2304]{1,0:T(8,128)} %collective-permute-done.20.refs_3_), custom_call_target="tpu_custom_call" | custom-call | flops 339738624 | bytes 2064384 | tf_op jit(solution)/shard_map/last_keep/pallas_call | solution.py:607
  416.8 3.9 add.277
  420.7 2.0 collective-permute-start.28
  427.2 34.1 %collective-permute-done.29 = f32[4,10368]{1,0:T(4,128)S(1)} collective-permute-done((f32[4,10368]{1,0:T(4,128)S(1)}, f32[4,10368]{1,0:T(4,128)S(1)}, u32[]{:S(2)}, u32[]{:S(2)}) %collective-permute-start.29) | collective-permute-done | bytes 165920 | tf_op jit(solution)/shard_map/ppermute | solution.py:1034
  461.4 4.8 collective-permute-done.28.refs_4_.refs_5_.refs_1_.refs_6_
  466.3 3.7 add.278
  470.7 3.2 collective-permute-start.30
  474.9 4.9 assemble.2
  479.8 16.6 %collective-permute-done.32 = f32[8,10368]{1,0:T(8,128)S(1)} collective-permute-done((f32[8,10368]{1,0:T(8,128)S(1)}, f32[8,10368]{1,0:T(8,128)S(1)}, u32[]{:S(2)}, u32[]{:S(2)}) %collective-permute-start.32) | collective-permute-done | bytes 331808 | tf_op jit(solution)/shard_map/ppermute | solution.py:1034
  497.7 3.3 add.279
  501.4 1.7 collective-permute-start.35
  503.2 1.7 collective-permute-start.33
  504.9 18.7 %collective-permute-done.33.refs_4_ = f32[36,2304]{1,0:T(8,128)S(1)} collective-permute-done((f32[36,2304]{1,0:T(8,128)}, f32[36,2304]{1,0:T(8,128)S(1)}, u32[]{:S(2)}, u32[]{:S(2)}) %collective-permute-start.33) | collective-permute-done | bytes 331808 | tf_op jit(solution)/shard_map/ppermute | solution.py:1027
  523.6 2.1 collective-permute-done.34.refs_3_.refs_8_
  526.5 3.0 add.280
  529.5 2.1 collective-permute-start.36
  531.6 16.2 %collective-permute-done.36.refs_9_ = f32[36,2304]{1,0:T(8,128)S(1)} collective-permute-done((f32[36,2304]{1,0:T(8,128)}, f32[36,2304]{1,0:T(8,128)S(1)}, u32[]{:S(2)}, u32[]{:S(2)}) %collective-permute-start.36) | collective-permute-done | bytes 331808 | tf_op jit(solution)/shard_map/ppermute | solution.py:1027
  549.1 3.7 assemble.3
  553.2 15.4 %modulation_back.1 = (f32[36,6912]{1,0:T(8,128)}, f32[1,6912]{1,0:T(1,128)}, f32[1001,1152]{1,0:T(8,128)}, f32[4,2304]{1,0:T(4,128)}) custom-call(s32[1]{0:T(128)} %bitcast.17.me_ref, f32[32,10368]{1,0:T(8,128)} %copy-done.4, f32[32,10368]{1,0:T(8,128)} %collective-permute-done.37.refs_1_.refs_5_.refs_9_, ...), custom_call_target="tpu_custom_call" | custom-call | flops 509607936 | bytes 1990656 | tf_op jit(solution)/shard_map/modulation_back/pallas_call | solution.py:826
  (181 shorter events, 39.6 us)
Async XLA Ops:
  5.0 8.8 %copy-start.28 = (f32[2304]{0:T(1024)S(1)}, f32[2304]{0:T(1024)}, u32[]{:S(2)}) copy-start(f32[2304]{0:T(1024)} %param.30) | copy-start | bytes 27652
  5.0 9.4 %copy-start.34 = (s32[4,16]{1,0:T(4,128)S(1)}, s32[4,16]{1,0:T(4,128)}, u32[]{:S(2)}) copy-start(s32[4,16]{1,0:T(4,128)} %param.24) | copy-start | bytes 772
  12.7 9.0 %copy-start.32 = (s32[1,1024]{1,0:T(1,128)S(1)}, s32[1,1024]{1,0:T(1,128)}, u32[]{:S(2)}) copy-start(s32[1,1024]{1,0:T(1,128)} %param.25) | copy-start | bytes 12292
  12.7 10.0 %copy-start.30 = (f32[1152]{0:T(1024)S(1)}, f32[1152]{0:T(1024)}, u32[]{:S(2)}) copy-start(f32[1152]{0:T(1024)} %param.32) | copy-start | bytes 13828
  12.7 10.6 %copy-start.29 = (f32[4608]{0:T(1024)S(1)}, f32[4608]{0:T(1024)}, u32[]{:S(2)}) copy-start(f32[4608]{0:T(1024)} %param.34) | copy-start | bytes 55300
  93.7 15.8 %collective-permute-start = (f32[576,1024]{1,0:T(8,128)}, f32[576,1024]{1,0:T(8,128)}, u32[]{:S(2)}, u32[]{:S(2)}) collective-permute-start(f32[576,1024]{1,0:T(8,128)} %get-tuple-element.275), channel_id=1, source_target_pairs={{0,16},{16,0},{1,17},{17,1},{2,18},{18,2},{3,19},{19,3},{4,20},{20... | collective-permute-start | bytes 7077896 | tf_op jit(solution)/shard_map/ppermute | solution.py:1029
  114.2 28.4 %collective-permute-start.1 = (f32[576,1536]{1,0:T(8,128)}, f32[576,1536]{1,0:T(8,128)}, u32[]{:S(2)}, u32[]{:S(2)}) collective-permute-start(f32[576,1536]{1,0:T(8,128)} %get-tuple-element.291), channel_id=1, source_target_pairs={{0,16},{16,0},{1,17},{17,1},{2,18},{18,2},{3,19},{19,3},{4,20},{20... | collective-permute-start | bytes 10616840 | tf_op jit(solution)/shard_map/ppermute | solution.py:1029
  114.2 28.4 %collective-permute-start.2 = (f32[288,1024]{1,0:T(8,128)}, f32[288,1024]{1,0:T(8,128)S(1)}, u32[]{:S(2)}, u32[]{:S(2)}) collective-permute-start(f32[288,1024]{1,0:T(8,128)} %get-tuple-element.292), channel_id=1, source_target_pairs={{0,1},{1,0},{2,3},{3,2},{4,5},{5,4},{6,7},{7,6},{8,9},{9,8},{10,11... | collective-permute-start | bytes 3538952 | tf_op jit(solution)/shard_map/ppermute | solution.py:1027
  142.6 7.4 %copy-start.5 = (f32[288,1024]{1,0:T(8,128)}, f32[288,1024]{1,0:T(8,128)S(1)}, u32[]{:S(2)}) copy-start(f32[288,1024]{1,0:T(8,128)S(1)} %collective-permute-done.2.refs_1_) | copy-start | bytes 3538948
  152.1 28.6 %collective-permute-start.3 = (f32[576,2048]{1,0:T(8,128)}, f32[576,2048]{1,0:T(8,128)}, u32[]{:S(2)}, u32[]{:S(2)}) collective-permute-start(f32[576,2048]{1,0:T(8,128)} %get-tuple-element.306), channel_id=1, source_target_pairs={{0,16},{16,0},{1,17},{17,1},{2,18},{18,2},{3,19},{19,3},{4,20},{20... | collective-permute-start | bytes 14155784 | tf_op jit(solution)/shard_map/ppermute | solution.py:1029
  152.1 28.6 %collective-permute-start.5 = (f32[288,1536]{1,0:T(8,128)}, f32[288,1536]{1,0:T(8,128)S(1)}, u32[]{:S(2)}, u32[]{:S(2)}) collective-permute-start(f32[288,1536]{1,0:T(8,128)} %get-tuple-element.308), channel_id=1, source_target_pairs={{0,1},{1,0},{2,3},{3,2},{4,5},{5,4},{6,7},{7,6},{8,9},{9,8},{10,11... | collective-permute-start | bytes 5308424 | tf_op jit(solution)/shard_map/ppermute | solution.py:1027
  152.2 23.7 %collective-permute-start.4 = (f32[144,1024]{1,0:T(8,128)}, f32[144,1024]{1,0:T(8,128)S(1)}, u32[]{:S(2)}, u32[]{:S(2)}) collective-permute-start(f32[144,1024]{1,0:T(8,128)} %add.272), channel_id=1, source_target_pairs={{0,2},{1,3},{2,0},{3,1},{4,6},{5,7},{6,4},{7,5},{8,10},{9,11},{10,... | collective-permute-start | bytes 1769480 | tf_op jit(solution)/shard_map/ppermute | solution.py:1027
  175.9 13.2 %copy-start.12 = (f32[144,1024]{1,0:T(8,128)}, f32[144,1024]{1,0:T(8,128)S(1)}, u32[]{:S(2)}) copy-start(f32[144,1024]{1,0:T(8,128)S(1)} %collective-permute-done.4.refs_2_) | copy-start | bytes 1769476
  180.7 8.4 %copy-start.2 = (f32[288,1536]{1,0:T(8,128)}, f32[288,1536]{1,0:T(8,128)S(1)}, u32[]{:S(2)}) copy-start(f32[288,1536]{1,0:T(8,128)S(1)} %collective-permute-done.5.refs_4_.refs_5_.refs_1_.refs_6_) | copy-start | bytes 5308420
  191.9 41.9 %collective-permute-start.6 = (f32[2304,1152]{1,0:T(8,128)}, f32[2304,1152]{1,0:T(8,128)}, u32[]{:S(2)}, u32[]{:S(2)}) collective-permute-start(f32[2304,1152]{1,0:T(8,128)} %bitcast.44), channel_id=1, source_target_pairs={{0,16},{16,0},{1,17},{17,1},{2,18},{18,2},{3,19},{19,3},{4,20},{20... | collective-permute-start | bytes 31850504 | tf_op jit(solution)/shard_map/ppermute | solution.py:1029
  192.0 41.8 %collective-permute-start.9 = (f32[288,2048]{1,0:T(8,128)}, f32[288,2048]{1,0:T(8,128)}, u32[]{:S(2)}, u32[]{:S(2)}) collective-permute-start(f32[288,2048]{1,0:T(8,128)} %get-tuple-element.335), channel_id=1, source_target_pairs={{0,1},{1,0},{2,3},{3,2},{4,5},{5,4},{6,7},{7,6},{8,9},{9,8},{10,11... | collective-permute-start | bytes 7077896 | tf_op jit(solution)/shard_map/ppermute | solution.py:1027
  192.5 41.3 %collective-permute-start.8 = (f32[144,1536]{1,0:T(8,128)}, f32[144,1536]{1,0:T(8,128)S(1)}, u32[]{:S(2)}, u32[]{:S(2)}) collective-permute-start(f32[144,1536]{1,0:T(8,128)} %get-tuple-element.334), channel_id=1, source_target_pairs={{0,2},{1,3},{2,0},{3,1},{4,6},{5,7},{6,4},{7,5},{8,10},{9,11},{10,... | collective-permute-start | bytes 2654216 | tf_op jit(solution)/shard_map/ppermute | solution.py:1027
  193.9 39.8 %collective-permute-start.7 = (f32[72,1024]{1,0:T(8,128)}, f32[72,1024]{1,0:T(8,128)S(1)}, u32[]{:S(2)}, u32[]{:S(2)}) collective-permute-start(f32[72,1024]{1,0:T(8,128)} %get-tuple-element.333), channel_id=1, source_target_pairs={{0,4},{1,5},{2,6},{3,7},{4,0},{5,1},{6,2},{7,3},{8,12},{9,13},{10,... | collective-permute-start | bytes 884744 | tf_op jit(solution)/shard_map/ppermute | solution.py:1027
  233.7 17.1 %copy-start.18 = (f32[72,1024]{1,0:T(8,128)}, f32[72,1024]{1,0:T(8,128)S(1)}, u32[]{:S(2)}) copy-start(f32[72,1024]{1,0:T(8,128)S(1)} %collective-permute-done.7.refs_3_) | copy-start | bytes 884740
  233.8 17.1 %copy-start.10 = (f32[144,1536]{1,0:T(8,128)}, f32[144,1536]{1,0:T(8,128)S(1)}, u32[]{:S(2)}) copy-start(f32[144,1536]{1,0:T(8,128)S(1)} %collective-permute-done.8.refs_6_.refs_2_.refs_7_) | copy-start | bytes 2654212
  250.9 7.6 %copy-start.31 = (f32[1152]{0:T(1024)S(1)}, f32[1152]{0:T(1024)}, u32[]{:S(2)}) copy-start(f32[1152]{0:T(1024)} %param.36) | copy-start | bytes 13828
  254.6 54.6 %collective-permute-start.13 = (f32[1152,768]{1,0:T(8,128)}, f32[1152,768]{1,0:T(8,128)}, u32[]{:S(2)}, u32[]{:S(2)}) collective-permute-start(f32[1152,768]{1,0:T(8,128)} %bitcast.49), channel_id=1, source_target_pairs={{0,1},{1,0},{2,3},{3,2},{4,5},{5,4},{6,7},{7,6},{8,9},{9,8},{10,11... | collective-permute-start | bytes 10616840 | tf_op jit(solution)/shard_map/ppermute | solution.py:1027
  256.2 53.0 %collective-permute-start.14 = (f32[1152,384]{1,0:T(8,128)}, f32[1152,384]{1,0:T(8,128)S(1)}, u32[]{:S(2)}, u32[]{:S(2)}) collective-permute-start(f32[1152,384]{1,0:T(8,128)} %bitcast.11), channel_id=1, source_target_pairs={{0,4},{1,5},{2,6},{3,7},{4,0},{5,1},{6,2},{7,3},{8,12},{9,13},{10,... | collective-permute-start | bytes 5308424 | tf_op jit(solution)/shard_map/ppermute | solution.py:1027
  256.2 53.0 %collective-permute-start.12 = (f32[144,2048]{1,0:T(8,128)}, f32[144,2048]{1,0:T(8,128)S(1)}, u32[]{:S(2)}, u32[]{:S(2)}) collective-permute-start(f32[144,2048]{1,0:T(8,128)} %get-tuple-element.365), channel_id=1, source_target_pairs={{0,2},{1,3},{2,0},{3,1},{4,6},{5,7},{6,4},{7,5},{8,10},{9,11},{10,... | collective-permute-start | bytes 3538952 | tf_op jit(solution)/shard_map/ppermute | solution.py:1027
  257.1 52.0 %collective-permute-start.11 = (f32[72,1536]{1,0:T(8,128)}, f32[72,1536]{1,0:T(8,128)S(1)}, u32[]{:S(2)}, u32[]{:S(2)}) collective-permute-start(f32[72,1536]{1,0:T(8,128)} %get-tuple-element.364), channel_id=1, source_target_pairs={{0,4},{1,5},{2,6},{3,7},{4,0},{5,1},{6,2},{7,3},{8,12},{9,13},{10,... | collective-permute-start | bytes 1327112 | tf_op jit(solution)/shard_map/ppermute | solution.py:1027
  259.1 48.0 %collective-permute-start.10 = (f32[36,1024]{1,0:T(8,128)}, f32[36,1024]{1,0:T(8,128)S(1)}, u32[]{:S(2)}, u32[]{:S(2)}) collective-permute-start(f32[36,1024]{1,0:T(8,128)} %get-tuple-element.363), channel_id=1, source_target_pairs={{0,8},{1,9},{2,10},{3,11},{4,12},{5,13},{6,14},{7,15},{8,0},{9,1},... | collective-permute-start | bytes 442376 | tf_op jit(solution)/shard_map/ppermute | solution.py:1027
  307.1 9.2 %copy-start.27 = (f32[36,1024]{1,0:T(8,128)}, f32[36,1024]{1,0:T(8,128)S(1)}, u32[]{:S(2)}) copy-start(f32[36,1024]{1,0:T(8,128)S(1)} %collective-permute-done.10.refs_4_) | copy-start | bytes 442372
  316.3 32.3 %collective-permute-start.15 = (f32[576,2304]{1,0:T(8,128)}, f32[576,2304]{1,0:T(8,128)}, u32[]{:S(2)}, u32[]{:S(2)}) collective-permute-start(f32[576,2304]{1,0:T(8,128)} %get-tuple-element.387), channel_id=1, source_target_pairs={{0,16},{16,0},{1,17},{17,1},{2,18},{18,2},{3,19},{19,3},{4,20},{20... | collective-permute-start | bytes 15925256 | tf_op jit(solution)/shard_map/ppermute | solution.py:1029
  316.3 32.3 %collective-permute-start.18 = (f32[576,768]{1,0:T(8,128)}, f32[576,768]{1,0:T(8,128)S(1)}, u32[]{:S(2)}, u32[]{:S(2)}) collective-permute-start(f32[576,768]{1,0:T(8,128)} %get-tuple-element.390), channel_id=1, source_target_pairs={{0,2},{1,3},{2,0},{3,1},{4,6},{5,7},{6,4},{7,5},{8,10},{9,11},{10,... | collective-permute-start | bytes 5308424 | tf_op jit(solution)/shard_map/ppermute | solution.py:1027
  317.0 29.3 %collective-permute-start.19 = (f32[576,384]{1,0:T(8,128)}, f32[576,384]{1,0:T(8,128)S(1)}, u32[]{:S(2)}, u32[]{:S(2)}) collective-permute-start(f32[576,384]{1,0:T(8,128)} %get-tuple-element.391), channel_id=1, source_target_pairs={{0,1},{1,0},{2,3},{3,2},{4,5},{5,4},{6,7},{7,6},{8,9},{9,8},{10,11... | collective-permute-start | bytes 2654216 | tf_op jit(solution)/shard_map/ppermute | solution.py:1027
  322.1 24.1 %collective-permute-start.17 = (f32[72,2048]{1,0:T(8,128)}, f32[72,2048]{1,0:T(8,128)}, u32[]{:S(2)}, u32[]{:S(2)}) collective-permute-start(f32[72,2048]{1,0:T(8,128)} %get-tuple-element.389), channel_id=1, source_target_pairs={{0,4},{1,5},{2,6},{3,7},{4,0},{5,1},{6,2},{7,3},{8,12},{9,13},{10,... | collective-permute-start | bytes 1769480 | tf_op jit(solution)/shard_map/ppermute | solution.py:1027
  324.1 22.2 %collective-permute-start.16 = (f32[36,1536]{1,0:T(8,128)}, f32[36,1536]{1,0:T(8,128)S(1)}, u32[]{:S(2)}, u32[]{:S(2)}) collective-permute-start(f32[36,1536]{1,0:T(8,128)} %get-tuple-element.388), channel_id=1, source_target_pairs={{0,8},{1,9},{2,10},{3,11},{4,12},{5,13},{6,14},{7,15},{8,0},{9,1},... | collective-permute-start | bytes 663560 | tf_op jit(solution)/shard_map/ppermute | solution.py:1027
  346.2 13.3 %copy-start.24 = (f32[36,1536]{1,0:T(8,128)}, f32[36,1536]{1,0:T(8,128)S(1)}, u32[]{:S(2)}) copy-start(f32[36,1536]{1,0:T(8,128)S(1)} %collective-permute-done.16.refs_9_) | copy-start | bytes 663556
  346.3 13.3 %copy-start.11 = (f32[576,384]{1,0:T(8,128)}, f32[576,384]{1,0:T(8,128)S(1)}, u32[]{:S(2)}) copy-start(f32[576,384]{1,0:T(8,128)S(1)} %collective-permute-done.19.refs_9_.refs_6_.refs_22_) | copy-start | bytes 2654212
  348.6 11.0 %copy-start.6 = (f32[576,768]{1,0:T(8,128)}, f32[576,768]{1,0:T(8,128)S(1)}, u32[]{:S(2)}) copy-start(f32[576,768]{1,0:T(8,128)S(1)} %collective-permute-done.18.refs_6_.refs_2_.refs_17_) | copy-start | bytes 5308420
  363.7 43.5 %collective-permute-start.20 = (f32[576,2304]{1,0:T(8,128)}, f32[576,2304]{1,0:T(8,128)}, u32[]{:S(2)}, u32[]{:S(2)}) collective-permute-start(f32[576,2304]{1,0:T(8,128)} %get-tuple-element.407), channel_id=1, source_target_pairs={{0,16},{16,0},{1,17},{17,1},{2,18},{18,2},{3,19},{19,3},{4,20},{20... | collective-permute-start | bytes 15925256 | tf_op jit(solution)/shard_map/ppermute | solution.py:1029
  366.9 40.3 %collective-permute-start.24 = (f32[288,2304]{1,0:T(8,128)}, f32[288,2304]{1,0:T(8,128)}, u32[]{:S(2)}, u32[]{:S(2)}) collective-permute-start(f32[288,2304]{1,0:T(8,128)} %get-tuple-element.411), channel_id=1, source_target_pairs={{0,1},{1,0},{2,3},{3,2},{4,5},{5,4},{6,7},{7,6},{8,9},{9,8},{10,11... | collective-permute-start | bytes 7962632 | tf_op jit(solution)/shard_map/ppermute | solution.py:1027
  372.1 27.5 %collective-permute-start.22 = (f32[288,768]{1,0:T(8,128)}, f32[288,768]{1,0:T(8,128)S(1)}, u32[]{:S(2)}, u32[]{:S(2)}) collective-permute-start(f32[288,768]{1,0:T(8,128)} %get-tuple-element.409), channel_id=1, source_target_pairs={{0,4},{1,5},{2,6},{3,7},{4,0},{5,1},{6,2},{7,3},{8,12},{9,13},{10,... | collective-permute-start | bytes 2654216 | tf_op jit(solution)/shard_map/ppermute | solution.py:1027
  372.2 26.9 %collective-permute-start.23 = (f32[288,384]{1,0:T(8,128)}, f32[288,384]{1,0:T(8,128)S(1)}, u32[]{:S(2)}, u32[]{:S(2)}) collective-permute-start(f32[288,384]{1,0:T(8,128)} %get-tuple-element.410), channel_id=1, source_target_pairs={{0,2},{1,3},{2,0},{3,1},{4,6},{5,7},{6,4},{7,5},{8,10},{9,11},{10,... | collective-permute-start | bytes 1327112 | tf_op jit(solution)/shard_map/ppermute | solution.py:1027
  374.2 24.8 %collective-permute-start.21 = (f32[36,2048]{1,0:T(8,128)}, f32[36,2048]{1,0:T(8,128)S(1)}, u32[]{:S(2)}, u32[]{:S(2)}) collective-permute-start(f32[36,2048]{1,0:T(8,128)} %get-tuple-element.408), channel_id=1, source_target_pairs={{0,8},{1,9},{2,10},{3,11},{4,12},{5,13},{6,14},{7,15},{8,0},{9,1},... | collective-permute-start | bytes 884744 | tf_op jit(solution)/shard_map/ppermute | solution.py:1027
  399.0 17.7 %copy-start.23 = (f32[36,2048]{1,0:T(8,128)}, f32[36,2048]{1,0:T(8,128)S(1)}, u32[]{:S(2)}) copy-start(f32[36,2048]{1,0:T(8,128)S(1)} %collective-permute-done.21.refs_14_) | copy-start | bytes 884740
  399.0 17.7 %copy-start.17 = (f32[288,384]{1,0:T(8,128)}, f32[288,384]{1,0:T(8,128)S(1)}, u32[]{:S(2)}) copy-start(f32[288,384]{1,0:T(8,128)S(1)} %collective-permute-done.23.refs_7_.refs_23_) | copy-start | bytes 1327108
  399.7 17.1 %copy-start.13 = (f32[288,768]{1,0:T(8,128)}, f32[288,768]{1,0:T(8,128)S(1)}, u32[]{:S(2)}) copy-start(f32[288,768]{1,0:T(8,128)S(1)} %collective-permute-done.22.refs_3_.refs_18_) | copy-start | bytes 2654212
  416.7 8.9 %copy-start.19 = (f32[4,10368]{1,0:T(4,128)S(1)}, f32[4,10368]{1,0:T(4,128)}, u32[]{:S(2)}) copy-start(f32[4,10368]{1,0:T(4,128)} %payload.1) | copy-start | bytes 497668
  420.7 45.5 %collective-permute-start.28 = (f32[288,2304]{1,0:T(8,128)}, f32[288,2304]{1,0:T(8,128)}, u32[]{:S(2)}, u32[]{:S(2)}) collective-permute-start(f32[288,2304]{1,0:T(8,128)} %get-tuple-element.436), channel_id=1, source_target_pairs={{0,1},{1,0},{2,3},{3,2},{4,5},{5,4},{6,7},{7,6},{8,9},{9,8},{10,11... | collective-permute-start | bytes 7962632 | tf_op jit(solution)/shard_map/ppermute | solution.py:1027
  422.7 38.7 %collective-permute-start.27 = (f32[144,2304]{1,0:T(8,128)}, f32[144,2304]{1,0:T(8,128)S(1)}, u32[]{:S(2)}, u32[]{:S(2)}) collective-permute-start(f32[144,2304]{1,0:T(8,128)} %get-tuple-element.435), channel_id=1, source_target_pairs={{0,2},{1,3},{2,0},{3,1},{4,6},{5,7},{6,4},{7,5},{8,10},{9,11},{10,... | collective-permute-start | bytes 3981320 | tf_op jit(solution)/shard_map/ppermute | solution.py:1027
  422.7 38.6 %collective-permute-start.25 = (f32[144,768]{1,0:T(8,128)}, f32[144,768]{1,0:T(8,128)S(1)}, u32[]{:S(2)}, u32[]{:S(2)}) collective-permute-start(f32[144,768]{1,0:T(8,128)} %get-tuple-element.433), channel_id=1, source_target_pairs={{0,8},{1,9},{2,10},{3,11},{4,12},{5,13},{6,14},{7,15},{8,0},{9,1},... | collective-permute-start | bytes 1327112 | tf_op jit(solution)/shard_map/ppermute | solution.py:1027
  424.3 37.0 %collective-permute-start.26 = (f32[144,384]{1,0:T(8,128)}, f32[144,384]{1,0:T(8,128)S(1)}, u32[]{:S(2)}, u32[]{:S(2)}) collective-permute-start(f32[144,384]{1,0:T(8,128)} %get-tuple-element.434), channel_id=1, source_target_pairs={{0,8},{1,9},{2,10},{3,11},{4,12},{5,13},{6,14},{7,15},{8,0},{9,1},... | collective-permute-start | bytes 663560 | tf_op jit(solution)/shard_map/ppermute | solution.py:1027
  425.6 35.7 %collective-permute-start.29 = (f32[4,10368]{1,0:T(4,128)S(1)}, f32[4,10368]{1,0:T(4,128)S(1)}, u32[]{:S(2)}, u32[]{:S(2)}) collective-permute-start(f32[4,10368]{1,0:T(4,128)S(1)} %copy-done.19), channel_id=1, source_target_pairs={{0,8},{1,9},{2,10},{3,11},{4,12},{5,13},{6,14},{7,15},{8,0},{9,1},... | collective-permute-start | bytes 497672 | tf_op jit(solution)/shard_map/ppermute | solution.py:1034
  461.3 8.6 %copy-start.25 = (f32[144,384]{1,0:T(8,128)}, f32[144,384]{1,0:T(8,128)S(1)}, u32[]{:S(2)}) copy-start(f32[144,384]{1,0:T(8,128)S(1)} %collective-permute-done.26.refs_24_) | copy-start | bytes 663556
  461.3 8.6 %copy-start.20 = (f32[144,768]{1,0:T(8,128)}, f32[144,768]{1,0:T(8,128)S(1)}, u32[]{:S(2)}) copy-start(f32[144,768]{1,0:T(8,128)S(1)} %collective-permute-done.25.refs_19_) | copy-start | bytes 1327108
  470.0 26.5 %collective-permute-start.31 = (f32[144,2304]{1,0:T(8,128)}, f32[144,2304]{1,0:T(8,128)S(1)}, u32[]{:S(2)}, u32[]{:S(2)}) collective-permute-start(f32[144,2304]{1,0:T(8,128)} %get-tuple-element.454), channel_id=1, source_target_pairs={{0,2},{1,3},{2,0},{3,1},{4,6},{5,7},{6,4},{7,5},{8,10},{9,11},{10,... | collective-permute-start | bytes 3981320 | tf_op jit(solution)/shard_map/ppermute | solution.py:1027
  470.7 25.8 %collective-permute-start.30 = (f32[72,2304]{1,0:T(8,128)}, f32[72,2304]{1,0:T(8,128)S(1)}, u32[]{:S(2)}, u32[]{:S(2)}) collective-permute-start(f32[72,2304]{1,0:T(8,128)} %get-tuple-element.453), channel_id=1, source_target_pairs={{0,4},{1,5},{2,6},{3,7},{4,0},{5,1},{6,2},{7,3},{8,12},{9,13},{10,... | collective-permute-start | bytes 1990664 | tf_op jit(solution)/shard_map/ppermute | solution.py:1027
  474.6 21.8 %collective-permute-start.32 = (f32[8,10368]{1,0:T(8,128)S(1)}, f32[8,10368]{1,0:T(8,128)S(1)}, u32[]{:S(2)}, u32[]{:S(2)}) collective-permute-start(f32[8,10368]{1,0:T(8,128)S(1)} %pad_maximum_fusion.2), channel_id=1, source_target_pairs={{0,4},{1,5},{2,6},{3,7},{4,0},{5,1},{6,2},{7,3},{8,12},{9,13},{10,... | collective-permute-start | bytes 995336 | tf_op jit(solution)/shard_map/ppermute | solution.py:1034
  501.1 24.6 %collective-permute-start.34 = (f32[72,2304]{1,0:T(8,128)}, f32[72,2304]{1,0:T(8,128)S(1)}, u32[]{:S(2)}, u32[]{:S(2)}) collective-permute-start(f32[72,2304]{1,0:T(8,128)} %get-tuple-element.467), channel_id=1, source_target_pairs={{0,4},{1,5},{2,6},{3,7},{4,0},{5,1},{6,2},{7,3},{8,12},{9,13},{10,... | collective-permute-start | bytes 1990664 | tf_op jit(solution)/shard_map/ppermute | solution.py:1027
  501.4 24.2 %collective-permute-start.35 = (f32[16,10368]{1,0:T(8,128)S(1)}, f32[16,10368]{1,0:T(8,128)S(1)}, u32[]{:S(2)}, u32[]{:S(2)}) collective-permute-start(f32[16,10368]{1,0:T(8,128)S(1)} %pad_maximum_fusion.1), channel_id=1, source_target_pairs={{0,2},{1,3},{2,0},{3,1},{4,6},{5,7},{6,4},{7,5},{8,10},{9,11},{10,... | collective-permute-start | bytes 1990664 | tf_op jit(solution)/shard_map/ppermute | solution.py:1034
  503.2 20.4 %collective-permute-start.33 = (f32[36,2304]{1,0:T(8,128)}, f32[36,2304]{1,0:T(8,128)S(1)}, u32[]{:S(2)}, u32[]{:S(2)}) collective-permute-start(f32[36,2304]{1,0:T(8,128)} %get-tuple-element.466), channel_id=1, source_target_pairs={{0,8},{1,9},{2,10},{3,11},{4,12},{5,13},{6,14},{7,15},{8,0},{9,1},... | collective-permute-start | bytes 995336 | tf_op jit(solution)/shard_map/ppermute | solution.py:1027
  523.6 5.9 %copy-start.21 = (f32[36,2304]{1,0:T(8,128)}, f32[36,2304]{1,0:T(8,128)S(1)}, u32[]{:S(2)}) copy-start(f32[36,2304]{1,0:T(8,128)S(1)} %collective-permute-done.33.refs_4_) | copy-start | bytes 995332
  526.5 21.3 %copy-start.4 = (f32[32,10368]{1,0:T(8,128)}, f32[32,10368]{1,0:T(8,128)S(1)}, u32[]{:S(2)}) copy-start(f32[32,10368]{1,0:T(8,128)S(1)} %pad_maximum_fusion.refs_0_.refs_4_.refs_8_) | copy-start | bytes 3981316
  529.5 18.3 %collective-permute-start.37 = (f32[32,10368]{1,0:T(8,128)S(1)}, f32[32,10368]{1,0:T(8,128)}, u32[]{:S(2)}, u32[]{:S(2)}) collective-permute-start(f32[32,10368]{1,0:T(8,128)S(1)} %pad_maximum_fusion.refs_0_.refs_4_.refs_8_), channel_id=1, source_target_pairs={{0,1},{1,0},{2,3},{3,2},{4,5},{5,4},{6,7},{7,6},{8,9},{9,8},{10,11... | collective-permute-start | bytes 3981320 | tf_op jit(solution)/shard_map/ppermute | solution.py:1034
  529.5 18.3 %collective-permute-start.36 = (f32[36,2304]{1,0:T(8,128)}, f32[36,2304]{1,0:T(8,128)S(1)}, u32[]{:S(2)}, u32[]{:S(2)}) collective-permute-start(f32[36,2304]{1,0:T(8,128)} %add.280), channel_id=1, source_target_pairs={{0,8},{1,9},{2,10},{3,11},{4,12},{5,13},{6,14},{7,15},{8,0},{9,1},... | collective-permute-start | bytes 995336 | tf_op jit(solution)/shard_map/ppermute | solution.py:1027
  547.8 5.0 collective-permute-start.38
  547.9 5.3 collective-permute-start.39
  553.2 20.6 %copy-start.1 = (bf16[1001,1152]{1,0:T(8,128)(2,1)S(1)}, bf16[1001,1152]{1,0:T(8,128)(2,1)}, u32[]{:S(2)}) copy-start(bf16[1001,1152]{1,0:T(8,128)(2,1)} %param.26) | copy-start | bytes 6918916
  (12 other events, 20.7 us)
